TPU v7x, 32 devices: a whole 2x2x4 slice. The times are simulated.
32 devices in a mesh: col: 4 (over z), hgt: 8 (over y, x, core).
Axes of the slice: x: 2, y: 2, z: 4, core: 2. Of those that a mesh axis runs over, the one named last changes fastest.
Arguments:
- efield_lattice_vector: float32 [3, 64, 192, 1024], P(None, 'col', 'hgt'), may hold values from -6 to 6
- hfield_lattice_vector: float32 [3, 64, 192, 1024], P(None, 'col', 'hgt'), may hold values from -6 to 6
- cell_temp: float32 [64, 192, 1024], P('col', 'hgt'), may hold values from -3 to 1
- region_tags: int32 [64, 192, 1024], P('col', 'hgt'), may hold values from 0 to 2
- block_owner: int32 [4, 8, 16, 24, 8, 1], P('col', 'hgt'), may hold values from 0 to 31; in each aligned block of 3072 rows (0 to 3071, 3072 to 6143, ..., all dimensions but the last counted through in order) at most 192 rows name the same one
- block_node: int32 [4, 8, 16, 24, 8], P('col', 'hgt'), may hold values from 0 to 383
- node_enthalpy: float32 [12288, 128], P(('col', 'hgt')), may hold values from -1.5 to 2.5
Outputs:
- e_out: float32 [3, 64, 192, 1024], P(None, 'col', 'hgt')
- h_out: float32 [3, 64, 192, 1024], P(None, 'col', 'hgt')
- node_temp: float32 [12288, 128], P(('col', 'hgt'))
Inputs may be any that keep to these rules, and one draw needn't show every extreme that they name: `block_owner`: among the margin blocks of one device, no partition is named by more than 192 blocks, a bound that the blocks of some device reach.
All inputs are finite; a program needn't handle non-finite values.
Results may differ from a plain program's by a relative error of at most 0.0003.
Values sent between devices are 32-bit elements; how exact they have to be, the bound alone decides.
No kernel may reach another device: no remote copies, remote signals or barrier semaphores. Data moves between devices by JAX's collectives and lax.ppermute only.
A program may use at most 320 MiB of HBM per device.

v0:
```python
import jax
import jax.numpy as jnp
from jax import lax
from jax.sharding import PartitionSpec as P

PTS = 128
STEPS = 4


def from_behind(block, axis, distance):
    devices = range(lax.axis_size(axis))
    route = [(i - distance, i) for i in devices if i - distance in devices]
    return lax.ppermute(block, axis, route)


def coefficients(cell_temp, region_tags):
    frac = jax.nn.sigmoid(2.0 * cell_temp)
    lean = region_tags == 0
    fat = region_tags == 1
    eps_frozen = jnp.where(lean, 4.0, jnp.where(fat, 2.5, 5.0))
    eps_thawed = jnp.where(lean, 50.0, jnp.where(fat, 6.0, 10.0))
    sig_frozen = jnp.where(lean, 0.2, jnp.where(fat, 0.05, 0.1))
    melted_conductance = jnp.where(lean, 8.0, jnp.where(fat, 0.4, 1.0))
    eps = eps_frozen + (eps_thawed - eps_frozen) * frac
    sigma = sig_frozen + (melted_conductance - sig_frozen) * frac
    loss = sigma * 0.55 / (2.0 * eps)
    ca = (1.0 - loss) / (1.0 + loss)
    cb = 0.55 / (eps * (1.0 + loss))
    return (sigma, ca, cb)


def forward(field, plane, axis):
    size = field.shape[axis]
    return jnp.concatenate([lax.slice_in_dim(field, 1, size, axis=axis), plane], axis) - field


def backward(field, plane, axis):
    size = field.shape[axis]
    return field - jnp.concatenate([plane, lax.slice_in_dim(field, 0, size - 1, axis=axis)], axis)


def curl(diff, comps, planes_x, planes_z, plane_y):
    fx, fy, fz = comps
    dx_y = diff(fy, planes_x[0], 0)
    dx_z = diff(fz, planes_x[1], 0)
    dz_x = diff(fx, planes_z[0], 1)
    dz_y = diff(fy, planes_z[1], 1)
    dy_x = diff(fx, plane_y, 2)
    dy_z = diff(fz, plane_y, 2)
    return jnp.stack([dy_z - dz_y, dz_x - dx_z, dx_y - dy_x])


def tissue_warmth_kelvin(heat_content_per_mass):
    return jnp.where(
        heat_content_per_mass < 0.0,
        heat_content_per_mass / 2.0,
        jnp.where(heat_content_per_mass > 1.0, (heat_content_per_mass - 1.0) / 3.0, 0.0),
    )


def per_device(
    efield_lattice_vector,
    hfield_lattice_vector,
    cell_temp,
    region_tags,
    block_owner,
    block_node,
    node_enthalpy,
):
    size_x, size_z, size_y = cell_temp.shape
    n_col = lax.axis_size("col")
    n_hgt = lax.axis_size("hgt")
    sigma, ca, cb = coefficients(cell_temp, region_tags)
    empty_height_plane = jnp.zeros((size_x, size_z, 1), jnp.float32)
    power = jnp.zeros(cell_temp.shape, jnp.float32)
    for step in range(STEPS):
        next_x = from_behind(efield_lattice_vector[1:3, :1], "col", -1)
        next_z = from_behind(efield_lattice_vector[0:2, :, :1], "hgt", -1)
        hfield_lattice_vector = hfield_lattice_vector - 0.55 * curl(
            forward,
            (efield_lattice_vector[0], efield_lattice_vector[1], efield_lattice_vector[2]),
            next_x,
            next_z,
            empty_height_plane,
        )
        prev_x = from_behind(hfield_lattice_vector[1:3, size_x - 1 :], "col", 1)
        previous_depth = from_behind(hfield_lattice_vector[0:2, :, size_z - 1 :], "hgt", 1)
        efield_lattice_vector = ca * efield_lattice_vector + cb * curl(
            backward,
            (hfield_lattice_vector[0], hfield_lattice_vector[1], hfield_lattice_vector[2]),
            prev_x,
            previous_depth,
            empty_height_plane,
        )
        power = power + sigma * (
            efield_lattice_vector[0] * efield_lattice_vector[0]
            + efield_lattice_vector[1] * efield_lattice_vector[1]
            + efield_lattice_vector[2] * efield_lattice_vector[2]
        )
    absorbed = power / STEPS
    blocks = absorbed.reshape(-1, PTS)
    count_blocks = blocks.shape[0]
    n_dev = n_col * n_hgt
    capacity = 2 * count_blocks // n_dev
    owners = block_owner.reshape(-1)
    nodes = block_node.reshape(-1).astype(jnp.float32)
    onehot = (owners[:, None] == jnp.arange(n_dev, dtype=jnp.int32)[None, :]).astype(jnp.int32)
    ranks = jnp.sum((jnp.cumsum(onehot, axis=0) - 1) * onehot, axis=1)
    where_to = owners * capacity + ranks
    send_vals = jnp.zeros((n_dev * capacity, PTS), jnp.float32).at[where_to].set(blocks)
    send_nodes = jnp.full((n_dev * capacity,), -1.0, jnp.float32).at[where_to].set(nodes)
    recv_vals, recv_nodes = (
        lax.all_to_all(send_vals, ("col", "hgt"), split_axis=0, concat_axis=0, tiled=True),
        lax.all_to_all(send_nodes, ("col", "hgt"), split_axis=0, concat_axis=0, tiled=True),
    )
    node_count = node_enthalpy.shape[0]
    choose_entries = (
        recv_nodes[:, None] == jnp.arange(node_count, dtype=jnp.float32)[None, :]
    ).astype(jnp.float32)
    heat = lax.dot_general(
        choose_entries,
        recv_vals,
        (((0,), (0,)), ((), ())),
        precision=lax.Precision.HIGHEST,
        preferred_element_type=jnp.float32,
    )
    heat_content_per_mass = node_enthalpy + 0.25 * heat
    return (
        efield_lattice_vector,
        hfield_lattice_vector,
        tissue_warmth_kelvin(heat_content_per_mass),
    )


def solution(mesh):
    placed = (
        P(None, "col", "hgt", None),
        P(None, "col", "hgt", None),
        P("col", "hgt", None),
        P("col", "hgt", None),
        P("col", "hgt", None, None, None, None),
        P("col", "hgt", None, None, None),
        P(("col", "hgt"), None),
    )
    return jax.shard_map(
        per_device,
        mesh=mesh,
        in_specs=placed,
        out_specs=(
            P(None, "col", "hgt", None),
            P(None, "col", "hgt", None),
            P(("col", "hgt"), None),
        ),
        check_vma=False,
    )
```

profile of v0, /device:TPU:0, one launch (start us, length us, event | category | flops | bytes accessed | tf_op | source)
XLA Modules:
  0.0 328.6 jit_solution(17052442611431933048)
XLA Ops:
  7.9 9.2 %reduce-window.6 = s32[32,24,128]{2,1,0:T(8,128)S(1)} reduce-window(s32[32,24,128]{2,1,0:T(8,128)S(1)} %fusion.62, s32[]{:T(128)} %constant.25.clone.1), window={size=1x1x128 pad=0_0x0_0x127_0}, to_apply=%region_0.1 | reduce-window | flops 12484608 | bytes 786436 | tf_op jit(solution)/shard_map/reduce-window
  18.3 11.8 %scatter_custom_fusion = f32[6144]{0:T(1024)S(1)} fusion(s32[3072]{0:T(1024)S(1)} %bitcast.302, f32[3072]{0:T(1024)S(1)} %reshape.150, f32[]{:T(128)} %constant.15.clone.1), kind=kCustom, calls=%fused_computation.180 | custom fusion | bytes 24580 | tf_op jit(solution)/shard_map/scatter | solution.py:111
  30.8 9.3 %all-to-all-start = ((f32[32,192,1]{1,2,0:T(1,128)}), f32[32,192,1]{1,2,0:T(1,128)}, u32[]{:S(2)}, u32[]{:S(2)}) async-start(f32[32,192,1]{1,2,0:T(1,128)} %all_to_all.19), calls=%async_computation | async-start | bytes 65536 | tf_op jit(solution)/shard_map/all_to_all | solution.py:114
  65.7 5.0 %fusion.22 = (f32[1,16,24,1024]{3,2,1,0:T(8,128)}, f32[1,16,24,1024]{3,2,1,0:T(8,128)}) fusion(f32[16,23,1024]{2,1,0:T(8,128)S(1)} %bitcast.290, f32[16,1,1024]{2,1,0:T(1,128)S(1)} %get-tuple-element.90, f32[16,24,1023]{2,1,0:T(8,128)S(1)} %bitcast.289, f32[3,16,24,1024]{3,2,1,0:T(8,128)S(1)} %fusion.1, f32[16,24,1023]{2,1,0:T(8,128)S(1)} %bitcast.285, ...), kind=kLoop, calls=%fused_computation.56 | loop fusion | flops 3145728 | bytes 14152704 | tf_op jit(solution)/shard_map/stack | solution.py:50
  79.2 8.5 %collective-permute-done.5 = f32[2,1,24,1024]{3,2,1,0:T(8,128)S(1)} collective-permute-done((f32[2,1,24,1024]{3,2,1,0:T(8,128)S(1)}, f32[2,1,24,1024]{3,2,1,0:T(8,128)S(1)}, u32[]{:S(2)}, u32[]{:S(2)}) %collective-permute-start.5) | collective-permute-done | bytes 196640 | tf_op jit(solution)/shard_map/ppermute | solution.py:13
  94.9 4.1 %collective-permute-start.7 = (f32[2,1,24,1024]{3,2,1,0:T(8,128)S(1)}, f32[2,1,24,1024]{3,2,1,0:T(8,128)S(1)}, u32[]{:S(2)}, u32[]{:S(2)}) collective-permute-start(f32[2,1,24,1024]{3,2,1,0:T(8,128)S(1)} %slice.624), channel_id=1, source_target_pairs={{0,8},{8,16},{16,24},{1,9},{9,17},{17,25},{2,10},{10,18},{18,26},{... | collective-permute-start | bytes 589832 | tf_op jit(solution)/shard_map/ppermute | solution.py:13
  105.7 4.4 %fusion.32 = (f32[1,16,24,1024]{3,2,1,0:T(8,128)}, f32[1,16,24,1024]{3,2,1,0:T(8,128)}) fusion(f32[16,23,1024]{2,1,0:T(8,128)S(1)} %bitcast.292, f32[16,1,1024]{2,1,0:T(1,128)S(1)} %get-tuple-element.86, f32[16,24,1023]{2,1,0:T(8,128)S(1)} %bitcast.291, f32[3,16,24,1024]{3,2,1,0:T(8,128)S(1)} %fusion.3, f32[16,24,1023]{2,1,0:T(8,128)S(1)} %bitcast.286, ...), kind=kLoop, calls=%fused_computation.74 | loop fusion | flops 3145728 | bytes 14152704 | tf_op jit(solution)/shard_map/stack | solution.py:50
  110.1 5.6 %fusion.4 = f32[3,16,24,1024]{3,2,1,0:T(8,128)S(1)} fusion(f32[1,16,24,1024]{3,2,1,0:T(8,128)} %get-tuple-element.35, f32[1,16,24,1024]{3,2,1,0:T(8,128)} %get-tuple-element.37, f32[1,16,24,1024]{3,2,1,0:T(8,128)} %get-tuple-element.34, f32[16,24,1024]{2,1,0:T(8,128)} %multiply_divide_fusion, f32[16,24,1024]{2,1,0:T(8,128)} %get-tuple-element.3, ...), kind=kLoop, calls=%fused_computation.11 | loop fusion | flops 11796480 | bytes 22020096 | tf_op jit(solution)/shard_map/add | solution.py:88
  121.2 6.8 %collective-permute-done.9 = f32[2,1,24,1024]{3,2,1,0:T(8,128)S(1)} collective-permute-done((f32[2,1,24,1024]{3,2,1,0:T(8,128)S(1)}, f32[2,1,24,1024]{3,2,1,0:T(8,128)S(1)}, u32[]{:S(2)}, u32[]{:S(2)}) %collective-permute-start.9) | collective-permute-done | bytes 196640 | tf_op jit(solution)/shard_map/ppermute | solution.py:13
  130.8 4.6 %fusion.37 = (f32[1,16,24,1024]{3,2,1,0:T(8,128)}, f32[1,16,24,1024]{3,2,1,0:T(8,128)}) fusion(f32[16,1,1024]{2,1,0:T(1,128)S(1)} %get-tuple-element.84, f32[16,23,1024]{2,1,0:T(8,128)S(1)} %slice.633, f32[16,24,1023]{2,1,0:T(8,128)S(1)} %slice.631, f32[3,16,24,1024]{3,2,1,0:T(8,128)S(1)} %fusion.4, f32[16,24,1023]{2,1,0:T(8,128)S(1)} %slice.644, ...), kind=kLoop, calls=%fused_computation.83 | loop fusion | flops 3145728 | bytes 14152704 | tf_op jit(solution)/shard_map/stack | solution.py:50
  135.4 4.9 %fusion.5 = f32[3,16,24,1024]{3,2,1,0:T(8,128)S(1)} fusion(f32[1,16,24,1024]{3,2,1,0:T(8,128)} %get-tuple-element.28, f32[1,16,24,1024]{3,2,1,0:T(8,128)} %get-tuple-element.30, f32[1,16,24,1024]{3,2,1,0:T(8,128)} %get-tuple-element.27, f32[1,16,24,1024]{3,2,1,0:T(8,128)} %copy-done.14, f32[1,16,24,1024]{3,2,1,0:T(8,128)} %copy-done.12, ...), kind=kLoop, calls=%fused_computation.13 | loop fusion | flops 14155776 | bytes 23592960 | tf_op jit(solution)/shard_map/sub | solution.py:79
  140.7 4.5 %collective-permute-start.11 = (f32[2,1,24,1024]{3,2,1,0:T(8,128)S(1)}, f32[2,1,24,1024]{3,2,1,0:T(8,128)S(1)}, u32[]{:S(2)}, u32[]{:S(2)}) collective-permute-start(f32[2,1,24,1024]{3,2,1,0:T(8,128)S(1)} %slice.654), channel_id=1, source_target_pairs={{0,8},{8,16},{16,24},{1,9},{9,17},{17,25},{2,10},{10,18},{18,26},{... | collective-permute-start | bytes 589832 | tf_op jit(solution)/shard_map/ppermute | solution.py:13
  153.6 5.8 %fusion.42 = (f32[1,16,24,1024]{3,2,1,0:T(8,128)}, f32[1,16,24,1024]{3,2,1,0:T(8,128)}) fusion(f32[16,23,1024]{2,1,0:T(8,128)} %bitcast.294, f32[16,1,1024]{2,1,0:T(1,128)S(1)} %get-tuple-element.82, f32[16,24,1023]{2,1,0:T(8,128)} %bitcast.293, f32[3,16,24,1024]{3,2,1,0:T(8,128)S(1)} %fusion.5, f32[16,24,1023]{2,1,0:T(8,128)} %bitcast.287, ...), kind=kLoop, calls=%fused_computation.92 | loop fusion | flops 3145728 | bytes 14152704 | tf_op jit(solution)/shard_map/stack | solution.py:50
  159.4 6.2 %fusion.6 = f32[3,16,24,1024]{3,2,1,0:T(8,128)S(1)} fusion(f32[1,16,24,1024]{3,2,1,0:T(8,128)} %get-tuple-element.21, f32[1,16,24,1024]{3,2,1,0:T(8,128)} %get-tuple-element.23, f32[1,16,24,1024]{3,2,1,0:T(8,128)} %get-tuple-element.20, f32[16,24,1024]{2,1,0:T(8,128)} %multiply_divide_fusion, f32[16,24,1024]{2,1,0:T(8,128)} %get-tuple-element.3, ...), kind=kLoop, calls=%fused_computation.15 | loop fusion | flops 17694720 | bytes 26738688 | tf_op jit(solution)/shard_map/add | solution.py:88
  172.6 4.7 %collective-permute-done.13 = f32[2,1,24,1024]{3,2,1,0:T(8,128)S(1)} collective-permute-done((f32[2,1,24,1024]{3,2,1,0:T(8,128)S(1)}, f32[2,1,24,1024]{3,2,1,0:T(8,128)S(1)}, u32[]{:S(2)}, u32[]{:S(2)}) %collective-permute-start.13) | collective-permute-done | bytes 196640 | tf_op jit(solution)/shard_map/ppermute | solution.py:13
  180.2 4.5 %fusion.47 = (f32[1,16,24,1024]{3,2,1,0:T(8,128)}, f32[1,16,24,1024]{3,2,1,0:T(8,128)}) fusion(f32[16,1,1024]{2,1,0:T(1,128)S(1)} %get-tuple-element.80, f32[16,23,1024]{2,1,0:T(8,128)S(1)} %slice.663, f32[16,24,1023]{2,1,0:T(8,128)S(1)} %slice.661, f32[3,16,24,1024]{3,2,1,0:T(8,128)S(1)} %fusion.6, f32[16,24,1023]{2,1,0:T(8,128)S(1)} %slice.674, ...), kind=kLoop, calls=%fused_computation.101 | loop fusion | flops 3145728 | bytes 14152704 | tf_op jit(solution)/shard_map/stack | solution.py:50
  184.7 8.0 %fusion.7 = f32[3,16,24,1024]{3,2,1,0:T(8,128)S(1)} fusion(f32[1,16,24,1024]{3,2,1,0:T(8,128)} %get-tuple-element.14, f32[1,16,24,1024]{3,2,1,0:T(8,128)} %get-tuple-element.16, f32[1,16,24,1024]{3,2,1,0:T(8,128)} %get-tuple-element.13, f32[1,16,24,1024]{3,2,1,0:T(8,128)} %get-tuple-element.28, f32[1,16,24,1024]{3,2,1,0:T(8,128)} %get-tuple-element.30, ...), kind=kLoop, calls=%fused_computation.17 | loop fusion | flops 18874368 | bytes 28311552 | tf_op jit(solution)/shard_map/sub | solution.py:79
  193.0 4.8 %collective-permute-start.15 = (f32[2,1,24,1024]{3,2,1,0:T(8,128)S(1)}, f32[2,1,24,1024]{3,2,1,0:T(8,128)S(1)}, u32[]{:S(2)}, u32[]{:S(2)}) collective-permute-start(f32[2,1,24,1024]{3,2,1,0:T(8,128)S(1)} %slice.684), channel_id=1, source_target_pairs={{0,8},{8,16},{16,24},{1,9},{9,17},{17,25},{2,10},{10,18},{18,26},{... | collective-permute-start | bytes 589832 | tf_op jit(solution)/shard_map/ppermute | solution.py:13
  205.8 5.8 %fusion.52 = (f32[1,16,24,1024]{3,2,1,0:T(8,128)}, f32[1,16,24,1024]{3,2,1,0:T(8,128)}) fusion(f32[16,23,1024]{2,1,0:T(8,128)} %bitcast.296, f32[16,1,1024]{2,1,0:T(1,128)S(1)} %get-tuple-element.78, f32[16,24,1023]{2,1,0:T(8,128)} %bitcast.295, f32[3,16,24,1024]{3,2,1,0:T(8,128)S(1)} %fusion.7, f32[16,24,1023]{2,1,0:T(8,128)} %bitcast.288, ...), kind=kLoop, calls=%fused_computation.110 | loop fusion | flops 3145728 | bytes 14152704 | tf_op jit(solution)/shard_map/stack | solution.py:50
  211.6 8.9 %fusion.8 = f32[3,16,24,1024]{3,2,1,0:T(8,128)S(1)} fusion(f32[1,16,24,1024]{3,2,1,0:T(8,128)} %get-tuple-element.7, f32[1,16,24,1024]{3,2,1,0:T(8,128)} %get-tuple-element.9, f32[1,16,24,1024]{3,2,1,0:T(8,128)} %get-tuple-element.6, f32[16,24,1024]{2,1,0:T(8,128)} %multiply_divide_fusion, f32[16,24,1024]{2,1,0:T(8,128)} %get-tuple-element.3, ...), kind=kLoop, calls=%fused_computation.19 | loop fusion | flops 23592960 | bytes 31457280 | tf_op jit(solution)/shard_map/add | solution.py:88
  226.8 10.2 %scatter_custom_fusion.1 = f32[6144,128]{1,0:T(8,128)} fusion(s32[3072]{0:T(1024)} %bitcast.303, f32[3072,128]{1,0:T(8,128)} %reshape.158, f32[]{:T(128)} %constant.14.clone.1), kind=kCustom, calls=%fused_computation.117 | custom fusion | bytes 3146240 | tf_op jit(solution)/shard_map/scatter | solution.py:110
  237.0 10.9 %all-to-all-start.1 = ((f32[32,192,128]{2,1,0:T(8,128)}), f32[32,192,128]{2,1,0:T(8,128)S(1)}, u32[]{:S(2)}, u32[]{:S(2)}) async-start(f32[32,192,128]{2,1,0:T(8,128)} %bitcast.78), calls=%async_computation.1 | async-start | bytes 6291456 | tf_op jit(solution)/shard_map/all_to_all | solution.py:113
  248.8 70.5 %all-to-all-done.1 = f32[32,192,128]{2,1,0:T(8,128)S(1)} async-done(((f32[32,192,128]{2,1,0:T(8,128)}), f32[32,192,128]{2,1,0:T(8,128)S(1)}, u32[]{:S(2)}, u32[]{:S(2)}) %all-to-all-start.1) | async-done | bytes 3145760 | tf_op jit(solution)/shard_map/all_to_all | solution.py:113
  319.4 9.0 %select_select_fusion = f32[384,128]{1,0:T(8,128)} fusion(f32[384,128]{1,0:T(8,128)S(1)} %copy-done.27, f32[6144,128]{1,0:T(8,128)S(1)} %bitcast.297, f32[6144]{0:T(1024)S(1)} %eq.64), kind=kOutput, calls=%fused_computation.161 | convolution fusion | flops 3626680320 | bytes 3563520 | tf_op jit(solution)/shard_map/dot_general | solution.py:120
  (197 shorter events, 98.8 us)
Async XLA Ops:
  1.9 48.0 %collective-permute-start = (f32[2,16,1,1024]{3,2,1,0:T(1,128)S(1)}, f32[2,16,1,1024]{3,2,1,0:T(1,128)S(1)}, u32[]{:S(2)}, u32[]{:S(2)}) collective-permute-start(f32[2,16,1,1024]{3,2,1,0:T(1,128)S(1)} %slice.448), channel_id=1, source_target_pairs={{1,0},{2,1},{3,2},{4,3},{5,4},{6,5},{7,6},{9,8},{10,9},{11,10},{12... | collective-permute-start | bytes 393224 | tf_op jit(solution)/shard_map/ppermute | solution.py:13
  4.2 45.7 %collective-permute-start.1 = (f32[2,1,24,1024]{3,2,1,0:T(8,128)S(1)}, f32[2,1,24,1024]{3,2,1,0:T(8,128)S(1)}, u32[]{:S(2)}, u32[]{:S(2)}) collective-permute-start(f32[2,1,24,1024]{3,2,1,0:T(8,128)S(1)} %slice.454), channel_id=1, source_target_pairs={{8,0},{16,8},{24,16},{9,1},{17,9},{25,17},{10,2},{18,10},{26,18},{... | collective-permute-start | bytes 589832 | tf_op jit(solution)/shard_map/ppermute | solution.py:13
  18.3 23.5 %copy-start.26 = (s32[3072,1]{0,1:T(1,128)}, s32[3072,1]{0,1:T(1,128)S(1)}, u32[]{:S(2)}) copy-start(s32[3072,1]{0,1:T(1,128)S(1)} %compare_select_fusion) | copy-start | bytes 36868
  30.8 206.2 %all-to-all-start = ((f32[32,192,1]{1,2,0:T(1,128)}), f32[32,192,1]{1,2,0:T(1,128)}, u32[]{:S(2)}, u32[]{:S(2)}) async-start(f32[32,192,1]{1,2,0:T(1,128)} %all_to_all.19), calls=%async_computation | async-start | bytes 65536 | tf_op jit(solution)/shard_map/all_to_all | solution.py:114
  53.3 38.9 %copy-start.1 = (f32[1,16,24,1024]{3,2,1,0:T(8,128)}, f32[1,16,24,1024]{3,2,1,0:T(8,128)S(1)}, u32[]{:S(2)}) copy-start(f32[1,16,24,1024]{3,2,1,0:T(8,128)S(1)} %get-tuple-element.55) | copy-start | bytes 4718596
  53.3 38.9 %copy-start.4 = (f32[1,16,24,1024]{3,2,1,0:T(8,128)}, f32[1,16,24,1024]{3,2,1,0:T(8,128)S(1)}, u32[]{:S(2)}) copy-start(f32[1,16,24,1024]{3,2,1,0:T(8,128)S(1)} %get-tuple-element.56) | copy-start | bytes 4718596
  56.3 8.3 %collective-permute-start.3 = (f32[2,1,24,1024]{3,2,1,0:T(8,128)S(1)}, f32[2,1,24,1024]{3,2,1,0:T(8,128)S(1)}, u32[]{:S(2)}, u32[]{:S(2)}) collective-permute-start(f32[2,1,24,1024]{3,2,1,0:T(8,128)S(1)} %slice.594), channel_id=1, source_target_pairs={{0,8},{8,16},{16,24},{1,9},{9,17},{17,25},{2,10},{10,18},{18,26},{... | collective-permute-start | bytes 589832 | tf_op jit(solution)/shard_map/ppermute | solution.py:13
  60.2 3.3 %collective-permute-start.2 = (f32[2,16,1,1024]{3,2,1,0:T(1,128)S(1)}, f32[2,16,1,1024]{3,2,1,0:T(1,128)S(1)}, u32[]{:S(2)}, u32[]{:S(2)}) collective-permute-start(f32[2,16,1,1024]{3,2,1,0:T(1,128)S(1)} %slice.588), channel_id=1, source_target_pairs={{0,1},{1,2},{2,3},{3,4},{4,5},{5,6},{6,7},{8,9},{9,10},{10,11},{11... | collective-permute-start | bytes 393224 | tf_op jit(solution)/shard_map/ppermute | solution.py:13
  74.4 4.7 %collective-permute-start.4 = (f32[2,16,1,1024]{3,2,1,0:T(1,128)S(1)}, f32[2,16,1,1024]{3,2,1,0:T(1,128)S(1)}, u32[]{:S(2)}, u32[]{:S(2)}) collective-permute-start(f32[2,16,1,1024]{3,2,1,0:T(1,128)S(1)} %slice.604), channel_id=1, source_target_pairs={{1,0},{2,1},{3,2},{4,3},{5,4},{6,5},{7,6},{9,8},{10,9},{11,10},{12... | collective-permute-start | bytes 393224 | tf_op jit(solution)/shard_map/ppermute | solution.py:13
  77.8 9.8 %collective-permute-start.5 = (f32[2,1,24,1024]{3,2,1,0:T(8,128)S(1)}, f32[2,1,24,1024]{3,2,1,0:T(8,128)S(1)}, u32[]{:S(2)}, u32[]{:S(2)}) collective-permute-start(f32[2,1,24,1024]{3,2,1,0:T(8,128)S(1)} %slice.610), channel_id=1, source_target_pairs={{8,0},{16,8},{24,16},{9,1},{17,9},{25,17},{10,2},{18,10},{26,18},{... | collective-permute-start | bytes 589832 | tf_op jit(solution)/shard_map/ppermute | solution.py:13
  94.9 8.5 %collective-permute-start.7 = (f32[2,1,24,1024]{3,2,1,0:T(8,128)S(1)}, f32[2,1,24,1024]{3,2,1,0:T(8,128)S(1)}, u32[]{:S(2)}, u32[]{:S(2)}) collective-permute-start(f32[2,1,24,1024]{3,2,1,0:T(8,128)S(1)} %slice.624), channel_id=1, source_target_pairs={{0,8},{8,16},{16,24},{1,9},{9,17},{17,25},{2,10},{10,18},{18,26},{... | collective-permute-start | bytes 589832 | tf_op jit(solution)/shard_map/ppermute | solution.py:13
  99.2 3.5 %collective-permute-start.6 = (f32[2,16,1,1024]{3,2,1,0:T(1,128)S(1)}, f32[2,16,1,1024]{3,2,1,0:T(1,128)S(1)}, u32[]{:S(2)}, u32[]{:S(2)}) collective-permute-start(f32[2,16,1,1024]{3,2,1,0:T(1,128)S(1)} %slice.618), channel_id=1, source_target_pairs={{0,1},{1,2},{2,3},{3,4},{4,5},{5,6},{6,7},{8,9},{9,10},{10,11},{11... | collective-permute-start | bytes 393224 | tf_op jit(solution)/shard_map/ppermute | solution.py:13
  116.0 5.2 %collective-permute-start.8 = (f32[2,16,1,1024]{3,2,1,0:T(1,128)S(1)}, f32[2,16,1,1024]{3,2,1,0:T(1,128)S(1)}, u32[]{:S(2)}, u32[]{:S(2)}) collective-permute-start(f32[2,16,1,1024]{3,2,1,0:T(1,128)S(1)} %slice.634), channel_id=1, source_target_pairs={{1,0},{2,1},{3,2},{4,3},{5,4},{6,5},{7,6},{9,8},{10,9},{11,10},{12... | collective-permute-start | bytes 393224 | tf_op jit(solution)/shard_map/ppermute | solution.py:13
  119.5 8.5 %collective-permute-start.9 = (f32[2,1,24,1024]{3,2,1,0:T(8,128)S(1)}, f32[2,1,24,1024]{3,2,1,0:T(8,128)S(1)}, u32[]{:S(2)}, u32[]{:S(2)}) collective-permute-start(f32[2,1,24,1024]{3,2,1,0:T(8,128)S(1)} %slice.640), channel_id=1, source_target_pairs={{8,0},{16,8},{24,16},{9,1},{17,9},{25,17},{10,2},{18,10},{26,18},{... | collective-permute-start | bytes 589832 | tf_op jit(solution)/shard_map/ppermute | solution.py:13
  140.7 9.7 %collective-permute-start.11 = (f32[2,1,24,1024]{3,2,1,0:T(8,128)S(1)}, f32[2,1,24,1024]{3,2,1,0:T(8,128)S(1)}, u32[]{:S(2)}, u32[]{:S(2)}) collective-permute-start(f32[2,1,24,1024]{3,2,1,0:T(8,128)S(1)} %slice.654), channel_id=1, source_target_pairs={{0,8},{8,16},{16,24},{1,9},{9,17},{17,25},{2,10},{10,18},{18,26},{... | collective-permute-start | bytes 589832 | tf_op jit(solution)/shard_map/ppermute | solution.py:13
  145.3 4.2 %collective-permute-start.10 = (f32[2,16,1,1024]{3,2,1,0:T(1,128)S(1)}, f32[2,16,1,1024]{3,2,1,0:T(1,128)S(1)}, u32[]{:S(2)}, u32[]{:S(2)}) collective-permute-start(f32[2,16,1,1024]{3,2,1,0:T(1,128)S(1)} %slice.648), channel_id=1, source_target_pairs={{0,1},{1,2},{2,3},{3,4},{4,5},{5,6},{6,7},{8,9},{9,10},{10,11},{11... | collective-permute-start | bytes 393224 | tf_op jit(solution)/shard_map/ppermute | solution.py:13
  165.9 6.7 %collective-permute-start.12 = (f32[2,16,1,1024]{3,2,1,0:T(1,128)S(1)}, f32[2,16,1,1024]{3,2,1,0:T(1,128)S(1)}, u32[]{:S(2)}, u32[]{:S(2)}) collective-permute-start(f32[2,16,1,1024]{3,2,1,0:T(1,128)S(1)} %slice.664), channel_id=1, source_target_pairs={{1,0},{2,1},{3,2},{4,3},{5,4},{6,5},{7,6},{9,8},{10,9},{11,10},{12... | collective-permute-start | bytes 393224 | tf_op jit(solution)/shard_map/ppermute | solution.py:13
  169.3 8.0 %collective-permute-start.13 = (f32[2,1,24,1024]{3,2,1,0:T(8,128)S(1)}, f32[2,1,24,1024]{3,2,1,0:T(8,128)S(1)}, u32[]{:S(2)}, u32[]{:S(2)}) collective-permute-start(f32[2,1,24,1024]{3,2,1,0:T(8,128)S(1)} %slice.670), channel_id=1, source_target_pairs={{8,0},{16,8},{24,16},{9,1},{17,9},{25,17},{10,2},{18,10},{26,18},{... | collective-permute-start | bytes 589832 | tf_op jit(solution)/shard_map/ppermute | solution.py:13
  192.7 13.1 %copy-start = (f32[3,16,24,1024]{3,2,1,0:T(8,128)}, f32[3,16,24,1024]{3,2,1,0:T(8,128)S(1)}, u32[]{:S(2)}) copy-start(f32[3,16,24,1024]{3,2,1,0:T(8,128)S(1)} %fusion.7) | copy-start | bytes 14155780
  193.0 9.9 %collective-permute-start.15 = (f32[2,1,24,1024]{3,2,1,0:T(8,128)S(1)}, f32[2,1,24,1024]{3,2,1,0:T(8,128)S(1)}, u32[]{:S(2)}, u32[]{:S(2)}) collective-permute-start(f32[2,1,24,1024]{3,2,1,0:T(8,128)S(1)} %slice.684), channel_id=1, source_target_pairs={{0,8},{8,16},{16,24},{1,9},{9,17},{17,25},{2,10},{10,18},{18,26},{... | collective-permute-start | bytes 589832 | tf_op jit(solution)/shard_map/ppermute | solution.py:13
  197.9 4.3 %collective-permute-start.14 = (f32[2,16,1,1024]{3,2,1,0:T(1,128)S(1)}, f32[2,16,1,1024]{3,2,1,0:T(1,128)S(1)}, u32[]{:S(2)}, u32[]{:S(2)}) collective-permute-start(f32[2,16,1,1024]{3,2,1,0:T(1,128)S(1)} %slice.678), channel_id=1, source_target_pairs={{0,1},{1,2},{2,3},{3,4},{4,5},{5,6},{6,7},{8,9},{9,10},{10,11},{11... | collective-permute-start | bytes 393224 | tf_op jit(solution)/shard_map/ppermute | solution.py:13
  211.6 11.1 %copy-start.21 = (pred[16,24,1024]{2,1,0:T(8,128)(4,1)S(1)}, pred[16,24,1024]{2,1,0:T(8,128)(4,1)}, u32[]{:S(2)}) copy-start(pred[16,24,1024]{2,1,0:T(8,128)(4,1)} %copy-done.20) | copy-start | bytes 1179652
  237.0 82.3 %copy-start.27 = (f32[384,128]{1,0:T(8,128)S(1)}, f32[384,128]{1,0:T(8,128)}, u32[]{:S(2)}) copy-start(f32[384,128]{1,0:T(8,128)} %param.13) | copy-start | bytes 589828
  237.0 82.3 %all-to-all-start.1 = ((f32[32,192,128]{2,1,0:T(8,128)}), f32[32,192,128]{2,1,0:T(8,128)S(1)}, u32[]{:S(2)}, u32[]{:S(2)}) async-start(f32[32,192,128]{2,1,0:T(8,128)} %bitcast.78), calls=%async_computation.1 | async-start | bytes 6291456 | tf_op jit(solution)/shard_map/all_to_all | solution.py:113
  (26 other events, 123.2 us)
where the time goes:
time: 332 us; the launch traced here: 329 us
  other arithmetic  110 us (33%)
  waiting for transfers between devices  96.2 us (29%)
  starting transfers between devices  57.5 us (17%)
  local copies, waits for them, and re-layouts  53.6 us (16%)
  matrix products  9.01 us (3%)
    all_to_all x1, waiting for transfers between devices, per_device(): lax.all_to_all(send_vals, ('col', 'hgt'), split_axis=0, concat_axis=0, ti...  70.5 us
    ppermute x16, starting transfers between devices, from_behind(): return lax.ppermute(block, axis, route)  37.3 us
    another operation x8, other arithmetic, curl(): return jnp.stack([dy_z - dz_y, dz_x - dx_z, dx_y - dy_x])  34.2 us
    ppermute x16, waiting for transfers between devices, from_behind(): return lax.ppermute(block, axis, route)  25.6 us
    add x4, other arithmetic, per_device(): ca * efield_lattice_vector  24.2 us
    sub x4, other arithmetic, per_device(): hfield_lattice_vector - 0.55 * curl(forward, (efield_lattice_vector[0], e...  16.3 us
    scatter x1, local copies, waits for them, and re-layouts, per_device(): jnp.full((n_dev * capacity,), -1.0, jnp.float32).at[where_to].set(nodes)  11.8 us
    all_to_all x1, starting transfers between devices, per_device(): lax.all_to_all(send_vals, ('col', 'hgt'), split_axis=0, concat_axis=0, ti...  10.9 us
  transfers between devices with their start and end apart: 18, of which 10 were waited for; matrix products, arithmetic and copies ran while one was open for 48% of the time, Pallas kernels for 0%

commit v1 on v0

v1 whole, which is shorter than its diff:
```python
import functools

import jax
import jax.numpy as jnp
from jax import lax
from jax.experimental import pallas as pl
from jax.experimental.pallas import tpu as pltpu
from jax.sharding import PartitionSpec as P

PTS = 128
STEPS = 4
COURANT = 0.55
LANES = 128
ROWS = 8
F32 = jnp.float32
VMEM_MIB = 16

WHOLE = pl.BlockSpec(memory_space=pltpu.VMEM)
SCALARS = pl.BlockSpec(memory_space=pltpu.SMEM)
FAR = pl.BlockSpec(memory_space=pltpu.HBM)


def vmem(*shape):
    return pltpu.VMEM(shape, F32)


def far(x):
    return pltpu.with_memory_space_constraint(x, pltpu.HBM)


def params(mib):
    return pltpu.CompilerParams(vmem_limit_bytes=mib << 20)


def cost(flops, moved):
    return pl.CostEstimate(flops=flops, bytes_accessed=moved, transcendentals=0)


def after_y(f):
    lane = lax.broadcasted_iota(jnp.int32, (ROWS, LANES), 1)
    n = f.shape[1] // LANES
    turned = [pltpu.roll(f[:, k * LANES : (k + 1) * LANES], LANES - 1, 1) for k in range(n)]
    turned.append(jnp.zeros((ROWS, LANES), F32))
    return jnp.concatenate([jnp.where(lane < LANES - 1, turned[k], turned[k + 1]) for k in range(n)], 1)


def before_y(f):
    lane = lax.broadcasted_iota(jnp.int32, (ROWS, LANES), 1)
    n = f.shape[1] // LANES
    turned = [jnp.zeros((ROWS, LANES), F32)]
    turned += [pltpu.roll(f[:, k * LANES : (k + 1) * LANES], 1, 1) for k in range(n)]
    return jnp.concatenate([jnp.where(lane > 0, turned[k + 1], turned[k]) for k in range(n)], 1)


def after_row(f, row):
    place = lax.broadcasted_iota(jnp.int32, f.shape, 0)
    return jnp.where(place < ROWS - 1, pltpu.roll(f, ROWS - 1, 0), jnp.broadcast_to(row, f.shape))


def before_row(f, row):
    place = lax.broadcasted_iota(jnp.int32, f.shape, 0)
    return jnp.where(place > 0, pltpu.roll(f, 1, 0), jnp.broadcast_to(row, f.shape))


def edges_kernel(e, h, fwd, back, sems):
    last = e.shape[1] - 1
    copies = [
        pltpu.make_async_copy(e.at[:, last], fwd.at[pl.ds(0, 3)], sems.at[0]),
        pltpu.make_async_copy(h.at[pl.ds(1, 2), last], fwd.at[pl.ds(3, 2)], sems.at[1]),
        pltpu.make_async_copy(e.at[pl.ds(1, 2), 0], back, sems.at[2]),
    ]
    for copy in copies:
        copy.start()
    for copy in copies:
        copy.wait()


def load_kernel(e_in, h_in, place, inside, e, h, fwd, back, diag_fwd, diag_back, sems):
    nx, nz = e_in.shape[1:3]
    e_copy = pltpu.make_async_copy(e_in, e.at[:, pl.ds(0, nx)], sems.at[0])
    h_copy = pltpu.make_async_copy(h_in, h.at[:, pl.ds(1, nx)], sems.at[1])
    e_copy.start()
    h_copy.start()
    e_copy.wait()
    h_copy.wait()

    def rows(x, carry):
        for comp in range(3):
            fwd[comp, pl.ds(x, 1), :] = e[comp, x, nz - 1 : nz, :]
        for comp in range(2):
            fwd[3 + comp, pl.ds(x, 1), :] = h[comp, x + 1, nz - 1 : nz, :]
            back[comp, pl.ds(x, 1), :] = e[comp, x, 0:1, :]
        return carry

    lax.fori_loop(0, nx, rows, 0)
    diag_fwd[...] = e[0, nx - 1, 0:1, :]
    diag_back[...] = e[2, 0, nz - 1 : nz, :]


def coefficients_kernel(temp_far, tags_far, ca, cb, sigma_out, temp, tags, sems):
    nx, nz, _ = temp.shape
    parts = 4
    size = nx // parts
    copies = []
    for part in range(parts):
        here = pl.ds(part * size, size)
        copies.append(pltpu.make_async_copy(temp_far.at[here], temp.at[here], sems.at[0, part]))
        copies.append(pltpu.make_async_copy(tags_far.at[here], tags.at[here], sems.at[1, part]))
    for copy in copies:
        copy.start()

    def plane(x, carry):
        for z in range(0, nz, ROWS):
            tag = tags[x, z : z + ROWS, :]
            lean = tag == 0
            fat = tag == 1
            frac = 1.0 / (1.0 + jnp.exp(-2.0 * temp[x, z : z + ROWS, :]))
            eps_low = jnp.where(lean, 4.0, jnp.where(fat, 2.5, 5.0))
            eps_rise = jnp.where(lean, 46.0, jnp.where(fat, 3.5, 5.0))
            sig_low = jnp.where(lean, 0.2, jnp.where(fat, 0.05, 0.1))
            sig_rise = jnp.where(lean, 7.8, jnp.where(fat, 0.35, 0.9))
            eps = eps_low + eps_rise * frac
            sigma = sig_low + sig_rise * frac
            half = (0.5 * COURANT) * sigma
            inverse = 1.0 / (eps + half)
            ca[x, z : z + ROWS, :] = (eps - half) * inverse
            cb[x, z : z + ROWS, :] = COURANT * inverse
            sigma_out[x, z : z + ROWS, :] = sigma
        return carry

    for part in range(parts):
        copies[2 * part].wait()
        copies[2 * part + 1].wait()
        lax.fori_loop(part * size, (part + 1) * size, plane, 0)


def step_kernel(first, last, *refs):
    inside, e_old, h_old, ca, cb, sigma = refs[:6]
    col_fwd, col_back, hgt_fwd, hgt_back, corner_x, corner_z, own_rows = refs[6:13]
    refs = refs[13:]
    if first:
        low_old = None
    else:
        low_old, power_old = refs[:2]
        refs = refs[2:]
    if last:
        e, h, power, low = refs
    else:
        e, h, power, low, to_fwd, to_back, rows_fwd, rows_back, diag_fwd, diag_back = refs
    nx = e.shape[1] - 1
    nz = e.shape[2]
    behind = inside[0]
    below = inside[1]

    for z in range(0, nz, ROWS):
        here = slice(z, z + ROWS)
        ex, ey, ez = (col_fwd[comp, here, :] for comp in range(3))
        row = col_fwd[0, z + ROWS : z + ROWS + 1, :] if z + ROWS < nz else corner_x[...]
        hy = col_fwd[3, here, :] if first else h[1, 0, here, :]
        hz = col_fwd[4, here, :] if first else h[2, 0, here, :]
        hy = hy - (COURANT * behind) * ((after_row(ex, row) - ex) - (e[2, 0, here, :] - ez))
        hz = hz - (COURANT * behind) * ((e[1, 0, here, :] - ey) - (after_y(ex) - ex))
        h[1, 0, here, :] = hy
        h[2, 0, here, :] = hz
        for comp in (1, 2):
            e[comp, nx, here, :] = col_back[comp - 1, here, :]

    for x in range(0, nx, ROWS):
        here = slice(x, x + ROWS)
        ex, ey, ez = (hgt_fwd[comp, here, :] for comp in range(3))
        row = hgt_fwd[2, x + ROWS : x + ROWS + 1, :] if x + ROWS < nx else corner_z[...]
        hx = hgt_fwd[3, here, :] if first else low_old[0, here, :]
        hy = hgt_fwd[4, here, :] if first else low_old[1, here, :]
        hx = hx - (COURANT * below) * ((after_y(ez) - ez) - (own_rows[1, here, :] - ey))
        hy = hy - (COURANT * below) * ((own_rows[0, here, :] - ex) - (after_row(ez, row) - ez))
        low[0, here, :] = hx
        low[1, here, :] = hy

    def plane(x, carry):
        here_x = pl.ds(x, 1)
        for z in range(0, nz, ROWS):
            here = slice(z, z + ROWS)
            ex, ey, ez = (e[comp, x, here, :] for comp in range(3))
            if z + ROWS < nz:
                row_x, row_y = (e[comp, x, z + ROWS : z + ROWS + 1, :] for comp in range(2))
            else:
                row_x, row_y = (hgt_back[comp, here_x, :] for comp in range(2))
            hx = h[0, x + 1, here, :] - COURANT * ((after_y(ez) - ez) - (after_row(ey, row_y) - ey))
            hy = h[1, x + 1, here, :] - COURANT * ((after_row(ex, row_x) - ex) - (e[2, x + 1, here, :] - ez))
            hz = h[2, x + 1, here, :] - COURANT * ((e[1, x + 1, here, :] - ey) - (after_y(ex) - ex))
            if z > 0:
                low_x, low_y = (h[comp, x + 1, z - 1 : z, :] for comp in range(2))
            else:
                low_x, low_y = (low[comp, here_x, :] for comp in range(2))
            h[0, x + 1, here, :] = hx
            h[1, x + 1, here, :] = hy
            h[2, x + 1, here, :] = hz
            keep = ca[x, here, :]
            drive = cb[x, here, :]
            ex = keep * ex + drive * ((hz - before_y(hz)) - (hy - before_row(hy, low_y)))
            ey = keep * ey + drive * ((hx - before_row(hx, low_x)) - (hz - h[2, x, here, :]))
            ez = keep * ez + drive * ((hy - h[1, x, here, :]) - (hx - before_y(hx)))
            e[0, x, here, :] = ex
            e[1, x, here, :] = ey
            e[2, x, here, :] = ez
            heat = sigma[x, here, :] * (ex * ex + ey * ey + ez * ez)
            power[x, here, :] = heat if first else power_old[x, here, :] + heat
        if not last:
            for comp in range(3):
                rows_fwd[comp, here_x, :] = e[comp, x, nz - 1 : nz, :]
            for comp in range(2):
                rows_back[comp, here_x, :] = e[comp, x, 0:1, :]
        return carry

    lax.fori_loop(0, nx, plane, 0)
    if not last:
        to_fwd[...] = e[:, nx - 1]
        to_back[...] = e[1:3, 0]
        diag_fwd[...] = e[0, nx - 1, 0:1, :]
        diag_back[...] = e[2, 0, nz - 1 : nz, :]


def places_kernel(n_col, n_hgt, cap, extra, owner, node, place, nodes_out):
    n_dev = n_col * n_hgt
    count = owner.shape[1]
    width = 256
    rows = lax.broadcasted_iota(jnp.int32, (n_dev, width), 0)
    before = lax.broadcasted_iota(jnp.int32, (width, width), 0)
    after = lax.broadcasted_iota(jnp.int32, (width, width), 1)
    upper = jnp.where(before <= after, 1.0, 0.0).astype(jnp.bfloat16)
    room_for = nodes_out.shape[0] // n_dev * LANES
    room = lax.broadcasted_iota(jnp.int32, (room_for, width), 0)
    total = jnp.zeros((n_dev, 1), F32)
    high = jnp.zeros((n_dev, room_for), F32)
    low = jnp.zeros((n_dev, room_for), F32)
    nt = (((1,), (1,)), ((), ()))
    for start in range(0, count, width):
        own = owner[:, start : start + width]
        target = lax.rem(own, n_hgt) * n_col + lax.div(own, n_hgt)
        hit = jnp.where(rows == target, 1.0, 0.0)
        running = total + jnp.dot(hit.astype(jnp.bfloat16), upper, preferred_element_type=F32)
        total = running[:, width - 1 : width]
        rank = jnp.sum(hit * running, axis=0, keepdims=True).astype(jnp.int32) - 1
        group = lax.div(target, n_col)
        place[:, start : start + width] = target * cap + group * extra + rank
        number = node[:, start : start + width]
        upper_part = lax.div(number, 16)
        lower_part = number - 16 * upper_part
        seat = jnp.where(room == rank, 1.0, 0.0).astype(jnp.bfloat16)
        high = high + lax.dot_general(
            (hit * upper_part.astype(F32)).astype(jnp.bfloat16), seat, nt, preferred_element_type=F32
        )
        low = low + lax.dot_general(
            (hit * lower_part.astype(F32)).astype(jnp.bfloat16), seat, nt, preferred_element_type=F32
        )
    taken = lax.broadcasted_iota(jnp.int32, (n_dev, room_for), 1).astype(F32) < total
    table = jnp.where(taken, 16.0 * high + low, -1.0)
    parts = room_for // LANES
    for part in range(parts):
        nodes_out[pl.ds(part, n_dev, stride=parts), :] = table[:, part * LANES : (part + 1) * LANES]


def pack_kernel(place, power, nodes, e, h, out, e_out, h_out, sems):
    nx, nz, ny = power.shape
    e_copy = pltpu.make_async_copy(e.at[:, pl.ds(0, nx)], e_out, sems.at[0])
    h_copy = pltpu.make_async_copy(h.at[:, pl.ds(1, nx)], h_out, sems.at[1])
    e_copy.start()
    h_copy.start()
    n_group, rows, _ = out.shape
    per_row = ny // PTS
    extra = nodes.shape[0] // n_group
    flat = out.reshape(n_group * rows, PTS)

    def clear(group, carry):
        out[group] = jnp.zeros((rows, PTS), F32)
        out[group, rows - extra : rows, :] = nodes[pl.ds(pl.multiple_of(group * extra, ROWS), extra), :]
        return carry

    lax.fori_loop(0, n_group, clear, 0)

    def plane(x, carry):
        for z in range(nz):
            for k in range(per_row):
                spot = place[x * (nz * per_row) + z * per_row + k]
                flat[pl.ds(spot, 1), :] = power[x, z : z + 1, k * PTS : (k + 1) * PTS]
        return carry

    lax.fori_loop(0, nx, plane, 0)
    e_copy.wait()
    h_copy.wait()


def collect_kernel(cap, blocks, out, chosen, split):
    n_from, rows, pts = blocks.shape
    n_part, node_count, _ = out.shape
    room = chosen.shape[1] // n_from
    parts = room // LANES
    ids = lax.broadcasted_iota(jnp.int32, (node_count, LANES), 0).astype(F32)
    split[...] = jnp.zeros(split.shape, split.dtype)
    for part in range(n_part):
        for source in range(n_from):
            for piece in range(parts):
                row = n_part * cap + part * parts + piece
                lanes = slice(source * room + piece * LANES, source * room + (piece + 1) * LANES)
                hit = ids == blocks[source, row : row + 1, :]
                chosen[:, lanes] = jnp.where(hit, 1.0, 0.0).astype(jnp.bfloat16)
            values = blocks[source, part * cap : (part + 1) * cap, :]
            high = values.astype(jnp.bfloat16)
            here = slice(source * room, source * room + cap)
            split[here, 0:pts] = high
            split[here, pts : 2 * pts] = (values - high.astype(F32)).astype(jnp.bfloat16)
        both = jnp.dot(chosen[...], split[...], preferred_element_type=F32)
        out[part] = both[:, 0:pts] + both[:, pts : 2 * pts]


def shifted(block, d_col, d_hgt):
    n_col = lax.axis_size("col")
    n_hgt = lax.axis_size("hgt")
    route = [
        (c * n_hgt + h, (c + d_col) * n_hgt + h + d_hgt)
        for c in range(n_col)
        for h in range(n_hgt)
        if 0 <= c + d_col < n_col and 0 <= h + d_hgt < n_hgt
    ]
    return lax.ppermute(block, ("col", "hgt"), route)


def tissue_warmth_kelvin(heat_content_per_mass):
    return jnp.where(
        heat_content_per_mass < 0.0,
        heat_content_per_mass / 2.0,
        jnp.where(heat_content_per_mass > 1.0, (heat_content_per_mass - 1.0) / 3.0, 0.0),
    )


def per_device(
    efield_lattice_vector,
    hfield_lattice_vector,
    cell_temp,
    region_tags,
    block_owner,
    block_node,
    node_enthalpy,
):
    nx, nz, ny = cell_temp.shape
    n_col = lax.axis_size("col")
    n_hgt = lax.axis_size("hgt")
    n_dev = n_col * n_hgt
    count = nx * nz * ny // PTS
    cap = 2 * count // n_dev
    node_count = node_enthalpy.shape[0]
    cells = nx * nz * ny
    sem = pltpu.SemaphoreType.DMA

    e_start = far(efield_lattice_vector)
    h_start = far(hfield_lattice_vector)
    to_fwd, to_back = pl.pallas_call(
        edges_kernel,
        out_shape=(vmem(5, nz, ny), vmem(2, nz, ny)),
        in_specs=[FAR, FAR],
        out_specs=(WHOLE, WHOLE),
        scratch_shapes=[sem((3,))],
        compiler_params=params(VMEM_MIB),
        cost_estimate=cost(0, 7 * nz * ny * 8),
        name="edges",
    )(e_start, h_start)
    col_fwd = shifted(to_fwd, 1, 0)
    col_back = shifted(to_back, -1, 0)
    room_for = -(-cap // LANES) * LANES
    extra = -(-(n_col * room_for // LANES) // ROWS) * ROWS
    place, send_nodes = pl.pallas_call(
        functools.partial(places_kernel, n_col, n_hgt, cap, extra),
        out_shape=(
            jax.ShapeDtypeStruct((1, count), jnp.int32),
            jax.ShapeDtypeStruct((n_hgt * extra, PTS), F32),
        ),
        in_specs=[WHOLE, WHOLE],
        out_specs=(WHOLE, WHOLE),
        compiler_params=params(VMEM_MIB),
        cost_estimate=cost(count * n_dev * 8, count * 16),
        name="places",
    )(block_owner.reshape(1, count), block_node.reshape(1, count))
    place = place.reshape(count)
    inside = jnp.stack([lax.axis_index("col") > 0, lax.axis_index("hgt") > 0]).astype(F32)
    e, h, rows_fwd, rows_back, diag_fwd, diag_back = pl.pallas_call(
        load_kernel,
        out_shape=(
            vmem(3, nx + 1, nz, ny),
            vmem(3, nx + 1, nz, ny),
            vmem(5, nx, ny),
            vmem(2, nx, ny),
            vmem(1, ny),
            vmem(1, ny),
        ),
        in_specs=[FAR, FAR, SCALARS, SCALARS],
        out_specs=(WHOLE,) * 6,
        scratch_shapes=[sem((2,))],
        compiler_params=params(VMEM_MIB),
        cost_estimate=cost(0, cells * 24),
        name="load",
    )(e_start, h_start, place, inside)
    hgt_fwd = shifted(rows_fwd, 0, 1)
    hgt_back = shifted(rows_back, 0, -1)
    corner_x = shifted(diag_fwd, 1, -1)
    corner_z = shifted(diag_back, -1, 1)

    ca, cb, sigma = pl.pallas_call(
        coefficients_kernel,
        out_shape=(vmem(nx, nz, ny),) * 3,
        in_specs=[FAR, FAR],
        out_specs=(WHOLE,) * 3,
        scratch_shapes=[
            pltpu.VMEM((nx, nz, ny), F32),
            pltpu.VMEM((nx, nz, ny), jnp.int32),
            sem((2, 4)),
        ],
        compiler_params=params(VMEM_MIB),
        cost_estimate=cost(cells * 40, cells * 20),
        name="coefficients",
    )(far(cell_temp), far(region_tags))
    low = power = None
    for step in range(STEPS):
        first = step == 0
        last = step == STEPS - 1
        out_shape = [vmem(3, nx + 1, nz, ny), vmem(3, nx + 1, nz, ny), vmem(nx, nz, ny), vmem(2, nx, ny)]
        if not last:
            out_shape += [
                vmem(3, nz, ny),
                vmem(2, nz, ny),
                vmem(3, nx, ny),
                vmem(2, nx, ny),
                vmem(1, ny),
                vmem(1, ny),
            ]
        args = [inside, e, h, ca, cb, sigma, col_fwd, col_back, hgt_fwd, hgt_back, corner_x, corner_z, rows_back]
        aliases = {1: 0, 2: 1}
        if not first:
            args += [low, power]
            aliases.update({13: 3, 14: 2})
        outs = pl.pallas_call(
            functools.partial(step_kernel, first, last),
            out_shape=tuple(out_shape),
            in_specs=[SCALARS] + [WHOLE] * (len(args) - 1),
            out_specs=(WHOLE,) * len(out_shape),
            input_output_aliases=aliases,
            compiler_params=params(VMEM_MIB),
            cost_estimate=cost(cells * 60, cells * 40),
            name=f"yee_step_{step}",
        )(*args)
        e, h, power, low = outs[:4]
        if not last:
            to_fwd, to_back, rows_fwd, rows_back, diag_fwd, diag_back = outs[4:]
            col_fwd = shifted(to_fwd, 1, 0)
            col_back = shifted(to_back, -1, 0)
            hgt_fwd = shifted(rows_fwd, 0, 1)
            hgt_back = shifted(rows_back, 0, -1)
            corner_x = shifted(diag_fwd, 1, -1)
            corner_z = shifted(diag_back, -1, 1)

    send, e_out, h_out = pl.pallas_call(
        pack_kernel,
        out_shape=(
            jax.ShapeDtypeStruct((n_hgt, n_col * cap + extra, PTS), F32),
            pltpu.HBM((3, nx, nz, ny), F32),
            pltpu.HBM((3, nx, nz, ny), F32),
        ),
        in_specs=[SCALARS, WHOLE, WHOLE, WHOLE, WHOLE],
        out_specs=(WHOLE, FAR, FAR),
        scratch_shapes=[sem((2,))],
        compiler_params=params(VMEM_MIB),
        cost_estimate=cost(cells, cells * 36),
        name="pack",
    )(place, power, send_nodes, e, h)
    blocks = lax.all_to_all(send, "hgt", split_axis=0, concat_axis=0, tiled=True)
    partial = pl.pallas_call(
        functools.partial(collect_kernel, cap),
        out_shape=jax.ShapeDtypeStruct((n_col, node_count, PTS), F32),
        in_specs=[WHOLE],
        out_specs=WHOLE,
        scratch_shapes=[
            pltpu.VMEM((node_count, n_hgt * room_for), jnp.bfloat16),
            pltpu.VMEM((n_hgt * room_for, 2 * PTS), jnp.bfloat16),
        ],
        compiler_params=params(VMEM_MIB),
        cost_estimate=cost(n_col * node_count * n_hgt * room_for * PTS * 4, cells * 8),
        name="collect",
    )(blocks)
    parts = lax.all_to_all(partial, "col", split_axis=0, concat_axis=0, tiled=True)
    heat = jnp.sum(parts, axis=0)
    heat_content_per_mass = node_enthalpy + (0.25 / STEPS) * heat
    return e_out, h_out, tissue_warmth_kelvin(heat_content_per_mass)


def solution(mesh):
    placed = (
        P(None, "col", "hgt", None),
        P(None, "col", "hgt", None),
        P("col", "hgt", None),
        P("col", "hgt", None),
        P("col", "hgt", None, None, None, None),
        P("col", "hgt", None, None, None),
        P(("col", "hgt"), None),
    )
    return jax.shard_map(
        per_device,
        mesh=mesh,
        in_specs=placed,
        out_specs=(
            P(None, "col", "hgt", None),
            P(None, "col", "hgt", None),
            P(("col", "hgt"), None),
        ),
        check_vma=False,
    )
```

time: 332 us -> 203 us (0.61)
  other arithmetic: 110 us -> 0.86 us
  waiting for transfers between devices: 96.2 us -> 9.11 us
  blocking collectives: 0 us -> 82.5 us
  local copies, waits for them, and re-layouts: 53.6 us -> 0.5 us
  Pallas kernels: 0 us -> 40.7 us
  starting transfers between devices: 57.5 us -> 67.3 us
  matrix products: 9.01 us -> 0 us
    all_to_all x0 -> x2, blocking collectives: none -> 82.5 us  [the longest x1 58 us: per_device(): lax.all_to_all(send, 'hgt', split_axis=0, concat_axis=0, tiled=True)]
    all_to_all x2 -> x0, waiting for transfers between devices: 70.5 us -> none  [the longest x1 70.5 us: per_device(): lax.all_to_all(send_vals, ('col', 'hgt'), split_axis=0, concat_axis=0, ti...]
    another operation x10 -> x0, other arithmetic: 43.6 us -> none  [the longest x8 34.2 us: curl(): return jnp.stack([dy_z - dz_y, dz_x - dx_z, dx_y - dy_x])]
    pallas_call x0 -> x10, Pallas kernels: none -> 40.7 us  [the longest x4 21.5 us: per_device(): pl.pallas_call(functools.partial(step_kernel, first, last), out_shape=tup...]
    ppermute x16 -> x24, starting transfers between devices: 37.3 us -> 67.3 us  [shifted(): return lax.ppermute(block, ('col', 'hgt'), route)]
    add x4 -> x0, other arithmetic: 24.2 us -> none  [per_device(): ca * efield_lattice_vector]
    scatter x2 -> x0, local copies, waits for them, and re-layouts: 22.1 us -> none  [the longest x1 11.8 us: per_device(): jnp.full((n_dev * capacity,), -1.0, jnp.float32).at[where_to].set(nodes)]
    all_to_all x2 -> x0, starting transfers between devices: 20.2 us -> none  [the longest x1 10.9 us: per_device(): lax.all_to_all(send_vals, ('col', 'hgt'), split_axis=0, concat_axis=0, ti...]
  transfers between devices with their start and end apart: 18 -> 24, of which waited for: 10 -> 5; matrix products, arithmetic and copies ran while one was open for 48% -> 0% of each run, Pallas kernels for 0% -> 5%
where the time goes in v1:
time: 203 us; the launch traced here: 202 us
  blocking collectives  82.5 us (41%)
  starting transfers between devices  67.3 us (33%)
  Pallas kernels  40.7 us (20%)
  waiting for transfers between devices  9.11 us (4%)
    ppermute x24, starting transfers between devices, shifted(): return lax.ppermute(block, ('col', 'hgt'), route)  67.3 us
    all_to_all x1, blocking collectives, per_device(): lax.all_to_all(send, 'hgt', split_axis=0, concat_axis=0, tiled=True)  58 us
    all_to_all x1, blocking collectives, per_device(): lax.all_to_all(partial, 'col', split_axis=0, concat_axis=0, tiled=True)  24.5 us
    pallas_call x4, Pallas kernels, per_device(): pl.pallas_call(functools.partial(step_kernel, first, last), out_shape=tup...  21.5 us
    ppermute x24, waiting for transfers between devices, shifted(): return lax.ppermute(block, ('col', 'hgt'), route)  9.11 us
    pallas_call x1, Pallas kernels, per_device(): pl.pallas_call(load_kernel, out_shape=(vmem(3, nx + 1, nz, ny), vmem(3, n...  4.69 us
    pallas_call x1, Pallas kernels, per_device(): pl.pallas_call(pack_kernel, out_shape=(jax.ShapeDtypeStruct((n_hgt, n_col...  4.49 us
  transfers between devices with their start and end apart: 24, of which 5 were waited for; matrix products, arithmetic and copies ran while one was open for 0% of the time, Pallas kernels for 5%

profile of v1, /device:TPU:0, one launch (start us, length us, event | category | flops | bytes accessed | tf_op | source)
XLA Modules:
  0.0 202.0 jit_solution(10435578962750446181)
XLA Ops:
  1.8 5.0 %collective-permute-start = (f32[5,24,1024]{2,1,0:T(8,128)S(1)}, f32[5,24,1024]{2,1,0:T(8,128)S(1)}, u32[]{:S(2)}, u32[]{:S(2)}) collective-permute-start(f32[5,24,1024]{2,1,0:T(8,128)S(1)} %get-tuple-element.58), channel_id=1, source_target_pairs={{0,8},{1,9},{2,10},{3,11},{4,12},{5,13},{6,14},{7,15},{8,16},{9,17... | collective-permute-start | bytes 1474568 | tf_op jit(solution)/shard_map/ppermute | solution.py:325
  7.3 2.8 %places.1 = (s32[1,3072]{1,0:T(1,128)S(1)}, f32[64,128]{1,0:T(8,128)S(1)}) custom-call(s32[1,3072]{1,0:T(1,128)S(1)} %reshape.15.owner, s32[1,3072]{1,0:T(1,128)S(1)} %reshape.16.node), custom_call_target="tpu_custom_call" | custom-call | flops 786432 | bytes 49152 | tf_op jit(solution)/shard_map/places/pallas_call | solution.py:371
  10.3 4.7 %load.1 = (f32[3,17,24,1024]{3,2,1,0:T(8,128)S(1)}, f32[3,17,24,1024]{3,2,1,0:T(8,128)S(1)}, f32[5,16,1024]{2,1,0:T(8,128)S(1)}, f32[2,16,1024]{2,1,0:T(8,128)S(...) custom-call(f32[3,16,24,1024]{3,2,1,0:T(8,128)} %e.1, f32[3,16,24,1024]{3,2,1,0:T(8,128)} %h.1, s32[3072]{0:T(1024)S(1)} %bitcast.9, ...), custom_call_target="tpu_custom_call" | custom-call | bytes 9437184 | tf_op jit(solution)/shard_map/load/pallas_call | solution.py:385
  15.0 1.5 collective-permute-start.2
  20.4 2.7 %coefficients.1 = (f32[16,24,1024]{2,1,0:T(8,128)S(1)}, f32[16,24,1024]{2,1,0:T(8,128)S(1)}, f32[16,24,1024]{2,1,0:T(8,128)S(1)}) custom-call(f32[16,24,1024]{2,1,0:T(8,128)} %temp_far.1, s32[16,24,1024]{2,1,0:T(8,128)} %tags_far.1), custom_call_target="tpu_custom_call" | custom-call | flops 15728640 | bytes 7864320 | tf_op jit(solution)/shard_map/coefficients/pallas_call | solution.py:407
  23.2 1.9 collective-permute-done.1.refs_7_
  25.0 5.4 %yee_step_0.1 = (f32[3,17,24,1024]{3,2,1,0:T(8,128)S(1)}, f32[3,17,24,1024]{3,2,1,0:T(8,128)S(1)}, f32[16,24,1024]{2,1,0:T(8,128)S(1)}, f32[2,16,1024]{2,1,0:T(8...) custom-call(f32[2]{0:T(128)S(1)} %add_convert_fusion.inside.refs_0_,, ...), custom_call_target="tpu_custom_call", output_to_operand_aliasing={{0}: (1, {}), {1}: (2, {})} | custom-call | flops 23592960 | bytes 15728640 | tf_op jit(solution)/shard_map/yee_step_0/pallas_call | solution.py:440
  30.5 7.7 %collective-permute-start.6 = (f32[3,24,1024]{2,1,0:T(8,128)S(1)}, f32[3,24,1024]{2,1,0:T(8,128)S(1)}, u32[]{:S(2)}, u32[]{:S(2)}) collective-permute-start(f32[3,24,1024]{2,1,0:T(8,128)S(1)} %get-tuple-element.66), channel_id=1, source_target_pairs={{0,8},{1,9},{2,10},{3,11},{4,12},{5,13},{6,14},{7,15},{8,16},{9,17... | collective-permute-start | bytes 884744 | tf_op jit(solution)/shard_map/ppermute | solution.py:325
  39.4 5.7 %collective-permute-start.8 = (f32[3,16,1024]{2,1,0:T(8,128)S(1)}, f32[3,16,1024]{2,1,0:T(8,128)S(1)}, u32[]{:S(2)}, u32[]{:S(2)}) collective-permute-start(f32[3,16,1024]{2,1,0:T(8,128)S(1)} %get-tuple-element.68), channel_id=1, source_target_pairs={{0,1},{1,2},{2,3},{3,4},{4,5},{5,6},{6,7},{8,9},{9,10},{10,11},{11... | collective-permute-start | bytes 589832 | tf_op jit(solution)/shard_map/ppermute | solution.py:325
  47.8 2.1 %collective-permute-done.9.refs_9_ = f32[2,16,1024]{2,1,0:T(8,128)S(1)} collective-permute-done((f32[2,16,1024]{2,1,0:T(8,128)S(1)}, f32[2,16,1024]{2,1,0:T(8,128)S(1)}, u32[]{:S(2)}, u32[]{:S(2)}) %collective-permute-start.9) | collective-permute-done | bytes 131104 | tf_op jit(solution)/shard_map/ppermute | solution.py:325
  51.0 5.5 %yee_step_1.1 = (f32[3,17,24,1024]{3,2,1,0:T(8,128)S(1)}, f32[3,17,24,1024]{3,2,1,0:T(8,128)S(1)}, f32[16,24,1024]{2,1,0:T(8,128)S(1)}, f32[2,16,1024]{2,1,0:T(8...) custom-call(f32[2]{0:T(128)S(1)} %add_convert_fusion.inside.refs_0_,, ...), custom_call_target="tpu_custom_call", output_to_operand_aliasing={{0}: (1, {}), {1}: (2, {}), {3}: (13, {}), {2}: (14, {})} | custom-call | flops 23592960 | bytes 15728640 | tf_op jit(solution)/shard_map/yee_step_1/pallas_call | solution.py:440
  56.5 7.7 %collective-permute-start.12 = (f32[3,24,1024]{2,1,0:T(8,128)S(1)}, f32[3,24,1024]{2,1,0:T(8,128)S(1)}, u32[]{:S(2)}, u32[]{:S(2)}) collective-permute-start(f32[3,24,1024]{2,1,0:T(8,128)S(1)} %get-tuple-element.76), channel_id=1, source_target_pairs={{0,8},{1,9},{2,10},{3,11},{4,12},{5,13},{6,14},{7,15},{8,16},{9,17... | collective-permute-start | bytes 884744 | tf_op jit(solution)/shard_map/ppermute | solution.py:325
  65.5 7.6 %collective-permute-start.14 = (f32[3,16,1024]{2,1,0:T(8,128)S(1)}, f32[3,16,1024]{2,1,0:T(8,128)S(1)}, u32[]{:S(2)}, u32[]{:S(2)}) collective-permute-start(f32[3,16,1024]{2,1,0:T(8,128)S(1)} %get-tuple-element.78), channel_id=1, source_target_pairs={{0,1},{1,2},{2,3},{3,4},{4,5},{5,6},{6,7},{8,9},{9,10},{10,11},{11... | collective-permute-start | bytes 589832 | tf_op jit(solution)/shard_map/ppermute | solution.py:325
  75.7 2.1 %collective-permute-done.15.refs_9_ = f32[2,16,1024]{2,1,0:T(8,128)S(1)} collective-permute-done((f32[2,16,1024]{2,1,0:T(8,128)S(1)}, f32[2,16,1024]{2,1,0:T(8,128)S(1)}, u32[]{:S(2)}, u32[]{:S(2)}) %collective-permute-start.15) | collective-permute-done | bytes 131104 | tf_op jit(solution)/shard_map/ppermute | solution.py:325
  77.8 5.5 %yee_step_2.1 = (f32[3,17,24,1024]{3,2,1,0:T(8,128)S(1)}, f32[3,17,24,1024]{3,2,1,0:T(8,128)S(1)}, f32[16,24,1024]{2,1,0:T(8,128)S(1)}, f32[2,16,1024]{2,1,0:T(8...) custom-call(f32[2]{0:T(128)S(1)} %add_convert_fusion.inside.refs_0_,, ...), custom_call_target="tpu_custom_call", output_to_operand_aliasing={{0}: (1, {}), {1}: (2, {}), {3}: (13, {}), {2}: (14, {})} | custom-call | flops 23592960 | bytes 15728640 | tf_op jit(solution)/shard_map/yee_step_2/pallas_call | solution.py:440
  83.4 8.7 %collective-permute-start.18 = (f32[3,24,1024]{2,1,0:T(8,128)S(1)}, f32[3,24,1024]{2,1,0:T(8,128)S(1)}, u32[]{:S(2)}, u32[]{:S(2)}) collective-permute-start(f32[3,24,1024]{2,1,0:T(8,128)S(1)} %get-tuple-element.86), channel_id=1, source_target_pairs={{0,8},{1,9},{2,10},{3,11},{4,12},{5,13},{6,14},{7,15},{8,16},{9,17... | collective-permute-start | bytes 884744 | tf_op jit(solution)/shard_map/ppermute | solution.py:325
  92.1 1.3 collective-permute-start.19
  93.4 7.8 %collective-permute-start.20 = (f32[3,16,1024]{2,1,0:T(8,128)S(1)}, f32[3,16,1024]{2,1,0:T(8,128)S(1)}, u32[]{:S(2)}, u32[]{:S(2)}) collective-permute-start(f32[3,16,1024]{2,1,0:T(8,128)S(1)} %get-tuple-element.88), channel_id=1, source_target_pairs={{0,1},{1,2},{2,3},{3,4},{4,5},{5,6},{6,7},{8,9},{9,10},{10,11},{11... | collective-permute-start | bytes 589832 | tf_op jit(solution)/shard_map/ppermute | solution.py:325
  103.9 2.0 collective-permute-done.21.refs_9_
  105.9 5.1 %yee_step_3.1 = (f32[3,17,24,1024]{3,2,1,0:T(8,128)S(1)}, f32[3,17,24,1024]{3,2,1,0:T(8,128)S(1)}, f32[16,24,1024]{2,1,0:T(8,128)S(1)}, f32[2,16,1024]{2,1,0:T(8,128)S(1)}) custom-call(f32[2]{0:T(128)S(1)} %add_convert_fusion.inside.refs_0_, ...), custom_call_target="tpu_custom_call", output_to_operand_aliasing={{0}: (1, {}), {1}: (2, {}), {3}: (13, {}), {2}: (14, {})} | custom-call | flops 23592960 | bytes 15728640 | tf_op jit(solution)/shard_map/yee_step_3/pallas_call | solution.py:440
  111.0 4.5 %pack.1 = (f32[8,776,128]{2,1,0:T(8,128)S(1)}, f32[3,16,24,1024]{3,2,1,0:T(8,128)}, f32[3,16,24,1024]{3,2,1,0:T(8,128)}) custom-call(s32[3072]{0:T(1024)S(1)} %bitcast.10, f32[16,24,1024]{2,1,0:T(8,128)S(1)} %get-tuple-element.94.power, f32[64,128]{1,0:T(8,128)S(1)} %get-tuple-element.95.nodes, f32[3,17,24,1024]{3,2,1,0:T(8,128)S(1)} %get-tuple-element.96.e, ...), custom_call_target="tpu_custom_call" | custom-call | flops 393216 | bytes 14155776 | tf_op jit(solution)/shard_map/pack/pallas_call | solution.py:460
  115.5 58.0 %all_to_all.10.blocks = f32[8,776,128]{2,1,0:T(8,128)S(1)} all-to-all(f32[8,776,128]{2,1,0:T(8,128)S(1)} %get-tuple-element.100), channel_id=1, replica_groups=mesh['col'=4,'hgt'=8] {'hgt'}, dimensions={0} | all-to-all | bytes 6356992 | tf_op jit(solution)/shard_map/all_to_all | solution.py:474
  173.5 3.2 %collect.1 = f32[4,384,128]{2,1,0:T(8,128)S(1)} custom-call(f32[8,776,128]{2,1,0:T(8,128)S(1)} %all_to_all.10.blocks), custom_call_target="tpu_custom_call" | custom-call | flops 1610612736 | bytes 3145728 | tf_op jit(solution)/shard_map/collect/pallas_call | solution.py:475
  176.7 24.5 %all_to_all.11 = f32[4,384,128]{2,1,0:T(8,128)S(1)} all-to-all(f32[4,384,128]{2,1,0:T(8,128)S(1)} %collect.1), channel_id=1, replica_groups=mesh['col'=4,'hgt'=8] {'col'}, dimensions={0} | all-to-all | bytes 1572864 | tf_op jit(solution)/shard_map/all_to_all | solution.py:488
  (49 shorter events, 18.0 us)
Async XLA Ops:
  1.8 23.2 %collective-permute-start = (f32[5,24,1024]{2,1,0:T(8,128)S(1)}, f32[5,24,1024]{2,1,0:T(8,128)S(1)}, u32[]{:S(2)}, u32[]{:S(2)}) collective-permute-start(f32[5,24,1024]{2,1,0:T(8,128)S(1)} %get-tuple-element.58), channel_id=1, source_target_pairs={{0,8},{1,9},{2,10},{3,11},{4,12},{5,13},{6,14},{7,15},{8,16},{9,17... | collective-permute-start | bytes 1474568 | tf_op jit(solution)/shard_map/ppermute | solution.py:325
  15.0 10.1 %collective-permute-start.2 = (f32[5,16,1024]{2,1,0:T(8,128)S(1)}, f32[5,16,1024]{2,1,0:T(8,128)S(1)}, u32[]{:S(2)}, u32[]{:S(2)}) collective-permute-start(f32[5,16,1024]{2,1,0:T(8,128)S(1)} %get-tuple-element.60), channel_id=1, source_target_pairs={{0,1},{1,2},{2,3},{3,4},{4,5},{5,6},{6,7},{8,9},{9,10},{10,11},{11... | collective-permute-start | bytes 983048 | tf_op jit(solution)/shard_map/ppermute | solution.py:325
  16.4 8.6 %collective-permute-start.1 = (f32[2,24,1024]{2,1,0:T(8,128)S(1)}, f32[2,24,1024]{2,1,0:T(8,128)S(1)}, u32[]{:S(2)}, u32[]{:S(2)}) collective-permute-start(f32[2,24,1024]{2,1,0:T(8,128)S(1)} %get-tuple-element.59), channel_id=1, source_target_pairs={{8,0},{9,1},{10,2},{11,3},{12,4},{13,5},{14,6},{15,7},{16,8},{17,9... | collective-permute-start | bytes 589832 | tf_op jit(solution)/shard_map/ppermute | solution.py:325
  17.7 5.4 %collective-permute-start.3 = (f32[2,16,1024]{2,1,0:T(8,128)S(1)}, f32[2,16,1024]{2,1,0:T(8,128)S(1)}, u32[]{:S(2)}, u32[]{:S(2)}) collective-permute-start(f32[2,16,1024]{2,1,0:T(8,128)S(1)} %get-tuple-element.61.refs_12_), channel_id=1, source_target_pairs={{1,0},{2,1},{3,2},{4,3},{5,4},{6,5},{7,6},{9,8},{10,9},{11,10},{12... | collective-permute-start | bytes 393224 | tf_op jit(solution)/shard_map/ppermute | solution.py:325
  19.0 0.7 collective-permute-start.4
  19.7 3.4 %collective-permute-start.5 = (f32[1,1024]{1,0:T(1,128)S(1)}, f32[1,1024]{1,0:T(1,128)S(1)}, u32[]{:S(2)}, u32[]{:S(2)}) collective-permute-start(f32[1,1024]{1,0:T(1,128)S(1)} %get-tuple-element.63), channel_id=1, source_target_pairs={{8,1},{9,2},{10,3},{11,4},{12,5},{13,6},{14,7},{16,9},{17,10},{18,... | collective-permute-start | bytes 12296 | tf_op jit(solution)/shard_map/ppermute | solution.py:325
  30.5 20.5 %collective-permute-start.6 = (f32[3,24,1024]{2,1,0:T(8,128)S(1)}, f32[3,24,1024]{2,1,0:T(8,128)S(1)}, u32[]{:S(2)}, u32[]{:S(2)}) collective-permute-start(f32[3,24,1024]{2,1,0:T(8,128)S(1)} %get-tuple-element.66), channel_id=1, source_target_pairs={{0,8},{1,9},{2,10},{3,11},{4,12},{5,13},{6,14},{7,15},{8,16},{9,17... | collective-permute-start | bytes 884744 | tf_op jit(solution)/shard_map/ppermute | solution.py:325
  38.1 12.8 %collective-permute-start.7 = (f32[2,24,1024]{2,1,0:T(8,128)S(1)}, f32[2,24,1024]{2,1,0:T(8,128)S(1)}, u32[]{:S(2)}, u32[]{:S(2)}) collective-permute-start(f32[2,24,1024]{2,1,0:T(8,128)S(1)} %get-tuple-element.67), channel_id=1, source_target_pairs={{8,0},{9,1},{10,2},{11,3},{12,4},{13,5},{14,6},{15,7},{16,8},{17,9... | collective-permute-start | bytes 589832 | tf_op jit(solution)/shard_map/ppermute | solution.py:325
  39.4 11.5 %collective-permute-start.8 = (f32[3,16,1024]{2,1,0:T(8,128)S(1)}, f32[3,16,1024]{2,1,0:T(8,128)S(1)}, u32[]{:S(2)}, u32[]{:S(2)}) collective-permute-start(f32[3,16,1024]{2,1,0:T(8,128)S(1)} %get-tuple-element.68), channel_id=1, source_target_pairs={{0,1},{1,2},{2,3},{3,4},{4,5},{5,6},{6,7},{8,9},{9,10},{10,11},{11... | collective-permute-start | bytes 589832 | tf_op jit(solution)/shard_map/ppermute | solution.py:325
  45.2 4.7 %collective-permute-start.9 = (f32[2,16,1024]{2,1,0:T(8,128)S(1)}, f32[2,16,1024]{2,1,0:T(8,128)S(1)}, u32[]{:S(2)}, u32[]{:S(2)}) collective-permute-start(f32[2,16,1024]{2,1,0:T(8,128)S(1)} %get-tuple-element.69.refs_12_), channel_id=1, source_target_pairs={{1,0},{2,1},{3,2},{4,3},{5,4},{6,5},{7,6},{9,8},{10,9},{11,10},{12... | collective-permute-start | bytes 393224 | tf_op jit(solution)/shard_map/ppermute | solution.py:325
  46.5 0.7 collective-permute-start.10
  47.2 0.7 collective-permute-start.11
  56.5 21.4 %collective-permute-start.12 = (f32[3,24,1024]{2,1,0:T(8,128)S(1)}, f32[3,24,1024]{2,1,0:T(8,128)S(1)}, u32[]{:S(2)}, u32[]{:S(2)}) collective-permute-start(f32[3,24,1024]{2,1,0:T(8,128)S(1)} %get-tuple-element.76), channel_id=1, source_target_pairs={{0,8},{1,9},{2,10},{3,11},{4,12},{5,13},{6,14},{7,15},{8,16},{9,17... | collective-permute-start | bytes 884744 | tf_op jit(solution)/shard_map/ppermute | solution.py:325
  64.2 13.6 %collective-permute-start.13 = (f32[2,24,1024]{2,1,0:T(8,128)S(1)}, f32[2,24,1024]{2,1,0:T(8,128)S(1)}, u32[]{:S(2)}, u32[]{:S(2)}) collective-permute-start(f32[2,24,1024]{2,1,0:T(8,128)S(1)} %get-tuple-element.77), channel_id=1, source_target_pairs={{8,0},{9,1},{10,2},{11,3},{12,4},{13,5},{14,6},{15,7},{16,8},{17,9... | collective-permute-start | bytes 589832 | tf_op jit(solution)/shard_map/ppermute | solution.py:325
  65.5 12.3 %collective-permute-start.14 = (f32[3,16,1024]{2,1,0:T(8,128)S(1)}, f32[3,16,1024]{2,1,0:T(8,128)S(1)}, u32[]{:S(2)}, u32[]{:S(2)}) collective-permute-start(f32[3,16,1024]{2,1,0:T(8,128)S(1)} %get-tuple-element.78), channel_id=1, source_target_pairs={{0,1},{1,2},{2,3},{3,4},{4,5},{5,6},{6,7},{8,9},{9,10},{10,11},{11... | collective-permute-start | bytes 589832 | tf_op jit(solution)/shard_map/ppermute | solution.py:325
  73.1 4.7 %collective-permute-start.15 = (f32[2,16,1024]{2,1,0:T(8,128)S(1)}, f32[2,16,1024]{2,1,0:T(8,128)S(1)}, u32[]{:S(2)}, u32[]{:S(2)}) collective-permute-start(f32[2,16,1024]{2,1,0:T(8,128)S(1)} %get-tuple-element.79.refs_12_), channel_id=1, source_target_pairs={{1,0},{2,1},{3,2},{4,3},{5,4},{6,5},{7,6},{9,8},{10,9},{11,10},{12... | collective-permute-start | bytes 393224 | tf_op jit(solution)/shard_map/ppermute | solution.py:325
  74.4 0.7 collective-permute-start.16
  75.1 0.7 collective-permute-start.17
  83.4 22.5 %collective-permute-start.18 = (f32[3,24,1024]{2,1,0:T(8,128)S(1)}, f32[3,24,1024]{2,1,0:T(8,128)S(1)}, u32[]{:S(2)}, u32[]{:S(2)}) collective-permute-start(f32[3,24,1024]{2,1,0:T(8,128)S(1)} %get-tuple-element.86), channel_id=1, source_target_pairs={{0,8},{1,9},{2,10},{3,11},{4,12},{5,13},{6,14},{7,15},{8,16},{9,17... | collective-permute-start | bytes 884744 | tf_op jit(solution)/shard_map/ppermute | solution.py:325
  92.1 13.8 %collective-permute-start.19 = (f32[2,24,1024]{2,1,0:T(8,128)S(1)}, f32[2,24,1024]{2,1,0:T(8,128)S(1)}, u32[]{:S(2)}, u32[]{:S(2)}) collective-permute-start(f32[2,24,1024]{2,1,0:T(8,128)S(1)} %get-tuple-element.87), channel_id=1, source_target_pairs={{8,0},{9,1},{10,2},{11,3},{12,4},{13,5},{14,6},{15,7},{16,8},{17,9... | collective-permute-start | bytes 589832 | tf_op jit(solution)/shard_map/ppermute | solution.py:325
  93.4 12.5 %collective-permute-start.20 = (f32[3,16,1024]{2,1,0:T(8,128)S(1)}, f32[3,16,1024]{2,1,0:T(8,128)S(1)}, u32[]{:S(2)}, u32[]{:S(2)}) collective-permute-start(f32[3,16,1024]{2,1,0:T(8,128)S(1)} %get-tuple-element.88), channel_id=1, source_target_pairs={{0,1},{1,2},{2,3},{3,4},{4,5},{5,6},{6,7},{8,9},{9,10},{10,11},{11... | collective-permute-start | bytes 589832 | tf_op jit(solution)/shard_map/ppermute | solution.py:325
  101.3 4.6 %collective-permute-start.21 = (f32[2,16,1024]{2,1,0:T(8,128)S(1)}, f32[2,16,1024]{2,1,0:T(8,128)S(1)}, u32[]{:S(2)}, u32[]{:S(2)}) collective-permute-start(f32[2,16,1024]{2,1,0:T(8,128)S(1)} %get-tuple-element.89.refs_12_), channel_id=1, source_target_pairs={{1,0},{2,1},{3,2},{4,3},{5,4},{6,5},{7,6},{9,8},{10,9},{11,10},{12... | collective-permute-start | bytes 393224 | tf_op jit(solution)/shard_map/ppermute | solution.py:325
  102.6 0.7 collective-permute-start.22
  103.2 0.7 collective-permute-start.23
  (3 other events, 40.4 us)

commit v2 on v1

v2 whole, which is shorter than its diff:
```python
import functools

import jax
import jax.numpy as jnp
from jax import lax
from jax.experimental import pallas as pl
from jax.experimental.pallas import tpu as pltpu
from jax.sharding import PartitionSpec as P

PTS = 128
STEPS = 4
COURANT = 0.55
LANES = 128
ROWS = 8
F32 = jnp.float32
VMEM_MIB = 16

WHOLE = pl.BlockSpec(memory_space=pltpu.VMEM)
SCALARS = pl.BlockSpec(memory_space=pltpu.SMEM)
FAR = pl.BlockSpec(memory_space=pltpu.HBM)


def vmem(*shape):
    return pltpu.VMEM(shape, F32)


def far(x):
    return pltpu.with_memory_space_constraint(x, pltpu.HBM)


def params(mib):
    return pltpu.CompilerParams(vmem_limit_bytes=mib << 20)


def cost(flops, moved):
    return pl.CostEstimate(flops=flops, bytes_accessed=moved, transcendentals=0)


def after_y(f):
    lane = lax.broadcasted_iota(jnp.int32, (ROWS, LANES), 1)
    n = f.shape[1] // LANES
    turned = [pltpu.roll(f[:, k * LANES : (k + 1) * LANES], LANES - 1, 1) for k in range(n)]
    turned.append(jnp.zeros((ROWS, LANES), F32))
    return jnp.concatenate([jnp.where(lane < LANES - 1, turned[k], turned[k + 1]) for k in range(n)], 1)


def before_y(f):
    lane = lax.broadcasted_iota(jnp.int32, (ROWS, LANES), 1)
    n = f.shape[1] // LANES
    turned = [jnp.zeros((ROWS, LANES), F32)]
    turned += [pltpu.roll(f[:, k * LANES : (k + 1) * LANES], 1, 1) for k in range(n)]
    return jnp.concatenate([jnp.where(lane > 0, turned[k + 1], turned[k]) for k in range(n)], 1)


def after_row(f, row):
    place = lax.broadcasted_iota(jnp.int32, f.shape, 0)
    return jnp.where(place < ROWS - 1, pltpu.roll(f, ROWS - 1, 0), jnp.broadcast_to(row, f.shape))


def before_row(f, row):
    place = lax.broadcasted_iota(jnp.int32, f.shape, 0)
    return jnp.where(place > 0, pltpu.roll(f, 1, 0), jnp.broadcast_to(row, f.shape))


def edge_kernel(e, back, sem):
    copy = pltpu.make_async_copy(e.at[pl.ds(1, 2), 0], back, sem)
    copy.start()
    copy.wait()


def load_kernel(e_in, order, e, back, sem):
    nx = e.shape[1]
    copy = pltpu.make_async_copy(e_in, e, sem)
    copy.start()
    copy.wait()

    def rows(x, carry):
        for comp in range(2):
            back[comp, pl.ds(x, 1), :] = e[comp, x, 0:1, :]
        return carry

    lax.fori_loop(0, nx, rows, 0)


def coefficients_kernel(temp_far, tags_far, h_far, ca, cb, sigma_out, h, temp, tags, sems):
    nx, nz, _ = temp.shape
    parts = 4
    size = nx // parts
    copies = []
    for part in range(parts):
        here = pl.ds(part * size, size)
        copies.append(pltpu.make_async_copy(temp_far.at[here], temp.at[here], sems.at[0, part]))
        copies.append(pltpu.make_async_copy(tags_far.at[here], tags.at[here], sems.at[1, part]))
    h_copy = pltpu.make_async_copy(h_far, h, sems.at[2, 0])
    for copy in copies:
        copy.start()
    h_copy.start()

    def plane(x, carry):
        for z in range(0, nz, ROWS):
            tag = tags[x, z : z + ROWS, :]
            lean = tag == 0
            fat = tag == 1
            frac = 1.0 / (1.0 + jnp.exp(-2.0 * temp[x, z : z + ROWS, :]))
            eps_low = jnp.where(lean, 4.0, jnp.where(fat, 2.5, 5.0))
            eps_rise = jnp.where(lean, 46.0, jnp.where(fat, 3.5, 5.0))
            sig_low = jnp.where(lean, 0.2, jnp.where(fat, 0.05, 0.1))
            sig_rise = jnp.where(lean, 7.8, jnp.where(fat, 0.35, 0.9))
            eps = eps_low + eps_rise * frac
            sigma = sig_low + sig_rise * frac
            half = (0.5 * COURANT) * sigma
            inverse = 1.0 / (eps + half)
            ca[x, z : z + ROWS, :] = (eps - half) * inverse
            cb[x, z : z + ROWS, :] = COURANT * inverse
            sigma_out[x, z : z + ROWS, :] = sigma
        return carry

    for part in range(parts):
        copies[2 * part].wait()
        copies[2 * part + 1].wait()
        lax.fori_loop(part * size, (part + 1) * size, plane, 0)
    h_copy.wait()


def over(first, stop, body):
    if stop - first == 1:
        body(first)
    else:

        def step(x, carry):
            body(x)
            return carry

        lax.fori_loop(first, stop, step, 0)


def h_tile(e, h, col, hgt, x, z):
    nz = e.shape[2]
    here = slice(z, z + ROWS)
    ex, ey, ez = (e[comp, x, here, :] for comp in range(3))
    if z + ROWS < nz:
        row_x, row_y = (e[comp, x, z + ROWS : z + ROWS + 1, :] for comp in range(2))
    else:
        row_x, row_y = (hgt[comp, pl.ds(x, 1), :] for comp in range(2))
    if col is None:
        next_y, next_z = (e[comp, x + 1, here, :] for comp in (1, 2))
    else:
        next_y, next_z = (col[comp, here, :] for comp in range(2))
    h[0, x, here, :] = h[0, x, here, :] - COURANT * ((after_y(ez) - ez) - (after_row(ey, row_y) - ey))
    hy = h[1, x, here, :] - COURANT * ((after_row(ex, row_x) - ex) - (next_z - ez))
    hz = h[2, x, here, :] - COURANT * ((next_y - ey) - (after_y(ex) - ex))
    h[1, x, here, :] = hy
    h[2, x, here, :] = hz
    return hy, hz


def e_tile(first, h, e, power, ca, cb, sigma, col, hgt, x, z):
    here = slice(z, z + ROWS)
    hx, hy, hz = (h[comp, x, here, :] for comp in range(3))
    if z > 0:
        row_x, row_y = (h[comp, x, z - 1 : z, :] for comp in range(2))
    else:
        row_x, row_y = (hgt[comp, pl.ds(x, 1), :] for comp in range(2))
    if col is None:
        past_y, past_z = (h[comp, x - 1, here, :] for comp in (1, 2))
    else:
        past_y, past_z = (col[comp, here, :] for comp in range(2))
    keep = ca[x, here, :]
    drive = cb[x, here, :]
    ex = keep * e[0, x, here, :] + drive * ((hz - before_y(hz)) - (hy - before_row(hy, row_y)))
    ey = keep * e[1, x, here, :] + drive * ((hx - before_row(hx, row_x)) - (hz - past_z))
    ez = keep * e[2, x, here, :] + drive * ((hy - past_y) - (hx - before_y(hx)))
    e[0, x, here, :] = ex
    e[1, x, here, :] = ey
    e[2, x, here, :] = ez
    heat = sigma[x, here, :] * (ex * ex + ey * ey + ez * ez)
    power[x, here, :] = heat if first else power[x, here, :] + heat
    return ey, ez


def h_inner_kernel(e, h_old, h):
    nx, nz = e.shape[1:3]

    def plane(x):
        for z in range(0, nz - ROWS, ROWS):
            h_tile(e, h, None, None, x, z)

    over(0, nx - 1, plane)


def h_plane_kernel(e, col, hgt, h_old, h, send):
    nx, nz = e.shape[1:3]
    for z in range(0, nz, ROWS):
        hy, hz = h_tile(e, h, col, hgt, nx - 1, z)
        send[0, z : z + ROWS, :] = hy
        send[1, z : z + ROWS, :] = hz


def h_rows_kernel(e, hgt, h_old, h, send):
    nx, nz = e.shape[1:3]

    def keep(x):
        for comp in range(2):
            send[comp, pl.ds(x, 1), :] = h[comp, x, nz - 1 : nz, :]

    def plane(x):
        h_tile(e, h, None, hgt, x, nz - ROWS)
        keep(x)

    over(0, nx - 1, plane)
    keep(nx - 1)


def e_inner_kernel(first, h, ca, cb, sigma, *refs):
    e, power = refs[-2:]
    nx, nz = e.shape[1:3]

    def plane(x):
        for z in range(ROWS, nz, ROWS):
            e_tile(first, h, e, power, ca, cb, sigma, None, None, x, z)

    over(1, nx, plane)


def e_plane_kernel(first, h, ca, cb, sigma, col, hgt, e_old, power_old, e, power, *send):
    nz = e.shape[2]
    for z in range(0, nz, ROWS):
        ey, ez = e_tile(first, h, e, power, ca, cb, sigma, col, hgt, 0, z)
        if send:
            send[0][0, z : z + ROWS, :] = ey
            send[0][1, z : z + ROWS, :] = ez


def e_rows_kernel(first, h, ca, cb, sigma, hgt, e_old, power_old, e, power, *send):
    nx = e.shape[1]

    def keep(x):
        if send:
            for comp in range(2):
                send[0][comp, pl.ds(x, 1), :] = e[comp, x, 0:1, :]

    def plane(x):
        e_tile(first, h, e, power, ca, cb, sigma, None, hgt, x, 0)
        keep(x)

    keep(0)
    over(1, nx, plane)


def places_kernel(n_col, n_hgt, cap, extra, owner, node, place, nodes_out):
    n_dev = n_col * n_hgt
    count = owner.shape[1]
    width = 256
    rows = lax.broadcasted_iota(jnp.int32, (n_dev, width), 0)
    before = lax.broadcasted_iota(jnp.int32, (width, width), 0)
    after = lax.broadcasted_iota(jnp.int32, (width, width), 1)
    upper = jnp.where(before <= after, 1.0, 0.0).astype(jnp.bfloat16)
    room_for = nodes_out.shape[0] // n_dev * LANES
    room = lax.broadcasted_iota(jnp.int32, (room_for, width), 0)
    total = jnp.zeros((n_dev, 1), F32)
    high = jnp.zeros((n_dev, room_for), F32)
    low = jnp.zeros((n_dev, room_for), F32)
    nt = (((1,), (1,)), ((), ()))
    for start in range(0, count, width):
        own = owner[:, start : start + width]
        target = lax.rem(own, n_hgt) * n_col + lax.div(own, n_hgt)
        hit = jnp.where(rows == target, 1.0, 0.0)
        running = total + jnp.dot(hit.astype(jnp.bfloat16), upper, preferred_element_type=F32)
        total = running[:, width - 1 : width]
        rank = jnp.sum(hit * running, axis=0, keepdims=True).astype(jnp.int32) - 1
        group = lax.div(target, n_col)
        place[:, start : start + width] = target * cap + group * extra + rank
        number = node[:, start : start + width]
        upper_part = lax.div(number, 16)
        lower_part = number - 16 * upper_part
        seat = jnp.where(room == rank, 1.0, 0.0).astype(jnp.bfloat16)
        high = high + lax.dot_general(
            (hit * upper_part.astype(F32)).astype(jnp.bfloat16), seat, nt, preferred_element_type=F32
        )
        low = low + lax.dot_general(
            (hit * lower_part.astype(F32)).astype(jnp.bfloat16), seat, nt, preferred_element_type=F32
        )
    taken = lax.broadcasted_iota(jnp.int32, (n_dev, room_for), 1).astype(F32) < total
    table = jnp.where(taken, 16.0 * high + low, -1.0)
    parts = room_for // LANES
    for part in range(parts):
        nodes_out[pl.ds(part, n_dev, stride=parts), :] = table[:, part * LANES : (part + 1) * LANES]


def pack_kernel(place, power, nodes, e, h, out, e_out, h_out, sems):
    nx, nz, ny = power.shape
    e_copy = pltpu.make_async_copy(e, e_out, sems.at[0])
    h_copy = pltpu.make_async_copy(h, h_out, sems.at[1])
    e_copy.start()
    h_copy.start()
    n_group, rows, _ = out.shape
    per_row = ny // PTS
    extra = nodes.shape[0] // n_group
    flat = out.reshape(n_group * rows, PTS)

    def clear(group, carry):
        out[group] = jnp.zeros((rows, PTS), F32)
        out[group, rows - extra : rows, :] = nodes[pl.ds(pl.multiple_of(group * extra, ROWS), extra), :]
        return carry

    lax.fori_loop(0, n_group, clear, 0)

    def plane(x, carry):
        for z in range(nz):
            for k in range(per_row):
                spot = place[x * (nz * per_row) + z * per_row + k]
                flat[pl.ds(spot, 1), :] = power[x, z : z + 1, k * PTS : (k + 1) * PTS]
        return carry

    lax.fori_loop(0, nx, plane, 0)
    e_copy.wait()
    h_copy.wait()


def collect_kernel(cap, blocks, out, chosen, split):
    n_from, rows, pts = blocks.shape
    n_part, node_count, _ = out.shape
    room = chosen.shape[1] // n_from
    parts = room // LANES
    ids = lax.broadcasted_iota(jnp.int32, (node_count, LANES), 0).astype(F32)
    split[...] = jnp.zeros(split.shape, split.dtype)
    for part in range(n_part):
        for source in range(n_from):
            for piece in range(parts):
                row = n_part * cap + part * parts + piece
                lanes = slice(source * room + piece * LANES, source * room + (piece + 1) * LANES)
                hit = ids == blocks[source, row : row + 1, :]
                chosen[:, lanes] = jnp.where(hit, 1.0, 0.0).astype(jnp.bfloat16)
            values = blocks[source, part * cap : (part + 1) * cap, :]
            high = values.astype(jnp.bfloat16)
            here = slice(source * room, source * room + cap)
            split[here, 0:pts] = high
            split[here, pts : 2 * pts] = (values - high.astype(F32)).astype(jnp.bfloat16)
        both = jnp.dot(chosen[...], split[...], preferred_element_type=F32)
        out[part] = both[:, 0:pts] + both[:, pts : 2 * pts]


def shifted(block, d_col, d_hgt):
    n_col = lax.axis_size("col")
    n_hgt = lax.axis_size("hgt")
    route = [
        (c * n_hgt + h, (c + d_col) * n_hgt + h + d_hgt)
        for c in range(n_col)
        for h in range(n_hgt)
        if 0 <= c + d_col < n_col and 0 <= h + d_hgt < n_hgt
    ]
    return lax.ppermute(block, ("col", "hgt"), route)


def tissue_warmth_kelvin(heat_content_per_mass):
    return jnp.where(
        heat_content_per_mass < 0.0,
        heat_content_per_mass / 2.0,
        jnp.where(heat_content_per_mass > 1.0, (heat_content_per_mass - 1.0) / 3.0, 0.0),
    )


def per_device(
    efield_lattice_vector,
    hfield_lattice_vector,
    cell_temp,
    region_tags,
    block_owner,
    block_node,
    node_enthalpy,
):
    nx, nz, ny = cell_temp.shape
    n_col = lax.axis_size("col")
    n_hgt = lax.axis_size("hgt")
    n_dev = n_col * n_hgt
    count = nx * nz * ny // PTS
    cap = 2 * count // n_dev
    node_count = node_enthalpy.shape[0]
    cells = nx * nz * ny
    sem = pltpu.SemaphoreType.DMA

    def kernel(body, outs, ins, args, name, work, aliases=None, scratch=()):
        return pl.pallas_call(
            body,
            out_shape=outs,
            in_specs=ins,
            out_specs=jax.tree.map(lambda out: WHOLE, outs),
            input_output_aliases=aliases or {},
            scratch_shapes=scratch,
            compiler_params=params(VMEM_MIB),
            cost_estimate=cost(work * cells, work * cells),
            name=name,
        )(*args)

    e_start = far(efield_lattice_vector)
    h_start = far(hfield_lattice_vector)
    owners = block_owner.reshape(1, count)
    nodes = block_node.reshape(1, count)
    field = vmem(3, nx, nz, ny)
    whole = vmem(nx, nz, ny)
    planes = vmem(2, nz, ny)
    rows = vmem(2, nx, ny)

    to_col = kernel(edge_kernel, planes, [FAR], [e_start], "edge", 1, scratch=[sem])
    col = shifted(to_col, -1, 0)
    e, to_hgt = kernel(load_kernel, (field, rows), [FAR, WHOLE], [e_start, owners + nodes], "load", 24, scratch=[sem])
    hgt = shifted(to_hgt, 0, -1)
    ca, cb, sigma, h = kernel(
        coefficients_kernel,
        (whole, whole, whole, field),
        [FAR] * 3,
        [far(cell_temp), far(region_tags), h_start],
        "coefficients",
        40,
        scratch=[pltpu.VMEM((nx, nz, ny), F32), pltpu.VMEM((nx, nz, ny), jnp.int32), sem((3, 4))],
    )
    room_for = -(-cap // LANES) * LANES
    extra = -(-(n_col * room_for // LANES) // ROWS) * ROWS
    place, send_nodes = kernel(
        functools.partial(places_kernel, n_col, n_hgt, cap, extra),
        (jax.ShapeDtypeStruct((1, count), jnp.int32), jax.ShapeDtypeStruct((n_hgt * extra, PTS), F32)),
        [WHOLE] * 2,
        [owners, nodes],
        "places",
        8,
    )
    power = None
    for step in range(STEPS):
        first = step == 0
        last = step == STEPS - 1
        h = kernel(h_inner_kernel, field, [WHOLE] * 2, [e, h], f"h_inner_{step}", 25, {1: 0})
        h, to_col = kernel(
            h_plane_kernel, (field, planes), [WHOLE] * 4, [e, col, hgt, h], f"h_plane_{step}", 2, {3: 0}
        )
        col = shifted(to_col, 1, 0)
        h, to_hgt = kernel(h_rows_kernel, (field, rows), [WHOLE] * 3, [e, hgt, h], f"h_rows_{step}", 12, {2: 0})
        hgt = shifted(to_hgt, 0, 1)
        media = [h, ca, cb, sigma]
        if first:
            e, power = kernel(
                functools.partial(e_inner_kernel, first),
                (field, whole),
                [WHOLE] * 5,
                media + [e],
                f"e_inner_{step}",
                30,
                {4: 0},
            )
        else:
            e, power = kernel(
                functools.partial(e_inner_kernel, first),
                (field, whole),
                [WHOLE] * 6,
                media + [e, power],
                f"e_inner_{step}",
                30,
                {4: 0, 5: 1},
            )
        outs = kernel(
            functools.partial(e_plane_kernel, first),
            (field, whole) if last else (field, whole, planes),
            [WHOLE] * 8,
            media + [col, hgt, e, power],
            f"e_plane_{step}",
            3,
            {6: 0, 7: 1},
        )
        e, power = outs[:2]
        if not last:
            col = shifted(outs[2], -1, 0)
        outs = kernel(
            functools.partial(e_rows_kernel, first),
            (field, whole) if last else (field, whole, rows),
            [WHOLE] * 7,
            media + [hgt, e, power],
            f"e_rows_{step}",
            15,
            {5: 0, 6: 1},
        )
        e, power = outs[:2]
        if not last:
            hgt = shifted(outs[2], 0, -1)

    send, e_out, h_out = pl.pallas_call(
        pack_kernel,
        out_shape=(
            jax.ShapeDtypeStruct((n_hgt, n_col * cap + extra, PTS), F32),
            pltpu.HBM((3, nx, nz, ny), F32),
            pltpu.HBM((3, nx, nz, ny), F32),
        ),
        in_specs=[SCALARS, WHOLE, WHOLE, WHOLE, WHOLE],
        out_specs=(WHOLE, FAR, FAR),
        scratch_shapes=[sem((2,))],
        compiler_params=params(VMEM_MIB),
        cost_estimate=cost(cells, cells * 36),
        name="pack",
    )(place.reshape(count), power, send_nodes, e, h)
    blocks = lax.all_to_all(send, "hgt", split_axis=0, concat_axis=0, tiled=True)
    partial = pl.pallas_call(
        functools.partial(collect_kernel, cap),
        out_shape=jax.ShapeDtypeStruct((n_col, node_count, PTS), F32),
        in_specs=[WHOLE],
        out_specs=WHOLE,
        scratch_shapes=[
            pltpu.VMEM((node_count, n_hgt * room_for), jnp.bfloat16),
            pltpu.VMEM((n_hgt * room_for, 2 * PTS), jnp.bfloat16),
        ],
        compiler_params=params(VMEM_MIB),
        cost_estimate=cost(n_col * node_count * n_hgt * room_for * PTS * 4, cells * 8),
        name="collect",
    )(blocks)
    parts = lax.all_to_all(partial, "col", split_axis=0, concat_axis=0, tiled=True)
    heat = jnp.sum(parts, axis=0)
    heat_content_per_mass = node_enthalpy + (0.25 / STEPS) * heat
    return e_out, h_out, tissue_warmth_kelvin(heat_content_per_mass)


def solution(mesh):
    placed = (
        P(None, "col", "hgt", None),
        P(None, "col", "hgt", None),
        P("col", "hgt", None),
        P("col", "hgt", None),
        P("col", "hgt", None, None, None, None),
        P("col", "hgt", None, None, None),
        P(("col", "hgt"), None),
    )
    return jax.shard_map(
        per_device,
        mesh=mesh,
        in_specs=placed,
        out_specs=(
            P(None, "col", "hgt", None),
            P(None, "col", "hgt", None),
            P(("col", "hgt"), None),
        ),
        check_vma=False,
    )
```

time: 203 us -> 166 us (0.82)
  starting transfers between devices: 67.3 us -> 43 us
  blocking collectives: 82.5 us -> 66.6 us
  Pallas kernels: 40.7 us -> 43.5 us
    ppermute x24 -> x16, starting transfers between devices: 67.3 us -> 43 us  [shifted(): return lax.ppermute(block, ('col', 'hgt'), route)]
    all_to_all x1, blocking collectives: 58 us -> 42.7 us  [per_device(): lax.all_to_all(send, 'hgt', split_axis=0, concat_axis=0, tiled=True)]
    pallas_call x8 -> x28, Pallas kernels: 33 us -> 35.8 us  [kernel(): pl.pallas_call(body, out_shape=outs, in_specs=ins, out_specs=jax.tree.map...]
    ppermute x24 -> x16, waiting for transfers between devices: 9.11 us -> 10.3 us  [shifted(): return lax.ppermute(block, ('col', 'hgt'), route)]
  transfers between devices with their start and end apart: 24 -> 16, of which waited for: 5 -> 6; matrix products, arithmetic and copies ran while one was open for 0% -> 0% of each run, Pallas kernels for 5% -> 19%
where the time goes in v2:
time: 166 us
  blocking collectives  66.6 us (40%)
  Pallas kernels  43.5 us (26%)
  starting transfers between devices  43 us (26%)
  waiting for transfers between devices  10.3 us (6%)
    ppermute x16, starting transfers between devices, shifted(): return lax.ppermute(block, ('col', 'hgt'), route)  43 us
    all_to_all x1, blocking collectives, per_device(): lax.all_to_all(send, 'hgt', split_axis=0, concat_axis=0, tiled=True)  42.7 us
    pallas_call x28, Pallas kernels, kernel(): pl.pallas_call(body, out_shape=outs, in_specs=ins, out_specs=jax.tree.map...  35.8 us
    all_to_all x1, blocking collectives, per_device(): lax.all_to_all(partial, 'col', split_axis=0, concat_axis=0, tiled=True)  23.9 us
    ppermute x16, waiting for transfers between devices, shifted(): return lax.ppermute(block, ('col', 'hgt'), route)  10.3 us
    pallas_call x1, Pallas kernels, per_device(): pl.pallas_call(pack_kernel, out_shape=(jax.ShapeDtypeStruct((n_hgt, n_col...  4.49 us
  transfers between devices with their start and end apart: 16, of which 6 were waited for; matrix products, arithmetic and copies ran while one was open for 0% of the time, Pallas kernels for 19%

profile of v2, /device:TPU:0, one launch (start us, length us, event | category | flops | bytes accessed | tf_op | source)
XLA Modules:
  0.0 165.8 jit_solution(8442587463158823391)
XLA Ops:
  3.5 2.4 %load.1 = (f32[3,16,24,1024]{3,2,1,0:T(8,128)S(1)}, f32[2,16,1024]{2,1,0:T(8,128)S(1)}) custom-call(f32[3,16,24,1024]{3,2,1,0:T(8,128)} %e.1, s32[1,3072]{1,0:T(1,128)S(1)} %add.7.order), custom_call_target="tpu_custom_call" | custom-call | flops 9437184 | bytes 9437184 | tf_op jit(solution)/shard_map/load/pallas_call | solution.py:383
  7.2 3.4 %coefficients.1 = (f32[16,24,1024]{2,1,0:T(8,128)S(1)}, f32[16,24,1024]{2,1,0:T(8,128)S(1)}, f32[16,24,1024]{2,1,0:T(8,128)S(1)}, f32[3,16,24,1024]{3,2,1,0:T(8,128)S(1)}) custom-call(f32[16,24,1024]{2,1,0:T(8,128)} %temp_far.1, s32[16,24,1024]{2,1,0:T(8,128)} %tags_far.1, f32[3,16,24,1024]{3,2,1,0:T(8,128)} %h_far.1), custom_call_target="tpu_custom_call" | custom-call | flops 15728640 | bytes 15728640 | tf_op jit(solution)/shard_map/coefficients/pallas_call | solution.py:383
  10.7 1.6 h_inner_0.1.h_old
  12.4 5.6 %collective-permute-start.3 = (f32[2,24,1024]{2,1,0:T(8,128)S(1)}, f32[2,24,1024]{2,1,0:T(8,128)S(1)}, u32[]{:S(2)}, u32[]{:S(2)}) collective-permute-start(f32[2,24,1024]{2,1,0:T(8,128)S(1)} %get-tuple-element.70), channel_id=1, source_target_pairs={{0,8},{1,9},{2,10},{3,11},{4,12},{5,13},{6,14},{7,15},{8,16},{9,17... | collective-permute-start | bytes 589832 | tf_op jit(solution)/shard_map/ppermute | solution.py:352
  19.4 2.8 %collective-permute-start.2 = (f32[2,16,1024]{2,1,0:T(8,128)S(1)}, f32[2,16,1024]{2,1,0:T(8,128)S(1)}, u32[]{:S(2)}, u32[]{:S(2)}) collective-permute-start(f32[2,16,1024]{2,1,0:T(8,128)S(1)} %get-tuple-element.69), channel_id=1, source_target_pairs={{0,1},{1,2},{2,3},{3,4},{4,5},{5,6},{6,7},{8,9},{9,10},{10,11},{11... | collective-permute-start | bytes 393224 | tf_op jit(solution)/shard_map/ppermute | solution.py:352
  22.2 1.8 %e_inner_0.1 = (f32[3,16,24,1024]{3,2,1,0:T(8,128)S(1)}, f32[16,24,1024]{2,1,0:T(8,128)S(1)}) custom-call(f32[3,16,24,1024]{3,2,1,0:T(8,128)S(1)} %get-tuple-element.65.h.h_old, f32[16,24,1024]{2,1,0:T(8,128)S(1)} %get-tuple-element.66.ca, f32[16,24,1024]{2,1,0:T(8,128)S(1)} %get-tuple-element.67.cb, ...), custom_call_target="tpu_custom_call", output_to_operand_aliasing={{0}: (4, {})} | custom-call | flops 11796480 | bytes 11796480 | tf_op jit(solution)/shard_map/e_inner_0/pallas_call | solution.py:383
  28.2 1.6 h_inner_1.1.h_old
  29.8 1.8 %collective-permute-done.4.hgt = f32[2,16,1024]{2,1,0:T(8,128)S(1)} collective-permute-done((f32[2,16,1024]{2,1,0:T(8,128)S(1)}, f32[2,16,1024]{2,1,0:T(8,128)S(1)}, u32[]{:S(2)}, u32[]{:S(2)}) %collective-permute-start.4) | collective-permute-done | bytes 131104 | tf_op jit(solution)/shard_map/ppermute | solution.py:352
  32.9 4.4 %collective-permute-start.7 = (f32[2,24,1024]{2,1,0:T(8,128)S(1)}, f32[2,24,1024]{2,1,0:T(8,128)S(1)}, u32[]{:S(2)}, u32[]{:S(2)}) collective-permute-start(f32[2,24,1024]{2,1,0:T(8,128)S(1)} %get-tuple-element.81), channel_id=1, source_target_pairs={{0,8},{1,9},{2,10},{3,11},{4,12},{5,13},{6,14},{7,15},{8,16},{9,17... | collective-permute-start | bytes 589832 | tf_op jit(solution)/shard_map/ppermute | solution.py:352
  38.7 4.8 %collective-permute-start.6 = (f32[2,16,1024]{2,1,0:T(8,128)S(1)}, f32[2,16,1024]{2,1,0:T(8,128)S(1)}, u32[]{:S(2)}, u32[]{:S(2)}) collective-permute-start(f32[2,16,1024]{2,1,0:T(8,128)S(1)} %get-tuple-element.80), channel_id=1, source_target_pairs={{0,1},{1,2},{2,3},{3,4},{4,5},{5,6},{6,7},{8,9},{9,10},{10,11},{11... | collective-permute-start | bytes 393224 | tf_op jit(solution)/shard_map/ppermute | solution.py:352
  43.6 1.8 %e_inner_1.1 = (f32[3,16,24,1024]{3,2,1,0:T(8,128)S(1)}, f32[16,24,1024]{2,1,0:T(8,128)S(1)}) custom-call(f32[3,16,24,1024]{3,2,1,0:T(8,128)S(1)} %get-tuple-element.79.h.h_old, f32[16,24,1024]{2,1,0:T(8,128)S(1)} %get-tuple-element.66.ca, f32[16,24,1024]{2,1,0:T(8,128)S(1)} %get-tuple-element.67.cb, ...), custom_call_target="tpu_custom_call", output_to_operand_aliasing={{0}: (4, {}), {1}: (5, {})} | custom-call | flops 11796480 | bytes 11796480 | tf_op jit(solution)/shard_map/e_inner_1/pallas_call | solution.py:383
  51.6 3.1 %collective-permute-done.9.col = f32[2,24,1024]{2,1,0:T(8,128)S(1)} collective-permute-done((f32[2,24,1024]{2,1,0:T(8,128)S(1)}, f32[2,24,1024]{2,1,0:T(8,128)S(1)}, u32[]{:S(2)}, u32[]{:S(2)}) %collective-permute-start.9) | collective-permute-done | bytes 196640 | tf_op jit(solution)/shard_map/ppermute | solution.py:352
  54.8 3.5 %collective-permute-start.11 = (f32[2,24,1024]{2,1,0:T(8,128)S(1)}, f32[2,24,1024]{2,1,0:T(8,128)S(1)}, u32[]{:S(2)}, u32[]{:S(2)}) collective-permute-start(f32[2,24,1024]{2,1,0:T(8,128)S(1)} %get-tuple-element.93), channel_id=1, source_target_pairs={{0,8},{1,9},{2,10},{3,11},{4,12},{5,13},{6,14},{7,15},{8,16},{9,17... | collective-permute-start | bytes 589832 | tf_op jit(solution)/shard_map/ppermute | solution.py:352
  59.7 4.0 %collective-permute-start.10 = (f32[2,16,1024]{2,1,0:T(8,128)S(1)}, f32[2,16,1024]{2,1,0:T(8,128)S(1)}, u32[]{:S(2)}, u32[]{:S(2)}) collective-permute-start(f32[2,16,1024]{2,1,0:T(8,128)S(1)} %get-tuple-element.92), channel_id=1, source_target_pairs={{0,1},{1,2},{2,3},{3,4},{4,5},{5,6},{6,7},{8,9},{9,10},{10,11},{11... | collective-permute-start | bytes 393224 | tf_op jit(solution)/shard_map/ppermute | solution.py:352
  63.7 1.8 %e_inner_2.1 = (f32[3,16,24,1024]{3,2,1,0:T(8,128)S(1)}, f32[16,24,1024]{2,1,0:T(8,128)S(1)}) custom-call(f32[3,16,24,1024]{3,2,1,0:T(8,128)S(1)} %get-tuple-element.91.h.h_old, f32[16,24,1024]{2,1,0:T(8,128)S(1)} %get-tuple-element.66.ca, f32[16,24,1024]{2,1,0:T(8,128)S(1)} %get-tuple-element.67.cb, ...), custom_call_target="tpu_custom_call", output_to_operand_aliasing={{0}: (4, {}), {1}: (5, {})} | custom-call | flops 11796480 | bytes 11796480 | tf_op jit(solution)/shard_map/e_inner_2/pallas_call | solution.py:383
  72.2 3.1 %collective-permute-done.13.col = f32[2,24,1024]{2,1,0:T(8,128)S(1)} collective-permute-done((f32[2,24,1024]{2,1,0:T(8,128)S(1)}, f32[2,24,1024]{2,1,0:T(8,128)S(1)}, u32[]{:S(2)}, u32[]{:S(2)}) %collective-permute-start.13) | collective-permute-done | bytes 196640 | tf_op jit(solution)/shard_map/ppermute | solution.py:352
  75.4 3.5 %collective-permute-start.15 = (f32[2,24,1024]{2,1,0:T(8,128)S(1)}, f32[2,24,1024]{2,1,0:T(8,128)S(1)}, u32[]{:S(2)}, u32[]{:S(2)}) collective-permute-start(f32[2,24,1024]{2,1,0:T(8,128)S(1)} %get-tuple-element.105), channel_id=1, source_target_pairs={{0,8},{1,9},{2,10},{3,11},{4,12},{5,13},{6,14},{7,15},{8,16},{9,17... | collective-permute-start | bytes 589832 | tf_op jit(solution)/shard_map/ppermute | solution.py:352
  80.3 4.1 %collective-permute-start.14 = (f32[2,16,1024]{2,1,0:T(8,128)S(1)}, f32[2,16,1024]{2,1,0:T(8,128)S(1)}, u32[]{:S(2)}, u32[]{:S(2)}) collective-permute-start(f32[2,16,1024]{2,1,0:T(8,128)S(1)} %get-tuple-element.104), channel_id=1, source_target_pairs={{0,1},{1,2},{2,3},{3,4},{4,5},{5,6},{6,7},{8,9},{9,10},{10,11},{11... | collective-permute-start | bytes 393224 | tf_op jit(solution)/shard_map/ppermute | solution.py:352
  84.4 2.8 %places.1 = (s32[1,3072]{1,0:T(1,128)S(1)}, f32[64,128]{1,0:T(8,128)S(1)}) custom-call(s32[1,3072]{1,0:T(1,128)S(1)} %reshape.35.owner, s32[1,3072]{1,0:T(1,128)S(1)} %reshape.36.node), custom_call_target="tpu_custom_call" | custom-call | flops 3145728 | bytes 3145728 | tf_op jit(solution)/shard_map/places/pallas_call | solution.py:383
  87.2 1.8 %e_inner_3.1 = (f32[3,16,24,1024]{3,2,1,0:T(8,128)S(1)}, f32[16,24,1024]{2,1,0:T(8,128)S(1)}) custom-call(f32[3,16,24,1024]{3,2,1,0:T(8,128)S(1)} %get-tuple-element.103.h, f32[16,24,1024]{2,1,0:T(8,128)S(1)} %get-tuple-element.66.ca, f32[16,24,1024]{2,1,0:T(8,128)S(1)} %get-tuple-element.67.cb, ...), custom_call_target="tpu_custom_call", output_to_operand_aliasing={{0}: (4, {}), {1}: (5, {})} | custom-call | flops 11796480 | bytes 11796480 | tf_op jit(solution)/shard_map/e_inner_3/pallas_call | solution.py:383
  90.7 4.5 %pack.1 = (f32[8,776,128]{2,1,0:T(8,128)S(1)}, f32[3,16,24,1024]{3,2,1,0:T(8,128)}, f32[3,16,24,1024]{3,2,1,0:T(8,128)}) custom-call(s32[3072]{0:T(1024)S(1)} %bitcast.7, f32[16,24,1024]{2,1,0:T(8,128)S(1)} %get-tuple-element.111.power, f32[64,128]{1,0:T(8,128)S(1)} %get-tuple-element.112.nodes, f32[3,16,24,1024]{3,2,1,0:T(8,128)S(1)} %get-tuple-element.113.e, ...), custom_call_target="tpu_custom_call" | custom-call | flops 393216 | bytes 14155776 | tf_op jit(solution)/shard_map/pack/pallas_call | solution.py:484
  95.2 42.7 %all_to_all.10.blocks = f32[8,776,128]{2,1,0:T(8,128)S(1)} all-to-all(f32[8,776,128]{2,1,0:T(8,128)S(1)} %get-tuple-element.116), channel_id=1, replica_groups=mesh['col'=4,'hgt'=8] {'hgt'}, dimensions={0} | all-to-all | bytes 6356992 | tf_op jit(solution)/shard_map/all_to_all | solution.py:498
  137.9 3.2 %collect.1 = f32[4,384,128]{2,1,0:T(8,128)S(1)} custom-call(f32[8,776,128]{2,1,0:T(8,128)S(1)} %all_to_all.10.blocks), custom_call_target="tpu_custom_call" | custom-call | flops 1610612736 | bytes 3145728 | tf_op jit(solution)/shard_map/collect/pallas_call | solution.py:499
  141.2 23.9 %all_to_all.11 = f32[4,384,128]{2,1,0:T(8,128)S(1)} all-to-all(f32[4,384,128]{2,1,0:T(8,128)S(1)} %collect.1), channel_id=1, replica_groups=mesh['col'=4,'hgt'=8] {'col'}, dimensions={0} | all-to-all | bytes 1572864 | tf_op jit(solution)/shard_map/all_to_all | solution.py:512
  (53 shorter events, 30.6 us)
Async XLA Ops:
  0.6 2.3 %copy-start.1 = (s32[1,1,16,24,8,1]{3,5,4,2,1,0:T(1,128)S(1)}, s32[1,1,16,24,8,1]{3,5,4,2,1,0:T(1,128)}, u32[]{:S(2)}) copy-start(s32[1,1,16,24,8,1]{3,5,4,2,1,0:T(1,128)} %param.11) | copy-start | bytes 36868
  0.6 2.6 %copy-start.2 = (s32[1,1,16,24,8]{3,4,2,1,0:T(8,128)S(1)}, s32[1,1,16,24,8]{3,4,2,1,0:T(8,128)}, u32[]{:S(2)}) copy-start(s32[1,1,16,24,8]{3,4,2,1,0:T(8,128)} %param.12) | copy-start | bytes 36868
  1.6 10.7 %collective-permute-start.1 = (f32[2,24,1024]{2,1,0:T(8,128)S(1)}, f32[2,24,1024]{2,1,0:T(8,128)S(1)}, u32[]{:S(2)}, u32[]{:S(2)}) collective-permute-start(f32[2,24,1024]{2,1,0:T(8,128)S(1)} %edge.1), channel_id=1, source_target_pairs={{8,0},{9,1},{10,2},{11,3},{12,4},{13,5},{14,6},{15,7},{16,8},{17,9... | collective-permute-start | bytes 589832 | tf_op jit(solution)/shard_map/ppermute | solution.py:352
  5.9 6.4 %collective-permute-start = (f32[2,16,1024]{2,1,0:T(8,128)S(1)}, f32[2,16,1024]{2,1,0:T(8,128)S(1)}, u32[]{:S(2)}, u32[]{:S(2)}) collective-permute-start(f32[2,16,1024]{2,1,0:T(8,128)S(1)} %get-tuple-element.62), channel_id=1, source_target_pairs={{1,0},{2,1},{3,2},{4,3},{5,4},{6,5},{7,6},{9,8},{10,9},{11,10},{12... | collective-permute-start | bytes 393224 | tf_op jit(solution)/shard_map/ppermute | solution.py:352
  12.4 11.5 %collective-permute-start.3 = (f32[2,24,1024]{2,1,0:T(8,128)S(1)}, f32[2,24,1024]{2,1,0:T(8,128)S(1)}, u32[]{:S(2)}, u32[]{:S(2)}) collective-permute-start(f32[2,24,1024]{2,1,0:T(8,128)S(1)} %get-tuple-element.70), channel_id=1, source_target_pairs={{0,8},{1,9},{2,10},{3,11},{4,12},{5,13},{6,14},{7,15},{8,16},{9,17... | collective-permute-start | bytes 589832 | tf_op jit(solution)/shard_map/ppermute | solution.py:352
  19.4 4.5 %collective-permute-start.2 = (f32[2,16,1024]{2,1,0:T(8,128)S(1)}, f32[2,16,1024]{2,1,0:T(8,128)S(1)}, u32[]{:S(2)}, u32[]{:S(2)}) collective-permute-start(f32[2,16,1024]{2,1,0:T(8,128)S(1)} %get-tuple-element.69), channel_id=1, source_target_pairs={{0,1},{1,2},{2,3},{3,4},{4,5},{5,6},{6,7},{8,9},{9,10},{10,11},{11... | collective-permute-start | bytes 393224 | tf_op jit(solution)/shard_map/ppermute | solution.py:352
  24.1 8.7 %collective-permute-start.5 = (f32[2,24,1024]{2,1,0:T(8,128)S(1)}, f32[2,24,1024]{2,1,0:T(8,128)S(1)}, u32[]{:S(2)}, u32[]{:S(2)}) collective-permute-start(f32[2,24,1024]{2,1,0:T(8,128)S(1)} %get-tuple-element.77), channel_id=1, source_target_pairs={{8,0},{9,1},{10,2},{11,3},{12,4},{13,5},{14,6},{15,7},{16,8},{17,9... | collective-permute-start | bytes 589832 | tf_op jit(solution)/shard_map/ppermute | solution.py:352
  26.9 4.7 %collective-permute-start.4 = (f32[2,16,1024]{2,1,0:T(8,128)S(1)}, f32[2,16,1024]{2,1,0:T(8,128)S(1)}, u32[]{:S(2)}, u32[]{:S(2)}) collective-permute-start(f32[2,16,1024]{2,1,0:T(8,128)S(1)} %get-tuple-element.76), channel_id=1, source_target_pairs={{1,0},{2,1},{3,2},{4,3},{5,4},{6,5},{7,6},{9,8},{10,9},{11,10},{12... | collective-permute-start | bytes 393224 | tf_op jit(solution)/shard_map/ppermute | solution.py:352
  32.9 12.5 %collective-permute-start.7 = (f32[2,24,1024]{2,1,0:T(8,128)S(1)}, f32[2,24,1024]{2,1,0:T(8,128)S(1)}, u32[]{:S(2)}, u32[]{:S(2)}) collective-permute-start(f32[2,24,1024]{2,1,0:T(8,128)S(1)} %get-tuple-element.81), channel_id=1, source_target_pairs={{0,8},{1,9},{2,10},{3,11},{4,12},{5,13},{6,14},{7,15},{8,16},{9,17... | collective-permute-start | bytes 589832 | tf_op jit(solution)/shard_map/ppermute | solution.py:352
  38.7 6.6 %collective-permute-start.6 = (f32[2,16,1024]{2,1,0:T(8,128)S(1)}, f32[2,16,1024]{2,1,0:T(8,128)S(1)}, u32[]{:S(2)}, u32[]{:S(2)}) collective-permute-start(f32[2,16,1024]{2,1,0:T(8,128)S(1)} %get-tuple-element.80), channel_id=1, source_target_pairs={{0,1},{1,2},{2,3},{3,4},{4,5},{5,6},{6,7},{8,9},{9,10},{10,11},{11... | collective-permute-start | bytes 393224 | tf_op jit(solution)/shard_map/ppermute | solution.py:352
  45.6 9.1 %collective-permute-start.9 = (f32[2,24,1024]{2,1,0:T(8,128)S(1)}, f32[2,24,1024]{2,1,0:T(8,128)S(1)}, u32[]{:S(2)}, u32[]{:S(2)}) collective-permute-start(f32[2,24,1024]{2,1,0:T(8,128)S(1)} %get-tuple-element.89), channel_id=1, source_target_pairs={{8,0},{9,1},{10,2},{11,3},{12,4},{13,5},{14,6},{15,7},{16,8},{17,9... | collective-permute-start | bytes 589832 | tf_op jit(solution)/shard_map/ppermute | solution.py:352
  48.4 3.2 %collective-permute-start.8 = (f32[2,16,1024]{2,1,0:T(8,128)S(1)}, f32[2,16,1024]{2,1,0:T(8,128)S(1)}, u32[]{:S(2)}, u32[]{:S(2)}) collective-permute-start(f32[2,16,1024]{2,1,0:T(8,128)S(1)} %get-tuple-element.88), channel_id=1, source_target_pairs={{1,0},{2,1},{3,2},{4,3},{5,4},{6,5},{7,6},{9,8},{10,9},{11,10},{12... | collective-permute-start | bytes 393224 | tf_op jit(solution)/shard_map/ppermute | solution.py:352
  54.8 10.7 %collective-permute-start.11 = (f32[2,24,1024]{2,1,0:T(8,128)S(1)}, f32[2,24,1024]{2,1,0:T(8,128)S(1)}, u32[]{:S(2)}, u32[]{:S(2)}) collective-permute-start(f32[2,24,1024]{2,1,0:T(8,128)S(1)} %get-tuple-element.93), channel_id=1, source_target_pairs={{0,8},{1,9},{2,10},{3,11},{4,12},{5,13},{6,14},{7,15},{8,16},{9,17... | collective-permute-start | bytes 589832 | tf_op jit(solution)/shard_map/ppermute | solution.py:352
  59.7 5.8 %collective-permute-start.10 = (f32[2,16,1024]{2,1,0:T(8,128)S(1)}, f32[2,16,1024]{2,1,0:T(8,128)S(1)}, u32[]{:S(2)}, u32[]{:S(2)}) collective-permute-start(f32[2,16,1024]{2,1,0:T(8,128)S(1)} %get-tuple-element.92), channel_id=1, source_target_pairs={{0,1},{1,2},{2,3},{3,4},{4,5},{5,6},{6,7},{8,9},{9,10},{10,11},{11... | collective-permute-start | bytes 393224 | tf_op jit(solution)/shard_map/ppermute | solution.py:352
  65.7 9.6 %collective-permute-start.13 = (f32[2,24,1024]{2,1,0:T(8,128)S(1)}, f32[2,24,1024]{2,1,0:T(8,128)S(1)}, u32[]{:S(2)}, u32[]{:S(2)}) collective-permute-start(f32[2,24,1024]{2,1,0:T(8,128)S(1)} %get-tuple-element.101), channel_id=1, source_target_pairs={{8,0},{9,1},{10,2},{11,3},{12,4},{13,5},{14,6},{15,7},{16,8},{17,9... | collective-permute-start | bytes 589832 | tf_op jit(solution)/shard_map/ppermute | solution.py:352
  68.5 3.6 %collective-permute-start.12 = (f32[2,16,1024]{2,1,0:T(8,128)S(1)}, f32[2,16,1024]{2,1,0:T(8,128)S(1)}, u32[]{:S(2)}, u32[]{:S(2)}) collective-permute-start(f32[2,16,1024]{2,1,0:T(8,128)S(1)} %get-tuple-element.100), channel_id=1, source_target_pairs={{1,0},{2,1},{3,2},{4,3},{5,4},{6,5},{7,6},{9,8},{10,9},{11,10},{12... | collective-permute-start | bytes 393224 | tf_op jit(solution)/shard_map/ppermute | solution.py:352
  75.4 13.6 %collective-permute-start.15 = (f32[2,24,1024]{2,1,0:T(8,128)S(1)}, f32[2,24,1024]{2,1,0:T(8,128)S(1)}, u32[]{:S(2)}, u32[]{:S(2)}) collective-permute-start(f32[2,24,1024]{2,1,0:T(8,128)S(1)} %get-tuple-element.105), channel_id=1, source_target_pairs={{0,8},{1,9},{2,10},{3,11},{4,12},{5,13},{6,14},{7,15},{8,16},{9,17... | collective-permute-start | bytes 589832 | tf_op jit(solution)/shard_map/ppermute | solution.py:352
  80.3 8.7 %collective-permute-start.14 = (f32[2,16,1024]{2,1,0:T(8,128)S(1)}, f32[2,16,1024]{2,1,0:T(8,128)S(1)}, u32[]{:S(2)}, u32[]{:S(2)}) collective-permute-start(f32[2,16,1024]{2,1,0:T(8,128)S(1)} %get-tuple-element.104), channel_id=1, source_target_pairs={{0,1},{1,2},{2,3},{3,4},{4,5},{5,6},{6,7},{8,9},{9,10},{10,11},{11... | collective-permute-start | bytes 393224 | tf_op jit(solution)/shard_map/ppermute | solution.py:352
  137.9 27.1 %copy-start = (f32[384,128]{1,0:T(8,128)S(1)}, f32[384,128]{1,0:T(8,128)}, u32[]{:S(2)}) copy-start(f32[384,128]{1,0:T(8,128)} %param.13) | copy-start | bytes 589828

commit v3 on v2

--- a/solution.py
+++ b/solution.py
@@ -62,27 +62,22 @@
     return jnp.where(place > 0, pltpu.roll(f, 1, 0), jnp.broadcast_to(row, f.shape))
 
 
-def edge_kernel(e, back, sem):
-    copy = pltpu.make_async_copy(e.at[pl.ds(1, 2), 0], back, sem)
-    copy.start()
-    copy.wait()
-
-
-def load_kernel(e_in, order, e, back, sem):
+def edge_kernel(e, to_col, to_hgt, low, sems):
     nx = e.shape[1]
-    copy = pltpu.make_async_copy(e_in, e, sem)
-    copy.start()
-    copy.wait()
-
-    def rows(x, carry):
+    col_copy = pltpu.make_async_copy(e.at[pl.ds(1, 2), 0], to_col, sems.at[0])
+    low_copy = pltpu.make_async_copy(e.at[pl.ds(0, 2), :, pl.ds(0, ROWS)], low, sems.at[1])
+    low_copy.start()
+    col_copy.start()
+    low_copy.wait()
+    for x in range(nx):
         for comp in range(2):
-            back[comp, pl.ds(x, 1), :] = e[comp, x, 0:1, :]
-        return carry
-
-    lax.fori_loop(0, nx, rows, 0)
-
-
-def coefficients_kernel(temp_far, tags_far, h_far, ca, cb, sigma_out, h, temp, tags, sems):
+            to_hgt[comp, x : x + 1, :] = low[comp, x, 0:1, :]
+    col_copy.wait()
+
+
+def load_kernel(
+    temp_far, tags_far, e_far, h_far, order, ca, cb, sigma_out, e, h, media_rows, e_rows, h_rows, temp, tags, sems
+):
     nx, nz, _ = temp.shape
     parts = 4
     size = nx // parts
@@ -91,9 +86,11 @@
         here = pl.ds(part * size, size)
         copies.append(pltpu.make_async_copy(temp_far.at[here], temp.at[here], sems.at[0, part]))
         copies.append(pltpu.make_async_copy(tags_far.at[here], tags.at[here], sems.at[1, part]))
-    h_copy = pltpu.make_async_copy(h_far, h, sems.at[2, 0])
+    e_copy = pltpu.make_async_copy(e_far, e, sems.at[2, 0])
+    h_copy = pltpu.make_async_copy(h_far, h, sems.at[2, 1])
     for copy in copies:
         copy.start()
+    e_copy.start()
     h_copy.start()
 
     def plane(x, carry):
@@ -113,13 +110,25 @@
             ca[x, z : z + ROWS, :] = (eps - half) * inverse
             cb[x, z : z + ROWS, :] = COURANT * inverse
             sigma_out[x, z : z + ROWS, :] = sigma
+        media_rows[0, pl.ds(x, 1), :] = ca[x, 0:1, :]
+        media_rows[1, pl.ds(x, 1), :] = cb[x, 0:1, :]
         return carry
 
     for part in range(parts):
         copies[2 * part].wait()
         copies[2 * part + 1].wait()
         lax.fori_loop(part * size, (part + 1) * size, plane, 0)
+    e_copy.wait()
     h_copy.wait()
+
+    def rows(x, carry):
+        for comp in range(3):
+            e_rows[comp, pl.ds(x, 1), :] = e[comp, x, nz - 1 : nz, :]
+        for comp in range(2):
+            h_rows[comp, pl.ds(x, 1), :] = h[comp, x, nz - 1 : nz, :]
+        return carry
+
+    lax.fori_loop(0, nx, rows, 0)
 
 
 def over(first, stop, body):
@@ -178,72 +187,77 @@
     return ey, ez
 
 
-def h_inner_kernel(e, h_old, h):
-    nx, nz = e.shape[1:3]
-
-    def plane(x):
-        for z in range(0, nz - ROWS, ROWS):
-            h_tile(e, h, None, None, x, z)
-
-    over(0, nx - 1, plane)
-
-
-def h_plane_kernel(e, col, hgt, h_old, h, send):
+def h_edge_kernel(e, col, hgt, e_rows, rows_old, h_old, h, to_col, to_hgt):
     nx, nz = e.shape[1:3]
     for z in range(0, nz, ROWS):
         hy, hz = h_tile(e, h, col, hgt, nx - 1, z)
-        send[0, z : z + ROWS, :] = hy
-        send[1, z : z + ROWS, :] = hz
-
-
-def h_rows_kernel(e, hgt, h_old, h, send):
+        to_col[0, z : z + ROWS, :] = hy
+        to_col[1, z : z + ROWS, :] = hz
+    for x in range(0, nx, ROWS):
+        here = slice(x, x + ROWS)
+        ex, ey, ez = (e_rows[comp, here, :] for comp in range(3))
+        row = e_rows[2, x + ROWS : x + ROWS + 1, :] if x + ROWS < nx else col[1, nz - 1 : nz, :]
+        to_hgt[0, here, :] = rows_old[0, here, :] - COURANT * ((after_y(ez) - ez) - (hgt[1, here, :] - ey))
+        to_hgt[1, here, :] = rows_old[1, here, :] - COURANT * ((hgt[0, here, :] - ex) - (after_row(ez, row) - ez))
+
+
+def h_rest_kernel(e, hgt, h_old, h, rows):
     nx, nz = e.shape[1:3]
 
     def keep(x):
-        for comp in range(2):
-            send[comp, pl.ds(x, 1), :] = h[comp, x, nz - 1 : nz, :]
+        for comp in range(3):
+            rows[comp, pl.ds(x, 1), :] = h[comp, x, 0:1, :]
 
     def plane(x):
-        h_tile(e, h, None, hgt, x, nz - ROWS)
+        for z in range(0, nz, ROWS):
+            h_tile(e, h, None, hgt, x, z)
         keep(x)
 
     over(0, nx - 1, plane)
     keep(nx - 1)
 
 
-def e_inner_kernel(first, h, ca, cb, sigma, *refs):
-    e, power = refs[-2:]
+def e_edge_kernel(first, h, ca, cb, sigma, col, hgt, media_rows, h_rows, rows_old, *refs):
+    e, power, to_col, to_hgt = refs[-4:]
     nx, nz = e.shape[1:3]
-
-    def plane(x):
-        for z in range(ROWS, nz, ROWS):
-            e_tile(first, h, e, power, ca, cb, sigma, None, None, x, z)
-
-    over(1, nx, plane)
-
-
-def e_plane_kernel(first, h, ca, cb, sigma, col, hgt, e_old, power_old, e, power, *send):
-    nz = e.shape[2]
     for z in range(0, nz, ROWS):
         ey, ez = e_tile(first, h, e, power, ca, cb, sigma, col, hgt, 0, z)
-        if send:
-            send[0][0, z : z + ROWS, :] = ey
-            send[0][1, z : z + ROWS, :] = ez
-
-
-def e_rows_kernel(first, h, ca, cb, sigma, hgt, e_old, power_old, e, power, *send):
-    nx = e.shape[1]
+        to_col[0, z : z + ROWS, :] = ey
+        to_col[1, z : z + ROWS, :] = ez
+    for x in range(0, nx, ROWS):
+        here = slice(x, x + ROWS)
+        hx, hy, hz = (h_rows[comp, here, :] for comp in range(3))
+        row = h_rows[2, x - 1 : x, :] if x > 0 else col[1, 0:1, :]
+        keep = media_rows[0, here, :]
+        drive = media_rows[1, here, :]
+        to_hgt[0, here, :] = keep * rows_old[0, here, :] + drive * ((hz - before_y(hz)) - (hy - hgt[1, here, :]))
+        to_hgt[1, here, :] = keep * rows_old[1, here, :] + drive * ((hx - hgt[0, here, :]) - (hz - before_row(hz, row)))
+
+
+def e_rest_kernel(first, h, ca, cb, sigma, hgt, e_old, power_old, e, power, rows):
+    nx, nz = e.shape[1:3]
 
     def keep(x):
-        if send:
-            for comp in range(2):
-                send[0][comp, pl.ds(x, 1), :] = e[comp, x, 0:1, :]
+        for comp in range(3):
+            rows[comp, pl.ds(x, 1), :] = e[comp, x, nz - 1 : nz, :]
 
     def plane(x):
-        e_tile(first, h, e, power, ca, cb, sigma, None, hgt, x, 0)
+        for z in range(0, nz, ROWS):
+            e_tile(first, h, e, power, ca, cb, sigma, None, hgt, x, z)
         keep(x)
 
     keep(0)
+    over(1, nx, plane)
+
+
+def e_last_kernel(first, h, ca, cb, sigma, col, hgt, e_old, power_old, e, power):
+    nx, nz = e.shape[1:3]
+
+    def plane(x):
+        for z in range(0, nz, ROWS):
+            e_tile(first, h, e, power, ca, cb, sigma, col if isinstance(x, int) else None, hgt, x, z)
+
+    plane(0)
     over(1, nx, plane)
 
 
@@ -258,8 +272,7 @@
     room_for = nodes_out.shape[0] // n_dev * LANES
     room = lax.broadcasted_iota(jnp.int32, (room_for, width), 0)
     total = jnp.zeros((n_dev, 1), F32)
-    high = jnp.zeros((n_dev, room_for), F32)
-    low = jnp.zeros((n_dev, room_for), F32)
+    parts_of = jnp.zeros((2 * n_dev, room_for), F32)
     nt = (((1,), (1,)), ((), ()))
     for start in range(0, count, width):
         own = owner[:, start : start + width]
@@ -274,14 +287,10 @@
         upper_part = lax.div(number, 16)
         lower_part = number - 16 * upper_part
         seat = jnp.where(room == rank, 1.0, 0.0).astype(jnp.bfloat16)
-        high = high + lax.dot_general(
-            (hit * upper_part.astype(F32)).astype(jnp.bfloat16), seat, nt, preferred_element_type=F32
-        )
-        low = low + lax.dot_general(
-            (hit * lower_part.astype(F32)).astype(jnp.bfloat16), seat, nt, preferred_element_type=F32
-        )
+        both = jnp.concatenate([hit * upper_part.astype(F32), hit * lower_part.astype(F32)], 0)
+        parts_of = parts_of + lax.dot_general(both.astype(jnp.bfloat16), seat, nt, preferred_element_type=F32)
     taken = lax.broadcasted_iota(jnp.int32, (n_dev, room_for), 1).astype(F32) < total
-    table = jnp.where(taken, 16.0 * high + low, -1.0)
+    table = jnp.where(taken, 16.0 * parts_of[:n_dev] + parts_of[n_dev:], -1.0)
     parts = room_for // LANES
     for part in range(parts):
         nodes_out[pl.ds(part, n_dev, stride=parts), :] = table[:, part * LANES : (part + 1) * LANES]
@@ -399,20 +408,22 @@
     field = vmem(3, nx, nz, ny)
     whole = vmem(nx, nz, ny)
     planes = vmem(2, nz, ny)
-    rows = vmem(2, nx, ny)
-
-    to_col = kernel(edge_kernel, planes, [FAR], [e_start], "edge", 1, scratch=[sem])
+    two_rows = vmem(2, nx, ny)
+    three_rows = vmem(3, nx, ny)
+
+    to_col, e_low = kernel(
+        edge_kernel, (planes, two_rows), [FAR], [e_start], "edge", 4, scratch=[vmem(2, nx, ROWS, ny), sem((2,))]
+    )
     col = shifted(to_col, -1, 0)
-    e, to_hgt = kernel(load_kernel, (field, rows), [FAR, WHOLE], [e_start, owners + nodes], "load", 24, scratch=[sem])
-    hgt = shifted(to_hgt, 0, -1)
-    ca, cb, sigma, h = kernel(
-        coefficients_kernel,
-        (whole, whole, whole, field),
-        [FAR] * 3,
-        [far(cell_temp), far(region_tags), h_start],
-        "coefficients",
-        40,
-        scratch=[pltpu.VMEM((nx, nz, ny), F32), pltpu.VMEM((nx, nz, ny), jnp.int32), sem((3, 4))],
+    hgt = shifted(e_low, 0, -1)
+    ca, cb, sigma, e, h, media_rows, e_rows, h_high = kernel(
+        load_kernel,
+        (whole, whole, whole, field, field, two_rows, three_rows, two_rows),
+        [FAR] * 4 + [WHOLE],
+        [far(cell_temp), far(region_tags), e_start, h_start, owners + nodes],
+        "load",
+        60,
+        scratch=[vmem(nx, nz, ny), pltpu.VMEM((nx, nz, ny), jnp.int32), sem((3, 4))],
     )
     room_for = -(-cap // LANES) * LANES
     extra = -(-(n_col * room_for // LANES) // ROWS) * ROWS
@@ -427,59 +438,55 @@
     power = None
     for step in range(STEPS):
         first = step == 0
-        last = step == STEPS - 1
-        h = kernel(h_inner_kernel, field, [WHOLE] * 2, [e, h], f"h_inner_{step}", 25, {1: 0})
-        h, to_col = kernel(
-            h_plane_kernel, (field, planes), [WHOLE] * 4, [e, col, hgt, h], f"h_plane_{step}", 2, {3: 0}
+        h, to_col, h_high = kernel(
+            h_edge_kernel,
+            (field, planes, two_rows),
+            [WHOLE] * 6,
+            [e, col, hgt, e_rows, h_high, h],
+            f"h_edge_{step}",
+            4,
+            {5: 0},
         )
+        e_hgt = hgt
         col = shifted(to_col, 1, 0)
-        h, to_hgt = kernel(h_rows_kernel, (field, rows), [WHOLE] * 3, [e, hgt, h], f"h_rows_{step}", 12, {2: 0})
-        hgt = shifted(to_hgt, 0, 1)
+        hgt = shifted(h_high, 0, 1)
+        h, h_rows = kernel(
+            h_rest_kernel, (field, three_rows), [WHOLE] * 3, [e, e_hgt, h], f"h_rest_{step}", 40, {2: 0}
+        )
         media = [h, ca, cb, sigma]
-        if first:
+        if step == STEPS - 1:
             e, power = kernel(
-                functools.partial(e_inner_kernel, first),
+                functools.partial(e_last_kernel, first),
                 (field, whole),
-                [WHOLE] * 5,
-                media + [e],
-                f"e_inner_{step}",
-                30,
-                {4: 0},
+                [WHOLE] * 8,
+                media + [col, hgt, e, power],
+                f"e_last_{step}",
+                50,
+                {6: 0, 7: 1},
             )
-        else:
-            e, power = kernel(
-                functools.partial(e_inner_kernel, first),
-                (field, whole),
-                [WHOLE] * 6,
-                media + [e, power],
-                f"e_inner_{step}",
-                30,
-                {4: 0, 5: 1},
-            )
-        outs = kernel(
-            functools.partial(e_plane_kernel, first),
-            (field, whole) if last else (field, whole, planes),
-            [WHOLE] * 8,
-            media + [col, hgt, e, power],
-            f"e_plane_{step}",
-            3,
-            {6: 0, 7: 1},
+            break
+        args = media + [col, hgt, media_rows, h_rows, e_low, e] + ([] if first else [power])
+        e, power, to_col, e_low = kernel(
+            functools.partial(e_edge_kernel, first),
+            (field, whole, planes, two_rows),
+            [WHOLE] * len(args),
+            args,
+            f"e_edge_{step}",
+            5,
+            {9: 0} if first else {9: 0, 10: 1},
         )
-        e, power = outs[:2]
-        if not last:
-            col = shifted(outs[2], -1, 0)
-        outs = kernel(
-            functools.partial(e_rows_kernel, first),
-            (field, whole) if last else (field, whole, rows),
+        h_hgt = hgt
+        col = shifted(to_col, -1, 0)
+        hgt = shifted(e_low, 0, -1)
+        e, power, e_rows = kernel(
+            functools.partial(e_rest_kernel, first),
+            (field, whole, three_rows),
             [WHOLE] * 7,
-            media + [hgt, e, power],
-            f"e_rows_{step}",
-            15,
+            media + [h_hgt, e, power],
+            f"e_rest_{step}",
+            45,
             {5: 0, 6: 1},
         )
-        e, power = outs[:2]
-        if not last:
-            hgt = shifted(outs[2], 0, -1)
 
     send, e_out, h_out = pl.pallas_call(
         pack_kernel,

time: 166 us -> 155 us (0.934)
  Pallas kernels: 43.5 us -> 34.3 us
  starting transfers between devices: 43 us -> 34.3 us
  waiting for transfers between devices: 10.3 us -> 18.8 us
  blocking collectives: 66.6 us -> 64.9 us
    pallas_call x28 -> x18, Pallas kernels: 35.8 us -> 26.7 us  [kernel(): pl.pallas_call(body, out_shape=outs, in_specs=ins, out_specs=jax.tree.map...]
    ppermute x16, starting transfers between devices: 43 us -> 34.3 us  [shifted(): return lax.ppermute(block, ('col', 'hgt'), route)]
    ppermute x16, waiting for transfers between devices: 10.3 us -> 18.8 us  [shifted(): return lax.ppermute(block, ('col', 'hgt'), route)]
  transfers between devices with their start and end apart: 16 -> 16, of which waited for: 6 -> 10; matrix products, arithmetic and copies ran while one was open for 0% -> 0% of each run, Pallas kernels for 19% -> 14%
where the time goes in v3:
time: 155 us
  blocking collectives  64.9 us (42%)
  Pallas kernels  34.3 us (22%)
  starting transfers between devices  34.3 us (22%)
  waiting for transfers between devices  18.8 us (12%)
    all_to_all x1, blocking collectives, per_device(): lax.all_to_all(send, 'hgt', split_axis=0, concat_axis=0, tiled=True)  42 us
    ppermute x16, starting transfers between devices, shifted(): return lax.ppermute(block, ('col', 'hgt'), route)  34.3 us
    pallas_call x18, Pallas kernels, kernel(): pl.pallas_call(body, out_shape=outs, in_specs=ins, out_specs=jax.tree.map...  26.7 us
    all_to_all x1, blocking collectives, per_device(): lax.all_to_all(partial, 'col', split_axis=0, concat_axis=0, tiled=True)  22.9 us
    ppermute x16, waiting for transfers between devices, shifted(): return lax.ppermute(block, ('col', 'hgt'), route)  18.8 us
    pallas_call x1, Pallas kernels, per_device(): pl.pallas_call(pack_kernel, out_shape=(jax.ShapeDtypeStruct((n_hgt, n_col...  4.49 us
    pallas_call x1, Pallas kernels, per_device(): pl.pallas_call(functools.partial(collect_kernel, cap), out_shape=jax.Shap...  3.21 us
  transfers between devices with their start and end apart: 16, of which 10 were waited for; matrix products, arithmetic and copies ran while one was open for 0% of the time, Pallas kernels for 14%

profile of v3, /device:TPU:0, one launch (start us, length us, event | category | flops | bytes accessed | tf_op | source)
XLA Modules:
  0.0 154.6 jit_solution(14342608437679449782)
XLA Ops:
  5.1 4.9 %load.1 = (f32[16,24,1024]{2,1,0:T(8,128)S(1)}, f32[16,24,1024]{2,1,0:T(8,128)S(1)}, f32[16,24,1024]{2,1,0:T(8,128)S(1)}, f32[3,16,24,1024]{3,2,1,0:T(8,128)S(1)...) custom-call(f32[16,24,1024]{2,1,0:T(8,128)} %temp_far.1, ...), custom_call_target="tpu_custom_call" | custom-call | flops 23592960 | bytes 23592960 | tf_op jit(solution)/shard_map/load/pallas_call | solution.py:392
  11.9 3.9 %collective-permute-start.3 = (f32[2,24,1024]{2,1,0:T(8,128)S(1)}, f32[2,24,1024]{2,1,0:T(8,128)S(1)}, u32[]{:S(2)}, u32[]{:S(2)}) collective-permute-start(f32[2,24,1024]{2,1,0:T(8,128)S(1)} %get-tuple-element.73), channel_id=1, source_target_pairs={{0,8},{1,9},{2,10},{3,11},{4,12},{5,13},{6,14},{7,15},{8,16},{9,17... | collective-permute-start | bytes 589832 | tf_op jit(solution)/shard_map/ppermute | solution.py:361
  15.8 2.8 %collective-permute-start.2 = (f32[2,16,1024]{2,1,0:T(8,128)S(1)}, f32[2,16,1024]{2,1,0:T(8,128)S(1)}, u32[]{:S(2)}, u32[]{:S(2)}) collective-permute-start(f32[2,16,1024]{2,1,0:T(8,128)S(1)} %get-tuple-element.72.rows_old), channel_id=1, source_target_pairs={{0,1},{1,2},{2,3},{3,4},{4,5},{5,6},{6,7},{8,9},{9,10},{10,11},{11... | collective-permute-start | bytes 393224 | tf_op jit(solution)/shard_map/ppermute | solution.py:361
  18.6 1.9 %h_rest_0.1 = (f32[3,16,24,1024]{3,2,1,0:T(8,128)S(1)}, f32[3,16,1024]{2,1,0:T(8,128)S(1)}) custom-call(f32[3,16,24,1024]{3,2,1,0:T(8,128)S(1)} %get-tuple-element.61.e.refs_0_, f32[2,16,1024]{2,1,0:T(8,128)S(1)} %collective-permute-done.hgt, f32[3,16,24,1024]{3,2,1,0:T(8,128)S(1)} %get-tuple-element.67.h_old), custom_call_target="tpu_custom_call", output_to_operand_aliasing={{0}: (2, {})} | custom-call | flops 15728640 | bytes 15728640 | tf_op jit(solution)/shard_map/h_rest_0/pallas_call | solution.py:392
  23.7 2.2 %e_rest_0.1 = (f32[3,16,24,1024]{3,2,1,0:T(8,128)S(1)}, f32[16,24,1024]{2,1,0:T(8,128)S(1)}, f32[3,16,1024]{2,1,0:T(8,128)S(1)}) custom-call(f32[3,16,24,1024]{3,2,1,0:T(8,128)S(1)} %get-tuple-element.68.h.h_old, f32[16,24,1024]{2,1,0:T(8,128)S(1)} %get-tuple-element.69.ca, ...), custom_call_target="tpu_custom_call", output_to_operand_aliasing={{0}: (5, {}), {1}: (6, {})} | custom-call | flops 17694720 | bytes 17694720 | tf_op jit(solution)/shard_map/e_rest_0/pallas_call | solution.py:392
  26.6 4.6 %collective-permute-done.5.col = f32[2,24,1024]{2,1,0:T(8,128)S(1)} collective-permute-done((f32[2,24,1024]{2,1,0:T(8,128)S(1)}, f32[2,24,1024]{2,1,0:T(8,128)S(1)}, u32[]{:S(2)}, u32[]{:S(2)}) %collective-permute-start.5) | collective-permute-done | bytes 196640 | tf_op jit(solution)/shard_map/ppermute | solution.py:361
  31.4 3.5 %collective-permute-start.7 = (f32[2,24,1024]{2,1,0:T(8,128)S(1)}, f32[2,24,1024]{2,1,0:T(8,128)S(1)}, u32[]{:S(2)}, u32[]{:S(2)}) collective-permute-start(f32[2,24,1024]{2,1,0:T(8,128)S(1)} %get-tuple-element.85), channel_id=1, source_target_pairs={{0,8},{1,9},{2,10},{3,11},{4,12},{5,13},{6,14},{7,15},{8,16},{9,17... | collective-permute-start | bytes 589832 | tf_op jit(solution)/shard_map/ppermute | solution.py:361
  34.9 2.3 %collective-permute-start.6 = (f32[2,16,1024]{2,1,0:T(8,128)S(1)}, f32[2,16,1024]{2,1,0:T(8,128)S(1)}, u32[]{:S(2)}, u32[]{:S(2)}) collective-permute-start(f32[2,16,1024]{2,1,0:T(8,128)S(1)} %get-tuple-element.84.rows_old), channel_id=1, source_target_pairs={{0,1},{1,2},{2,3},{3,4},{4,5},{5,6},{6,7},{8,9},{9,10},{10,11},{11... | collective-permute-start | bytes 393224 | tf_op jit(solution)/shard_map/ppermute | solution.py:361
  37.2 1.9 %h_rest_1.1 = (f32[3,16,24,1024]{3,2,1,0:T(8,128)S(1)}, f32[3,16,1024]{2,1,0:T(8,128)S(1)}) custom-call(f32[3,16,24,1024]{3,2,1,0:T(8,128)S(1)} %get-tuple-element.78.e.refs_0_, f32[2,16,1024]{2,1,0:T(8,128)S(1)} %collective-permute-done.4.hgt, f32[3,16,24,1024]{3,2,1,0:T(8,128)S(1)} %get-tuple-element.82.h_old), custom_call_target="tpu_custom_call", output_to_operand_aliasing={{0}: (2, {})} | custom-call | flops 15728640 | bytes 15728640 | tf_op jit(solution)/shard_map/h_rest_1/pallas_call | solution.py:392
  42.6 2.3 %e_rest_1.1 = (f32[3,16,24,1024]{3,2,1,0:T(8,128)S(1)}, f32[16,24,1024]{2,1,0:T(8,128)S(1)}, f32[3,16,1024]{2,1,0:T(8,128)S(1)}) custom-call(f32[3,16,24,1024]{3,2,1,0:T(8,128)S(1)} %get-tuple-element.83.h.h_old, f32[16,24,1024]{2,1,0:T(8,128)S(1)} %get-tuple-element.69.ca, ...), custom_call_target="tpu_custom_call", output_to_operand_aliasing={{0}: (5, {}), {1}: (6, {})} | custom-call | flops 17694720 | bytes 17694720 | tf_op jit(solution)/shard_map/e_rest_1/pallas_call | solution.py:392
  45.2 4.7 %collective-permute-done.9.col = f32[2,24,1024]{2,1,0:T(8,128)S(1)} collective-permute-done((f32[2,24,1024]{2,1,0:T(8,128)S(1)}, f32[2,24,1024]{2,1,0:T(8,128)S(1)}, u32[]{:S(2)}, u32[]{:S(2)}) %collective-permute-start.9) | collective-permute-done | bytes 196640 | tf_op jit(solution)/shard_map/ppermute | solution.py:361
  50.0 3.5 %collective-permute-start.11 = (f32[2,24,1024]{2,1,0:T(8,128)S(1)}, f32[2,24,1024]{2,1,0:T(8,128)S(1)}, u32[]{:S(2)}, u32[]{:S(2)}) collective-permute-start(f32[2,24,1024]{2,1,0:T(8,128)S(1)} %get-tuple-element.97), channel_id=1, source_target_pairs={{0,8},{1,9},{2,10},{3,11},{4,12},{5,13},{6,14},{7,15},{8,16},{9,17... | collective-permute-start | bytes 589832 | tf_op jit(solution)/shard_map/ppermute | solution.py:361
  53.5 2.3 %collective-permute-start.10 = (f32[2,16,1024]{2,1,0:T(8,128)S(1)}, f32[2,16,1024]{2,1,0:T(8,128)S(1)}, u32[]{:S(2)}, u32[]{:S(2)}) collective-permute-start(f32[2,16,1024]{2,1,0:T(8,128)S(1)} %get-tuple-element.96.rows_old), channel_id=1, source_target_pairs={{0,1},{1,2},{2,3},{3,4},{4,5},{5,6},{6,7},{8,9},{9,10},{10,11},{11... | collective-permute-start | bytes 393224 | tf_op jit(solution)/shard_map/ppermute | solution.py:361
  55.8 1.9 %h_rest_2.1 = (f32[3,16,24,1024]{3,2,1,0:T(8,128)S(1)}, f32[3,16,1024]{2,1,0:T(8,128)S(1)}) custom-call(f32[3,16,24,1024]{3,2,1,0:T(8,128)S(1)} %get-tuple-element.90.e.refs_0_, f32[2,16,1024]{2,1,0:T(8,128)S(1)} %collective-permute-done.8.hgt, f32[3,16,24,1024]{3,2,1,0:T(8,128)S(1)} %get-tuple-element.94.h_old), custom_call_target="tpu_custom_call", output_to_operand_aliasing={{0}: (2, {})} | custom-call | flops 15728640 | bytes 15728640 | tf_op jit(solution)/shard_map/h_rest_2/pallas_call | solution.py:392
  61.2 2.3 %e_rest_2.1 = (f32[3,16,24,1024]{3,2,1,0:T(8,128)S(1)}, f32[16,24,1024]{2,1,0:T(8,128)S(1)}, f32[3,16,1024]{2,1,0:T(8,128)S(1)}) custom-call(f32[3,16,24,1024]{3,2,1,0:T(8,128)S(1)} %get-tuple-element.95.h.h_old, f32[16,24,1024]{2,1,0:T(8,128)S(1)} %get-tuple-element.69.ca, ...), custom_call_target="tpu_custom_call", output_to_operand_aliasing={{0}: (5, {}), {1}: (6, {})} | custom-call | flops 17694720 | bytes 17694720 | tf_op jit(solution)/shard_map/e_rest_2/pallas_call | solution.py:392
  64.0 4.7 %collective-permute-done.13.col = f32[2,24,1024]{2,1,0:T(8,128)S(1)} collective-permute-done((f32[2,24,1024]{2,1,0:T(8,128)S(1)}, f32[2,24,1024]{2,1,0:T(8,128)S(1)}, u32[]{:S(2)}, u32[]{:S(2)}) %collective-permute-start.13) | collective-permute-done | bytes 196640 | tf_op jit(solution)/shard_map/ppermute | solution.py:361
  68.8 3.2 %collective-permute-start.14 = (f32[2,24,1024]{2,1,0:T(8,128)S(1)}, f32[2,24,1024]{2,1,0:T(8,128)S(1)}, u32[]{:S(2)}, u32[]{:S(2)}) collective-permute-start(f32[2,24,1024]{2,1,0:T(8,128)S(1)} %get-tuple-element.108), channel_id=1, source_target_pairs={{0,8},{1,9},{2,10},{3,11},{4,12},{5,13},{6,14},{7,15},{8,16},{9,17... | collective-permute-start | bytes 589832 | tf_op jit(solution)/shard_map/ppermute | solution.py:361
  72.0 2.6 %collective-permute-start.15 = (f32[2,16,1024]{2,1,0:T(8,128)S(1)}, f32[2,16,1024]{2,1,0:T(8,128)S(1)}, u32[]{:S(2)}, u32[]{:S(2)}) collective-permute-start(f32[2,16,1024]{2,1,0:T(8,128)S(1)} %get-tuple-element.109), channel_id=1, source_target_pairs={{0,1},{1,2},{2,3},{3,4},{4,5},{5,6},{6,7},{8,9},{9,10},{10,11},{11... | collective-permute-start | bytes 393224 | tf_op jit(solution)/shard_map/ppermute | solution.py:361
  76.1 2.6 %h_rest_3.1 = (f32[3,16,24,1024]{3,2,1,0:T(8,128)S(1)}, f32[3,16,1024]{2,1,0:T(8,128)}) custom-call(f32[3,16,24,1024]{3,2,1,0:T(8,128)S(1)} %get-tuple-element.102.e.e_old, f32[2,16,1024]{2,1,0:T(8,128)S(1)} %collective-permute-done.12.hgt, f32[3,16,24,1024]{3,2,1,0:T(8,128)S(1)} %get-tuple-element.106.h_old), custom_call_target="tpu_custom_call", output_to_operand_aliasing={{0}: (2, {})} | custom-call | flops 15728640 | bytes 15728640 | tf_op jit(solution)/shard_map/h_rest_3/pallas_call | solution.py:392
  78.7 2.5 %e_last_3.1 = (f32[3,16,24,1024]{3,2,1,0:T(8,128)S(1)}, f32[16,24,1024]{2,1,0:T(8,128)S(1)}) custom-call(f32[3,16,24,1024]{3,2,1,0:T(8,128)S(1)} %get-tuple-element.107.h, f32[16,24,1024]{2,1,0:T(8,128)S(1)} %get-tuple-element.69.ca, f32[16,24,1024]{2,1,0:T(8,128)S(1)} %get-tuple-element.70.cb, ...), custom_call_target="tpu_custom_call", output_to_operand_aliasing={{0}: (6, {}), {1}: (7, {})} | custom-call | flops 19660800 | bytes 19660800 | tf_op jit(solution)/shard_map/e_last_3/pallas_call | solution.py:392
  81.2 4.5 %pack.1 = (f32[8,776,128]{2,1,0:T(8,128)S(1)}, f32[3,16,24,1024]{3,2,1,0:T(8,128)}, f32[3,16,24,1024]{3,2,1,0:T(8,128)}) custom-call(s32[3072]{0:T(1024)S(1)} %bitcast.7, f32[16,24,1024]{2,1,0:T(8,128)S(1)} %get-tuple-element.111.power, f32[64,128]{1,0:T(8,128)S(1)} %get-tuple-element.112.nodes, f32[3,16,24,1024]{3,2,1,0:T(8,128)S(1)} %get-tuple-element.113.e, ...), custom_call_target="tpu_custom_call" | custom-call | flops 393216 | bytes 14155776 | tf_op jit(solution)/shard_map/pack/pallas_call | solution.py:491
  85.7 42.0 %all_to_all.10.blocks = f32[8,776,128]{2,1,0:T(8,128)S(1)} all-to-all(f32[8,776,128]{2,1,0:T(8,128)S(1)} %get-tuple-element.116), channel_id=1, replica_groups=mesh['col'=4,'hgt'=8] {'hgt'}, dimensions={0} | all-to-all | bytes 6356992 | tf_op jit(solution)/shard_map/all_to_all | solution.py:505
  127.7 3.2 %collect.1 = f32[4,384,128]{2,1,0:T(8,128)S(1)} custom-call(f32[8,776,128]{2,1,0:T(8,128)S(1)} %all_to_all.10.blocks), custom_call_target="tpu_custom_call" | custom-call | flops 1610612736 | bytes 3145728 | tf_op jit(solution)/shard_map/collect/pallas_call | solution.py:506
  130.9 22.9 %all_to_all.11 = f32[4,384,128]{2,1,0:T(8,128)S(1)} all-to-all(f32[4,384,128]{2,1,0:T(8,128)S(1)} %collect.1), channel_id=1, replica_groups=mesh['col'=4,'hgt'=8] {'col'}, dimensions={0} | all-to-all | bytes 1572864 | tf_op jit(solution)/shard_map/all_to_all | solution.py:519
  (43 shorter events, 20.5 us)
Async XLA Ops:
  0.6 3.9 %copy-start.1 = (s32[1,1,16,24,8,1]{3,5,4,2,1,0:T(1,128)S(1)}, s32[1,1,16,24,8,1]{3,5,4,2,1,0:T(1,128)}, u32[]{:S(2)}) copy-start(s32[1,1,16,24,8,1]{3,5,4,2,1,0:T(1,128)} %param.11) | copy-start | bytes 36868
  0.6 4.2 %copy-start.2 = (s32[1,1,16,24,8]{3,4,2,1,0:T(8,128)S(1)}, s32[1,1,16,24,8]{3,4,2,1,0:T(8,128)}, u32[]{:S(2)}) copy-start(s32[1,1,16,24,8]{3,4,2,1,0:T(8,128)} %param.12) | copy-start | bytes 36868
  2.0 9.8 %collective-permute-start.1 = (f32[2,24,1024]{2,1,0:T(8,128)S(1)}, f32[2,24,1024]{2,1,0:T(8,128)S(1)}, u32[]{:S(2)}, u32[]{:S(2)}) collective-permute-start(f32[2,24,1024]{2,1,0:T(8,128)S(1)} %get-tuple-element.63), channel_id=1, source_target_pairs={{8,0},{9,1},{10,2},{11,3},{12,4},{13,5},{14,6},{15,7},{16,8},{17,9... | collective-permute-start | bytes 589832 | tf_op jit(solution)/shard_map/ppermute | solution.py:361
  3.3 6.8 %collective-permute-start = (f32[2,16,1024]{2,1,0:T(8,128)S(1)}, f32[2,16,1024]{2,1,0:T(8,128)S(1)}, u32[]{:S(2)}, u32[]{:S(2)}) collective-permute-start(f32[2,16,1024]{2,1,0:T(8,128)S(1)} %get-tuple-element.62.rows_old), channel_id=1, source_target_pairs={{1,0},{2,1},{3,2},{4,3},{5,4},{6,5},{7,6},{9,8},{10,9},{11,10},{12... | collective-permute-start | bytes 393224 | tf_op jit(solution)/shard_map/ppermute | solution.py:361
  11.9 9.0 %collective-permute-start.3 = (f32[2,24,1024]{2,1,0:T(8,128)S(1)}, f32[2,24,1024]{2,1,0:T(8,128)S(1)}, u32[]{:S(2)}, u32[]{:S(2)}) collective-permute-start(f32[2,24,1024]{2,1,0:T(8,128)S(1)} %get-tuple-element.73), channel_id=1, source_target_pairs={{0,8},{1,9},{2,10},{3,11},{4,12},{5,13},{6,14},{7,15},{8,16},{9,17... | collective-permute-start | bytes 589832 | tf_op jit(solution)/shard_map/ppermute | solution.py:361
  15.8 4.7 %collective-permute-start.2 = (f32[2,16,1024]{2,1,0:T(8,128)S(1)}, f32[2,16,1024]{2,1,0:T(8,128)S(1)}, u32[]{:S(2)}, u32[]{:S(2)}) collective-permute-start(f32[2,16,1024]{2,1,0:T(8,128)S(1)} %get-tuple-element.72.rows_old), channel_id=1, source_target_pairs={{0,1},{1,2},{2,3},{3,4},{4,5},{5,6},{6,7},{8,9},{9,10},{10,11},{11... | collective-permute-start | bytes 393224 | tf_op jit(solution)/shard_map/ppermute | solution.py:361
  21.1 10.1 %collective-permute-start.5 = (f32[2,24,1024]{2,1,0:T(8,128)S(1)}, f32[2,24,1024]{2,1,0:T(8,128)S(1)}, u32[]{:S(2)}, u32[]{:S(2)}) collective-permute-start(f32[2,24,1024]{2,1,0:T(8,128)S(1)} %get-tuple-element.80), channel_id=1, source_target_pairs={{8,0},{9,1},{10,2},{11,3},{12,4},{13,5},{14,6},{15,7},{16,8},{17,9... | collective-permute-start | bytes 589832 | tf_op jit(solution)/shard_map/ppermute | solution.py:361
  22.4 4.2 %collective-permute-start.4 = (f32[2,16,1024]{2,1,0:T(8,128)S(1)}, f32[2,16,1024]{2,1,0:T(8,128)S(1)}, u32[]{:S(2)}, u32[]{:S(2)}) collective-permute-start(f32[2,16,1024]{2,1,0:T(8,128)S(1)} %get-tuple-element.79.rows_old), channel_id=1, source_target_pairs={{1,0},{2,1},{3,2},{4,3},{5,4},{6,5},{7,6},{9,8},{10,9},{11,10},{12... | collective-permute-start | bytes 393224 | tf_op jit(solution)/shard_map/ppermute | solution.py:361
  31.4 8.4 %collective-permute-start.7 = (f32[2,24,1024]{2,1,0:T(8,128)S(1)}, f32[2,24,1024]{2,1,0:T(8,128)S(1)}, u32[]{:S(2)}, u32[]{:S(2)}) collective-permute-start(f32[2,24,1024]{2,1,0:T(8,128)S(1)} %get-tuple-element.85), channel_id=1, source_target_pairs={{0,8},{1,9},{2,10},{3,11},{4,12},{5,13},{6,14},{7,15},{8,16},{9,17... | collective-permute-start | bytes 589832 | tf_op jit(solution)/shard_map/ppermute | solution.py:361
  34.9 4.2 %collective-permute-start.6 = (f32[2,16,1024]{2,1,0:T(8,128)S(1)}, f32[2,16,1024]{2,1,0:T(8,128)S(1)}, u32[]{:S(2)}, u32[]{:S(2)}) collective-permute-start(f32[2,16,1024]{2,1,0:T(8,128)S(1)} %get-tuple-element.84.rows_old), channel_id=1, source_target_pairs={{0,1},{1,2},{2,3},{3,4},{4,5},{5,6},{6,7},{8,9},{9,10},{10,11},{11... | collective-permute-start | bytes 393224 | tf_op jit(solution)/shard_map/ppermute | solution.py:361
  40.0 9.8 %collective-permute-start.9 = (f32[2,24,1024]{2,1,0:T(8,128)S(1)}, f32[2,24,1024]{2,1,0:T(8,128)S(1)}, u32[]{:S(2)}, u32[]{:S(2)}) collective-permute-start(f32[2,24,1024]{2,1,0:T(8,128)S(1)} %get-tuple-element.92), channel_id=1, source_target_pairs={{8,0},{9,1},{10,2},{11,3},{12,4},{13,5},{14,6},{15,7},{16,8},{17,9... | collective-permute-start | bytes 589832 | tf_op jit(solution)/shard_map/ppermute | solution.py:361
  41.3 3.9 %collective-permute-start.8 = (f32[2,16,1024]{2,1,0:T(8,128)S(1)}, f32[2,16,1024]{2,1,0:T(8,128)S(1)}, u32[]{:S(2)}, u32[]{:S(2)}) collective-permute-start(f32[2,16,1024]{2,1,0:T(8,128)S(1)} %get-tuple-element.91.rows_old), channel_id=1, source_target_pairs={{1,0},{2,1},{3,2},{4,3},{5,4},{6,5},{7,6},{9,8},{10,9},{11,10},{12... | collective-permute-start | bytes 393224 | tf_op jit(solution)/shard_map/ppermute | solution.py:361
  50.0 8.4 %collective-permute-start.11 = (f32[2,24,1024]{2,1,0:T(8,128)S(1)}, f32[2,24,1024]{2,1,0:T(8,128)S(1)}, u32[]{:S(2)}, u32[]{:S(2)}) collective-permute-start(f32[2,24,1024]{2,1,0:T(8,128)S(1)} %get-tuple-element.97), channel_id=1, source_target_pairs={{0,8},{1,9},{2,10},{3,11},{4,12},{5,13},{6,14},{7,15},{8,16},{9,17... | collective-permute-start | bytes 589832 | tf_op jit(solution)/shard_map/ppermute | solution.py:361
  53.5 4.2 %collective-permute-start.10 = (f32[2,16,1024]{2,1,0:T(8,128)S(1)}, f32[2,16,1024]{2,1,0:T(8,128)S(1)}, u32[]{:S(2)}, u32[]{:S(2)}) collective-permute-start(f32[2,16,1024]{2,1,0:T(8,128)S(1)} %get-tuple-element.96.rows_old), channel_id=1, source_target_pairs={{0,1},{1,2},{2,3},{3,4},{4,5},{5,6},{6,7},{8,9},{9,10},{10,11},{11... | collective-permute-start | bytes 393224 | tf_op jit(solution)/shard_map/ppermute | solution.py:361
  58.6 10.1 %collective-permute-start.13 = (f32[2,24,1024]{2,1,0:T(8,128)S(1)}, f32[2,24,1024]{2,1,0:T(8,128)S(1)}, u32[]{:S(2)}, u32[]{:S(2)}) collective-permute-start(f32[2,24,1024]{2,1,0:T(8,128)S(1)} %get-tuple-element.104), channel_id=1, source_target_pairs={{8,0},{9,1},{10,2},{11,3},{12,4},{13,5},{14,6},{15,7},{16,8},{17,9... | collective-permute-start | bytes 589832 | tf_op jit(solution)/shard_map/ppermute | solution.py:361
  59.9 4.1 %collective-permute-start.12 = (f32[2,16,1024]{2,1,0:T(8,128)S(1)}, f32[2,16,1024]{2,1,0:T(8,128)S(1)}, u32[]{:S(2)}, u32[]{:S(2)}) collective-permute-start(f32[2,16,1024]{2,1,0:T(8,128)S(1)} %get-tuple-element.103), channel_id=1, source_target_pairs={{1,0},{2,1},{3,2},{4,3},{5,4},{6,5},{7,6},{9,8},{10,9},{11,10},{12... | collective-permute-start | bytes 393224 | tf_op jit(solution)/shard_map/ppermute | solution.py:361
  68.8 9.9 %collective-permute-start.14 = (f32[2,24,1024]{2,1,0:T(8,128)S(1)}, f32[2,24,1024]{2,1,0:T(8,128)S(1)}, u32[]{:S(2)}, u32[]{:S(2)}) collective-permute-start(f32[2,24,1024]{2,1,0:T(8,128)S(1)} %get-tuple-element.108), channel_id=1, source_target_pairs={{0,8},{1,9},{2,10},{3,11},{4,12},{5,13},{6,14},{7,15},{8,16},{9,17... | collective-permute-start | bytes 589832 | tf_op jit(solution)/shard_map/ppermute | solution.py:361
  72.0 6.7 %collective-permute-start.15 = (f32[2,16,1024]{2,1,0:T(8,128)S(1)}, f32[2,16,1024]{2,1,0:T(8,128)S(1)}, u32[]{:S(2)}, u32[]{:S(2)}) collective-permute-start(f32[2,16,1024]{2,1,0:T(8,128)S(1)} %get-tuple-element.109), channel_id=1, source_target_pairs={{0,1},{1,2},{2,3},{3,4},{4,5},{5,6},{6,7},{8,9},{9,10},{10,11},{11... | collective-permute-start | bytes 393224 | tf_op jit(solution)/shard_map/ppermute | solution.py:361
  127.7 26.2 %copy-start = (f32[384,128]{1,0:T(8,128)S(1)}, f32[384,128]{1,0:T(8,128)}, u32[]{:S(2)}) copy-start(f32[384,128]{1,0:T(8,128)} %param.13) | copy-start | bytes 589828

commit v4 on v3

--- a/solution.py
+++ b/solution.py
@@ -261,7 +261,7 @@
     over(1, nx, plane)
 
 
-def places_kernel(n_col, n_hgt, cap, extra, owner, node, place, nodes_out):
+def places_kernel(n_col, n_hgt, near, far_cap, extra, my_col, owner, node, place, near_nodes, far_nodes):
     n_dev = n_col * n_hgt
     count = owner.shape[1]
     width = 256
@@ -269,50 +269,72 @@
     before = lax.broadcasted_iota(jnp.int32, (width, width), 0)
     after = lax.broadcasted_iota(jnp.int32, (width, width), 1)
     upper = jnp.where(before <= after, 1.0, 0.0).astype(jnp.bfloat16)
-    room_for = nodes_out.shape[0] // n_dev * LANES
+    room_for = 2 * LANES
+    near_rows = n_col * near + extra
+    far_rows = n_hgt * far_cap + extra
     room = lax.broadcasted_iota(jnp.int32, (room_for, width), 0)
     total = jnp.zeros((n_dev, 1), F32)
     parts_of = jnp.zeros((2 * n_dev, room_for), F32)
     nt = (((1,), (1,)), ((), ()))
     for start in range(0, count, width):
         own = owner[:, start : start + width]
-        target = lax.rem(own, n_hgt) * n_col + lax.div(own, n_hgt)
-        hit = jnp.where(rows == target, 1.0, 0.0)
+        own_col = lax.div(own, n_hgt)
+        own_hgt = lax.rem(own, n_hgt)
+        hit = jnp.where(rows == own, 1.0, 0.0)
         running = total + jnp.dot(hit.astype(jnp.bfloat16), upper, preferred_element_type=F32)
         total = running[:, width - 1 : width]
         rank = jnp.sum(hit * running, axis=0, keepdims=True).astype(jnp.int32) - 1
-        group = lax.div(target, n_col)
-        place[:, start : start + width] = target * cap + group * extra + rank
+        place[:, start : start + width] = jnp.where(
+            rank < near,
+            own_hgt * near_rows + lax.rem(own_col - my_col[0] + n_col, n_col) * near + rank,
+            n_hgt * near_rows + own_col * far_rows + own_hgt * far_cap + (rank - near),
+        )
+        rank = jnp.where(rank < near, rank, rank + (LANES - near))
         number = node[:, start : start + width]
         upper_part = lax.div(number, 16)
         lower_part = number - 16 * upper_part
         seat = jnp.where(room == rank, 1.0, 0.0).astype(jnp.bfloat16)
         both = jnp.concatenate([hit * upper_part.astype(F32), hit * lower_part.astype(F32)], 0)
         parts_of = parts_of + lax.dot_general(both.astype(jnp.bfloat16), seat, nt, preferred_element_type=F32)
-    taken = lax.broadcasted_iota(jnp.int32, (n_dev, room_for), 1).astype(F32) < total
-    table = jnp.where(taken, 16.0 * parts_of[:n_dev] + parts_of[n_dev:], -1.0)
-    parts = room_for // LANES
-    for part in range(parts):
-        nodes_out[pl.ds(part, n_dev, stride=parts), :] = table[:, part * LANES : (part + 1) * LANES]
-
-
-def pack_kernel(place, power, nodes, e, h, out, e_out, h_out, sems):
+    seat_of = lax.broadcasted_iota(jnp.int32, (n_dev, LANES), 1).astype(F32)
+    table = 16.0 * parts_of[:n_dev] + parts_of[n_dev:]
+    near_taken = (seat_of < near) & (seat_of < total)
+    far_taken = (seat_of < far_cap) & (seat_of + near < total)
+    near_table = jnp.where(near_taken, table[:, :LANES], -1.0)
+    far_table = jnp.where(far_taken, table[:, LANES:], -1.0)
+    near_nodes[...] = jnp.full(near_nodes.shape, -1.0, F32)
+    far_nodes[...] = jnp.full(far_nodes.shape, -1.0, F32)
+    for group in range(n_col):
+        mine = slice(group * n_hgt, (group + 1) * n_hgt)
+        far_nodes[group, 0:n_hgt, :] = far_table[mine, :]
+        slot = lax.rem(group - my_col[0] + n_col, n_col)
+        for part in range(n_hgt):
+            near_nodes[part, pl.ds(slot, 1), :] = near_table[group * n_hgt + part : group * n_hgt + part + 1, :]
+
+
+def pack_kernel(place, power, near_nodes, far_nodes, e, h, near_out, far_out, e_out, h_out, flat, sems):
     nx, nz, ny = power.shape
     e_copy = pltpu.make_async_copy(e, e_out, sems.at[0])
     h_copy = pltpu.make_async_copy(h, h_out, sems.at[1])
     e_copy.start()
     h_copy.start()
-    n_group, rows, _ = out.shape
     per_row = ny // PTS
-    extra = nodes.shape[0] // n_group
-    flat = out.reshape(n_group * rows, PTS)
-
-    def clear(group, carry):
-        out[group] = jnp.zeros((rows, PTS), F32)
-        out[group, rows - extra : rows, :] = nodes[pl.ds(pl.multiple_of(group * extra, ROWS), extra), :]
+    begin = 0
+    chunk = 8 * ROWS
+
+    def clear(i, carry):
+        flat[pl.ds(pl.multiple_of(i * chunk, chunk), chunk), :] = jnp.zeros((chunk, PTS), F32)
         return carry
 
-    lax.fori_loop(0, n_group, clear, 0)
+    lax.fori_loop(0, flat.shape[0] // chunk, clear, 0)
+    for at in range(flat.shape[0] // chunk * chunk, flat.shape[0], ROWS):
+        flat[at : at + ROWS, :] = jnp.zeros((ROWS, PTS), F32)
+    for table in (near_nodes, far_nodes):
+        groups, extra, _ = table.shape
+        rows = (near_out if table is near_nodes else far_out).shape[1]
+        for group in range(groups):
+            begin += rows
+            flat[begin - extra : begin, :] = table[group]
 
     def plane(x, carry):
         for z in range(nz):
@@ -322,31 +344,74 @@
         return carry
 
     lax.fori_loop(0, nx, plane, 0)
+    begin = 0
+    copies = []
+    for out in (near_out, far_out):
+        groups, rows, _ = out.shape
+        first = 0 if out is near_out else near_out.shape[0] * near_out.shape[1]
+        for group in range(groups):
+            copies.append(
+                pltpu.make_async_copy(flat.at[pl.ds(first + group * rows, rows)], out.at[group], sems.at[2 + len(copies)])
+            )
+    for copy in copies:
+        copy.start()
+    for copy in copies:
+        copy.wait()
     e_copy.wait()
     h_copy.wait()
 
 
-def collect_kernel(cap, blocks, out, chosen, split):
-    n_from, rows, pts = blocks.shape
-    n_part, node_count, _ = out.shape
-    room = chosen.shape[1] // n_from
-    parts = room // LANES
+def summed(blocks, first, cap, node_row, chosen, split, node_count):
     ids = lax.broadcasted_iota(jnp.int32, (node_count, LANES), 0).astype(F32)
+    n_from, _, pts = blocks.shape
+    many = len(first)
+    for source in range(n_from):
+        for i in range(many):
+            seat = (source * many + i) * LANES
+            row = node_row[i]
+            hit = ids == blocks[source, row : row + 1, :]
+            chosen[:, seat : seat + LANES] = jnp.where(hit, 1.0, 0.0).astype(jnp.bfloat16)
+            values = blocks[source, first[i] : first[i] + cap, :]
+            high = values.astype(jnp.bfloat16)
+            split[seat : seat + cap, 0:pts] = high
+            split[seat : seat + cap, pts : 2 * pts] = (values - high.astype(F32)).astype(jnp.bfloat16)
+    both = jnp.dot(chosen[...], split[...], preferred_element_type=F32)
+    return both[:, 0:pts] + both[:, pts : 2 * pts]
+
+
+def collect_kernel(cap, blocks, *refs):
+    *outs, chosen, split = refs
+    if cap < LANES:
+        split[...] = jnp.zeros(split.shape, split.dtype)
+    for part, out in enumerate(outs):
+        out[...] = summed(blocks, [part * cap], cap, [len(outs) * cap + part], chosen, split, out.shape[0])
+
+
+def regroup_kernel(cap, blocks, order, out):
+    n_from = blocks.shape[0]
+    n_part = out.shape[0]
+    out[:, n_from * cap :, :] = jnp.full((n_part, out.shape[1] - n_from * cap, PTS), -1.0, F32)
+    for source in range(n_from):
+        for part in range(n_part):
+            out[part, source * cap : (source + 1) * cap, :] = blocks[source, part * cap : (part + 1) * cap, :]
+            row = n_part * cap + part
+            out[part, n_from * cap + source : n_from * cap + source + 1, :] = blocks[source, row : row + 1, :]
+
+
+def collect_far_kernel(cap, n_mid, blocks, out, chosen, split):
     split[...] = jnp.zeros(split.shape, split.dtype)
-    for part in range(n_part):
-        for source in range(n_from):
-            for piece in range(parts):
-                row = n_part * cap + part * parts + piece
-                lanes = slice(source * room + piece * LANES, source * room + (piece + 1) * LANES)
-                hit = ids == blocks[source, row : row + 1, :]
-                chosen[:, lanes] = jnp.where(hit, 1.0, 0.0).astype(jnp.bfloat16)
-            values = blocks[source, part * cap : (part + 1) * cap, :]
-            high = values.astype(jnp.bfloat16)
-            here = slice(source * room, source * room + cap)
-            split[here, 0:pts] = high
-            split[here, pts : 2 * pts] = (values - high.astype(F32)).astype(jnp.bfloat16)
-        both = jnp.dot(chosen[...], split[...], preferred_element_type=F32)
-        out[part] = both[:, 0:pts] + both[:, pts : 2 * pts]
+    first = [i * cap for i in range(n_mid)]
+    node_row = [n_mid * cap + i for i in range(n_mid)]
+    out[...] = summed(blocks, first, cap, node_row, chosen, split, out.shape[0])
+
+
+def finish_kernel(enthalpy, *refs):
+    *parts, out = refs
+    heat = parts[0][...]
+    for part in parts[1:]:
+        heat = heat + part[...]
+    content = enthalpy[...] + (0.25 / STEPS) * heat
+    out[...] = jnp.where(content < 0.0, content / 2.0, jnp.where(content > 1.0, (content - 1.0) / 3.0, 0.0))
 
 
 def shifted(block, d_col, d_hgt):
@@ -359,14 +424,6 @@
         if 0 <= c + d_col < n_col and 0 <= h + d_hgt < n_hgt
     ]
     return lax.ppermute(block, ("col", "hgt"), route)
-
-
-def tissue_warmth_kelvin(heat_content_per_mass):
-    return jnp.where(
-        heat_content_per_mass < 0.0,
-        heat_content_per_mass / 2.0,
-        jnp.where(heat_content_per_mass > 1.0, (heat_content_per_mass - 1.0) / 3.0, 0.0),
-    )
 
 
 def per_device(
@@ -403,6 +460,7 @@
 
     e_start = far(efield_lattice_vector)
     h_start = far(hfield_lattice_vector)
+    my_col = lax.axis_index("col").astype(jnp.int32).reshape(1)
     owners = block_owner.reshape(1, count)
     nodes = block_node.reshape(1, count)
     field = vmem(3, nx, nz, ny)
@@ -420,18 +478,19 @@
         load_kernel,
         (whole, whole, whole, field, field, two_rows, three_rows, two_rows),
         [FAR] * 4 + [WHOLE],
-        [far(cell_temp), far(region_tags), e_start, h_start, owners + nodes],
+        [far(cell_temp), far(region_tags), e_start, h_start, owners + nodes + my_col],
         "load",
         60,
         scratch=[vmem(nx, nz, ny), pltpu.VMEM((nx, nz, ny), jnp.int32), sem((3, 4))],
     )
-    room_for = -(-cap // LANES) * LANES
-    extra = -(-(n_col * room_for // LANES) // ROWS) * ROWS
-    place, send_nodes = kernel(
-        functools.partial(places_kernel, n_col, n_hgt, cap, extra),
-        (jax.ShapeDtypeStruct((1, count), jnp.int32), jax.ShapeDtypeStruct((n_hgt * extra, PTS), F32)),
-        [WHOLE] * 2,
-        [owners, nodes],
+    near = 2 * cap // 3 // ROWS * ROWS
+    far_cap = -(-(cap - near) // ROWS) * ROWS
+    extra = -(-max(n_col, n_hgt) // ROWS) * ROWS
+    place, near_nodes, far_nodes = kernel(
+        functools.partial(places_kernel, n_col, n_hgt, near, far_cap, extra),
+        (jax.ShapeDtypeStruct((1, count), jnp.int32), vmem(n_hgt, extra, PTS), vmem(n_col, extra, PTS)),
+        [SCALARS, WHOLE, WHOLE],
+        [my_col, owners, nodes],
         "places",
         8,
     )
@@ -488,38 +547,76 @@
             {5: 0, 6: 1},
         )
 
-    send, e_out, h_out = pl.pallas_call(
+    near_rows = n_col * near + extra
+    far_rows = n_hgt * far_cap + extra
+    near_send, far_send, e_out, h_out = pl.pallas_call(
         pack_kernel,
         out_shape=(
-            jax.ShapeDtypeStruct((n_hgt, n_col * cap + extra, PTS), F32),
+            pltpu.HBM((n_hgt, near_rows, PTS), F32),
+            pltpu.HBM((n_col, far_rows, PTS), F32),
             pltpu.HBM((3, nx, nz, ny), F32),
             pltpu.HBM((3, nx, nz, ny), F32),
         ),
-        in_specs=[SCALARS, WHOLE, WHOLE, WHOLE, WHOLE],
-        out_specs=(WHOLE, FAR, FAR),
-        scratch_shapes=[sem((2,))],
+        in_specs=[SCALARS] + [WHOLE] * 5,
+        out_specs=(FAR, FAR, FAR, FAR),
+        scratch_shapes=[vmem(n_hgt * near_rows + n_col * far_rows, PTS), sem((2 + n_hgt + n_col,))],
         compiler_params=params(VMEM_MIB),
         cost_estimate=cost(cells, cells * 36),
         name="pack",
-    )(place.reshape(count), power, send_nodes, e, h)
-    blocks = lax.all_to_all(send, "hgt", split_axis=0, concat_axis=0, tiled=True)
-    partial = pl.pallas_call(
-        functools.partial(collect_kernel, cap),
-        out_shape=jax.ShapeDtypeStruct((n_col, node_count, PTS), F32),
-        in_specs=[WHOLE],
-        out_specs=WHOLE,
-        scratch_shapes=[
-            pltpu.VMEM((node_count, n_hgt * room_for), jnp.bfloat16),
-            pltpu.VMEM((n_hgt * room_for, 2 * PTS), jnp.bfloat16),
-        ],
-        compiler_params=params(VMEM_MIB),
-        cost_estimate=cost(n_col * node_count * n_hgt * room_for * PTS * 4, cells * 8),
-        name="collect",
-    )(blocks)
-    parts = lax.all_to_all(partial, "col", split_axis=0, concat_axis=0, tiled=True)
-    heat = jnp.sum(parts, axis=0)
-    heat_content_per_mass = node_enthalpy + (0.25 / STEPS) * heat
-    return e_out, h_out, tissue_warmth_kelvin(heat_content_per_mass)
+    )(place.reshape(count), power, near_nodes, far_nodes, e, h)
+
+    def swap(x, axis):
+        return lax.all_to_all(x, axis, split_axis=0, concat_axis=0, tiled=True)
+
+    def one_hot_space(sources):
+        return [
+            pltpu.VMEM((node_count, sources * LANES), jnp.bfloat16),
+            pltpu.VMEM((sources * LANES, 2 * PTS), jnp.bfloat16),
+        ]
+
+    near_blocks = swap(near_send, "hgt")
+    far_blocks = swap(far_send, "col")
+    node_rows = jax.ShapeDtypeStruct((node_count, PTS), F32)
+    partial = kernel(
+        functools.partial(collect_kernel, near),
+        (node_rows,) * n_col,
+        [WHOLE],
+        [near_blocks],
+        "collect",
+        100,
+        scratch=one_hot_space(n_hgt),
+    )
+    parts = [partial[0]]
+    for turn in range(1, n_col):
+        route = [(c, (c + turn) % n_col) for c in range(n_col)]
+        parts.append(lax.ppermute(partial[turn], "col", route))
+    far_again = kernel(
+        functools.partial(regroup_kernel, far_cap),
+        jax.ShapeDtypeStruct((n_hgt, n_col * far_cap + ROWS, PTS), F32),
+        [WHOLE, FAR],
+        [far_blocks, partial[0]],
+        "regroup",
+        0,
+    )
+    far_final = swap(far_again, "hgt")
+    far_heat = kernel(
+        functools.partial(collect_far_kernel, far_cap, n_col),
+        node_rows,
+        [WHOLE],
+        [far_final],
+        "collect_far",
+        10,
+        scratch=one_hot_space(n_dev),
+    )
+    node_temp = kernel(
+        finish_kernel,
+        node_rows,
+        [WHOLE] * (2 + n_col),
+        [node_enthalpy, *parts, far_heat],
+        "finish",
+        1,
+    )
+    return e_out, h_out, node_temp
 
 
 def solution(mesh):

time: 155 us -> 174 us (1.12); the launches traced: 155 us -> 172 us
  waiting for transfers between devices: 18.8 us -> 54.6 us
  blocking collectives: 64.9 us -> 30.8 us
  starting transfers between devices: 34.3 us -> 44.4 us
  local copies, waits for them, and re-layouts: 0.5 us -> 3.49 us
  Pallas kernels: 34.3 us -> 37.2 us
    all_to_all x0 -> x2, waiting for transfers between devices: none -> 34.4 us  [swap(): return lax.all_to_all(x, axis, split_axis=0, concat_axis=0, tiled=True)]
    all_to_all x2 -> x1, blocking collectives: 64.9 us -> 30.8 us  [swap(): return lax.all_to_all(x, axis, split_axis=0, concat_axis=0, tiled=True)]
    all_to_all x0 -> x2, starting transfers between devices: none -> 7.08 us  [swap(): return lax.all_to_all(x, axis, split_axis=0, concat_axis=0, tiled=True)]
    pallas_call x18 -> x22, Pallas kernels: 26.7 us -> 31.8 us  [kernel(): pl.pallas_call(body, out_shape=outs, in_specs=ins, out_specs=jax.tree.map...]
    ppermute x0 -> x3, starting transfers between devices: none -> 3.87 us  [per_device(): parts.append(lax.ppermute(partial[turn], 'col', route))]
    unnamed x8 -> x14, local copies, waits for them, and re-layouts: 0.22 us -> 3.21 us
    pallas_call x2 -> x1, Pallas kernels: 7.7 us -> 5.44 us  [per_device(): pl.pallas_call(pack_kernel, out_shape=(pltpu.HBM((n_hgt, near_rows, PTS),...]
  transfers between devices with their start and end apart: 16 -> 21, of which waited for: 10 -> 12; matrix products, arithmetic and copies ran while one was open for 0% -> 0% of each run, Pallas kernels for 14% -> 15%
where the time goes in v4:
time: 174 us; the launch traced here: 172 us
  waiting for transfers between devices  54.6 us (31%)
  starting transfers between devices  44.4 us (26%)
  Pallas kernels  37.2 us (21%)
  blocking collectives  30.8 us (18%)
  local copies, waits for them, and re-layouts  3.49 us (2%)
    all_to_all x2, waiting for transfers between devices, swap(): return lax.all_to_all(x, axis, split_axis=0, concat_axis=0, tiled=True)  34.4 us
    ppermute x16, starting transfers between devices, shifted(): return lax.ppermute(block, ('col', 'hgt'), route)  33.5 us
    pallas_call x22, Pallas kernels, kernel(): pl.pallas_call(body, out_shape=outs, in_specs=ins, out_specs=jax.tree.map...  31.8 us
    all_to_all x1, blocking collectives, swap(): return lax.all_to_all(x, axis, split_axis=0, concat_axis=0, tiled=True)  30.8 us
    ppermute x16, waiting for transfers between devices, shifted(): return lax.ppermute(block, ('col', 'hgt'), route)  19.9 us
    all_to_all x2, starting transfers between devices, swap(): return lax.all_to_all(x, axis, split_axis=0, concat_axis=0, tiled=True)  7.08 us
    pallas_call x1, Pallas kernels, per_device(): pl.pallas_call(pack_kernel, out_shape=(pltpu.HBM((n_hgt, near_rows, PTS),...  5.44 us
    ppermute x3, starting transfers between devices, per_device(): parts.append(lax.ppermute(partial[turn], 'col', route))  3.87 us
  transfers between devices with their start and end apart: 21, of which 12 were waited for; matrix products, arithmetic and copies ran while one was open for 0% of the time, Pallas kernels for 15%

profile of v4, /device:TPU:0, one launch (start us, length us, event | category | flops | bytes accessed | tf_op | source)
XLA Modules:
  0.0 171.6 jit_solution(15205759522281845529)
XLA Ops:
  5.1 4.9 %load.1 = (f32[16,24,1024]{2,1,0:T(8,128)S(1)}, f32[16,24,1024]{2,1,0:T(8,128)S(1)}, f32[16,24,1024]{2,1,0:T(8,128)S(1)}, f32[3,16,24,1024]{3,2,1,0:T(8,128)S(1)...) custom-call(f32[16,24,1024]{2,1,0:T(8,128)} %temp_far.1, ...), custom_call_target="tpu_custom_call" | custom-call | flops 23592960 | bytes 23592960 | tf_op jit(solution)/shard_map/load/pallas_call | solution.py:449
  10.1 3.5 %collective-permute-done.1.col = f32[2,24,1024]{2,1,0:T(8,128)S(1)} collective-permute-done((f32[2,24,1024]{2,1,0:T(8,128)S(1)}, f32[2,24,1024]{2,1,0:T(8,128)S(1)}, u32[]{:S(2)}, u32[]{:S(2)}) %collective-permute-start.1) | collective-permute-done | bytes 196640 | tf_op jit(solution)/shard_map/ppermute | solution.py:426
  13.7 4.1 %collective-permute-start.3 = (f32[2,24,1024]{2,1,0:T(8,128)S(1)}, f32[2,24,1024]{2,1,0:T(8,128)S(1)}, u32[]{:S(2)}, u32[]{:S(2)}) collective-permute-start(f32[2,24,1024]{2,1,0:T(8,128)S(1)} %get-tuple-element.79), channel_id=1, source_target_pairs={{0,8},{1,9},{2,10},{3,11},{4,12},{5,13},{6,14},{7,15},{8,16},{9,17... | collective-permute-start | bytes 589832 | tf_op jit(solution)/shard_map/ppermute | solution.py:426
  25.1 2.2 %e_rest_0.1 = (f32[3,16,24,1024]{3,2,1,0:T(8,128)S(1)}, f32[16,24,1024]{2,1,0:T(8,128)S(1)}, f32[3,16,1024]{2,1,0:T(8,128)S(1)}) custom-call(f32[3,16,24,1024]{3,2,1,0:T(8,128)S(1)} %get-tuple-element.74.h.h_old, f32[16,24,1024]{2,1,0:T(8,128)S(1)} %get-tuple-element.75.ca, ...), custom_call_target="tpu_custom_call", output_to_operand_aliasing={{0}: (5, {}), {1}: (6, {})} | custom-call | flops 17694720 | bytes 17694720 | tf_op jit(solution)/shard_map/e_rest_0/pallas_call | solution.py:449
  27.9 4.7 %collective-permute-done.5.col = f32[2,24,1024]{2,1,0:T(8,128)S(1)} collective-permute-done((f32[2,24,1024]{2,1,0:T(8,128)S(1)}, f32[2,24,1024]{2,1,0:T(8,128)S(1)}, u32[]{:S(2)}, u32[]{:S(2)}) %collective-permute-start.5) | collective-permute-done | bytes 196640 | tf_op jit(solution)/shard_map/ppermute | solution.py:426
  32.7 3.5 %collective-permute-start.7 = (f32[2,24,1024]{2,1,0:T(8,128)S(1)}, f32[2,24,1024]{2,1,0:T(8,128)S(1)}, u32[]{:S(2)}, u32[]{:S(2)}) collective-permute-start(f32[2,24,1024]{2,1,0:T(8,128)S(1)} %get-tuple-element.91), channel_id=1, source_target_pairs={{0,8},{1,9},{2,10},{3,11},{4,12},{5,13},{6,14},{7,15},{8,16},{9,17... | collective-permute-start | bytes 589832 | tf_op jit(solution)/shard_map/ppermute | solution.py:426
  36.2 2.3 %collective-permute-start.6 = (f32[2,16,1024]{2,1,0:T(8,128)S(1)}, f32[2,16,1024]{2,1,0:T(8,128)S(1)}, u32[]{:S(2)}, u32[]{:S(2)}) collective-permute-start(f32[2,16,1024]{2,1,0:T(8,128)S(1)} %get-tuple-element.90.rows_old), channel_id=1, source_target_pairs={{0,1},{1,2},{2,3},{3,4},{4,5},{5,6},{6,7},{8,9},{9,10},{10,11},{11... | collective-permute-start | bytes 393224 | tf_op jit(solution)/shard_map/ppermute | solution.py:426
  43.9 2.4 %e_rest_1.1 = (f32[3,16,24,1024]{3,2,1,0:T(8,128)S(1)}, f32[16,24,1024]{2,1,0:T(8,128)S(1)}, f32[3,16,1024]{2,1,0:T(8,128)S(1)}) custom-call(f32[3,16,24,1024]{3,2,1,0:T(8,128)S(1)} %get-tuple-element.89.h.h_old, f32[16,24,1024]{2,1,0:T(8,128)S(1)} %get-tuple-element.75.ca, ...), custom_call_target="tpu_custom_call", output_to_operand_aliasing={{0}: (5, {}), {1}: (6, {})} | custom-call | flops 17694720 | bytes 17694720 | tf_op jit(solution)/shard_map/e_rest_1/pallas_call | solution.py:449
  46.3 4.3 %collective-permute-done.9.col = f32[2,24,1024]{2,1,0:T(8,128)S(1)} collective-permute-done((f32[2,24,1024]{2,1,0:T(8,128)S(1)}, f32[2,24,1024]{2,1,0:T(8,128)S(1)}, u32[]{:S(2)}, u32[]{:S(2)}) %collective-permute-start.9) | collective-permute-done | bytes 196640 | tf_op jit(solution)/shard_map/ppermute | solution.py:426
  50.7 3.6 %collective-permute-start.11 = (f32[2,24,1024]{2,1,0:T(8,128)S(1)}, f32[2,24,1024]{2,1,0:T(8,128)S(1)}, u32[]{:S(2)}, u32[]{:S(2)}) collective-permute-start(f32[2,24,1024]{2,1,0:T(8,128)S(1)} %get-tuple-element.103), channel_id=1, source_target_pairs={{0,8},{1,9},{2,10},{3,11},{4,12},{5,13},{6,14},{7,15},{8,16},{9,17... | collective-permute-start | bytes 589832 | tf_op jit(solution)/shard_map/ppermute | solution.py:426
  54.4 2.1 %collective-permute-start.10 = (f32[2,16,1024]{2,1,0:T(8,128)S(1)}, f32[2,16,1024]{2,1,0:T(8,128)S(1)}, u32[]{:S(2)}, u32[]{:S(2)}) collective-permute-start(f32[2,16,1024]{2,1,0:T(8,128)S(1)} %get-tuple-element.102.rows_old), channel_id=1, source_target_pairs={{0,1},{1,2},{2,3},{3,4},{4,5},{5,6},{6,7},{8,9},{9,10},{10,11},{11... | collective-permute-start | bytes 393224 | tf_op jit(solution)/shard_map/ppermute | solution.py:426
  61.9 2.4 %e_rest_2.1 = (f32[3,16,24,1024]{3,2,1,0:T(8,128)S(1)}, f32[16,24,1024]{2,1,0:T(8,128)S(1)}, f32[3,16,1024]{2,1,0:T(8,128)S(1)}) custom-call(f32[3,16,24,1024]{3,2,1,0:T(8,128)S(1)} %get-tuple-element.101.h.h_old, f32[16,24,1024]{2,1,0:T(8,128)S(1)} %get-tuple-element.75.ca, ...), custom_call_target="tpu_custom_call", output_to_operand_aliasing={{0}: (5, {}), {1}: (6, {})} | custom-call | flops 17694720 | bytes 17694720 | tf_op jit(solution)/shard_map/e_rest_2/pallas_call | solution.py:449
  64.4 4.7 %collective-permute-done.13.col = f32[2,24,1024]{2,1,0:T(8,128)S(1)} collective-permute-done((f32[2,24,1024]{2,1,0:T(8,128)S(1)}, f32[2,24,1024]{2,1,0:T(8,128)S(1)}, u32[]{:S(2)}, u32[]{:S(2)}) %collective-permute-start.13) | collective-permute-done | bytes 196640 | tf_op jit(solution)/shard_map/ppermute | solution.py:426
  69.2 3.0 %collective-permute-start.14 = (f32[2,24,1024]{2,1,0:T(8,128)S(1)}, f32[2,24,1024]{2,1,0:T(8,128)S(1)}, u32[]{:S(2)}, u32[]{:S(2)}) collective-permute-start(f32[2,24,1024]{2,1,0:T(8,128)S(1)} %get-tuple-element.114), channel_id=1, source_target_pairs={{0,8},{1,9},{2,10},{3,11},{4,12},{5,13},{6,14},{7,15},{8,16},{9,17... | collective-permute-start | bytes 589832 | tf_op jit(solution)/shard_map/ppermute | solution.py:426
  72.3 2.7 %collective-permute-start.15 = (f32[2,16,1024]{2,1,0:T(8,128)S(1)}, f32[2,16,1024]{2,1,0:T(8,128)S(1)}, u32[]{:S(2)}, u32[]{:S(2)}) collective-permute-start(f32[2,16,1024]{2,1,0:T(8,128)S(1)} %get-tuple-element.115), channel_id=1, source_target_pairs={{0,1},{1,2},{2,3},{3,4},{4,5},{5,6},{6,7},{8,9},{9,10},{10,11},{11... | collective-permute-start | bytes 393224 | tf_op jit(solution)/shard_map/ppermute | solution.py:426
  76.6 2.6 %h_rest_3.1 = (f32[3,16,24,1024]{3,2,1,0:T(8,128)S(1)}, f32[3,16,1024]{2,1,0:T(8,128)}) custom-call(f32[3,16,24,1024]{3,2,1,0:T(8,128)S(1)} %get-tuple-element.108.e.e_old, f32[2,16,1024]{2,1,0:T(8,128)S(1)} %collective-permute-done.12.hgt, f32[3,16,24,1024]{3,2,1,0:T(8,128)S(1)} %get-tuple-element.112.h_old), custom_call_target="tpu_custom_call", output_to_operand_aliasing={{0}: (2, {})} | custom-call | flops 15728640 | bytes 15728640 | tf_op jit(solution)/shard_map/h_rest_3/pallas_call | solution.py:449
  79.2 2.4 %e_last_3.1 = (f32[3,16,24,1024]{3,2,1,0:T(8,128)S(1)}, f32[16,24,1024]{2,1,0:T(8,128)S(1)}) custom-call(f32[3,16,24,1024]{3,2,1,0:T(8,128)S(1)} %get-tuple-element.113.h, f32[16,24,1024]{2,1,0:T(8,128)S(1)} %get-tuple-element.75.ca, f32[16,24,1024]{2,1,0:T(8,128)S(1)} %get-tuple-element.76.cb, ...), custom_call_target="tpu_custom_call", output_to_operand_aliasing={{0}: (6, {}), {1}: (7, {})} | custom-call | flops 19660800 | bytes 19660800 | tf_op jit(solution)/shard_map/e_last_3/pallas_call | solution.py:449
  81.6 5.4 %pack.1 = (f32[8,520,128]{2,1,0:T(8,128)}, f32[4,520,128]{2,1,0:T(8,128)}, f32[3,16,24,1024]{3,2,1,0:T(8,128)}, f32[3,16,24,1024]{3,2,1,0:T(8,128)}) custom-call(s32[3072]{0:T(1024)S(1)} %bitcast.8, f32[16,24,1024]{2,1,0:T(8,128)S(1)} %get-tuple-element.117.power, f32[8,8,128]{2,1,0:T(8,128)S(1)} %get-tuple-element.118.near_nodes, ...), custom_call_target="tpu_custom_call" | custom-call | flops 393216 | bytes 14155776 | tf_op jit(solution)/shard_map/pack/pallas_call | solution.py:552
  87.1 30.8 %all_to_all.15.blocks = f32[8,520,128]{2,1,0:T(8,128)S(1)} all-to-all(f32[8,520,128]{2,1,0:T(8,128)} %get-tuple-element.123), channel_id=1, replica_groups=mesh['col'=4,'hgt'=8] {'hgt'}, dimensions={0} | all-to-all | bytes 4259840 | tf_op jit(solution)/shard_map/all_to_all | solution.py:569
  117.9 3.5 %all-to-all-start.1 = ((f32[4,520,128]{2,1,0:T(8,128)}), f32[4,520,128]{2,1,0:T(8,128)S(1)}, u32[]{:S(2)}, u32[]{:S(2)}) async-start(f32[4,520,128]{2,1,0:T(8,128)} %get-tuple-element.128), calls=%async_computation.1 | async-start | bytes 2129920 | tf_op jit(solution)/shard_map/all_to_all | solution.py:569
  125.2 22.6 %all-to-all-done.1.blocks = f32[4,520,128]{2,1,0:T(8,128)S(1)} async-done(((f32[4,520,128]{2,1,0:T(8,128)}), f32[4,520,128]{2,1,0:T(8,128)S(1)}, u32[]{:S(2)}, u32[]{:S(2)}) %all-to-all-start.1) | async-done | bytes 1064992 | tf_op jit(solution)/shard_map/all_to_all | solution.py:569
  148.9 3.6 %all-to-all-start.2 = ((f32[8,264,128]{2,1,0:T(8,128)}), f32[8,264,128]{2,1,0:T(8,128)S(1)}, u32[]{:S(2)}, u32[]{:S(2)}) async-start(f32[8,264,128]{2,1,0:T(8,128)} %regroup.1), calls=%async_computation.2 | async-start | bytes 2162688 | tf_op jit(solution)/shard_map/all_to_all | solution.py:569
  152.6 2.0 %collective-permute-start.17 = (f32[384,128]{1,0:T(8,128)}, f32[384,128]{1,0:T(8,128)S(1)}, u32[]{:S(2)}, u32[]{:S(2)}) collective-permute-start(f32[384,128]{1,0:T(8,128)} %copy-done.2), channel_id=1, source_target_pairs={{0,16},{8,24},{16,0},{24,8},{1,17},{9,25},{17,1},{25,9},{2,18},{10... | collective-permute-start | bytes 589832 | tf_op jit(solution)/shard_map/ppermute | solution.py:592
  156.4 11.8 %all-to-all-done.2.blocks = f32[8,264,128]{2,1,0:T(8,128)S(1)} async-done(((f32[8,264,128]{2,1,0:T(8,128)}), f32[8,264,128]{2,1,0:T(8,128)S(1)}, u32[]{:S(2)}, u32[]{:S(2)}) %all-to-all-start.2) | async-done | bytes 1081376 | tf_op jit(solution)/shard_map/all_to_all | solution.py:569
  (59 shorter events, 35.4 us)
Async XLA Ops:
  0.6 4.0 %copy-start.4 = (s32[1,1,16,24,8,1]{3,5,4,2,1,0:T(1,128)S(1)}, s32[1,1,16,24,8,1]{3,5,4,2,1,0:T(1,128)}, u32[]{:S(2)}) copy-start(s32[1,1,16,24,8,1]{3,5,4,2,1,0:T(1,128)} %param.11) | copy-start | bytes 36868
  0.6 4.2 %copy-start.5 = (s32[1,1,16,24,8]{3,4,2,1,0:T(8,128)S(1)}, s32[1,1,16,24,8]{3,4,2,1,0:T(8,128)}, u32[]{:S(2)}) copy-start(s32[1,1,16,24,8]{3,4,2,1,0:T(8,128)} %param.12) | copy-start | bytes 36868
  2.0 8.1 %collective-permute-start = (f32[2,16,1024]{2,1,0:T(8,128)S(1)}, f32[2,16,1024]{2,1,0:T(8,128)S(1)}, u32[]{:S(2)}, u32[]{:S(2)}) collective-permute-start(f32[2,16,1024]{2,1,0:T(8,128)S(1)} %get-tuple-element.68.rows_old), channel_id=1, source_target_pairs={{1,0},{2,1},{3,2},{4,3},{5,4},{6,5},{7,6},{9,8},{10,9},{11,10},{12... | collective-permute-start | bytes 393224 | tf_op jit(solution)/shard_map/ppermute | solution.py:426
  3.3 10.3 %collective-permute-start.1 = (f32[2,24,1024]{2,1,0:T(8,128)S(1)}, f32[2,24,1024]{2,1,0:T(8,128)S(1)}, u32[]{:S(2)}, u32[]{:S(2)}) collective-permute-start(f32[2,24,1024]{2,1,0:T(8,128)S(1)} %get-tuple-element.69), channel_id=1, source_target_pairs={{8,0},{9,1},{10,2},{11,3},{12,4},{13,5},{14,6},{15,7},{16,8},{17,9... | collective-permute-start | bytes 589832 | tf_op jit(solution)/shard_map/ppermute | solution.py:426
  13.7 8.5 %collective-permute-start.3 = (f32[2,24,1024]{2,1,0:T(8,128)S(1)}, f32[2,24,1024]{2,1,0:T(8,128)S(1)}, u32[]{:S(2)}, u32[]{:S(2)}) collective-permute-start(f32[2,24,1024]{2,1,0:T(8,128)S(1)} %get-tuple-element.79), channel_id=1, source_target_pairs={{0,8},{1,9},{2,10},{3,11},{4,12},{5,13},{6,14},{7,15},{8,16},{9,17... | collective-permute-start | bytes 589832 | tf_op jit(solution)/shard_map/ppermute | solution.py:426
  17.9 3.7 %collective-permute-start.2 = (f32[2,16,1024]{2,1,0:T(8,128)S(1)}, f32[2,16,1024]{2,1,0:T(8,128)S(1)}, u32[]{:S(2)}, u32[]{:S(2)}) collective-permute-start(f32[2,16,1024]{2,1,0:T(8,128)S(1)} %get-tuple-element.78.rows_old), channel_id=1, source_target_pairs={{0,1},{1,2},{2,3},{3,4},{4,5},{5,6},{6,7},{8,9},{9,10},{10,11},{11... | collective-permute-start | bytes 393224 | tf_op jit(solution)/shard_map/ppermute | solution.py:426
  22.5 10.1 %collective-permute-start.5 = (f32[2,24,1024]{2,1,0:T(8,128)S(1)}, f32[2,24,1024]{2,1,0:T(8,128)S(1)}, u32[]{:S(2)}, u32[]{:S(2)}) collective-permute-start(f32[2,24,1024]{2,1,0:T(8,128)S(1)} %get-tuple-element.86), channel_id=1, source_target_pairs={{8,0},{9,1},{10,2},{11,3},{12,4},{13,5},{14,6},{15,7},{16,8},{17,9... | collective-permute-start | bytes 589832 | tf_op jit(solution)/shard_map/ppermute | solution.py:426
  23.8 4.1 %collective-permute-start.4 = (f32[2,16,1024]{2,1,0:T(8,128)S(1)}, f32[2,16,1024]{2,1,0:T(8,128)S(1)}, u32[]{:S(2)}, u32[]{:S(2)}) collective-permute-start(f32[2,16,1024]{2,1,0:T(8,128)S(1)} %get-tuple-element.85.rows_old), channel_id=1, source_target_pairs={{1,0},{2,1},{3,2},{4,3},{5,4},{6,5},{7,6},{9,8},{10,9},{11,10},{12... | collective-permute-start | bytes 393224 | tf_op jit(solution)/shard_map/ppermute | solution.py:426
  32.7 8.4 %collective-permute-start.7 = (f32[2,24,1024]{2,1,0:T(8,128)S(1)}, f32[2,24,1024]{2,1,0:T(8,128)S(1)}, u32[]{:S(2)}, u32[]{:S(2)}) collective-permute-start(f32[2,24,1024]{2,1,0:T(8,128)S(1)} %get-tuple-element.91), channel_id=1, source_target_pairs={{0,8},{1,9},{2,10},{3,11},{4,12},{5,13},{6,14},{7,15},{8,16},{9,17... | collective-permute-start | bytes 589832 | tf_op jit(solution)/shard_map/ppermute | solution.py:426
  36.2 4.2 %collective-permute-start.6 = (f32[2,16,1024]{2,1,0:T(8,128)S(1)}, f32[2,16,1024]{2,1,0:T(8,128)S(1)}, u32[]{:S(2)}, u32[]{:S(2)}) collective-permute-start(f32[2,16,1024]{2,1,0:T(8,128)S(1)} %get-tuple-element.90.rows_old), channel_id=1, source_target_pairs={{0,1},{1,2},{2,3},{3,4},{4,5},{5,6},{6,7},{8,9},{9,10},{10,11},{11... | collective-permute-start | bytes 393224 | tf_op jit(solution)/shard_map/ppermute | solution.py:426
  41.3 9.2 %collective-permute-start.9 = (f32[2,24,1024]{2,1,0:T(8,128)S(1)}, f32[2,24,1024]{2,1,0:T(8,128)S(1)}, u32[]{:S(2)}, u32[]{:S(2)}) collective-permute-start(f32[2,24,1024]{2,1,0:T(8,128)S(1)} %get-tuple-element.98), channel_id=1, source_target_pairs={{8,0},{9,1},{10,2},{11,3},{12,4},{13,5},{14,6},{15,7},{16,8},{17,9... | collective-permute-start | bytes 589832 | tf_op jit(solution)/shard_map/ppermute | solution.py:426
  42.6 3.7 %collective-permute-start.8 = (f32[2,16,1024]{2,1,0:T(8,128)S(1)}, f32[2,16,1024]{2,1,0:T(8,128)S(1)}, u32[]{:S(2)}, u32[]{:S(2)}) collective-permute-start(f32[2,16,1024]{2,1,0:T(8,128)S(1)} %get-tuple-element.97.rows_old), channel_id=1, source_target_pairs={{1,0},{2,1},{3,2},{4,3},{5,4},{6,5},{7,6},{9,8},{10,9},{11,10},{12... | collective-permute-start | bytes 393224 | tf_op jit(solution)/shard_map/ppermute | solution.py:426
  50.7 8.4 %collective-permute-start.11 = (f32[2,24,1024]{2,1,0:T(8,128)S(1)}, f32[2,24,1024]{2,1,0:T(8,128)S(1)}, u32[]{:S(2)}, u32[]{:S(2)}) collective-permute-start(f32[2,24,1024]{2,1,0:T(8,128)S(1)} %get-tuple-element.103), channel_id=1, source_target_pairs={{0,8},{1,9},{2,10},{3,11},{4,12},{5,13},{6,14},{7,15},{8,16},{9,17... | collective-permute-start | bytes 589832 | tf_op jit(solution)/shard_map/ppermute | solution.py:426
  54.4 4.1 %collective-permute-start.10 = (f32[2,16,1024]{2,1,0:T(8,128)S(1)}, f32[2,16,1024]{2,1,0:T(8,128)S(1)}, u32[]{:S(2)}, u32[]{:S(2)}) collective-permute-start(f32[2,16,1024]{2,1,0:T(8,128)S(1)} %get-tuple-element.102.rows_old), channel_id=1, source_target_pairs={{0,1},{1,2},{2,3},{3,4},{4,5},{5,6},{6,7},{8,9},{9,10},{10,11},{11... | collective-permute-start | bytes 393224 | tf_op jit(solution)/shard_map/ppermute | solution.py:426
  59.3 9.8 %collective-permute-start.13 = (f32[2,24,1024]{2,1,0:T(8,128)S(1)}, f32[2,24,1024]{2,1,0:T(8,128)S(1)}, u32[]{:S(2)}, u32[]{:S(2)}) collective-permute-start(f32[2,24,1024]{2,1,0:T(8,128)S(1)} %get-tuple-element.110), channel_id=1, source_target_pairs={{8,0},{9,1},{10,2},{11,3},{12,4},{13,5},{14,6},{15,7},{16,8},{17,9... | collective-permute-start | bytes 589832 | tf_op jit(solution)/shard_map/ppermute | solution.py:426
  60.6 3.8 %collective-permute-start.12 = (f32[2,16,1024]{2,1,0:T(8,128)S(1)}, f32[2,16,1024]{2,1,0:T(8,128)S(1)}, u32[]{:S(2)}, u32[]{:S(2)}) collective-permute-start(f32[2,16,1024]{2,1,0:T(8,128)S(1)} %get-tuple-element.109), channel_id=1, source_target_pairs={{1,0},{2,1},{3,2},{4,3},{5,4},{6,5},{7,6},{9,8},{10,9},{11,10},{12... | collective-permute-start | bytes 393224 | tf_op jit(solution)/shard_map/ppermute | solution.py:426
  69.2 10.0 %collective-permute-start.14 = (f32[2,24,1024]{2,1,0:T(8,128)S(1)}, f32[2,24,1024]{2,1,0:T(8,128)S(1)}, u32[]{:S(2)}, u32[]{:S(2)}) collective-permute-start(f32[2,24,1024]{2,1,0:T(8,128)S(1)} %get-tuple-element.114), channel_id=1, source_target_pairs={{0,8},{1,9},{2,10},{3,11},{4,12},{5,13},{6,14},{7,15},{8,16},{9,17... | collective-permute-start | bytes 589832 | tf_op jit(solution)/shard_map/ppermute | solution.py:426
  72.3 6.9 %collective-permute-start.15 = (f32[2,16,1024]{2,1,0:T(8,128)S(1)}, f32[2,16,1024]{2,1,0:T(8,128)S(1)}, u32[]{:S(2)}, u32[]{:S(2)}) collective-permute-start(f32[2,16,1024]{2,1,0:T(8,128)S(1)} %get-tuple-element.115), channel_id=1, source_target_pairs={{0,1},{1,2},{2,3},{3,4},{4,5},{5,6},{6,7},{8,9},{9,10},{10,11},{11... | collective-permute-start | bytes 393224 | tf_op jit(solution)/shard_map/ppermute | solution.py:426
  117.9 30.0 %all-to-all-start.1 = ((f32[4,520,128]{2,1,0:T(8,128)}), f32[4,520,128]{2,1,0:T(8,128)S(1)}, u32[]{:S(2)}, u32[]{:S(2)}) async-start(f32[4,520,128]{2,1,0:T(8,128)} %get-tuple-element.128), calls=%async_computation.1 | async-start | bytes 2129920 | tf_op jit(solution)/shard_map/all_to_all | solution.py:569
  148.9 19.3 %all-to-all-start.2 = ((f32[8,264,128]{2,1,0:T(8,128)}), f32[8,264,128]{2,1,0:T(8,128)S(1)}, u32[]{:S(2)}, u32[]{:S(2)}) async-start(f32[8,264,128]{2,1,0:T(8,128)} %regroup.1), calls=%async_computation.2 | async-start | bytes 2162688 | tf_op jit(solution)/shard_map/all_to_all | solution.py:569
  152.5 17.2 %collective-permute-start.16 = (f32[384,128]{1,0:T(8,128)}, f32[384,128]{1,0:T(8,128)S(1)}, u32[]{:S(2)}, u32[]{:S(2)}) collective-permute-start(f32[384,128]{1,0:T(8,128)} %copy-done.3), channel_id=1, source_target_pairs={{0,8},{8,16},{16,24},{24,0},{1,9},{9,17},{17,25},{25,1},{2,10},{10... | collective-permute-start | bytes 589832 | tf_op jit(solution)/shard_map/ppermute | solution.py:592
  152.6 17.4 %collective-permute-start.17 = (f32[384,128]{1,0:T(8,128)}, f32[384,128]{1,0:T(8,128)S(1)}, u32[]{:S(2)}, u32[]{:S(2)}) collective-permute-start(f32[384,128]{1,0:T(8,128)} %copy-done.2), channel_id=1, source_target_pairs={{0,16},{8,24},{16,0},{24,8},{1,17},{9,25},{17,1},{25,9},{2,18},{10... | collective-permute-start | bytes 589832 | tf_op jit(solution)/shard_map/ppermute | solution.py:592
  154.6 15.4 %collective-permute-start.18 = (f32[384,128]{1,0:T(8,128)}, f32[384,128]{1,0:T(8,128)S(1)}, u32[]{:S(2)}, u32[]{:S(2)}) collective-permute-start(f32[384,128]{1,0:T(8,128)} %copy-done.1), channel_id=1, source_target_pairs={{0,24},{8,0},{16,8},{24,16},{1,25},{9,1},{17,9},{25,17},{2,26},{10... | collective-permute-start | bytes 589832 | tf_op jit(solution)/shard_map/ppermute | solution.py:592
  169.9 0.9 copy-start
  (3 other events, 2.1 us)

commit v5 on v4

--- a/solution.py
+++ b/solution.py
@@ -13,7 +13,7 @@
 LANES = 128
 ROWS = 8
 F32 = jnp.float32
-VMEM_MIB = 16
+VMEM_MIB = 20
 
 WHOLE = pl.BlockSpec(memory_space=pltpu.VMEM)
 SCALARS = pl.BlockSpec(memory_space=pltpu.SMEM)
@@ -261,7 +261,7 @@
     over(1, nx, plane)
 
 
-def places_kernel(n_col, n_hgt, near, far_cap, extra, my_col, owner, node, place, near_nodes, far_nodes):
+def places_kernel(n_col, n_hgt, cap, my_col, owner, node, place, mine_nodes, pair_nodes, other_nodes):
     n_dev = n_col * n_hgt
     count = owner.shape[1]
     width = 256
@@ -269,57 +269,79 @@
     before = lax.broadcasted_iota(jnp.int32, (width, width), 0)
     after = lax.broadcasted_iota(jnp.int32, (width, width), 1)
     upper = jnp.where(before <= after, 1.0, 0.0).astype(jnp.bfloat16)
-    room_for = 2 * LANES
-    near_rows = n_col * near + extra
-    far_rows = n_hgt * far_cap + extra
+    per = -(-cap // LANES)
+    room_for = per * LANES
     room = lax.broadcasted_iota(jnp.int32, (room_for, width), 0)
     total = jnp.zeros((n_dev, 1), F32)
     parts_of = jnp.zeros((2 * n_dev, room_for), F32)
     nt = (((1,), (1,)), ((), ()))
+    begins, heights = starts_of(n_col, n_hgt, cap)
     for start in range(0, count, width):
         own = owner[:, start : start + width]
-        own_col = lax.div(own, n_hgt)
-        own_hgt = lax.rem(own, n_hgt)
         hit = jnp.where(rows == own, 1.0, 0.0)
         running = total + jnp.dot(hit.astype(jnp.bfloat16), upper, preferred_element_type=F32)
         total = running[:, width - 1 : width]
         rank = jnp.sum(hit * running, axis=0, keepdims=True).astype(jnp.int32) - 1
-        place[:, start : start + width] = jnp.where(
-            rank < near,
-            own_hgt * near_rows + lax.rem(own_col - my_col[0] + n_col, n_col) * near + rank,
-            n_hgt * near_rows + own_col * far_rows + own_hgt * far_cap + (rank - near),
+        turn = lax.bitwise_xor(lax.div(own, n_hgt), my_col[0])
+        own_hgt = lax.rem(own, n_hgt)
+        begin = jnp.where(
+            turn == 0,
+            begins[0] + own_hgt * heights[0],
+            jnp.where(
+                turn == 1,
+                begins[1] + own_hgt * heights[1],
+                begins[2] + own_hgt * heights[2] + (turn - 2) * cap,
+            ),
         )
-        rank = jnp.where(rank < near, rank, rank + (LANES - near))
+        place[:, start : start + width] = begin + rank
         number = node[:, start : start + width]
         upper_part = lax.div(number, 16)
         lower_part = number - 16 * upper_part
         seat = jnp.where(room == rank, 1.0, 0.0).astype(jnp.bfloat16)
         both = jnp.concatenate([hit * upper_part.astype(F32), hit * lower_part.astype(F32)], 0)
         parts_of = parts_of + lax.dot_general(both.astype(jnp.bfloat16), seat, nt, preferred_element_type=F32)
-    seat_of = lax.broadcasted_iota(jnp.int32, (n_dev, LANES), 1).astype(F32)
-    table = 16.0 * parts_of[:n_dev] + parts_of[n_dev:]
-    near_taken = (seat_of < near) & (seat_of < total)
-    far_taken = (seat_of < far_cap) & (seat_of + near < total)
-    near_table = jnp.where(near_taken, table[:, :LANES], -1.0)
-    far_table = jnp.where(far_taken, table[:, LANES:], -1.0)
-    near_nodes[...] = jnp.full(near_nodes.shape, -1.0, F32)
-    far_nodes[...] = jnp.full(far_nodes.shape, -1.0, F32)
+    taken = lax.broadcasted_iota(jnp.int32, (n_dev, room_for), 1).astype(F32) < total
+    table = jnp.where(taken, 16.0 * parts_of[:n_dev] + parts_of[n_dev:], -1.0)
+    for ref in (mine_nodes, pair_nodes, other_nodes):
+        ref[...] = jnp.full(ref.shape, -1.0, F32)
     for group in range(n_col):
-        mine = slice(group * n_hgt, (group + 1) * n_hgt)
-        far_nodes[group, 0:n_hgt, :] = far_table[mine, :]
-        slot = lax.rem(group - my_col[0] + n_col, n_col)
+        turn = lax.bitwise_xor(jnp.int32(group), my_col[0])
         for part in range(n_hgt):
-            near_nodes[part, pl.ds(slot, 1), :] = near_table[group * n_hgt + part : group * n_hgt + part + 1, :]
-
-
-def pack_kernel(place, power, near_nodes, far_nodes, e, h, near_out, far_out, e_out, h_out, flat, sems):
+            at = group * n_hgt + part
+            for piece in range(per):
+                row = table[at : at + 1, piece * LANES : (piece + 1) * LANES]
+
+                @pl.when(turn == 0)
+                def _():
+                    mine_nodes[part, piece : piece + 1, :] = row
+
+                @pl.when(turn == 1)
+                def _():
+                    pair_nodes[part, piece : piece + 1, :] = row
+
+                @pl.when(turn > 1)
+                def _():
+                    other_nodes[part, pl.ds((turn - 2) * per + piece, 1), :] = row
+
+
+def table_rows(parts, cap):
+    return -(-parts * -(-cap // LANES) // ROWS) * ROWS
+
+
+def starts_of(n_col, n_hgt, cap):
+    one = cap + table_rows(1, cap)
+    heights = [one, one, (n_col - 2) * cap + table_rows(n_col - 2, cap)]
+    return [0, n_hgt * heights[0], n_hgt * (heights[0] + heights[1])], heights
+
+
+def pack_kernel(cap, place, power, mine_nodes, pair_nodes, other_nodes, e, h, mine, pair, other, e_out, h_out, flat, sems):
     nx, nz, ny = power.shape
     e_copy = pltpu.make_async_copy(e, e_out, sems.at[0])
     h_copy = pltpu.make_async_copy(h, h_out, sems.at[1])
     e_copy.start()
     h_copy.start()
     per_row = ny // PTS
-    begin = 0
+    outs = (mine, pair, other)
     chunk = 8 * ROWS
 
     def clear(i, carry):
@@ -329,12 +351,15 @@
     lax.fori_loop(0, flat.shape[0] // chunk, clear, 0)
     for at in range(flat.shape[0] // chunk * chunk, flat.shape[0], ROWS):
         flat[at : at + ROWS, :] = jnp.zeros((ROWS, PTS), F32)
-    for table in (near_nodes, far_nodes):
-        groups, extra, _ = table.shape
-        rows = (near_out if table is near_nodes else far_out).shape[1]
+    begin = 0
+    begins = []
+    heights = [cap + mine_nodes.shape[1], pair.shape[1], other.shape[1]]
+    for out, rows, table in zip(outs, heights, (mine_nodes, pair_nodes, other_nodes)):
+        groups = out.shape[0]
+        begins.append(begin)
         for group in range(groups):
             begin += rows
-            flat[begin - extra : begin, :] = table[group]
+            flat[begin - table.shape[1] : begin, :] = table[group]
 
     def plane(x, carry):
         for z in range(nz):
@@ -344,15 +369,12 @@
         return carry
 
     lax.fori_loop(0, nx, plane, 0)
-    begin = 0
     copies = []
-    for out in (near_out, far_out):
-        groups, rows, _ = out.shape
-        first = 0 if out is near_out else near_out.shape[0] * near_out.shape[1]
-        for group in range(groups):
-            copies.append(
-                pltpu.make_async_copy(flat.at[pl.ds(first + group * rows, rows)], out.at[group], sems.at[2 + len(copies)])
-            )
+    for out, rows, first in zip(outs, heights, begins):
+        for group in range(out.shape[0]):
+            source = flat.at[pl.ds(first + group * rows, rows)]
+            target = out.at[group, pl.ds(0, rows)]
+            copies.append(pltpu.make_async_copy(source, target, sems.at[2 + len(copies)]))
     for copy in copies:
         copy.start()
     for copy in copies:
@@ -364,13 +386,16 @@
 def summed(blocks, first, cap, node_row, chosen, split, node_count):
     ids = lax.broadcasted_iota(jnp.int32, (node_count, LANES), 0).astype(F32)
     n_from, _, pts = blocks.shape
+    per = -(-cap // LANES)
     many = len(first)
     for source in range(n_from):
         for i in range(many):
-            seat = (source * many + i) * LANES
-            row = node_row[i]
-            hit = ids == blocks[source, row : row + 1, :]
-            chosen[:, seat : seat + LANES] = jnp.where(hit, 1.0, 0.0).astype(jnp.bfloat16)
+            seat = (source * many + i) * per * LANES
+            for piece in range(per):
+                row = node_row[i] + piece
+                lanes = slice(seat + piece * LANES, seat + (piece + 1) * LANES)
+                hit = ids == blocks[source, row : row + 1, :]
+                chosen[:, lanes] = jnp.where(hit, 1.0, 0.0).astype(jnp.bfloat16)
             values = blocks[source, first[i] : first[i] + cap, :]
             high = values.astype(jnp.bfloat16)
             split[seat : seat + cap, 0:pts] = high
@@ -381,28 +406,28 @@
 
 def collect_kernel(cap, blocks, *refs):
     *outs, chosen, split = refs
-    if cap < LANES:
-        split[...] = jnp.zeros(split.shape, split.dtype)
+    per = -(-cap // LANES)
+    split[...] = jnp.zeros(split.shape, split.dtype)
     for part, out in enumerate(outs):
-        out[...] = summed(blocks, [part * cap], cap, [len(outs) * cap + part], chosen, split, out.shape[0])
-
-
-def regroup_kernel(cap, blocks, order, out):
-    n_from = blocks.shape[0]
-    n_part = out.shape[0]
-    out[:, n_from * cap :, :] = jnp.full((n_part, out.shape[1] - n_from * cap, PTS), -1.0, F32)
-    for source in range(n_from):
-        for part in range(n_part):
-            out[part, source * cap : (source + 1) * cap, :] = blocks[source, part * cap : (part + 1) * cap, :]
-            row = n_part * cap + part
-            out[part, n_from * cap + source : n_from * cap + source + 1, :] = blocks[source, row : row + 1, :]
-
-
-def collect_far_kernel(cap, n_mid, blocks, out, chosen, split):
+        out[...] = summed(blocks, [part * cap], cap, [len(outs) * cap + part * per], chosen, split, out.shape[0])
+
+
+def merge_kernel(pair, order, mine_old, mine, sems):
+    rows = pair.shape[1]
+    copies = [
+        pltpu.make_async_copy(pair.at[group], mine.at[group, pl.ds(rows, rows)], sems.at[group])
+        for group in range(mine.shape[0])
+    ]
+    for copy in copies:
+        copy.start()
+    for copy in copies:
+        copy.wait()
+
+
+def collect_mine_kernel(cap, blocks, out, chosen, split):
+    half = blocks.shape[1] // 2
     split[...] = jnp.zeros(split.shape, split.dtype)
-    first = [i * cap for i in range(n_mid)]
-    node_row = [n_mid * cap + i for i in range(n_mid)]
-    out[...] = summed(blocks, first, cap, node_row, chosen, split, out.shape[0])
+    out[...] = summed(blocks, [0, half], cap, [cap, half + cap], chosen, split, out.shape[0])
 
 
 def finish_kernel(enthalpy, *refs):
@@ -483,12 +508,15 @@
         60,
         scratch=[vmem(nx, nz, ny), pltpu.VMEM((nx, nz, ny), jnp.int32), sem((3, 4))],
     )
-    near = 2 * cap // 3 // ROWS * ROWS
-    far_cap = -(-(cap - near) // ROWS) * ROWS
-    extra = -(-max(n_col, n_hgt) // ROWS) * ROWS
-    place, near_nodes, far_nodes = kernel(
-        functools.partial(places_kernel, n_col, n_hgt, near, far_cap, extra),
-        (jax.ShapeDtypeStruct((1, count), jnp.int32), vmem(n_hgt, extra, PTS), vmem(n_col, extra, PTS)),
+    begins, heights = starts_of(n_col, n_hgt, cap)
+    place, mine_nodes, pair_nodes, other_nodes = kernel(
+        functools.partial(places_kernel, n_col, n_hgt, cap),
+        (
+            jax.ShapeDtypeStruct((1, count), jnp.int32),
+            vmem(n_hgt, table_rows(1, cap), PTS),
+            vmem(n_hgt, table_rows(1, cap), PTS),
+            vmem(n_hgt, table_rows(n_col - 2, cap), PTS),
+        ),
         [SCALARS, WHOLE, WHOLE],
         [my_col, owners, nodes],
         "places",
@@ -547,74 +575,69 @@
             {5: 0, 6: 1},
         )
 
-    near_rows = n_col * near + extra
-    far_rows = n_hgt * far_cap + extra
-    near_send, far_send, e_out, h_out = pl.pallas_call(
-        pack_kernel,
+    mine, pair, other, e_out, h_out = pl.pallas_call(
+        functools.partial(pack_kernel, cap),
         out_shape=(
-            pltpu.HBM((n_hgt, near_rows, PTS), F32),
-            pltpu.HBM((n_col, far_rows, PTS), F32),
+            pltpu.HBM((n_hgt, 2 * heights[0], PTS), F32),
+            pltpu.HBM((n_hgt, heights[1], PTS), F32),
+            pltpu.HBM((n_hgt, heights[2], PTS), F32),
             pltpu.HBM((3, nx, nz, ny), F32),
             pltpu.HBM((3, nx, nz, ny), F32),
         ),
-        in_specs=[SCALARS] + [WHOLE] * 5,
-        out_specs=(FAR, FAR, FAR, FAR),
-        scratch_shapes=[vmem(n_hgt * near_rows + n_col * far_rows, PTS), sem((2 + n_hgt + n_col,))],
+        in_specs=[SCALARS] + [WHOLE] * 6,
+        out_specs=(FAR,) * 5,
+        scratch_shapes=[vmem(n_hgt * sum(heights), PTS), sem((2 + 3 * n_hgt,))],
         compiler_params=params(VMEM_MIB),
         cost_estimate=cost(cells, cells * 36),
         name="pack",
-    )(place.reshape(count), power, near_nodes, far_nodes, e, h)
+    )(place.reshape(count), power, mine_nodes, pair_nodes, other_nodes, e, h)
 
     def swap(x, axis):
         return lax.all_to_all(x, axis, split_axis=0, concat_axis=0, tiled=True)
 
+    def across(x, turn):
+        return lax.ppermute(x, "col", [(c, c ^ turn) for c in range(n_col)])
+
     def one_hot_space(sources):
-        return [
-            pltpu.VMEM((node_count, sources * LANES), jnp.bfloat16),
-            pltpu.VMEM((sources * LANES, 2 * PTS), jnp.bfloat16),
-        ]
-
-    near_blocks = swap(near_send, "hgt")
-    far_blocks = swap(far_send, "col")
+        seats = sources * -(-cap // LANES) * LANES
+        return [pltpu.VMEM((node_count, seats), jnp.bfloat16), pltpu.VMEM((seats, 2 * PTS), jnp.bfloat16)]
+
     node_rows = jax.ShapeDtypeStruct((node_count, PTS), F32)
-    partial = kernel(
-        functools.partial(collect_kernel, near),
-        (node_rows,) * n_col,
+    from_pair = across(pair, 1)
+    other_blocks = swap(other, "hgt")
+    sums = kernel(
+        functools.partial(collect_kernel, cap),
+        (node_rows,) * (n_col - 2),
         [WHOLE],
-        [near_blocks],
-        "collect",
-        100,
+        [other_blocks],
+        "collect_other",
+        1,
         scratch=one_hot_space(n_hgt),
     )
-    parts = [partial[0]]
-    for turn in range(1, n_col):
-        route = [(c, (c + turn) % n_col) for c in range(n_col)]
-        parts.append(lax.ppermute(partial[turn], "col", route))
-    far_again = kernel(
-        functools.partial(regroup_kernel, far_cap),
-        jax.ShapeDtypeStruct((n_hgt, n_col * far_cap + ROWS, PTS), F32),
-        [WHOLE, FAR],
-        [far_blocks, partial[0]],
-        "regroup",
-        0,
-    )
-    far_final = swap(far_again, "hgt")
-    far_heat = kernel(
-        functools.partial(collect_far_kernel, far_cap, n_col),
+    parts = [across(sums[turn - 2], turn) for turn in range(2, n_col)]
+    mine = pl.pallas_call(
+        merge_kernel,
+        out_shape=pltpu.HBM((n_hgt, 2 * heights[0], PTS), F32),
+        in_specs=[pl.BlockSpec(memory_space=pl.ANY), pl.BlockSpec(memory_space=pl.ANY), FAR],
+        out_specs=FAR,
+        input_output_aliases={2: 0},
+        scratch_shapes=[sem((n_hgt,))],
+        compiler_params=params(VMEM_MIB),
+        cost_estimate=cost(1, 1),
+        name="merge",
+    )(from_pair, sums[0], mine)
+    mine_blocks = swap(mine, "hgt")
+    own = kernel(
+        functools.partial(collect_mine_kernel, cap),
         node_rows,
         [WHOLE],
-        [far_final],
-        "collect_far",
-        10,
-        scratch=one_hot_space(n_dev),
+        [mine_blocks],
+        "collect_mine",
+        1,
+        scratch=one_hot_space(2 * n_hgt),
     )
     node_temp = kernel(
-        finish_kernel,
-        node_rows,
-        [WHOLE] * (2 + n_col),
-        [node_enthalpy, *parts, far_heat],
-        "finish",
-        1,
+        finish_kernel, node_rows, [WHOLE] * (n_col), [node_enthalpy, own, *parts], "finish", 1
     )
     return e_out, h_out, node_temp
 

time: 174 us -> 144 us (0.83); the launches traced: 172 us -> 144 us
  blocking collectives: 30.8 us -> 0 us
  waiting for transfers between devices: 54.6 us -> 59.5 us
  local copies, waits for them, and re-layouts: 3.49 us -> 0.51 us
    all_to_all x1 -> x0, blocking collectives: 30.8 us -> none  [swap(): return lax.all_to_all(x, axis, split_axis=0, concat_axis=0, tiled=True)]
    all_to_all x2, waiting for transfers between devices: 34.4 us -> 39.6 us  [swap(): return lax.all_to_all(x, axis, split_axis=0, concat_axis=0, tiled=True)]
    unnamed x14 -> x8, local copies, waits for them, and re-layouts: 3.21 us -> 0.22 us
    pallas_call x1 -> x2, Pallas kernels: 5.44 us -> 6.62 us  [the longest x1 5.61 us: per_device(): pl.pallas_call(functools.partial(pack_kernel, cap), out_shape=(pltpu.HBM(...]
    pallas_call x22 -> x21, Pallas kernels: 31.8 us -> 31.4 us  [kernel(): pl.pallas_call(body, out_shape=outs, in_specs=ins, out_specs=jax.tree.map...]
  transfers between devices with their start and end apart: 21 -> 21, of which waited for: 12 -> 11; matrix products, arithmetic and copies ran while one was open for 0% -> 0% of each run, Pallas kernels for 15% -> 18%
where the time goes in v5:
time: 144 us
  waiting for transfers between devices  59.5 us (41%)
  starting transfers between devices  44.4 us (31%)
  Pallas kernels  38 us (26%)
    all_to_all x2, waiting for transfers between devices, swap(): return lax.all_to_all(x, axis, split_axis=0, concat_axis=0, tiled=True)  39.6 us
    ppermute x16, starting transfers between devices, shifted(): return lax.ppermute(block, ('col', 'hgt'), route)  33.5 us
    pallas_call x21, Pallas kernels, kernel(): pl.pallas_call(body, out_shape=outs, in_specs=ins, out_specs=jax.tree.map...  31.4 us
    ppermute x16, waiting for transfers between devices, shifted(): return lax.ppermute(block, ('col', 'hgt'), route)  19.9 us
    all_to_all x2, starting transfers between devices, swap(): return lax.all_to_all(x, axis, split_axis=0, concat_axis=0, tiled=True)  7.46 us
    pallas_call x1, Pallas kernels, per_device(): pl.pallas_call(functools.partial(pack_kernel, cap), out_shape=(pltpu.HBM(...  5.61 us
    ppermute x3, starting transfers between devices, across(): return lax.ppermute(x, 'col', [(c, c ^ turn) for c in range(n_col)])  3.44 us
  transfers between devices with their start and end apart: 21, of which 11 were waited for; matrix products, arithmetic and copies ran while one was open for 0% of the time, Pallas kernels for 18%

profile of v5, /device:TPU:0, one launch (start us, length us, event | category | flops | bytes accessed | tf_op | source)
XLA Modules:
  0.0 143.5 jit_solution(8310077171691775694)
XLA Ops:
  5.1 4.9 %load.1 = (f32[16,24,1024]{2,1,0:T(8,128)S(1)}, f32[16,24,1024]{2,1,0:T(8,128)S(1)}, f32[16,24,1024]{2,1,0:T(8,128)S(1)}, f32[3,16,24,1024]{3,2,1,0:T(8,128)S(1)...) custom-call(f32[16,24,1024]{2,1,0:T(8,128)} %temp_far.1, ...), custom_call_target="tpu_custom_call" | custom-call | flops 23592960 | bytes 23592960 | tf_op jit(solution)/shard_map/load/pallas_call | solution.py:474
  10.1 3.5 %collective-permute-done.1.col = f32[2,24,1024]{2,1,0:T(8,128)S(1)} collective-permute-done((f32[2,24,1024]{2,1,0:T(8,128)S(1)}, f32[2,24,1024]{2,1,0:T(8,128)S(1)}, u32[]{:S(2)}, u32[]{:S(2)}) %collective-permute-start.1) | collective-permute-done | bytes 196640 | tf_op jit(solution)/shard_map/ppermute | solution.py:451
  13.7 4.1 %collective-permute-start.3 = (f32[2,24,1024]{2,1,0:T(8,128)S(1)}, f32[2,24,1024]{2,1,0:T(8,128)S(1)}, u32[]{:S(2)}, u32[]{:S(2)}) collective-permute-start(f32[2,24,1024]{2,1,0:T(8,128)S(1)} %get-tuple-element.79), channel_id=1, source_target_pairs={{0,8},{1,9},{2,10},{3,11},{4,12},{5,13},{6,14},{7,15},{8,16},{9,17... | collective-permute-start | bytes 589832 | tf_op jit(solution)/shard_map/ppermute | solution.py:451
  19.6 1.9 %h_rest_0.1 = (f32[3,16,24,1024]{3,2,1,0:T(8,128)S(1)}, f32[3,16,1024]{2,1,0:T(8,128)S(1)}) custom-call(f32[3,16,24,1024]{3,2,1,0:T(8,128)S(1)} %get-tuple-element.67.e.refs_0_, f32[2,16,1024]{2,1,0:T(8,128)S(1)} %collective-permute-done.hgt, f32[3,16,24,1024]{3,2,1,0:T(8,128)S(1)} %get-tuple-element.73.h_old), custom_call_target="tpu_custom_call", output_to_operand_aliasing={{0}: (2, {})} | custom-call | flops 15728640 | bytes 15728640 | tf_op jit(solution)/shard_map/h_rest_0/pallas_call | solution.py:474
  25.1 2.2 %e_rest_0.1 = (f32[3,16,24,1024]{3,2,1,0:T(8,128)S(1)}, f32[16,24,1024]{2,1,0:T(8,128)S(1)}, f32[3,16,1024]{2,1,0:T(8,128)S(1)}) custom-call(f32[3,16,24,1024]{3,2,1,0:T(8,128)S(1)} %get-tuple-element.74.h.h_old, f32[16,24,1024]{2,1,0:T(8,128)S(1)} %get-tuple-element.75.ca, ...), custom_call_target="tpu_custom_call", output_to_operand_aliasing={{0}: (5, {}), {1}: (6, {})} | custom-call | flops 17694720 | bytes 17694720 | tf_op jit(solution)/shard_map/e_rest_0/pallas_call | solution.py:474
  27.9 4.7 %collective-permute-done.5.col = f32[2,24,1024]{2,1,0:T(8,128)S(1)} collective-permute-done((f32[2,24,1024]{2,1,0:T(8,128)S(1)}, f32[2,24,1024]{2,1,0:T(8,128)S(1)}, u32[]{:S(2)}, u32[]{:S(2)}) %collective-permute-start.5) | collective-permute-done | bytes 196640 | tf_op jit(solution)/shard_map/ppermute | solution.py:451
  32.7 3.5 %collective-permute-start.7 = (f32[2,24,1024]{2,1,0:T(8,128)S(1)}, f32[2,24,1024]{2,1,0:T(8,128)S(1)}, u32[]{:S(2)}, u32[]{:S(2)}) collective-permute-start(f32[2,24,1024]{2,1,0:T(8,128)S(1)} %get-tuple-element.91), channel_id=1, source_target_pairs={{0,8},{1,9},{2,10},{3,11},{4,12},{5,13},{6,14},{7,15},{8,16},{9,17... | collective-permute-start | bytes 589832 | tf_op jit(solution)/shard_map/ppermute | solution.py:451
  36.2 2.3 %collective-permute-start.6 = (f32[2,16,1024]{2,1,0:T(8,128)S(1)}, f32[2,16,1024]{2,1,0:T(8,128)S(1)}, u32[]{:S(2)}, u32[]{:S(2)}) collective-permute-start(f32[2,16,1024]{2,1,0:T(8,128)S(1)} %get-tuple-element.90.rows_old), channel_id=1, source_target_pairs={{0,1},{1,2},{2,3},{3,4},{4,5},{5,6},{6,7},{8,9},{9,10},{10,11},{11... | collective-permute-start | bytes 393224 | tf_op jit(solution)/shard_map/ppermute | solution.py:451
  43.9 2.4 %e_rest_1.1 = (f32[3,16,24,1024]{3,2,1,0:T(8,128)S(1)}, f32[16,24,1024]{2,1,0:T(8,128)S(1)}, f32[3,16,1024]{2,1,0:T(8,128)S(1)}) custom-call(f32[3,16,24,1024]{3,2,1,0:T(8,128)S(1)} %get-tuple-element.89.h.h_old, f32[16,24,1024]{2,1,0:T(8,128)S(1)} %get-tuple-element.75.ca, ...), custom_call_target="tpu_custom_call", output_to_operand_aliasing={{0}: (5, {}), {1}: (6, {})} | custom-call | flops 17694720 | bytes 17694720 | tf_op jit(solution)/shard_map/e_rest_1/pallas_call | solution.py:474
  46.3 4.3 %collective-permute-done.9.col = f32[2,24,1024]{2,1,0:T(8,128)S(1)} collective-permute-done((f32[2,24,1024]{2,1,0:T(8,128)S(1)}, f32[2,24,1024]{2,1,0:T(8,128)S(1)}, u32[]{:S(2)}, u32[]{:S(2)}) %collective-permute-start.9) | collective-permute-done | bytes 196640 | tf_op jit(solution)/shard_map/ppermute | solution.py:451
  50.7 3.6 %collective-permute-start.11 = (f32[2,24,1024]{2,1,0:T(8,128)S(1)}, f32[2,24,1024]{2,1,0:T(8,128)S(1)}, u32[]{:S(2)}, u32[]{:S(2)}) collective-permute-start(f32[2,24,1024]{2,1,0:T(8,128)S(1)} %get-tuple-element.103), channel_id=1, source_target_pairs={{0,8},{1,9},{2,10},{3,11},{4,12},{5,13},{6,14},{7,15},{8,16},{9,17... | collective-permute-start | bytes 589832 | tf_op jit(solution)/shard_map/ppermute | solution.py:451
  54.4 2.1 %collective-permute-start.10 = (f32[2,16,1024]{2,1,0:T(8,128)S(1)}, f32[2,16,1024]{2,1,0:T(8,128)S(1)}, u32[]{:S(2)}, u32[]{:S(2)}) collective-permute-start(f32[2,16,1024]{2,1,0:T(8,128)S(1)} %get-tuple-element.102.rows_old), channel_id=1, source_target_pairs={{0,1},{1,2},{2,3},{3,4},{4,5},{5,6},{6,7},{8,9},{9,10},{10,11},{11... | collective-permute-start | bytes 393224 | tf_op jit(solution)/shard_map/ppermute | solution.py:451
  61.9 2.4 %e_rest_2.1 = (f32[3,16,24,1024]{3,2,1,0:T(8,128)S(1)}, f32[16,24,1024]{2,1,0:T(8,128)S(1)}, f32[3,16,1024]{2,1,0:T(8,128)S(1)}) custom-call(f32[3,16,24,1024]{3,2,1,0:T(8,128)S(1)} %get-tuple-element.101.h.h_old, f32[16,24,1024]{2,1,0:T(8,128)S(1)} %get-tuple-element.75.ca, ...), custom_call_target="tpu_custom_call", output_to_operand_aliasing={{0}: (5, {}), {1}: (6, {})} | custom-call | flops 17694720 | bytes 17694720 | tf_op jit(solution)/shard_map/e_rest_2/pallas_call | solution.py:474
  64.4 4.7 %collective-permute-done.13.col = f32[2,24,1024]{2,1,0:T(8,128)S(1)} collective-permute-done((f32[2,24,1024]{2,1,0:T(8,128)S(1)}, f32[2,24,1024]{2,1,0:T(8,128)S(1)}, u32[]{:S(2)}, u32[]{:S(2)}) %collective-permute-start.13) | collective-permute-done | bytes 196640 | tf_op jit(solution)/shard_map/ppermute | solution.py:451
  69.2 3.0 %collective-permute-start.14 = (f32[2,24,1024]{2,1,0:T(8,128)S(1)}, f32[2,24,1024]{2,1,0:T(8,128)S(1)}, u32[]{:S(2)}, u32[]{:S(2)}) collective-permute-start(f32[2,24,1024]{2,1,0:T(8,128)S(1)} %get-tuple-element.114), channel_id=1, source_target_pairs={{0,8},{1,9},{2,10},{3,11},{4,12},{5,13},{6,14},{7,15},{8,16},{9,17... | collective-permute-start | bytes 589832 | tf_op jit(solution)/shard_map/ppermute | solution.py:451
  72.3 2.7 %collective-permute-start.15 = (f32[2,16,1024]{2,1,0:T(8,128)S(1)}, f32[2,16,1024]{2,1,0:T(8,128)S(1)}, u32[]{:S(2)}, u32[]{:S(2)}) collective-permute-start(f32[2,16,1024]{2,1,0:T(8,128)S(1)} %get-tuple-element.115), channel_id=1, source_target_pairs={{0,1},{1,2},{2,3},{3,4},{4,5},{5,6},{6,7},{8,9},{9,10},{10,11},{11... | collective-permute-start | bytes 393224 | tf_op jit(solution)/shard_map/ppermute | solution.py:451
  75.0 2.2 %places.1 = (s32[1,3072]{1,0:T(1,128)S(1)}, f32[8,8,128]{2,1,0:T(8,128)S(1)}, f32[8,8,128]{2,1,0:T(8,128)S(1)}, f32[8,8,128]{2,1,0:T(8,128)S(1)}) custom-call(s32[1]{0:T(128)} %bitcast.my_col, s32[1,3072]{1,0:T(1,128)S(1)} %reshape.46.owner, s32[1,3072]{1,0:T(1,128)S(1)} %reshape.47.node), custom_call_target="tpu_custom_call" | custom-call | flops 3145728 | bytes 3145728 | tf_op jit(solution)/shard_map/places/pallas_call | solution.py:474
  77.2 2.6 %h_rest_3.1 = (f32[3,16,24,1024]{3,2,1,0:T(8,128)S(1)}, f32[3,16,1024]{2,1,0:T(8,128)}) custom-call(f32[3,16,24,1024]{3,2,1,0:T(8,128)S(1)} %get-tuple-element.108.e.e_old, f32[2,16,1024]{2,1,0:T(8,128)S(1)} %collective-permute-done.12.hgt, f32[3,16,24,1024]{3,2,1,0:T(8,128)S(1)} %get-tuple-element.112.h_old), custom_call_target="tpu_custom_call", output_to_operand_aliasing={{0}: (2, {})} | custom-call | flops 15728640 | bytes 15728640 | tf_op jit(solution)/shard_map/h_rest_3/pallas_call | solution.py:474
  79.8 2.4 %e_last_3.1 = (f32[3,16,24,1024]{3,2,1,0:T(8,128)S(1)}, f32[16,24,1024]{2,1,0:T(8,128)S(1)}) custom-call(f32[3,16,24,1024]{3,2,1,0:T(8,128)S(1)} %get-tuple-element.113.h, f32[16,24,1024]{2,1,0:T(8,128)S(1)} %get-tuple-element.75.ca, f32[16,24,1024]{2,1,0:T(8,128)S(1)} %get-tuple-element.76.cb, ...), custom_call_target="tpu_custom_call", output_to_operand_aliasing={{0}: (6, {}), {1}: (7, {})} | custom-call | flops 19660800 | bytes 19660800 | tf_op jit(solution)/shard_map/e_last_3/pallas_call | solution.py:474
  82.2 5.6 %pack.1 = (f32[8,400,128]{2,1,0:T(8,128)}, f32[8,200,128]{2,1,0:T(8,128)}, f32[8,392,128]{2,1,0:T(8,128)}, f32[3,16,24,1024]{3,2,1,0:T(8,128)}, f32[3,16,24,1024]{3,2,1,0:T(8,128)}) custom-call(s32[3072]{0:T(1024)S(1)} %bitcast.8, f32[16,24,1024]{2,1,0:T(8,128)S(1)} %get-tuple-element.117.power, f32[8,8,128]{2,1,0:T(8,128)S(1)} %get-tuple-element.118.mine_nodes, ...), custom_call_target="tpu_custom_call" | custom-call | flops 393216 | bytes 14155776 | tf_op jit(solution)/shard_map/pack/pallas_call | solution.py:578
  87.9 3.9 %all-to-all-start = ((f32[8,392,128]{2,1,0:T(8,128)}), f32[8,392,128]{2,1,0:T(8,128)S(1)}, u32[]{:S(2)}, u32[]{:S(2)}) async-start(f32[8,392,128]{2,1,0:T(8,128)} %get-tuple-element.125), calls=%async_computation | async-start | bytes 3211264 | tf_op jit(solution)/shard_map/all_to_all | solution.py:596
  92.7 20.4 %all-to-all-done.blocks = f32[8,392,128]{2,1,0:T(8,128)S(1)} async-done(((f32[8,392,128]{2,1,0:T(8,128)}), f32[8,392,128]{2,1,0:T(8,128)S(1)}, u32[]{:S(2)}, u32[]{:S(2)}) %all-to-all-start) | async-done | bytes 1605664 | tf_op jit(solution)/shard_map/all_to_all | solution.py:596
  115.8 3.6 %all-to-all-start.1 = ((f32[8,400,128]{2,1,0:T(8,128)}), f32[8,400,128]{2,1,0:T(8,128)S(1)}, u32[]{:S(2)}, u32[]{:S(2)}) async-start(f32[8,400,128]{2,1,0:T(8,128)} %merge.1), calls=%async_computation.1 | async-start | bytes 3276800 | tf_op jit(solution)/shard_map/all_to_all | solution.py:596
  121.9 19.2 %all-to-all-done.1.blocks = f32[8,400,128]{2,1,0:T(8,128)S(1)} async-done(((f32[8,400,128]{2,1,0:T(8,128)}), f32[8,400,128]{2,1,0:T(8,128)S(1)}, u32[]{:S(2)}, u32[]{:S(2)}) %all-to-all-start.1) | async-done | bytes 1638432 | tf_op jit(solution)/shard_map/all_to_all | solution.py:596
  (52 shorter events, 30.3 us)
Async XLA Ops:
  0.6 4.0 %copy-start.1 = (s32[1,1,16,24,8,1]{3,5,4,2,1,0:T(1,128)S(1)}, s32[1,1,16,24,8,1]{3,5,4,2,1,0:T(1,128)}, u32[]{:S(2)}) copy-start(s32[1,1,16,24,8,1]{3,5,4,2,1,0:T(1,128)} %param.11) | copy-start | bytes 36868
  0.6 4.2 %copy-start.2 = (s32[1,1,16,24,8]{3,4,2,1,0:T(8,128)S(1)}, s32[1,1,16,24,8]{3,4,2,1,0:T(8,128)}, u32[]{:S(2)}) copy-start(s32[1,1,16,24,8]{3,4,2,1,0:T(8,128)} %param.12) | copy-start | bytes 36868
  2.0 8.1 %collective-permute-start = (f32[2,16,1024]{2,1,0:T(8,128)S(1)}, f32[2,16,1024]{2,1,0:T(8,128)S(1)}, u32[]{:S(2)}, u32[]{:S(2)}) collective-permute-start(f32[2,16,1024]{2,1,0:T(8,128)S(1)} %get-tuple-element.68.rows_old), channel_id=1, source_target_pairs={{1,0},{2,1},{3,2},{4,3},{5,4},{6,5},{7,6},{9,8},{10,9},{11,10},{12... | collective-permute-start | bytes 393224 | tf_op jit(solution)/shard_map/ppermute | solution.py:451
  3.3 10.3 %collective-permute-start.1 = (f32[2,24,1024]{2,1,0:T(8,128)S(1)}, f32[2,24,1024]{2,1,0:T(8,128)S(1)}, u32[]{:S(2)}, u32[]{:S(2)}) collective-permute-start(f32[2,24,1024]{2,1,0:T(8,128)S(1)} %get-tuple-element.69), channel_id=1, source_target_pairs={{8,0},{9,1},{10,2},{11,3},{12,4},{13,5},{14,6},{15,7},{16,8},{17,9... | collective-permute-start | bytes 589832 | tf_op jit(solution)/shard_map/ppermute | solution.py:451
  13.7 8.5 %collective-permute-start.3 = (f32[2,24,1024]{2,1,0:T(8,128)S(1)}, f32[2,24,1024]{2,1,0:T(8,128)S(1)}, u32[]{:S(2)}, u32[]{:S(2)}) collective-permute-start(f32[2,24,1024]{2,1,0:T(8,128)S(1)} %get-tuple-element.79), channel_id=1, source_target_pairs={{0,8},{1,9},{2,10},{3,11},{4,12},{5,13},{6,14},{7,15},{8,16},{9,17... | collective-permute-start | bytes 589832 | tf_op jit(solution)/shard_map/ppermute | solution.py:451
  17.9 3.7 %collective-permute-start.2 = (f32[2,16,1024]{2,1,0:T(8,128)S(1)}, f32[2,16,1024]{2,1,0:T(8,128)S(1)}, u32[]{:S(2)}, u32[]{:S(2)}) collective-permute-start(f32[2,16,1024]{2,1,0:T(8,128)S(1)} %get-tuple-element.78.rows_old), channel_id=1, source_target_pairs={{0,1},{1,2},{2,3},{3,4},{4,5},{5,6},{6,7},{8,9},{9,10},{10,11},{11... | collective-permute-start | bytes 393224 | tf_op jit(solution)/shard_map/ppermute | solution.py:451
  22.5 10.1 %collective-permute-start.5 = (f32[2,24,1024]{2,1,0:T(8,128)S(1)}, f32[2,24,1024]{2,1,0:T(8,128)S(1)}, u32[]{:S(2)}, u32[]{:S(2)}) collective-permute-start(f32[2,24,1024]{2,1,0:T(8,128)S(1)} %get-tuple-element.86), channel_id=1, source_target_pairs={{8,0},{9,1},{10,2},{11,3},{12,4},{13,5},{14,6},{15,7},{16,8},{17,9... | collective-permute-start | bytes 589832 | tf_op jit(solution)/shard_map/ppermute | solution.py:451
  23.8 4.1 %collective-permute-start.4 = (f32[2,16,1024]{2,1,0:T(8,128)S(1)}, f32[2,16,1024]{2,1,0:T(8,128)S(1)}, u32[]{:S(2)}, u32[]{:S(2)}) collective-permute-start(f32[2,16,1024]{2,1,0:T(8,128)S(1)} %get-tuple-element.85.rows_old), channel_id=1, source_target_pairs={{1,0},{2,1},{3,2},{4,3},{5,4},{6,5},{7,6},{9,8},{10,9},{11,10},{12... | collective-permute-start | bytes 393224 | tf_op jit(solution)/shard_map/ppermute | solution.py:451
  32.7 8.4 %collective-permute-start.7 = (f32[2,24,1024]{2,1,0:T(8,128)S(1)}, f32[2,24,1024]{2,1,0:T(8,128)S(1)}, u32[]{:S(2)}, u32[]{:S(2)}) collective-permute-start(f32[2,24,1024]{2,1,0:T(8,128)S(1)} %get-tuple-element.91), channel_id=1, source_target_pairs={{0,8},{1,9},{2,10},{3,11},{4,12},{5,13},{6,14},{7,15},{8,16},{9,17... | collective-permute-start | bytes 589832 | tf_op jit(solution)/shard_map/ppermute | solution.py:451
  36.2 4.2 %collective-permute-start.6 = (f32[2,16,1024]{2,1,0:T(8,128)S(1)}, f32[2,16,1024]{2,1,0:T(8,128)S(1)}, u32[]{:S(2)}, u32[]{:S(2)}) collective-permute-start(f32[2,16,1024]{2,1,0:T(8,128)S(1)} %get-tuple-element.90.rows_old), channel_id=1, source_target_pairs={{0,1},{1,2},{2,3},{3,4},{4,5},{5,6},{6,7},{8,9},{9,10},{10,11},{11... | collective-permute-start | bytes 393224 | tf_op jit(solution)/shard_map/ppermute | solution.py:451
  41.3 9.2 %collective-permute-start.9 = (f32[2,24,1024]{2,1,0:T(8,128)S(1)}, f32[2,24,1024]{2,1,0:T(8,128)S(1)}, u32[]{:S(2)}, u32[]{:S(2)}) collective-permute-start(f32[2,24,1024]{2,1,0:T(8,128)S(1)} %get-tuple-element.98), channel_id=1, source_target_pairs={{8,0},{9,1},{10,2},{11,3},{12,4},{13,5},{14,6},{15,7},{16,8},{17,9... | collective-permute-start | bytes 589832 | tf_op jit(solution)/shard_map/ppermute | solution.py:451
  42.6 3.7 %collective-permute-start.8 = (f32[2,16,1024]{2,1,0:T(8,128)S(1)}, f32[2,16,1024]{2,1,0:T(8,128)S(1)}, u32[]{:S(2)}, u32[]{:S(2)}) collective-permute-start(f32[2,16,1024]{2,1,0:T(8,128)S(1)} %get-tuple-element.97.rows_old), channel_id=1, source_target_pairs={{1,0},{2,1},{3,2},{4,3},{5,4},{6,5},{7,6},{9,8},{10,9},{11,10},{12... | collective-permute-start | bytes 393224 | tf_op jit(solution)/shard_map/ppermute | solution.py:451
  50.7 8.4 %collective-permute-start.11 = (f32[2,24,1024]{2,1,0:T(8,128)S(1)}, f32[2,24,1024]{2,1,0:T(8,128)S(1)}, u32[]{:S(2)}, u32[]{:S(2)}) collective-permute-start(f32[2,24,1024]{2,1,0:T(8,128)S(1)} %get-tuple-element.103), channel_id=1, source_target_pairs={{0,8},{1,9},{2,10},{3,11},{4,12},{5,13},{6,14},{7,15},{8,16},{9,17... | collective-permute-start | bytes 589832 | tf_op jit(solution)/shard_map/ppermute | solution.py:451
  54.4 4.1 %collective-permute-start.10 = (f32[2,16,1024]{2,1,0:T(8,128)S(1)}, f32[2,16,1024]{2,1,0:T(8,128)S(1)}, u32[]{:S(2)}, u32[]{:S(2)}) collective-permute-start(f32[2,16,1024]{2,1,0:T(8,128)S(1)} %get-tuple-element.102.rows_old), channel_id=1, source_target_pairs={{0,1},{1,2},{2,3},{3,4},{4,5},{5,6},{6,7},{8,9},{9,10},{10,11},{11... | collective-permute-start | bytes 393224 | tf_op jit(solution)/shard_map/ppermute | solution.py:451
  59.3 9.8 %collective-permute-start.13 = (f32[2,24,1024]{2,1,0:T(8,128)S(1)}, f32[2,24,1024]{2,1,0:T(8,128)S(1)}, u32[]{:S(2)}, u32[]{:S(2)}) collective-permute-start(f32[2,24,1024]{2,1,0:T(8,128)S(1)} %get-tuple-element.110), channel_id=1, source_target_pairs={{8,0},{9,1},{10,2},{11,3},{12,4},{13,5},{14,6},{15,7},{16,8},{17,9... | collective-permute-start | bytes 589832 | tf_op jit(solution)/shard_map/ppermute | solution.py:451
  60.6 3.8 %collective-permute-start.12 = (f32[2,16,1024]{2,1,0:T(8,128)S(1)}, f32[2,16,1024]{2,1,0:T(8,128)S(1)}, u32[]{:S(2)}, u32[]{:S(2)}) collective-permute-start(f32[2,16,1024]{2,1,0:T(8,128)S(1)} %get-tuple-element.109), channel_id=1, source_target_pairs={{1,0},{2,1},{3,2},{4,3},{5,4},{6,5},{7,6},{9,8},{10,9},{11,10},{12... | collective-permute-start | bytes 393224 | tf_op jit(solution)/shard_map/ppermute | solution.py:451
  69.2 10.6 %collective-permute-start.14 = (f32[2,24,1024]{2,1,0:T(8,128)S(1)}, f32[2,24,1024]{2,1,0:T(8,128)S(1)}, u32[]{:S(2)}, u32[]{:S(2)}) collective-permute-start(f32[2,24,1024]{2,1,0:T(8,128)S(1)} %get-tuple-element.114), channel_id=1, source_target_pairs={{0,8},{1,9},{2,10},{3,11},{4,12},{5,13},{6,14},{7,15},{8,16},{9,17... | collective-permute-start | bytes 589832 | tf_op jit(solution)/shard_map/ppermute | solution.py:451
  72.3 7.5 %collective-permute-start.15 = (f32[2,16,1024]{2,1,0:T(8,128)S(1)}, f32[2,16,1024]{2,1,0:T(8,128)S(1)}, u32[]{:S(2)}, u32[]{:S(2)}) collective-permute-start(f32[2,16,1024]{2,1,0:T(8,128)S(1)} %get-tuple-element.115), channel_id=1, source_target_pairs={{0,1},{1,2},{2,3},{3,4},{4,5},{5,6},{6,7},{8,9},{9,10},{10,11},{11... | collective-permute-start | bytes 393224 | tf_op jit(solution)/shard_map/ppermute | solution.py:451
  87.9 25.2 %all-to-all-start = ((f32[8,392,128]{2,1,0:T(8,128)}), f32[8,392,128]{2,1,0:T(8,128)S(1)}, u32[]{:S(2)}, u32[]{:S(2)}) async-start(f32[8,392,128]{2,1,0:T(8,128)} %get-tuple-element.125), calls=%async_computation | async-start | bytes 3211264 | tf_op jit(solution)/shard_map/all_to_all | solution.py:596
  91.7 23.1 %collective-permute-start.16 = (f32[8,200,128]{2,1,0:T(8,128)}, f32[8,200,128]{2,1,0:T(8,128)S(1)}, u32[]{:S(2)}, u32[]{:S(2)}) collective-permute-start(f32[8,200,128]{2,1,0:T(8,128)} %get-tuple-element.124), channel_id=1, source_target_pairs={{0,8},{8,0},{16,24},{24,16},{1,9},{9,1},{17,25},{25,17},{2,10},{10... | collective-permute-start | bytes 2457608 | tf_op jit(solution)/shard_map/ppermute | solution.py:599
  114.8 28.0 %copy-start = (f32[384,128]{1,0:T(8,128)S(1)}, f32[384,128]{1,0:T(8,128)}, u32[]{:S(2)}) copy-start(f32[384,128]{1,0:T(8,128)} %enthalpy.1) | copy-start | bytes 589828
  115.8 25.3 %all-to-all-start.1 = ((f32[8,400,128]{2,1,0:T(8,128)}), f32[8,400,128]{2,1,0:T(8,128)S(1)}, u32[]{:S(2)}, u32[]{:S(2)}) async-start(f32[8,400,128]{2,1,0:T(8,128)} %merge.1), calls=%async_computation.1 | async-start | bytes 3276800 | tf_op jit(solution)/shard_map/all_to_all | solution.py:596
  119.4 23.3 %collective-permute-start.18 = (f32[384,128]{1,0:T(8,128)S(1)}, f32[384,128]{1,0:T(8,128)S(1)}, u32[]{:S(2)}, u32[]{:S(2)}) collective-permute-start(f32[384,128]{1,0:T(8,128)S(1)} %get-tuple-element.128), channel_id=1, source_target_pairs={{0,24},{8,16},{16,8},{24,0},{1,25},{9,17},{17,9},{25,1},{2,26},{10... | collective-permute-start | bytes 589832 | tf_op jit(solution)/shard_map/ppermute | solution.py:599
  120.1 22.7 %collective-permute-start.17 = (f32[384,128]{1,0:T(8,128)S(1)}, f32[384,128]{1,0:T(8,128)S(1)}, u32[]{:S(2)}, u32[]{:S(2)}) collective-permute-start(f32[384,128]{1,0:T(8,128)S(1)} %get-tuple-element.126.order), channel_id=1, source_target_pairs={{0,16},{8,24},{16,0},{24,8},{1,17},{9,25},{17,1},{25,9},{2,18},{10... | collective-permute-start | bytes 589832 | tf_op jit(solution)/shard_map/ppermute | solution.py:599

commit v6 on v5

--- a/solution.py
+++ b/solution.py
@@ -201,12 +201,13 @@
         to_hgt[1, here, :] = rows_old[1, here, :] - COURANT * ((hgt[0, here, :] - ex) - (after_row(ez, row) - ez))
 
 
-def h_rest_kernel(e, hgt, h_old, h, rows):
+def h_rest_kernel(e, hgt, h_old, h, *rows):
     nx, nz = e.shape[1:3]
 
     def keep(x):
-        for comp in range(3):
-            rows[comp, pl.ds(x, 1), :] = h[comp, x, 0:1, :]
+        if rows:
+            for comp in range(3):
+                rows[0][comp, pl.ds(x, 1), :] = h[comp, x, 0:1, :]
 
     def plane(x):
         for z in range(0, nz, ROWS):
@@ -250,8 +251,10 @@
     over(1, nx, plane)
 
 
-def e_last_kernel(first, h, ca, cb, sigma, col, hgt, e_old, power_old, e, power):
+def e_last_kernel(first, h, ca, cb, sigma, col, hgt, e_old, power_old, e, power, h_out, sem):
     nx, nz = e.shape[1:3]
+    copy = pltpu.make_async_copy(h, h_out, sem)
+    copy.start()
 
     def plane(x):
         for z in range(0, nz, ROWS):
@@ -259,9 +262,10 @@
 
     plane(0)
     over(1, nx, plane)
-
-
-def places_kernel(n_col, n_hgt, cap, my_col, owner, node, place, mine_nodes, pair_nodes, other_nodes):
+    copy.wait()
+
+
+def places_kernel(n_col, n_hgt, cap, my_col, owner, node, place, flat):
     n_dev = n_col * n_hgt
     count = owner.shape[1]
     width = 256
@@ -302,26 +306,31 @@
         parts_of = parts_of + lax.dot_general(both.astype(jnp.bfloat16), seat, nt, preferred_element_type=F32)
     taken = lax.broadcasted_iota(jnp.int32, (n_dev, room_for), 1).astype(F32) < total
     table = jnp.where(taken, 16.0 * parts_of[:n_dev] + parts_of[n_dev:], -1.0)
-    for ref in (mine_nodes, pair_nodes, other_nodes):
-        ref[...] = jnp.full(ref.shape, -1.0, F32)
+    chunk = 8 * ROWS
+
+    def clear(i, carry):
+        flat[pl.ds(pl.multiple_of(i * chunk, chunk), chunk), :] = jnp.zeros((chunk, PTS), F32)
+        return carry
+
+    lax.fori_loop(0, flat.shape[0] // chunk, clear, 0)
+    for at in range(flat.shape[0] // chunk * chunk, flat.shape[0], ROWS):
+        flat[at : at + ROWS, :] = jnp.zeros((ROWS, PTS), F32)
+    behind = [cap, cap, (n_col - 2) * cap]
+    for begin, height, skip in zip(begins, heights, behind):
+        for part in range(n_hgt):
+            at = begin + part * height
+            flat[at + skip : at + height, :] = jnp.full((height - skip, PTS), -1.0, F32)
     for group in range(n_col):
         turn = lax.bitwise_xor(jnp.int32(group), my_col[0])
+        kind = jnp.minimum(turn, 2)
+        begin = jnp.where(kind == 0, begins[0], jnp.where(kind == 1, begins[1], begins[2]))
+        height = jnp.where(kind == 2, heights[2], heights[0])
+        skip = jnp.where(kind == 2, behind[2] + (turn - 2) * per, cap)
         for part in range(n_hgt):
             at = group * n_hgt + part
             for piece in range(per):
                 row = table[at : at + 1, piece * LANES : (piece + 1) * LANES]
-
-                @pl.when(turn == 0)
-                def _():
-                    mine_nodes[part, piece : piece + 1, :] = row
-
-                @pl.when(turn == 1)
-                def _():
-                    pair_nodes[part, piece : piece + 1, :] = row
-
-                @pl.when(turn > 1)
-                def _():
-                    other_nodes[part, pl.ds((turn - 2) * per + piece, 1), :] = row
+                flat[pl.ds(begin + part * height + skip + piece, 1), :] = row
 
 
 def table_rows(parts, cap):
@@ -334,32 +343,11 @@
     return [0, n_hgt * heights[0], n_hgt * (heights[0] + heights[1])], heights
 
 
-def pack_kernel(cap, place, power, mine_nodes, pair_nodes, other_nodes, e, h, mine, pair, other, e_out, h_out, flat, sems):
+def pack_kernel(heights, place, power, flat_old, e, mine, pair, other, e_out, flat, sems):
     nx, nz, ny = power.shape
     e_copy = pltpu.make_async_copy(e, e_out, sems.at[0])
-    h_copy = pltpu.make_async_copy(h, h_out, sems.at[1])
     e_copy.start()
-    h_copy.start()
     per_row = ny // PTS
-    outs = (mine, pair, other)
-    chunk = 8 * ROWS
-
-    def clear(i, carry):
-        flat[pl.ds(pl.multiple_of(i * chunk, chunk), chunk), :] = jnp.zeros((chunk, PTS), F32)
-        return carry
-
-    lax.fori_loop(0, flat.shape[0] // chunk, clear, 0)
-    for at in range(flat.shape[0] // chunk * chunk, flat.shape[0], ROWS):
-        flat[at : at + ROWS, :] = jnp.zeros((ROWS, PTS), F32)
-    begin = 0
-    begins = []
-    heights = [cap + mine_nodes.shape[1], pair.shape[1], other.shape[1]]
-    for out, rows, table in zip(outs, heights, (mine_nodes, pair_nodes, other_nodes)):
-        groups = out.shape[0]
-        begins.append(begin)
-        for group in range(groups):
-            begin += rows
-            flat[begin - table.shape[1] : begin, :] = table[group]
 
     def plane(x, carry):
         for z in range(nz):
@@ -370,17 +358,17 @@
 
     lax.fori_loop(0, nx, plane, 0)
     copies = []
-    for out, rows, first in zip(outs, heights, begins):
+    first = 0
+    for out, rows in zip((mine, pair, other), heights):
         for group in range(out.shape[0]):
-            source = flat.at[pl.ds(first + group * rows, rows)]
             target = out.at[group, pl.ds(0, rows)]
-            copies.append(pltpu.make_async_copy(source, target, sems.at[2 + len(copies)]))
+            copies.append(pltpu.make_async_copy(flat.at[pl.ds(first, rows)], target, sems.at[1 + len(copies)]))
+            first += rows
     for copy in copies:
         copy.start()
     for copy in copies:
         copy.wait()
     e_copy.wait()
-    h_copy.wait()
 
 
 def summed(blocks, first, cap, node_row, chosen, split, node_count):
@@ -412,7 +400,7 @@
         out[...] = summed(blocks, [part * cap], cap, [len(outs) * cap + part * per], chosen, split, out.shape[0])
 
 
-def merge_kernel(pair, order, mine_old, mine, sems):
+def merge_kernel(pair, mine_old, mine, sems):
     rows = pair.shape[1]
     copies = [
         pltpu.make_async_copy(pair.at[group], mine.at[group, pl.ds(rows, rows)], sems.at[group])
@@ -509,14 +497,9 @@
         scratch=[vmem(nx, nz, ny), pltpu.VMEM((nx, nz, ny), jnp.int32), sem((3, 4))],
     )
     begins, heights = starts_of(n_col, n_hgt, cap)
-    place, mine_nodes, pair_nodes, other_nodes = kernel(
+    place, flat = kernel(
         functools.partial(places_kernel, n_col, n_hgt, cap),
-        (
-            jax.ShapeDtypeStruct((1, count), jnp.int32),
-            vmem(n_hgt, table_rows(1, cap), PTS),
-            vmem(n_hgt, table_rows(1, cap), PTS),
-            vmem(n_hgt, table_rows(n_col - 2, cap), PTS),
-        ),
+        (jax.ShapeDtypeStruct((1, count), jnp.int32), vmem(n_hgt * sum(heights), PTS)),
         [SCALARS, WHOLE, WHOLE],
         [my_col, owners, nodes],
         "places",
@@ -537,22 +520,24 @@
         e_hgt = hgt
         col = shifted(to_col, 1, 0)
         hgt = shifted(h_high, 0, 1)
-        h, h_rows = kernel(
-            h_rest_kernel, (field, three_rows), [WHOLE] * 3, [e, e_hgt, h], f"h_rest_{step}", 40, {2: 0}
-        )
+        last = step == STEPS - 1
+        outs = (field,) if last else (field, three_rows)
+        h, *h_rows = kernel(h_rest_kernel, outs, [WHOLE] * 3, [e, e_hgt, h], f"h_rest_{step}", 40, {2: 0})
         media = [h, ca, cb, sigma]
-        if step == STEPS - 1:
-            e, power = kernel(
+        if last:
+            e, power, h_out = pl.pallas_call(
                 functools.partial(e_last_kernel, first),
-                (field, whole),
-                [WHOLE] * 8,
-                media + [col, hgt, e, power],
-                f"e_last_{step}",
-                50,
-                {6: 0, 7: 1},
-            )
+                out_shape=(field, whole, pltpu.HBM((3, nx, nz, ny), F32)),
+                in_specs=[WHOLE] * 8,
+                out_specs=(WHOLE, WHOLE, FAR),
+                input_output_aliases={6: 0, 7: 1},
+                scratch_shapes=[sem],
+                compiler_params=params(VMEM_MIB),
+                cost_estimate=cost(cells * 50, cells * 50),
+                name="e_last",
+            )(*media, col, hgt, e, power)
             break
-        args = media + [col, hgt, media_rows, h_rows, e_low, e] + ([] if first else [power])
+        args = media + [col, hgt, media_rows, *h_rows, e_low, e] + ([] if first else [power])
         e, power, to_col, e_low = kernel(
             functools.partial(e_edge_kernel, first),
             (field, whole, planes, two_rows),
@@ -575,22 +560,23 @@
             {5: 0, 6: 1},
         )
 
-    mine, pair, other, e_out, h_out = pl.pallas_call(
-        functools.partial(pack_kernel, cap),
+    mine, pair, other, e_out, _ = pl.pallas_call(
+        functools.partial(pack_kernel, heights),
         out_shape=(
             pltpu.HBM((n_hgt, 2 * heights[0], PTS), F32),
             pltpu.HBM((n_hgt, heights[1], PTS), F32),
             pltpu.HBM((n_hgt, heights[2], PTS), F32),
             pltpu.HBM((3, nx, nz, ny), F32),
-            pltpu.HBM((3, nx, nz, ny), F32),
+            vmem(n_hgt * sum(heights), PTS),
         ),
-        in_specs=[SCALARS] + [WHOLE] * 6,
-        out_specs=(FAR,) * 5,
-        scratch_shapes=[vmem(n_hgt * sum(heights), PTS), sem((2 + 3 * n_hgt,))],
+        in_specs=[SCALARS] + [WHOLE] * 3,
+        out_specs=(FAR,) * 4 + (WHOLE,),
+        input_output_aliases={2: 4},
+        scratch_shapes=[sem((1 + 3 * n_hgt,))],
         compiler_params=params(VMEM_MIB),
         cost_estimate=cost(cells, cells * 36),
         name="pack",
-    )(place.reshape(count), power, mine_nodes, pair_nodes, other_nodes, e, h)
+    )(place.reshape(count), power, flat, e)
 
     def swap(x, axis):
         return lax.all_to_all(x, axis, split_axis=0, concat_axis=0, tiled=True)
@@ -618,14 +604,14 @@
     mine = pl.pallas_call(
         merge_kernel,
         out_shape=pltpu.HBM((n_hgt, 2 * heights[0], PTS), F32),
-        in_specs=[pl.BlockSpec(memory_space=pl.ANY), pl.BlockSpec(memory_space=pl.ANY), FAR],
+        in_specs=[pl.BlockSpec(memory_space=pl.ANY), FAR],
         out_specs=FAR,
-        input_output_aliases={2: 0},
+        input_output_aliases={1: 0},
         scratch_shapes=[sem((n_hgt,))],
         compiler_params=params(VMEM_MIB),
         cost_estimate=cost(1, 1),
         name="merge",
-    )(from_pair, sums[0], mine)
+    )(from_pair, mine)
     mine_blocks = swap(mine, "hgt")
     own = kernel(
         functools.partial(collect_mine_kernel, cap),

time: 144 us -> 141 us (0.979)
  waiting for transfers between devices: 59.5 us -> 56.1 us
    all_to_all x2, waiting for transfers between devices: 39.6 us -> 16 us  [swap(): return lax.all_to_all(x, axis, split_axis=0, concat_axis=0, tiled=True)]
    ppermute x3, waiting for transfers between devices: 0.01 us -> 19.9 us  [across(): return lax.ppermute(x, 'col', [(c, c ^ turn) for c in range(n_col)])]
    pallas_call x21 -> x20, Pallas kernels: 31.4 us -> 28.7 us  [kernel(): pl.pallas_call(body, out_shape=outs, in_specs=ins, out_specs=jax.tree.map...]
    pallas_call x1 -> x2, Pallas kernels: 5.61 us -> 7.45 us  [the longest x1 5.11 us: per_device(): pl.pallas_call(functools.partial(pack_kernel, heights), out_shape=(pltpu....]
  transfers between devices with their start and end apart: 21 -> 21, of which waited for: 11 -> 11; matrix products, arithmetic and copies ran while one was open for 0% -> 0% of each run, Pallas kernels for 18% -> 19%
where the time goes in v6:
time: 141 us; the launch traced here: 140 us
  waiting for transfers between devices  56.1 us (40%)
  starting transfers between devices  45.5 us (32%)
  Pallas kernels  37.1 us (26%)
    ppermute x16, starting transfers between devices, shifted(): return lax.ppermute(block, ('col', 'hgt'), route)  33.5 us
    pallas_call x20, Pallas kernels, kernel(): pl.pallas_call(body, out_shape=outs, in_specs=ins, out_specs=jax.tree.map...  28.7 us
    ppermute x16, waiting for transfers between devices, shifted(): return lax.ppermute(block, ('col', 'hgt'), route)  20.2 us
    ppermute x3, waiting for transfers between devices, across(): return lax.ppermute(x, 'col', [(c, c ^ turn) for c in range(n_col)])  19.9 us
    all_to_all x2, waiting for transfers between devices, swap(): return lax.all_to_all(x, axis, split_axis=0, concat_axis=0, tiled=True)  16 us
    all_to_all x2, starting transfers between devices, swap(): return lax.all_to_all(x, axis, split_axis=0, concat_axis=0, tiled=True)  7.73 us
    pallas_call x1, Pallas kernels, per_device(): pl.pallas_call(functools.partial(pack_kernel, heights), out_shape=(pltpu....  5.11 us
    ppermute x3, starting transfers between devices, across(): return lax.ppermute(x, 'col', [(c, c ^ turn) for c in range(n_col)])  4.28 us
  transfers between devices with their start and end apart: 21, of which 11 were waited for; matrix products, arithmetic and copies ran while one was open for 0% of the time, Pallas kernels for 19%

profile of v6, /device:TPU:0, one launch (start us, length us, event | category | flops | bytes accessed | tf_op | source)
XLA Modules:
  0.0 140.3 jit_solution(15873579465421913350)
XLA Ops:
  5.1 4.9 %load.1 = (f32[16,24,1024]{2,1,0:T(8,128)S(1)}, f32[16,24,1024]{2,1,0:T(8,128)S(1)}, f32[16,24,1024]{2,1,0:T(8,128)S(1)}, f32[3,16,24,1024]{3,2,1,0:T(8,128)S(1)...) custom-call(f32[16,24,1024]{2,1,0:T(8,128)} %temp_far.1, ...), custom_call_target="tpu_custom_call" | custom-call | flops 23592960 | bytes 23592960 | tf_op jit(solution)/shard_map/load/pallas_call | solution.py:462
  10.1 3.5 %collective-permute-done.1.col = f32[2,24,1024]{2,1,0:T(8,128)S(1)} collective-permute-done((f32[2,24,1024]{2,1,0:T(8,128)S(1)}, f32[2,24,1024]{2,1,0:T(8,128)S(1)}, u32[]{:S(2)}, u32[]{:S(2)}) %collective-permute-start.1) | collective-permute-done | bytes 196640 | tf_op jit(solution)/shard_map/ppermute | solution.py:439
  13.8 4.1 %collective-permute-start.3 = (f32[2,24,1024]{2,1,0:T(8,128)S(1)}, f32[2,24,1024]{2,1,0:T(8,128)S(1)}, u32[]{:S(2)}, u32[]{:S(2)}) collective-permute-start(f32[2,24,1024]{2,1,0:T(8,128)S(1)} %get-tuple-element.76), channel_id=1, source_target_pairs={{0,8},{1,9},{2,10},{3,11},{4,12},{5,13},{6,14},{7,15},{8,16},{9,17... | collective-permute-start | bytes 589832 | tf_op jit(solution)/shard_map/ppermute | solution.py:439
  19.6 1.9 %h_rest_0.1 = (f32[3,16,24,1024]{3,2,1,0:T(8,128)S(1)}, f32[3,16,1024]{2,1,0:T(8,128)S(1)}) custom-call(f32[3,16,24,1024]{3,2,1,0:T(8,128)S(1)} %get-tuple-element.64.e.refs_0_, f32[2,16,1024]{2,1,0:T(8,128)S(1)} %collective-permute-done.hgt, f32[3,16,24,1024]{3,2,1,0:T(8,128)S(1)} %get-tuple-element.70.h_old), custom_call_target="tpu_custom_call", output_to_operand_aliasing={{0}: (2, {})} | custom-call | flops 15728640 | bytes 15728640 | tf_op jit(solution)/shard_map/h_rest_0/pallas_call | solution.py:462
  25.1 2.2 %e_rest_0.1 = (f32[3,16,24,1024]{3,2,1,0:T(8,128)S(1)}, f32[16,24,1024]{2,1,0:T(8,128)S(1)}, f32[3,16,1024]{2,1,0:T(8,128)S(1)}) custom-call(f32[3,16,24,1024]{3,2,1,0:T(8,128)S(1)} %get-tuple-element.71.h.h_old, f32[16,24,1024]{2,1,0:T(8,128)S(1)} %get-tuple-element.72.ca, ...), custom_call_target="tpu_custom_call", output_to_operand_aliasing={{0}: (5, {}), {1}: (6, {})} | custom-call | flops 17694720 | bytes 17694720 | tf_op jit(solution)/shard_map/e_rest_0/pallas_call | solution.py:462
  27.9 4.7 %collective-permute-done.5.col = f32[2,24,1024]{2,1,0:T(8,128)S(1)} collective-permute-done((f32[2,24,1024]{2,1,0:T(8,128)S(1)}, f32[2,24,1024]{2,1,0:T(8,128)S(1)}, u32[]{:S(2)}, u32[]{:S(2)}) %collective-permute-start.5) | collective-permute-done | bytes 196640 | tf_op jit(solution)/shard_map/ppermute | solution.py:439
  32.7 3.5 %collective-permute-start.7 = (f32[2,24,1024]{2,1,0:T(8,128)S(1)}, f32[2,24,1024]{2,1,0:T(8,128)S(1)}, u32[]{:S(2)}, u32[]{:S(2)}) collective-permute-start(f32[2,24,1024]{2,1,0:T(8,128)S(1)} %get-tuple-element.88), channel_id=1, source_target_pairs={{0,8},{1,9},{2,10},{3,11},{4,12},{5,13},{6,14},{7,15},{8,16},{9,17... | collective-permute-start | bytes 589832 | tf_op jit(solution)/shard_map/ppermute | solution.py:439
  36.2 2.3 %collective-permute-start.6 = (f32[2,16,1024]{2,1,0:T(8,128)S(1)}, f32[2,16,1024]{2,1,0:T(8,128)S(1)}, u32[]{:S(2)}, u32[]{:S(2)}) collective-permute-start(f32[2,16,1024]{2,1,0:T(8,128)S(1)} %get-tuple-element.87.rows_old), channel_id=1, source_target_pairs={{0,1},{1,2},{2,3},{3,4},{4,5},{5,6},{6,7},{8,9},{9,10},{10,11},{11... | collective-permute-start | bytes 393224 | tf_op jit(solution)/shard_map/ppermute | solution.py:439
  43.9 2.3 %e_rest_1.1 = (f32[3,16,24,1024]{3,2,1,0:T(8,128)S(1)}, f32[16,24,1024]{2,1,0:T(8,128)S(1)}, f32[3,16,1024]{2,1,0:T(8,128)S(1)}) custom-call(f32[3,16,24,1024]{3,2,1,0:T(8,128)S(1)} %get-tuple-element.86.h.h_old, f32[16,24,1024]{2,1,0:T(8,128)S(1)} %get-tuple-element.72.ca, ...), custom_call_target="tpu_custom_call", output_to_operand_aliasing={{0}: (5, {}), {1}: (6, {})} | custom-call | flops 17694720 | bytes 17694720 | tf_op jit(solution)/shard_map/e_rest_1/pallas_call | solution.py:462
  46.2 4.4 %collective-permute-done.9.col = f32[2,24,1024]{2,1,0:T(8,128)S(1)} collective-permute-done((f32[2,24,1024]{2,1,0:T(8,128)S(1)}, f32[2,24,1024]{2,1,0:T(8,128)S(1)}, u32[]{:S(2)}, u32[]{:S(2)}) %collective-permute-start.9) | collective-permute-done | bytes 196640 | tf_op jit(solution)/shard_map/ppermute | solution.py:439
  50.7 3.6 %collective-permute-start.11 = (f32[2,24,1024]{2,1,0:T(8,128)S(1)}, f32[2,24,1024]{2,1,0:T(8,128)S(1)}, u32[]{:S(2)}, u32[]{:S(2)}) collective-permute-start(f32[2,24,1024]{2,1,0:T(8,128)S(1)} %get-tuple-element.100), channel_id=1, source_target_pairs={{0,8},{1,9},{2,10},{3,11},{4,12},{5,13},{6,14},{7,15},{8,16},{9,17... | collective-permute-start | bytes 589832 | tf_op jit(solution)/shard_map/ppermute | solution.py:439
  54.4 2.1 %collective-permute-start.10 = (f32[2,16,1024]{2,1,0:T(8,128)S(1)}, f32[2,16,1024]{2,1,0:T(8,128)S(1)}, u32[]{:S(2)}, u32[]{:S(2)}) collective-permute-start(f32[2,16,1024]{2,1,0:T(8,128)S(1)} %get-tuple-element.99.rows_old), channel_id=1, source_target_pairs={{0,1},{1,2},{2,3},{3,4},{4,5},{5,6},{6,7},{8,9},{9,10},{10,11},{11... | collective-permute-start | bytes 393224 | tf_op jit(solution)/shard_map/ppermute | solution.py:439
  61.9 2.3 %e_rest_2.1 = (f32[3,16,24,1024]{3,2,1,0:T(8,128)S(1)}, f32[16,24,1024]{2,1,0:T(8,128)S(1)}, f32[3,16,1024]{2,1,0:T(8,128)S(1)}) custom-call(f32[3,16,24,1024]{3,2,1,0:T(8,128)S(1)} %get-tuple-element.98.h.h_old, f32[16,24,1024]{2,1,0:T(8,128)S(1)} %get-tuple-element.72.ca, ...), custom_call_target="tpu_custom_call", output_to_operand_aliasing={{0}: (5, {}), {1}: (6, {})} | custom-call | flops 17694720 | bytes 17694720 | tf_op jit(solution)/shard_map/e_rest_2/pallas_call | solution.py:462
  64.4 4.7 %collective-permute-done.13.col = f32[2,24,1024]{2,1,0:T(8,128)S(1)} collective-permute-done((f32[2,24,1024]{2,1,0:T(8,128)S(1)}, f32[2,24,1024]{2,1,0:T(8,128)S(1)}, u32[]{:S(2)}, u32[]{:S(2)}) %collective-permute-start.13) | collective-permute-done | bytes 196640 | tf_op jit(solution)/shard_map/ppermute | solution.py:439
  69.2 3.0 %collective-permute-start.14 = (f32[2,24,1024]{2,1,0:T(8,128)S(1)}, f32[2,24,1024]{2,1,0:T(8,128)S(1)}, u32[]{:S(2)}, u32[]{:S(2)}) collective-permute-start(f32[2,24,1024]{2,1,0:T(8,128)S(1)} %get-tuple-element.110), channel_id=1, source_target_pairs={{0,8},{1,9},{2,10},{3,11},{4,12},{5,13},{6,14},{7,15},{8,16},{9,17... | collective-permute-start | bytes 589832 | tf_op jit(solution)/shard_map/ppermute | solution.py:439
  72.3 2.7 %collective-permute-start.15 = (f32[2,16,1024]{2,1,0:T(8,128)S(1)}, f32[2,16,1024]{2,1,0:T(8,128)S(1)}, u32[]{:S(2)}, u32[]{:S(2)}) collective-permute-start(f32[2,16,1024]{2,1,0:T(8,128)S(1)} %get-tuple-element.111), channel_id=1, source_target_pairs={{0,1},{1,2},{2,3},{3,4},{4,5},{5,6},{6,7},{8,9},{9,10},{10,11},{11... | collective-permute-start | bytes 393224 | tf_op jit(solution)/shard_map/ppermute | solution.py:439
  75.0 2.2 %places.1 = (s32[1,3072]{1,0:T(1,128)S(1)}, f32[6336,128]{1,0:T(8,128)S(1)}) custom-call(s32[1]{0:T(128)} %bitcast.my_col, s32[1,3072]{1,0:T(1,128)S(1)} %reshape.46.owner, s32[1,3072]{1,0:T(1,128)S(1)} %reshape.47.node), custom_call_target="tpu_custom_call" | custom-call | flops 3145728 | bytes 3145728 | tf_op jit(solution)/shard_map/places/pallas_call | solution.py:462
  79.1 2.3 %e_last.1 = (f32[3,16,24,1024]{3,2,1,0:T(8,128)S(1)}, f32[16,24,1024]{2,1,0:T(8,128)S(1)}, f32[3,16,24,1024]{3,2,1,0:T(8,128)}) custom-call(f32[3,16,24,1024]{3,2,1,0:T(8,128)S(1)} %h_rest_3.1.h, f32[16,24,1024]{2,1,0:T(8,128)S(1)} %get-tuple-element.72.ca, f32[16,24,1024]{2,1,0:T(8,128)S(1)} %get-tuple-element.73.cb, ...), custom_call_target="tpu_custom_call", output_to_operand_aliasing={{0}: (6, {}), {1}: (7, {})} | custom-call | flops 19660800 | bytes 19660800 | tf_op jit(solution)/shard_map/e_last/pallas_call | solution.py:528
  81.4 5.1 %pack.1 = (f32[8,400,128]{2,1,0:T(8,128)}, f32[8,200,128]{2,1,0:T(8,128)}, f32[8,392,128]{2,1,0:T(8,128)}, f32[3,16,24,1024]{3,2,1,0:T(8,128)}, f32[6336,128]{1,0:T(8,128)S(1)}) custom-call(s32[3072]{0:T(1024)S(1)} %bitcast.8, f32[16,24,1024]{2,1,0:T(8,128)S(1)} %get-tuple-element.113.power, ...), custom_call_target="tpu_custom_call", output_to_operand_aliasing={{4}: (2, {})} | custom-call | flops 393216 | bytes 14155776 | tf_op jit(solution)/shard_map/pack/pallas_call | solution.py:563
  86.5 3.9 %all-to-all-start.1 = ((f32[8,392,128]{2,1,0:T(8,128)}), f32[8,392,128]{2,1,0:T(8,128)S(1)}, u32[]{:S(2)}, u32[]{:S(2)}) async-start(f32[8,392,128]{2,1,0:T(8,128)} %get-tuple-element.120), calls=%async_computation.1 | async-start | bytes 3211264 | tf_op jit(solution)/shard_map/all_to_all | solution.py:582
  91.4 19.9 %collective-permute-done.16.pair = f32[8,200,128]{2,1,0:T(8,128)S(1)} collective-permute-done((f32[8,200,128]{2,1,0:T(8,128)}, f32[8,200,128]{2,1,0:T(8,128)S(1)}, u32[]{:S(2)}, u32[]{:S(2)}) %collective-permute-start.16) | collective-permute-done | bytes 819232 | tf_op jit(solution)/shard_map/ppermute | solution.py:585
  112.3 3.9 %all-to-all-start = ((f32[8,400,128]{2,1,0:T(8,128)}), f32[8,400,128]{2,1,0:T(8,128)S(1)}, u32[]{:S(2)}, u32[]{:S(2)}) async-start(f32[8,400,128]{2,1,0:T(8,128)} %merge.1), calls=%async_computation | async-start | bytes 3276800 | tf_op jit(solution)/shard_map/all_to_all | solution.py:582
  116.1 2.4 %collect_other.1 = (f32[384,128]{1,0:T(8,128)}, f32[384,128]{1,0:T(8,128)}) custom-call(f32[8,392,128]{2,1,0:T(8,128)S(1)} %all-to-all-done.1.blocks), custom_call_target="tpu_custom_call" | custom-call | flops 393216 | bytes 393216 | tf_op jit(solution)/shard_map/collect_other/pallas_call | solution.py:462
  121.8 16.0 %all-to-all-done.blocks = f32[8,400,128]{2,1,0:T(8,128)S(1)} async-done(((f32[8,400,128]{2,1,0:T(8,128)}), f32[8,400,128]{2,1,0:T(8,128)S(1)}, u32[]{:S(2)}, u32[]{:S(2)}) %all-to-all-start) | async-done | bytes 1638432 | tf_op jit(solution)/shard_map/all_to_all | solution.py:582
  (52 shorter events, 31.4 us)
Async XLA Ops:
  0.6 3.9 %copy-start.1 = (s32[1,1,16,24,8,1]{3,5,4,2,1,0:T(1,128)S(1)}, s32[1,1,16,24,8,1]{3,5,4,2,1,0:T(1,128)}, u32[]{:S(2)}) copy-start(s32[1,1,16,24,8,1]{3,5,4,2,1,0:T(1,128)} %param.11) | copy-start | bytes 36868
  0.6 4.2 %copy-start.2 = (s32[1,1,16,24,8]{3,4,2,1,0:T(8,128)S(1)}, s32[1,1,16,24,8]{3,4,2,1,0:T(8,128)}, u32[]{:S(2)}) copy-start(s32[1,1,16,24,8]{3,4,2,1,0:T(8,128)} %param.12) | copy-start | bytes 36868
  2.0 8.1 %collective-permute-start = (f32[2,16,1024]{2,1,0:T(8,128)S(1)}, f32[2,16,1024]{2,1,0:T(8,128)S(1)}, u32[]{:S(2)}, u32[]{:S(2)}) collective-permute-start(f32[2,16,1024]{2,1,0:T(8,128)S(1)} %get-tuple-element.65.rows_old), channel_id=1, source_target_pairs={{1,0},{2,1},{3,2},{4,3},{5,4},{6,5},{7,6},{9,8},{10,9},{11,10},{12... | collective-permute-start | bytes 393224 | tf_op jit(solution)/shard_map/ppermute | solution.py:439
  3.3 10.3 %collective-permute-start.1 = (f32[2,24,1024]{2,1,0:T(8,128)S(1)}, f32[2,24,1024]{2,1,0:T(8,128)S(1)}, u32[]{:S(2)}, u32[]{:S(2)}) collective-permute-start(f32[2,24,1024]{2,1,0:T(8,128)S(1)} %get-tuple-element.66), channel_id=1, source_target_pairs={{8,0},{9,1},{10,2},{11,3},{12,4},{13,5},{14,6},{15,7},{16,8},{17,9... | collective-permute-start | bytes 589832 | tf_op jit(solution)/shard_map/ppermute | solution.py:439
  13.8 8.5 %collective-permute-start.3 = (f32[2,24,1024]{2,1,0:T(8,128)S(1)}, f32[2,24,1024]{2,1,0:T(8,128)S(1)}, u32[]{:S(2)}, u32[]{:S(2)}) collective-permute-start(f32[2,24,1024]{2,1,0:T(8,128)S(1)} %get-tuple-element.76), channel_id=1, source_target_pairs={{0,8},{1,9},{2,10},{3,11},{4,12},{5,13},{6,14},{7,15},{8,16},{9,17... | collective-permute-start | bytes 589832 | tf_op jit(solution)/shard_map/ppermute | solution.py:439
  17.9 3.7 %collective-permute-start.2 = (f32[2,16,1024]{2,1,0:T(8,128)S(1)}, f32[2,16,1024]{2,1,0:T(8,128)S(1)}, u32[]{:S(2)}, u32[]{:S(2)}) collective-permute-start(f32[2,16,1024]{2,1,0:T(8,128)S(1)} %get-tuple-element.75.rows_old), channel_id=1, source_target_pairs={{0,1},{1,2},{2,3},{3,4},{4,5},{5,6},{6,7},{8,9},{9,10},{10,11},{11... | collective-permute-start | bytes 393224 | tf_op jit(solution)/shard_map/ppermute | solution.py:439
  22.5 10.1 %collective-permute-start.5 = (f32[2,24,1024]{2,1,0:T(8,128)S(1)}, f32[2,24,1024]{2,1,0:T(8,128)S(1)}, u32[]{:S(2)}, u32[]{:S(2)}) collective-permute-start(f32[2,24,1024]{2,1,0:T(8,128)S(1)} %get-tuple-element.83), channel_id=1, source_target_pairs={{8,0},{9,1},{10,2},{11,3},{12,4},{13,5},{14,6},{15,7},{16,8},{17,9... | collective-permute-start | bytes 589832 | tf_op jit(solution)/shard_map/ppermute | solution.py:439
  23.8 4.1 %collective-permute-start.4 = (f32[2,16,1024]{2,1,0:T(8,128)S(1)}, f32[2,16,1024]{2,1,0:T(8,128)S(1)}, u32[]{:S(2)}, u32[]{:S(2)}) collective-permute-start(f32[2,16,1024]{2,1,0:T(8,128)S(1)} %get-tuple-element.82.rows_old), channel_id=1, source_target_pairs={{1,0},{2,1},{3,2},{4,3},{5,4},{6,5},{7,6},{9,8},{10,9},{11,10},{12... | collective-permute-start | bytes 393224 | tf_op jit(solution)/shard_map/ppermute | solution.py:439
  32.7 8.4 %collective-permute-start.7 = (f32[2,24,1024]{2,1,0:T(8,128)S(1)}, f32[2,24,1024]{2,1,0:T(8,128)S(1)}, u32[]{:S(2)}, u32[]{:S(2)}) collective-permute-start(f32[2,24,1024]{2,1,0:T(8,128)S(1)} %get-tuple-element.88), channel_id=1, source_target_pairs={{0,8},{1,9},{2,10},{3,11},{4,12},{5,13},{6,14},{7,15},{8,16},{9,17... | collective-permute-start | bytes 589832 | tf_op jit(solution)/shard_map/ppermute | solution.py:439
  36.2 4.2 %collective-permute-start.6 = (f32[2,16,1024]{2,1,0:T(8,128)S(1)}, f32[2,16,1024]{2,1,0:T(8,128)S(1)}, u32[]{:S(2)}, u32[]{:S(2)}) collective-permute-start(f32[2,16,1024]{2,1,0:T(8,128)S(1)} %get-tuple-element.87.rows_old), channel_id=1, source_target_pairs={{0,1},{1,2},{2,3},{3,4},{4,5},{5,6},{6,7},{8,9},{9,10},{10,11},{11... | collective-permute-start | bytes 393224 | tf_op jit(solution)/shard_map/ppermute | solution.py:439
  41.3 9.3 %collective-permute-start.9 = (f32[2,24,1024]{2,1,0:T(8,128)S(1)}, f32[2,24,1024]{2,1,0:T(8,128)S(1)}, u32[]{:S(2)}, u32[]{:S(2)}) collective-permute-start(f32[2,24,1024]{2,1,0:T(8,128)S(1)} %get-tuple-element.95), channel_id=1, source_target_pairs={{8,0},{9,1},{10,2},{11,3},{12,4},{13,5},{14,6},{15,7},{16,8},{17,9... | collective-permute-start | bytes 589832 | tf_op jit(solution)/shard_map/ppermute | solution.py:439
  42.6 3.6 %collective-permute-start.8 = (f32[2,16,1024]{2,1,0:T(8,128)S(1)}, f32[2,16,1024]{2,1,0:T(8,128)S(1)}, u32[]{:S(2)}, u32[]{:S(2)}) collective-permute-start(f32[2,16,1024]{2,1,0:T(8,128)S(1)} %get-tuple-element.94.rows_old), channel_id=1, source_target_pairs={{1,0},{2,1},{3,2},{4,3},{5,4},{6,5},{7,6},{9,8},{10,9},{11,10},{12... | collective-permute-start | bytes 393224 | tf_op jit(solution)/shard_map/ppermute | solution.py:439
  50.7 8.4 %collective-permute-start.11 = (f32[2,24,1024]{2,1,0:T(8,128)S(1)}, f32[2,24,1024]{2,1,0:T(8,128)S(1)}, u32[]{:S(2)}, u32[]{:S(2)}) collective-permute-start(f32[2,24,1024]{2,1,0:T(8,128)S(1)} %get-tuple-element.100), channel_id=1, source_target_pairs={{0,8},{1,9},{2,10},{3,11},{4,12},{5,13},{6,14},{7,15},{8,16},{9,17... | collective-permute-start | bytes 589832 | tf_op jit(solution)/shard_map/ppermute | solution.py:439
  54.4 4.1 %collective-permute-start.10 = (f32[2,16,1024]{2,1,0:T(8,128)S(1)}, f32[2,16,1024]{2,1,0:T(8,128)S(1)}, u32[]{:S(2)}, u32[]{:S(2)}) collective-permute-start(f32[2,16,1024]{2,1,0:T(8,128)S(1)} %get-tuple-element.99.rows_old), channel_id=1, source_target_pairs={{0,1},{1,2},{2,3},{3,4},{4,5},{5,6},{6,7},{8,9},{9,10},{10,11},{11... | collective-permute-start | bytes 393224 | tf_op jit(solution)/shard_map/ppermute | solution.py:439
  59.3 9.8 %collective-permute-start.13 = (f32[2,24,1024]{2,1,0:T(8,128)S(1)}, f32[2,24,1024]{2,1,0:T(8,128)S(1)}, u32[]{:S(2)}, u32[]{:S(2)}) collective-permute-start(f32[2,24,1024]{2,1,0:T(8,128)S(1)} %get-tuple-element.107), channel_id=1, source_target_pairs={{8,0},{9,1},{10,2},{11,3},{12,4},{13,5},{14,6},{15,7},{16,8},{17,9... | collective-permute-start | bytes 589832 | tf_op jit(solution)/shard_map/ppermute | solution.py:439
  60.6 3.8 %collective-permute-start.12 = (f32[2,16,1024]{2,1,0:T(8,128)S(1)}, f32[2,16,1024]{2,1,0:T(8,128)S(1)}, u32[]{:S(2)}, u32[]{:S(2)}) collective-permute-start(f32[2,16,1024]{2,1,0:T(8,128)S(1)} %get-tuple-element.106), channel_id=1, source_target_pairs={{1,0},{2,1},{3,2},{4,3},{5,4},{6,5},{7,6},{9,8},{10,9},{11,10},{12... | collective-permute-start | bytes 393224 | tf_op jit(solution)/shard_map/ppermute | solution.py:439
  69.2 9.8 %collective-permute-start.14 = (f32[2,24,1024]{2,1,0:T(8,128)S(1)}, f32[2,24,1024]{2,1,0:T(8,128)S(1)}, u32[]{:S(2)}, u32[]{:S(2)}) collective-permute-start(f32[2,24,1024]{2,1,0:T(8,128)S(1)} %get-tuple-element.110), channel_id=1, source_target_pairs={{0,8},{1,9},{2,10},{3,11},{4,12},{5,13},{6,14},{7,15},{8,16},{9,17... | collective-permute-start | bytes 589832 | tf_op jit(solution)/shard_map/ppermute | solution.py:439
  72.3 6.8 %collective-permute-start.15 = (f32[2,16,1024]{2,1,0:T(8,128)S(1)}, f32[2,16,1024]{2,1,0:T(8,128)S(1)}, u32[]{:S(2)}, u32[]{:S(2)}) collective-permute-start(f32[2,16,1024]{2,1,0:T(8,128)S(1)} %get-tuple-element.111), channel_id=1, source_target_pairs={{0,1},{1,2},{2,3},{3,4},{4,5},{5,6},{6,7},{8,9},{9,10},{10,11},{11... | collective-permute-start | bytes 393224 | tf_op jit(solution)/shard_map/ppermute | solution.py:439
  86.5 25.7 %all-to-all-start.1 = ((f32[8,392,128]{2,1,0:T(8,128)}), f32[8,392,128]{2,1,0:T(8,128)S(1)}, u32[]{:S(2)}, u32[]{:S(2)}) async-start(f32[8,392,128]{2,1,0:T(8,128)} %get-tuple-element.120), calls=%async_computation.1 | async-start | bytes 3211264 | tf_op jit(solution)/shard_map/all_to_all | solution.py:582
  90.4 20.9 %collective-permute-start.16 = (f32[8,200,128]{2,1,0:T(8,128)}, f32[8,200,128]{2,1,0:T(8,128)S(1)}, u32[]{:S(2)}, u32[]{:S(2)}) collective-permute-start(f32[8,200,128]{2,1,0:T(8,128)} %get-tuple-element.118), channel_id=1, source_target_pairs={{0,8},{8,0},{16,24},{24,16},{1,9},{9,1},{17,25},{25,17},{2,10},{10... | collective-permute-start | bytes 2457608 | tf_op jit(solution)/shard_map/ppermute | solution.py:585
  111.3 28.3 %copy-start = (f32[384,128]{1,0:T(8,128)S(1)}, f32[384,128]{1,0:T(8,128)}, u32[]{:S(2)}) copy-start(f32[384,128]{1,0:T(8,128)} %enthalpy.1) | copy-start | bytes 589828
  112.3 25.6 %all-to-all-start = ((f32[8,400,128]{2,1,0:T(8,128)}), f32[8,400,128]{2,1,0:T(8,128)S(1)}, u32[]{:S(2)}, u32[]{:S(2)}) async-start(f32[8,400,128]{2,1,0:T(8,128)} %merge.1), calls=%async_computation | async-start | bytes 3276800 | tf_op jit(solution)/shard_map/all_to_all | solution.py:582
  118.5 21.0 %collective-permute-start.17 = (f32[384,128]{1,0:T(8,128)}, f32[384,128]{1,0:T(8,128)S(1)}, u32[]{:S(2)}, u32[]{:S(2)}) collective-permute-start(f32[384,128]{1,0:T(8,128)} %get-tuple-element.121), channel_id=1, source_target_pairs={{0,16},{8,24},{16,0},{24,8},{1,17},{9,25},{17,1},{25,9},{2,18},{10... | collective-permute-start | bytes 589832 | tf_op jit(solution)/shard_map/ppermute | solution.py:585
  120.1 19.5 %collective-permute-start.18 = (f32[384,128]{1,0:T(8,128)}, f32[384,128]{1,0:T(8,128)S(1)}, u32[]{:S(2)}, u32[]{:S(2)}) collective-permute-start(f32[384,128]{1,0:T(8,128)} %get-tuple-element.122), channel_id=1, source_target_pairs={{0,24},{8,16},{16,8},{24,0},{1,25},{9,17},{17,9},{25,1},{2,26},{10... | collective-permute-start | bytes 589832 | tf_op jit(solution)/shard_map/ppermute | solution.py:585

commit v7 on v6

--- a/solution.py
+++ b/solution.py
@@ -75,23 +75,38 @@
     col_copy.wait()
 
 
-def load_kernel(
-    temp_far, tags_far, e_far, h_far, order, ca, cb, sigma_out, e, h, media_rows, e_rows, h_rows, temp, tags, sems
-):
+def load_kernel(e_far, h_far, order, e, h, e_rows, h_rows, sems):
+    nx, nz = e.shape[1:3]
+    e_copy = pltpu.make_async_copy(e_far, e, sems.at[0])
+    h_copy = pltpu.make_async_copy(h_far, h, sems.at[1])
+    e_copy.start()
+    h_copy.start()
+
+    def take(field, rows):
+        def body(x, carry):
+            for comp in range(rows.shape[0]):
+                rows[comp, pl.ds(x, 1), :] = field[comp, x, nz - 1 : nz, :]
+            return carry
+
+        lax.fori_loop(0, nx, body, 0)
+
+    e_copy.wait()
+    take(e, e_rows)
+    h_copy.wait()
+    take(h, h_rows)
+
+
+def coefficients_kernel(temp_far, tags_far, order, ca, cb, sigma_out, media_rows, temp, tags, sems):
     nx, nz, _ = temp.shape
-    parts = 4
+    parts = 8
     size = nx // parts
     copies = []
     for part in range(parts):
         here = pl.ds(part * size, size)
         copies.append(pltpu.make_async_copy(temp_far.at[here], temp.at[here], sems.at[0, part]))
         copies.append(pltpu.make_async_copy(tags_far.at[here], tags.at[here], sems.at[1, part]))
-    e_copy = pltpu.make_async_copy(e_far, e, sems.at[2, 0])
-    h_copy = pltpu.make_async_copy(h_far, h, sems.at[2, 1])
     for copy in copies:
         copy.start()
-    e_copy.start()
-    h_copy.start()
 
     def plane(x, carry):
         for z in range(0, nz, ROWS):
@@ -118,17 +133,6 @@
         copies[2 * part].wait()
         copies[2 * part + 1].wait()
         lax.fori_loop(part * size, (part + 1) * size, plane, 0)
-    e_copy.wait()
-    h_copy.wait()
-
-    def rows(x, carry):
-        for comp in range(3):
-            e_rows[comp, pl.ds(x, 1), :] = e[comp, x, nz - 1 : nz, :]
-        for comp in range(2):
-            h_rows[comp, pl.ds(x, 1), :] = h[comp, x, nz - 1 : nz, :]
-        return carry
-
-    lax.fori_loop(0, nx, rows, 0)
 
 
 def over(first, stop, body):
@@ -218,7 +222,7 @@
     keep(nx - 1)
 
 
-def e_edge_kernel(first, h, ca, cb, sigma, col, hgt, media_rows, h_rows, rows_old, *refs):
+def e_edge_kernel(first, order, h, ca, cb, sigma, col, hgt, media_rows, h_rows, rows_old, *refs):
     e, power, to_col, to_hgt = refs[-4:]
     nx, nz = e.shape[1:3]
     for z in range(0, nz, ROWS):
@@ -487,14 +491,14 @@
     )
     col = shifted(to_col, -1, 0)
     hgt = shifted(e_low, 0, -1)
-    ca, cb, sigma, e, h, media_rows, e_rows, h_high = kernel(
+    e, h, e_rows, h_high = kernel(
         load_kernel,
-        (whole, whole, whole, field, field, two_rows, three_rows, two_rows),
-        [FAR] * 4 + [WHOLE],
-        [far(cell_temp), far(region_tags), e_start, h_start, owners + nodes + my_col],
+        (field, field, three_rows, two_rows),
+        [FAR] * 2 + [WHOLE],
+        [e_start, h_start, owners + nodes + my_col],
         "load",
-        60,
-        scratch=[vmem(nx, nz, ny), pltpu.VMEM((nx, nz, ny), jnp.int32), sem((3, 4))],
+        40,
+        scratch=[sem((2,))],
     )
     begins, heights = starts_of(n_col, n_hgt, cap)
     place, flat = kernel(
@@ -520,6 +524,16 @@
         e_hgt = hgt
         col = shifted(to_col, 1, 0)
         hgt = shifted(h_high, 0, 1)
+        if first:
+            ca, cb, sigma, media_rows = kernel(
+                coefficients_kernel,
+                (whole, whole, whole, two_rows),
+                [FAR] * 2 + [WHOLE],
+                [far(cell_temp), far(region_tags), h_high],
+                "coefficients",
+                40,
+                scratch=[vmem(nx, nz, ny), pltpu.VMEM((nx, nz, ny), jnp.int32), sem((2, 8))],
+            )
         last = step == STEPS - 1
         outs = (field,) if last else (field, three_rows)
         h, *h_rows = kernel(h_rest_kernel, outs, [WHOLE] * 3, [e, e_hgt, h], f"h_rest_{step}", 40, {2: 0})
@@ -537,15 +551,16 @@
                 name="e_last",
             )(*media, col, hgt, e, power)
             break
-        args = media + [col, hgt, media_rows, *h_rows, e_low, e] + ([] if first else [power])
+        order = place if step == 1 else my_col
+        args = [order] + media + [col, hgt, media_rows, *h_rows, e_low, e] + ([] if first else [power])
         e, power, to_col, e_low = kernel(
             functools.partial(e_edge_kernel, first),
             (field, whole, planes, two_rows),
-            [WHOLE] * len(args),
+            [WHOLE if step == 1 else SCALARS] + [WHOLE] * (len(args) - 1),
             args,
             f"e_edge_{step}",
             5,
-            {9: 0} if first else {9: 0, 10: 1},
+            {10: 0} if first else {10: 0, 11: 1},
         )
         h_hgt = hgt
         col = shifted(to_col, -1, 0)

time: 141 us -> 144 us (1.021)
  starting transfers between devices: 45.5 us -> 48.2 us
  Pallas kernels: 37.1 us -> 38.8 us
  waiting for transfers between devices: 56.1 us -> 54.5 us
    all_to_all x2, starting transfers between devices: 7.73 us -> 9.49 us  [swap(): return lax.all_to_all(x, axis, split_axis=0, concat_axis=0, tiled=True)]
    pallas_call x20 -> x21, Pallas kernels: 28.7 us -> 30.4 us  [kernel(): pl.pallas_call(body, out_shape=outs, in_specs=ins, out_specs=jax.tree.map...]
  transfers between devices with their start and end apart: 21 -> 21, of which waited for: 11 -> 10; matrix products, arithmetic and copies ran while one was open for 0% -> 0% of each run, Pallas kernels for 19% -> 20%
where the time goes in v7:
time: 144 us; the launch traced here: 143 us
  waiting for transfers between devices  54.5 us (38%)
  starting transfers between devices  48.2 us (33%)
  Pallas kernels  38.8 us (27%)
    ppermute x16, starting transfers between devices, shifted(): return lax.ppermute(block, ('col', 'hgt'), route)  34.1 us
    pallas_call x21, Pallas kernels, kernel(): pl.pallas_call(body, out_shape=outs, in_specs=ins, out_specs=jax.tree.map...  30.4 us
    ppermute x3, waiting for transfers between devices, across(): return lax.ppermute(x, 'col', [(c, c ^ turn) for c in range(n_col)])  19.7 us
    ppermute x16, waiting for transfers between devices, shifted(): return lax.ppermute(block, ('col', 'hgt'), route)  19 us
    all_to_all x2, waiting for transfers between devices, swap(): return lax.all_to_all(x, axis, split_axis=0, concat_axis=0, tiled=True)  15.8 us
    all_to_all x2, starting transfers between devices, swap(): return lax.all_to_all(x, axis, split_axis=0, concat_axis=0, tiled=True)  9.49 us
    pallas_call x1, Pallas kernels, per_device(): pl.pallas_call(functools.partial(pack_kernel, heights), out_shape=(pltpu....  5.11 us
    ppermute x3, starting transfers between devices, across(): return lax.ppermute(x, 'col', [(c, c ^ turn) for c in range(n_col)])  4.68 us
  transfers between devices with their start and end apart: 21, of which 10 were waited for; matrix products, arithmetic and copies ran while one was open for 0% of the time, Pallas kernels for 20%

profile of v7, /device:TPU:0, one launch (start us, length us, event | category | flops | bytes accessed | tf_op | source)
XLA Modules:
  0.0 143.2 jit_solution(3648484463838850312)
XLA Ops:
  5.1 3.9 %load.1 = (f32[3,16,24,1024]{3,2,1,0:T(8,128)S(1)}, f32[3,16,24,1024]{3,2,1,0:T(8,128)S(1)}, f32[3,16,1024]{2,1,0:T(8,128)S(1)}, f32[2,16,1024]{2,1,0:T(8,128)S(1)}) custom-call(f32[3,16,24,1024]{3,2,1,0:T(8,128)} %e.1, f32[3,16,24,1024]{3,2,1,0:T(8,128)} %h_far.1, s32[1,3072]{1,0:T(1,128)S(1)} %add_add_fusion.order), custom_call_target="tpu_custom_call" | custom-call | flops 15728640 | bytes 15728640 | tf_op jit(solution)/shard_map/load/pallas_call | solution.py:466
  9.1 4.5 %collective-permute-done.1.col = f32[2,24,1024]{2,1,0:T(8,128)S(1)} collective-permute-done((f32[2,24,1024]{2,1,0:T(8,128)S(1)}, f32[2,24,1024]{2,1,0:T(8,128)S(1)}, u32[]{:S(2)}, u32[]{:S(2)}) %collective-permute-start.1) | collective-permute-done | bytes 196640 | tf_op jit(solution)/shard_map/ppermute | solution.py:443
  13.8 4.1 %collective-permute-start.3 = (f32[2,24,1024]{2,1,0:T(8,128)S(1)}, f32[2,24,1024]{2,1,0:T(8,128)S(1)}, u32[]{:S(2)}, u32[]{:S(2)}) collective-permute-start(f32[2,24,1024]{2,1,0:T(8,128)S(1)} %get-tuple-element.76), channel_id=1, source_target_pairs={{0,8},{1,9},{2,10},{3,11},{4,12},{5,13},{6,14},{7,15},{8,16},{9,17... | collective-permute-start | bytes 589832 | tf_op jit(solution)/shard_map/ppermute | solution.py:443
  19.6 2.7 %coefficients.1 = (f32[16,24,1024]{2,1,0:T(8,128)S(1)}, f32[16,24,1024]{2,1,0:T(8,128)S(1)}, f32[16,24,1024]{2,1,0:T(8,128)S(1)}, f32[2,16,1024]{2,1,0:T(8,128)S(1)}) custom-call(f32[16,24,1024]{2,1,0:T(8,128)} %temp_far.1, s32[16,24,1024]{2,1,0:T(8,128)} %tags_far.1, f32[2,16,1024]{2,1,0:T(8,128)S(1)} %get-tuple-element.72.order.rows_old), custom_call_target="tpu_custom_call" | custom-call | flops 15728640 | bytes 15728640 | tf_op jit(solution)/shard_map/coefficients/pallas_call | solution.py:466
  27.1 2.2 %e_rest_0.1 = (f32[3,16,24,1024]{3,2,1,0:T(8,128)S(1)}, f32[16,24,1024]{2,1,0:T(8,128)S(1)}, f32[3,16,1024]{2,1,0:T(8,128)S(1)}) custom-call(f32[3,16,24,1024]{3,2,1,0:T(8,128)S(1)} %get-tuple-element.71.h.h_old, f32[16,24,1024]{2,1,0:T(8,128)S(1)} %get-tuple-element.73.ca, ...), custom_call_target="tpu_custom_call", output_to_operand_aliasing={{0}: (5, {}), {1}: (6, {})} | custom-call | flops 17694720 | bytes 17694720 | tf_op jit(solution)/shard_map/e_rest_0/pallas_call | solution.py:466
  30.6 2.4 %collective-permute-done.5.col = f32[2,24,1024]{2,1,0:T(8,128)S(1)} collective-permute-done((f32[2,24,1024]{2,1,0:T(8,128)S(1)}, f32[2,24,1024]{2,1,0:T(8,128)S(1)}, u32[]{:S(2)}, u32[]{:S(2)}) %collective-permute-start.5) | collective-permute-done | bytes 196640 | tf_op jit(solution)/shard_map/ppermute | solution.py:443
  33.1 3.5 %collective-permute-start.7 = (f32[2,24,1024]{2,1,0:T(8,128)S(1)}, f32[2,24,1024]{2,1,0:T(8,128)S(1)}, u32[]{:S(2)}, u32[]{:S(2)}) collective-permute-start(f32[2,24,1024]{2,1,0:T(8,128)S(1)} %get-tuple-element.88), channel_id=1, source_target_pairs={{0,8},{1,9},{2,10},{3,11},{4,12},{5,13},{6,14},{7,15},{8,16},{9,17... | collective-permute-start | bytes 589832 | tf_op jit(solution)/shard_map/ppermute | solution.py:443
  36.6 3.6 %collective-permute-start.6 = (f32[2,16,1024]{2,1,0:T(8,128)S(1)}, f32[2,16,1024]{2,1,0:T(8,128)S(1)}, u32[]{:S(2)}, u32[]{:S(2)}) collective-permute-start(f32[2,16,1024]{2,1,0:T(8,128)S(1)} %get-tuple-element.87.rows_old), channel_id=1, source_target_pairs={{0,1},{1,2},{2,3},{3,4},{4,5},{5,6},{6,7},{8,9},{9,10},{10,11},{11... | collective-permute-start | bytes 393224 | tf_op jit(solution)/shard_map/ppermute | solution.py:443
  47.1 2.3 %e_rest_1.1 = (f32[3,16,24,1024]{3,2,1,0:T(8,128)S(1)}, f32[16,24,1024]{2,1,0:T(8,128)S(1)}, f32[3,16,1024]{2,1,0:T(8,128)S(1)}) custom-call(f32[3,16,24,1024]{3,2,1,0:T(8,128)S(1)} %get-tuple-element.86.h.h_old, f32[16,24,1024]{2,1,0:T(8,128)S(1)} %get-tuple-element.73.ca, ...), custom_call_target="tpu_custom_call", output_to_operand_aliasing={{0}: (5, {}), {1}: (6, {})} | custom-call | flops 17694720 | bytes 17694720 | tf_op jit(solution)/shard_map/e_rest_1/pallas_call | solution.py:466
  49.6 4.6 %collective-permute-done.9.col = f32[2,24,1024]{2,1,0:T(8,128)S(1)} collective-permute-done((f32[2,24,1024]{2,1,0:T(8,128)S(1)}, f32[2,24,1024]{2,1,0:T(8,128)S(1)}, u32[]{:S(2)}, u32[]{:S(2)}) %collective-permute-start.9) | collective-permute-done | bytes 196640 | tf_op jit(solution)/shard_map/ppermute | solution.py:443
  54.3 2.7 %collective-permute-start.11 = (f32[2,24,1024]{2,1,0:T(8,128)S(1)}, f32[2,24,1024]{2,1,0:T(8,128)S(1)}, u32[]{:S(2)}, u32[]{:S(2)}) collective-permute-start(f32[2,24,1024]{2,1,0:T(8,128)S(1)} %get-tuple-element.100), channel_id=1, source_target_pairs={{0,8},{1,9},{2,10},{3,11},{4,12},{5,13},{6,14},{7,15},{8,16},{9,17... | collective-permute-start | bytes 589832 | tf_op jit(solution)/shard_map/ppermute | solution.py:443
  57.0 2.2 %collective-permute-start.10 = (f32[2,16,1024]{2,1,0:T(8,128)S(1)}, f32[2,16,1024]{2,1,0:T(8,128)S(1)}, u32[]{:S(2)}, u32[]{:S(2)}) collective-permute-start(f32[2,16,1024]{2,1,0:T(8,128)S(1)} %get-tuple-element.99.rows_old), channel_id=1, source_target_pairs={{0,1},{1,2},{2,3},{3,4},{4,5},{5,6},{6,7},{8,9},{9,10},{10,11},{11... | collective-permute-start | bytes 393224 | tf_op jit(solution)/shard_map/ppermute | solution.py:443
  64.7 2.3 %e_rest_2.1 = (f32[3,16,24,1024]{3,2,1,0:T(8,128)S(1)}, f32[16,24,1024]{2,1,0:T(8,128)S(1)}, f32[3,16,1024]{2,1,0:T(8,128)S(1)}) custom-call(f32[3,16,24,1024]{3,2,1,0:T(8,128)S(1)} %get-tuple-element.98.h.h_old, f32[16,24,1024]{2,1,0:T(8,128)S(1)} %get-tuple-element.73.ca, ...), custom_call_target="tpu_custom_call", output_to_operand_aliasing={{0}: (5, {}), {1}: (6, {})} | custom-call | flops 17694720 | bytes 17694720 | tf_op jit(solution)/shard_map/e_rest_2/pallas_call | solution.py:466
  67.7 4.5 %collective-permute-done.13.col = f32[2,24,1024]{2,1,0:T(8,128)S(1)} collective-permute-done((f32[2,24,1024]{2,1,0:T(8,128)S(1)}, f32[2,24,1024]{2,1,0:T(8,128)S(1)}, u32[]{:S(2)}, u32[]{:S(2)}) %collective-permute-start.13) | collective-permute-done | bytes 196640 | tf_op jit(solution)/shard_map/ppermute | solution.py:443
  72.3 2.8 %collective-permute-start.14 = (f32[2,24,1024]{2,1,0:T(8,128)S(1)}, f32[2,24,1024]{2,1,0:T(8,128)S(1)}, u32[]{:S(2)}, u32[]{:S(2)}) collective-permute-start(f32[2,24,1024]{2,1,0:T(8,128)S(1)} %get-tuple-element.110), channel_id=1, source_target_pairs={{0,8},{1,9},{2,10},{3,11},{4,12},{5,13},{6,14},{7,15},{8,16},{9,17... | collective-permute-start | bytes 589832 | tf_op jit(solution)/shard_map/ppermute | solution.py:443
  75.2 3.0 %collective-permute-start.15 = (f32[2,16,1024]{2,1,0:T(8,128)S(1)}, f32[2,16,1024]{2,1,0:T(8,128)S(1)}, u32[]{:S(2)}, u32[]{:S(2)}) collective-permute-start(f32[2,16,1024]{2,1,0:T(8,128)S(1)} %get-tuple-element.111), channel_id=1, source_target_pairs={{0,1},{1,2},{2,3},{3,4},{4,5},{5,6},{6,7},{8,9},{9,10},{10,11},{11... | collective-permute-start | bytes 393224 | tf_op jit(solution)/shard_map/ppermute | solution.py:443
  80.1 2.3 %e_last.1 = (f32[3,16,24,1024]{3,2,1,0:T(8,128)S(1)}, f32[16,24,1024]{2,1,0:T(8,128)S(1)}, f32[3,16,24,1024]{3,2,1,0:T(8,128)}) custom-call(f32[3,16,24,1024]{3,2,1,0:T(8,128)S(1)} %h_rest_3.1.h, f32[16,24,1024]{2,1,0:T(8,128)S(1)} %get-tuple-element.73.ca, f32[16,24,1024]{2,1,0:T(8,128)S(1)} %get-tuple-element.74.cb, ...), custom_call_target="tpu_custom_call", output_to_operand_aliasing={{0}: (6, {}), {1}: (7, {})} | custom-call | flops 19660800 | bytes 19660800 | tf_op jit(solution)/shard_map/e_last/pallas_call | solution.py:542
  82.5 5.1 %pack.1 = (f32[8,400,128]{2,1,0:T(8,128)}, f32[8,200,128]{2,1,0:T(8,128)}, f32[8,392,128]{2,1,0:T(8,128)}, f32[3,16,24,1024]{3,2,1,0:T(8,128)}, f32[6336,128]{1,0:T(8,128)S(1)}) custom-call(s32[3072]{0:T(1024)S(1)} %bitcast.8, f32[16,24,1024]{2,1,0:T(8,128)S(1)} %get-tuple-element.113.power, ...), custom_call_target="tpu_custom_call", output_to_operand_aliasing={{4}: (2, {})} | custom-call | flops 393216 | bytes 14155776 | tf_op jit(solution)/shard_map/pack/pallas_call | solution.py:578
  87.6 5.6 %all-to-all-start.1 = ((f32[8,392,128]{2,1,0:T(8,128)}), f32[8,392,128]{2,1,0:T(8,128)S(1)}, u32[]{:S(2)}, u32[]{:S(2)}) async-start(f32[8,392,128]{2,1,0:T(8,128)} %get-tuple-element.120), calls=%async_computation.1 | async-start | bytes 3211264 | tf_op jit(solution)/shard_map/all_to_all | solution.py:597
  94.4 19.7 %collective-permute-done.16.pair = f32[8,200,128]{2,1,0:T(8,128)S(1)} collective-permute-done((f32[8,200,128]{2,1,0:T(8,128)}, f32[8,200,128]{2,1,0:T(8,128)S(1)}, u32[]{:S(2)}, u32[]{:S(2)}) %collective-permute-start.16) | collective-permute-done | bytes 819232 | tf_op jit(solution)/shard_map/ppermute | solution.py:600
  115.1 3.9 %all-to-all-start = ((f32[8,400,128]{2,1,0:T(8,128)}), f32[8,400,128]{2,1,0:T(8,128)S(1)}, u32[]{:S(2)}, u32[]{:S(2)}) async-start(f32[8,400,128]{2,1,0:T(8,128)} %merge.1), calls=%async_computation | async-start | bytes 3276800 | tf_op jit(solution)/shard_map/all_to_all | solution.py:597
  119.0 2.4 %collect_other.1 = (f32[384,128]{1,0:T(8,128)}, f32[384,128]{1,0:T(8,128)}) custom-call(f32[8,392,128]{2,1,0:T(8,128)S(1)} %all-to-all-done.1.blocks), custom_call_target="tpu_custom_call" | custom-call | flops 393216 | bytes 393216 | tf_op jit(solution)/shard_map/collect_other/pallas_call | solution.py:466
  122.1 2.8 %collective-permute-start.18 = (f32[384,128]{1,0:T(8,128)}, f32[384,128]{1,0:T(8,128)S(1)}, u32[]{:S(2)}, u32[]{:S(2)}) collective-permute-start(f32[384,128]{1,0:T(8,128)} %get-tuple-element.122), channel_id=1, source_target_pairs={{0,24},{8,16},{16,8},{24,0},{1,25},{9,17},{17,9},{25,1},{2,26},{10... | collective-permute-start | bytes 589832 | tf_op jit(solution)/shard_map/ppermute | solution.py:600
  124.9 15.8 %all-to-all-done.blocks = f32[8,400,128]{2,1,0:T(8,128)S(1)} async-done(((f32[8,400,128]{2,1,0:T(8,128)}), f32[8,400,128]{2,1,0:T(8,128)S(1)}, u32[]{:S(2)}, u32[]{:S(2)}) %all-to-all-start) | async-done | bytes 1638432 | tf_op jit(solution)/shard_map/all_to_all | solution.py:597
  (53 shorter events, 33.1 us)
Async XLA Ops:
  0.6 4.0 %copy-start.1 = (s32[1,1,16,24,8,1]{3,5,4,2,1,0:T(1,128)S(1)}, s32[1,1,16,24,8,1]{3,5,4,2,1,0:T(1,128)}, u32[]{:S(2)}) copy-start(s32[1,1,16,24,8,1]{3,5,4,2,1,0:T(1,128)} %param.11) | copy-start | bytes 36868
  0.6 4.2 %copy-start.2 = (s32[1,1,16,24,8]{3,4,2,1,0:T(8,128)S(1)}, s32[1,1,16,24,8]{3,4,2,1,0:T(8,128)}, u32[]{:S(2)}) copy-start(s32[1,1,16,24,8]{3,4,2,1,0:T(8,128)} %param.12) | copy-start | bytes 36868
  2.0 7.1 %collective-permute-start = (f32[2,16,1024]{2,1,0:T(8,128)S(1)}, f32[2,16,1024]{2,1,0:T(8,128)S(1)}, u32[]{:S(2)}, u32[]{:S(2)}) collective-permute-start(f32[2,16,1024]{2,1,0:T(8,128)S(1)} %get-tuple-element.65.rows_old), channel_id=1, source_target_pairs={{1,0},{2,1},{3,2},{4,3},{5,4},{6,5},{7,6},{9,8},{10,9},{11,10},{12... | collective-permute-start | bytes 393224 | tf_op jit(solution)/shard_map/ppermute | solution.py:443
  3.3 10.3 %collective-permute-start.1 = (f32[2,24,1024]{2,1,0:T(8,128)S(1)}, f32[2,24,1024]{2,1,0:T(8,128)S(1)}, u32[]{:S(2)}, u32[]{:S(2)}) collective-permute-start(f32[2,24,1024]{2,1,0:T(8,128)S(1)} %get-tuple-element.66), channel_id=1, source_target_pairs={{8,0},{9,1},{10,2},{11,3},{12,4},{13,5},{14,6},{15,7},{16,8},{17,9... | collective-permute-start | bytes 589832 | tf_op jit(solution)/shard_map/ppermute | solution.py:443
  13.8 10.5 %collective-permute-start.3 = (f32[2,24,1024]{2,1,0:T(8,128)S(1)}, f32[2,24,1024]{2,1,0:T(8,128)S(1)}, u32[]{:S(2)}, u32[]{:S(2)}) collective-permute-start(f32[2,24,1024]{2,1,0:T(8,128)S(1)} %get-tuple-element.76), channel_id=1, source_target_pairs={{0,8},{1,9},{2,10},{3,11},{4,12},{5,13},{6,14},{7,15},{8,16},{9,17... | collective-permute-start | bytes 589832 | tf_op jit(solution)/shard_map/ppermute | solution.py:443
  17.9 6.4 %collective-permute-start.2 = (f32[2,16,1024]{2,1,0:T(8,128)S(1)}, f32[2,16,1024]{2,1,0:T(8,128)S(1)}, u32[]{:S(2)}, u32[]{:S(2)}) collective-permute-start(f32[2,16,1024]{2,1,0:T(8,128)S(1)} %get-tuple-element.72.order.rows_old), channel_id=1, source_target_pairs={{0,1},{1,2},{2,3},{3,4},{4,5},{5,6},{6,7},{8,9},{9,10},{10,11},{11... | collective-permute-start | bytes 393224 | tf_op jit(solution)/shard_map/ppermute | solution.py:443
  24.5 8.5 %collective-permute-start.5 = (f32[2,24,1024]{2,1,0:T(8,128)S(1)}, f32[2,24,1024]{2,1,0:T(8,128)S(1)}, u32[]{:S(2)}, u32[]{:S(2)}) collective-permute-start(f32[2,24,1024]{2,1,0:T(8,128)S(1)} %get-tuple-element.83), channel_id=1, source_target_pairs={{8,0},{9,1},{10,2},{11,3},{12,4},{13,5},{14,6},{15,7},{16,8},{17,9... | collective-permute-start | bytes 589832 | tf_op jit(solution)/shard_map/ppermute | solution.py:443
  25.8 4.8 %collective-permute-start.4 = (f32[2,16,1024]{2,1,0:T(8,128)S(1)}, f32[2,16,1024]{2,1,0:T(8,128)S(1)}, u32[]{:S(2)}, u32[]{:S(2)}) collective-permute-start(f32[2,16,1024]{2,1,0:T(8,128)S(1)} %get-tuple-element.82.rows_old), channel_id=1, source_target_pairs={{1,0},{2,1},{3,2},{4,3},{5,4},{6,5},{7,6},{9,8},{10,9},{11,10},{12... | collective-permute-start | bytes 393224 | tf_op jit(solution)/shard_map/ppermute | solution.py:443
  33.1 11.2 %collective-permute-start.7 = (f32[2,24,1024]{2,1,0:T(8,128)S(1)}, f32[2,24,1024]{2,1,0:T(8,128)S(1)}, u32[]{:S(2)}, u32[]{:S(2)}) collective-permute-start(f32[2,24,1024]{2,1,0:T(8,128)S(1)} %get-tuple-element.88), channel_id=1, source_target_pairs={{0,8},{1,9},{2,10},{3,11},{4,12},{5,13},{6,14},{7,15},{8,16},{9,17... | collective-permute-start | bytes 589832 | tf_op jit(solution)/shard_map/ppermute | solution.py:443
  36.6 7.7 %collective-permute-start.6 = (f32[2,16,1024]{2,1,0:T(8,128)S(1)}, f32[2,16,1024]{2,1,0:T(8,128)S(1)}, u32[]{:S(2)}, u32[]{:S(2)}) collective-permute-start(f32[2,16,1024]{2,1,0:T(8,128)S(1)} %get-tuple-element.87.rows_old), channel_id=1, source_target_pairs={{0,1},{1,2},{2,3},{3,4},{4,5},{5,6},{6,7},{8,9},{9,10},{10,11},{11... | collective-permute-start | bytes 393224 | tf_op jit(solution)/shard_map/ppermute | solution.py:443
  44.5 9.6 %collective-permute-start.9 = (f32[2,24,1024]{2,1,0:T(8,128)S(1)}, f32[2,24,1024]{2,1,0:T(8,128)S(1)}, u32[]{:S(2)}, u32[]{:S(2)}) collective-permute-start(f32[2,24,1024]{2,1,0:T(8,128)S(1)} %get-tuple-element.95), channel_id=1, source_target_pairs={{8,0},{9,1},{10,2},{11,3},{12,4},{13,5},{14,6},{15,7},{16,8},{17,9... | collective-permute-start | bytes 589832 | tf_op jit(solution)/shard_map/ppermute | solution.py:443
  45.8 3.8 %collective-permute-start.8 = (f32[2,16,1024]{2,1,0:T(8,128)S(1)}, f32[2,16,1024]{2,1,0:T(8,128)S(1)}, u32[]{:S(2)}, u32[]{:S(2)}) collective-permute-start(f32[2,16,1024]{2,1,0:T(8,128)S(1)} %get-tuple-element.94.rows_old), channel_id=1, source_target_pairs={{1,0},{2,1},{3,2},{4,3},{5,4},{6,5},{7,6},{9,8},{10,9},{11,10},{12... | collective-permute-start | bytes 393224 | tf_op jit(solution)/shard_map/ppermute | solution.py:443
  54.3 7.6 %collective-permute-start.11 = (f32[2,24,1024]{2,1,0:T(8,128)S(1)}, f32[2,24,1024]{2,1,0:T(8,128)S(1)}, u32[]{:S(2)}, u32[]{:S(2)}) collective-permute-start(f32[2,24,1024]{2,1,0:T(8,128)S(1)} %get-tuple-element.100), channel_id=1, source_target_pairs={{0,8},{1,9},{2,10},{3,11},{4,12},{5,13},{6,14},{7,15},{8,16},{9,17... | collective-permute-start | bytes 589832 | tf_op jit(solution)/shard_map/ppermute | solution.py:443
  57.0 4.2 %collective-permute-start.10 = (f32[2,16,1024]{2,1,0:T(8,128)S(1)}, f32[2,16,1024]{2,1,0:T(8,128)S(1)}, u32[]{:S(2)}, u32[]{:S(2)}) collective-permute-start(f32[2,16,1024]{2,1,0:T(8,128)S(1)} %get-tuple-element.99.rows_old), channel_id=1, source_target_pairs={{0,1},{1,2},{2,3},{3,4},{4,5},{5,6},{6,7},{8,9},{9,10},{10,11},{11... | collective-permute-start | bytes 393224 | tf_op jit(solution)/shard_map/ppermute | solution.py:443
  62.1 10.1 %collective-permute-start.13 = (f32[2,24,1024]{2,1,0:T(8,128)S(1)}, f32[2,24,1024]{2,1,0:T(8,128)S(1)}, u32[]{:S(2)}, u32[]{:S(2)}) collective-permute-start(f32[2,24,1024]{2,1,0:T(8,128)S(1)} %get-tuple-element.107), channel_id=1, source_target_pairs={{8,0},{9,1},{10,2},{11,3},{12,4},{13,5},{14,6},{15,7},{16,8},{17,9... | collective-permute-start | bytes 589832 | tf_op jit(solution)/shard_map/ppermute | solution.py:443
  63.4 4.2 %collective-permute-start.12 = (f32[2,16,1024]{2,1,0:T(8,128)S(1)}, f32[2,16,1024]{2,1,0:T(8,128)S(1)}, u32[]{:S(2)}, u32[]{:S(2)}) collective-permute-start(f32[2,16,1024]{2,1,0:T(8,128)S(1)} %get-tuple-element.106), channel_id=1, source_target_pairs={{1,0},{2,1},{3,2},{4,3},{5,4},{6,5},{7,6},{9,8},{10,9},{11,10},{12... | collective-permute-start | bytes 393224 | tf_op jit(solution)/shard_map/ppermute | solution.py:443
  72.3 7.8 %collective-permute-start.14 = (f32[2,24,1024]{2,1,0:T(8,128)S(1)}, f32[2,24,1024]{2,1,0:T(8,128)S(1)}, u32[]{:S(2)}, u32[]{:S(2)}) collective-permute-start(f32[2,24,1024]{2,1,0:T(8,128)S(1)} %get-tuple-element.110), channel_id=1, source_target_pairs={{0,8},{1,9},{2,10},{3,11},{4,12},{5,13},{6,14},{7,15},{8,16},{9,17... | collective-permute-start | bytes 589832 | tf_op jit(solution)/shard_map/ppermute | solution.py:443
  75.2 4.9 %collective-permute-start.15 = (f32[2,16,1024]{2,1,0:T(8,128)S(1)}, f32[2,16,1024]{2,1,0:T(8,128)S(1)}, u32[]{:S(2)}, u32[]{:S(2)}) collective-permute-start(f32[2,16,1024]{2,1,0:T(8,128)S(1)} %get-tuple-element.111), channel_id=1, source_target_pairs={{0,1},{1,2},{2,3},{3,4},{4,5},{5,6},{6,7},{8,9},{9,10},{10,11},{11... | collective-permute-start | bytes 393224 | tf_op jit(solution)/shard_map/ppermute | solution.py:443
  87.6 27.5 %all-to-all-start.1 = ((f32[8,392,128]{2,1,0:T(8,128)}), f32[8,392,128]{2,1,0:T(8,128)S(1)}, u32[]{:S(2)}, u32[]{:S(2)}) async-start(f32[8,392,128]{2,1,0:T(8,128)} %get-tuple-element.120), calls=%async_computation.1 | async-start | bytes 3211264 | tf_op jit(solution)/shard_map/all_to_all | solution.py:597
  93.2 20.9 %collective-permute-start.16 = (f32[8,200,128]{2,1,0:T(8,128)}, f32[8,200,128]{2,1,0:T(8,128)S(1)}, u32[]{:S(2)}, u32[]{:S(2)}) collective-permute-start(f32[8,200,128]{2,1,0:T(8,128)} %get-tuple-element.118), channel_id=1, source_target_pairs={{0,8},{8,0},{16,24},{24,16},{1,9},{9,1},{17,25},{25,17},{2,10},{10... | collective-permute-start | bytes 2457608 | tf_op jit(solution)/shard_map/ppermute | solution.py:600
  114.1 28.3 %copy-start = (f32[384,128]{1,0:T(8,128)S(1)}, f32[384,128]{1,0:T(8,128)}, u32[]{:S(2)}) copy-start(f32[384,128]{1,0:T(8,128)} %enthalpy.1) | copy-start | bytes 589828
  115.1 25.6 %all-to-all-start = ((f32[8,400,128]{2,1,0:T(8,128)}), f32[8,400,128]{2,1,0:T(8,128)S(1)}, u32[]{:S(2)}, u32[]{:S(2)}) async-start(f32[8,400,128]{2,1,0:T(8,128)} %merge.1), calls=%async_computation | async-start | bytes 3276800 | tf_op jit(solution)/shard_map/all_to_all | solution.py:597
  121.4 21.0 %collective-permute-start.17 = (f32[384,128]{1,0:T(8,128)}, f32[384,128]{1,0:T(8,128)S(1)}, u32[]{:S(2)}, u32[]{:S(2)}) collective-permute-start(f32[384,128]{1,0:T(8,128)} %get-tuple-element.121), channel_id=1, source_target_pairs={{0,16},{8,24},{16,0},{24,8},{1,17},{9,25},{17,1},{25,9},{2,18},{10... | collective-permute-start | bytes 589832 | tf_op jit(solution)/shard_map/ppermute | solution.py:600
  122.1 20.3 %collective-permute-start.18 = (f32[384,128]{1,0:T(8,128)}, f32[384,128]{1,0:T(8,128)S(1)}, u32[]{:S(2)}, u32[]{:S(2)}) collective-permute-start(f32[384,128]{1,0:T(8,128)} %get-tuple-element.122), channel_id=1, source_target_pairs={{0,24},{8,16},{16,8},{24,0},{1,25},{9,17},{17,9},{25,1},{2,26},{10... | collective-permute-start | bytes 589832 | tf_op jit(solution)/shard_map/ppermute | solution.py:600

commit v8 on v6

--- a/solution.py
+++ b/solution.py
@@ -62,22 +62,36 @@
     return jnp.where(place > 0, pltpu.roll(f, 1, 0), jnp.broadcast_to(row, f.shape))
 
 
-def edge_kernel(e, to_col, to_hgt, low, sems):
-    nx = e.shape[1]
-    col_copy = pltpu.make_async_copy(e.at[pl.ds(1, 2), 0], to_col, sems.at[0])
-    low_copy = pltpu.make_async_copy(e.at[pl.ds(0, 2), :, pl.ds(0, ROWS)], low, sems.at[1])
-    low_copy.start()
-    col_copy.start()
-    low_copy.wait()
-    for x in range(nx):
-        for comp in range(2):
-            to_hgt[comp, x : x + 1, :] = low[comp, x, 0:1, :]
-    col_copy.wait()
+def on(predicate, even, odd):
+    pl.when(predicate)(even)
+    pl.when(jnp.logical_not(predicate))(odd)
+
+
+def edge_kernel(spot, e, h, order, col_even, col_odd, sems):
+    last = e.shape[1] - 1
+
+    def send(fwd, back):
+        def run():
+            copies = [
+                pltpu.make_async_copy(e.at[:, last], fwd.at[pl.ds(0, 3)], sems.at[0]),
+                pltpu.make_async_copy(h.at[pl.ds(1, 2), last], fwd.at[pl.ds(3, 2)], sems.at[1]),
+                pltpu.make_async_copy(e.at[:, 0], back.at[pl.ds(0, 3)], sems.at[2]),
+                pltpu.make_async_copy(e.at[pl.ds(1, 2), 0], back.at[pl.ds(3, 2)], sems.at[3]),
+            ]
+            for copy in copies:
+                copy.start()
+            for copy in copies:
+                copy.wait()
+
+        return run
+
+    on(lax.rem(spot[0], 2) == 0, send(col_even, col_odd), send(col_odd, col_even))
 
 
 def load_kernel(
-    temp_far, tags_far, e_far, h_far, order, ca, cb, sigma_out, e, h, media_rows, e_rows, h_rows, temp, tags, sems
+    spot, temp_far, tags_far, e_far, h_far, ca, cb, sigma_out, e, h, own_rows, *refs
 ):
+    hgt_even, hgt_odd, diag_even, diag_odd, temp, tags, sems = refs
     nx, nz, _ = temp.shape
     parts = 4
     size = nx // parts
@@ -110,8 +124,6 @@
             ca[x, z : z + ROWS, :] = (eps - half) * inverse
             cb[x, z : z + ROWS, :] = COURANT * inverse
             sigma_out[x, z : z + ROWS, :] = sigma
-        media_rows[0, pl.ds(x, 1), :] = ca[x, 0:1, :]
-        media_rows[1, pl.ds(x, 1), :] = cb[x, 0:1, :]
         return carry
 
     for part in range(parts):
@@ -121,14 +133,41 @@
     e_copy.wait()
     h_copy.wait()
 
-    def rows(x, carry):
-        for comp in range(3):
-            e_rows[comp, pl.ds(x, 1), :] = e[comp, x, nz - 1 : nz, :]
-        for comp in range(2):
-            h_rows[comp, pl.ds(x, 1), :] = h[comp, x, nz - 1 : nz, :]
-        return carry
-
-    lax.fori_loop(0, nx, rows, 0)
+    pass_on(spot, e, own_rows, hgt_even, hgt_odd, diag_even, diag_odd, h)
+
+
+def pass_on(spot, e, own_rows, hgt_even, hgt_odd, diag_even, diag_odd, h=None):
+    nx, nz = e.shape[1:3]
+
+    def send(fwd, back):
+        def run():
+            def rows(x, carry):
+                for comp in range(3):
+                    fwd[comp, pl.ds(x, 1), :] = e[comp, x, nz - 1 : nz, :]
+                    low = e[comp, x, 0:1, :]
+                    back[comp, pl.ds(x, 1), :] = low
+                    if comp < 2:
+                        own_rows[comp, pl.ds(x, 1), :] = low
+                if h is not None:
+                    for comp in range(2):
+                        fwd[3 + comp, pl.ds(x, 1), :] = h[comp, x, nz - 1 : nz, :]
+                        back[3 + comp, pl.ds(x, 1), :] = e[comp, x, 0:1, :]
+                return carry
+
+            lax.fori_loop(0, nx, rows, 0)
+
+        return run
+
+    on(lax.rem(spot[1], 2) == 0, send(hgt_even, hgt_odd), send(hgt_odd, hgt_even))
+
+    def corners(fwd, back):
+        def run():
+            fwd[...] = e[0, nx - 1, 0:1, :]
+            back[...] = e[2, 0, nz - 1 : nz, :]
+
+        return run
+
+    on(lax.rem(spot[0], 2) == 0, corners(diag_even, diag_odd), corners(diag_odd, diag_even))
 
 
 def over(first, stop, body):
@@ -154,7 +193,7 @@
     if col is None:
         next_y, next_z = (e[comp, x + 1, here, :] for comp in (1, 2))
     else:
-        next_y, next_z = (col[comp, here, :] for comp in range(2))
+        next_y, next_z = (col[comp, here, :] for comp in (1, 2))
     h[0, x, here, :] = h[0, x, here, :] - COURANT * ((after_y(ez) - ez) - (after_row(ey, row_y) - ey))
     hy = h[1, x, here, :] - COURANT * ((after_row(ex, row_x) - ex) - (next_z - ez))
     hz = h[2, x, here, :] - COURANT * ((next_y - ey) - (after_y(ex) - ex))
@@ -187,82 +226,91 @@
     return ey, ez
 
 
-def h_edge_kernel(e, col, hgt, e_rows, rows_old, h_old, h, to_col, to_hgt):
+def step_kernel(first, last, *refs):
+    spot, h_old, e_old, ca, cb, sigma, own_old, col_even, col_odd, hgt_even, hgt_odd, diag_even, diag_odd = refs[:13]
+    refs = refs[13:]
+    if not first:
+        beyond_old, below_old, power_old = refs[:3]
+        refs = refs[3:]
+    h, e, power, beyond, below = refs[:5]
+    refs = refs[5:]
+    if last:
+        h_out = refs[0]
+        refs = refs[1:]
+    else:
+        own_rows, to_col_even, to_col_odd, to_hgt_even, to_hgt_odd, to_diag_even, to_diag_odd = refs[:7]
+        refs = refs[7:]
+    col_fwd, col_back, hgt_fwd, hgt_back, corner_x, corner_z = refs[:6]
     nx, nz = e.shape[1:3]
+    first_col = lax.rem(spot[0], 2) == 0
+    first_hgt = lax.rem(spot[1], 2) == 0
+
+    def take(pairs):
+        def run():
+            for target, source in pairs:
+                target[...] = source[0 : target.shape[0]]
+
+        return run
+
+    on(
+        first_col,
+        take([(col_fwd, col_odd), (col_back, col_even), (corner_x, diag_odd), (corner_z, diag_even)]),
+        take([(col_fwd, col_even), (col_back, col_odd), (corner_x, diag_even), (corner_z, diag_odd)]),
+    )
+    on(
+        first_hgt,
+        take([(hgt_fwd, hgt_odd), (hgt_back, hgt_even)]),
+        take([(hgt_fwd, hgt_even), (hgt_back, hgt_odd)]),
+    )
+    inside_x = COURANT * jnp.where(spot[0] > 0, 1.0, 0.0)
+    inside_z = COURANT * jnp.where(spot[1] > 0, 1.0, 0.0)
+
     for z in range(0, nz, ROWS):
-        hy, hz = h_tile(e, h, col, hgt, nx - 1, z)
-        to_col[0, z : z + ROWS, :] = hy
-        to_col[1, z : z + ROWS, :] = hz
+        here = slice(z, z + ROWS)
+        ex, ey, ez = (col_fwd[comp, here, :] for comp in range(3))
+        row = col_fwd[0, z + ROWS : z + ROWS + 1, :] if z + ROWS < nz else corner_x[...]
+        hy = col_fwd[3, here, :] if first else beyond_old[0, here, :]
+        hz = col_fwd[4, here, :] if first else beyond_old[1, here, :]
+        beyond[0, here, :] = hy - inside_x * ((after_row(ex, row) - ex) - (e[2, 0, here, :] - ez))
+        beyond[1, here, :] = hz - inside_x * ((e[1, 0, here, :] - ey) - (after_y(ex) - ex))
     for x in range(0, nx, ROWS):
         here = slice(x, x + ROWS)
-        ex, ey, ez = (e_rows[comp, here, :] for comp in range(3))
-        row = e_rows[2, x + ROWS : x + ROWS + 1, :] if x + ROWS < nx else col[1, nz - 1 : nz, :]
-        to_hgt[0, here, :] = rows_old[0, here, :] - COURANT * ((after_y(ez) - ez) - (hgt[1, here, :] - ey))
-        to_hgt[1, here, :] = rows_old[1, here, :] - COURANT * ((hgt[0, here, :] - ex) - (after_row(ez, row) - ez))
-
-
-def h_rest_kernel(e, hgt, h_old, h, *rows):
-    nx, nz = e.shape[1:3]
-
-    def keep(x):
-        if rows:
-            for comp in range(3):
-                rows[0][comp, pl.ds(x, 1), :] = h[comp, x, 0:1, :]
-
-    def plane(x):
+        ex, ey, ez = (hgt_fwd[comp, here, :] for comp in range(3))
+        row = hgt_fwd[2, x + ROWS : x + ROWS + 1, :] if x + ROWS < nx else corner_z[...]
+        hx = hgt_fwd[3, here, :] if first else below_old[0, here, :]
+        hy = hgt_fwd[4, here, :] if first else below_old[1, here, :]
+        below[0, here, :] = hx - inside_z * ((after_y(ez) - ez) - (own_old[1, here, :] - ey))
+        below[1, here, :] = hy - inside_z * ((own_old[0, here, :] - ex) - (after_row(ez, row) - ez))
+
+    def h_plane(x):
         for z in range(0, nz, ROWS):
-            h_tile(e, h, None, hgt, x, z)
-        keep(x)
-
-    over(0, nx - 1, plane)
-    keep(nx - 1)
-
-
-def e_edge_kernel(first, h, ca, cb, sigma, col, hgt, media_rows, h_rows, rows_old, *refs):
-    e, power, to_col, to_hgt = refs[-4:]
-    nx, nz = e.shape[1:3]
-    for z in range(0, nz, ROWS):
-        ey, ez = e_tile(first, h, e, power, ca, cb, sigma, col, hgt, 0, z)
-        to_col[0, z : z + ROWS, :] = ey
-        to_col[1, z : z + ROWS, :] = ez
-    for x in range(0, nx, ROWS):
-        here = slice(x, x + ROWS)
-        hx, hy, hz = (h_rows[comp, here, :] for comp in range(3))
-        row = h_rows[2, x - 1 : x, :] if x > 0 else col[1, 0:1, :]
-        keep = media_rows[0, here, :]
-        drive = media_rows[1, here, :]
-        to_hgt[0, here, :] = keep * rows_old[0, here, :] + drive * ((hz - before_y(hz)) - (hy - hgt[1, here, :]))
-        to_hgt[1, here, :] = keep * rows_old[1, here, :] + drive * ((hx - hgt[0, here, :]) - (hz - before_row(hz, row)))
-
-
-def e_rest_kernel(first, h, ca, cb, sigma, hgt, e_old, power_old, e, power, rows):
-    nx, nz = e.shape[1:3]
-
-    def keep(x):
-        for comp in range(3):
-            rows[comp, pl.ds(x, 1), :] = e[comp, x, nz - 1 : nz, :]
-
-    def plane(x):
+            h_tile(e, h, col_back if isinstance(x, int) else None, hgt_back, x, z)
+
+    over(0, nx - 1, h_plane)
+    h_plane(nx - 1)
+    if last:
+        copy = pltpu.make_async_copy(h, h_out, refs[6])
+        copy.start()
+
+    def e_plane(x):
         for z in range(0, nz, ROWS):
-            e_tile(first, h, e, power, ca, cb, sigma, None, hgt, x, z)
-        keep(x)
-
-    keep(0)
-    over(1, nx, plane)
-
-
-def e_last_kernel(first, h, ca, cb, sigma, col, hgt, e_old, power_old, e, power, h_out, sem):
-    nx, nz = e.shape[1:3]
-    copy = pltpu.make_async_copy(h, h_out, sem)
-    copy.start()
-
-    def plane(x):
-        for z in range(0, nz, ROWS):
-            e_tile(first, h, e, power, ca, cb, sigma, col if isinstance(x, int) else None, hgt, x, z)
-
-    plane(0)
-    over(1, nx, plane)
-    copy.wait()
+            e_tile(first, h, e, power, ca, cb, sigma, beyond if isinstance(x, int) else None, below, x, z)
+
+    e_plane(0)
+    over(1, nx, e_plane)
+    if last:
+        copy.wait()
+        return
+
+    def send(fwd, back):
+        def run():
+            fwd[...] = e[:, nx - 1]
+            back[...] = e[:, 0]
+
+        return run
+
+    on(first_col, send(to_col_even, to_col_odd), send(to_col_odd, to_col_even))
+    pass_on(spot, e, own_rows, to_hgt_even, to_hgt_odd, to_diag_even, to_diag_odd)
 
 
 def places_kernel(n_col, n_hgt, cap, my_col, owner, node, place, flat):
@@ -427,15 +475,16 @@
     out[...] = jnp.where(content < 0.0, content / 2.0, jnp.where(content > 1.0, (content - 1.0) / 3.0, 0.0))
 
 
-def shifted(block, d_col, d_hgt):
+def swapped(block, d_col, d_hgt, odd):
     n_col = lax.axis_size("col")
     n_hgt = lax.axis_size("hgt")
-    route = [
-        (c * n_hgt + h, (c + d_col) * n_hgt + h + d_hgt)
-        for c in range(n_col)
-        for h in range(n_hgt)
-        if 0 <= c + d_col < n_col and 0 <= h + d_hgt < n_hgt
-    ]
+    route = []
+    for c in range(n_col):
+        for h in range(n_hgt):
+            place = c if d_col else h
+            if place % 2 == odd and 0 <= c + d_col < n_col and 0 <= h + d_hgt < n_hgt:
+                pair = (c * n_hgt + h, (c + d_col) * n_hgt + h + d_hgt)
+                route += [pair, pair[::-1]]
     return lax.ppermute(block, ("col", "hgt"), route)
 
 
@@ -473,92 +522,88 @@
 
     e_start = far(efield_lattice_vector)
     h_start = far(hfield_lattice_vector)
-    my_col = lax.axis_index("col").astype(jnp.int32).reshape(1)
+    spot = jnp.stack([lax.axis_index("col"), lax.axis_index("hgt")]).astype(jnp.int32)
     owners = block_owner.reshape(1, count)
     nodes = block_node.reshape(1, count)
     field = vmem(3, nx, nz, ny)
     whole = vmem(nx, nz, ny)
-    planes = vmem(2, nz, ny)
-    two_rows = vmem(2, nx, ny)
-    three_rows = vmem(3, nx, ny)
-
-    to_col, e_low = kernel(
-        edge_kernel, (planes, two_rows), [FAR], [e_start], "edge", 4, scratch=[vmem(2, nx, ROWS, ny), sem((2,))]
-    )
-    col = shifted(to_col, -1, 0)
-    hgt = shifted(e_low, 0, -1)
-    ca, cb, sigma, e, h, media_rows, e_rows, h_high = kernel(
+    pair_planes = vmem(2, nz, ny)
+    pair_rows = vmem(2, nx, ny)
+    row = vmem(1, ny)
+
+    def exchange(to_col_even, to_col_odd, to_hgt_even, to_hgt_odd, to_diag_even, to_diag_odd):
+        return (
+            swapped(to_col_even, 1, 0, 0) if to_col_even is not None else None,
+            swapped(to_col_odd, 1, 0, 1) if to_col_odd is not None else None,
+            swapped(to_hgt_even, 0, 1, 0),
+            swapped(to_hgt_odd, 0, 1, 1),
+            swapped(to_diag_even, 1, -1, 0),
+            swapped(to_diag_odd, 1, -1, 1),
+        )
+
+    to_col_even, to_col_odd = kernel(
+        edge_kernel,
+        (vmem(5, nz, ny), vmem(5, nz, ny)),
+        [SCALARS, FAR, FAR, WHOLE],
+        [spot, e_start, h_start, owners + nodes],
+        "edge",
+        4,
+        scratch=[sem((4,))],
+    )
+    col = (swapped(to_col_even, 1, 0, 0), swapped(to_col_odd, 1, 0, 1))
+    ca, cb, sigma, e, h, own_rows, *sends = kernel(
         load_kernel,
-        (whole, whole, whole, field, field, two_rows, three_rows, two_rows),
-        [FAR] * 4 + [WHOLE],
-        [far(cell_temp), far(region_tags), e_start, h_start, owners + nodes + my_col],
+        (whole, whole, whole, field, field, pair_rows, vmem(5, nx, ny), vmem(5, nx, ny), row, row),
+        [SCALARS] + [FAR] * 4,
+        [spot, far(cell_temp), far(region_tags), e_start, h_start],
         "load",
         60,
         scratch=[vmem(nx, nz, ny), pltpu.VMEM((nx, nz, ny), jnp.int32), sem((3, 4))],
     )
+    others = exchange(None, None, *sends)[2:]
     begins, heights = starts_of(n_col, n_hgt, cap)
     place, flat = kernel(
         functools.partial(places_kernel, n_col, n_hgt, cap),
         (jax.ShapeDtypeStruct((1, count), jnp.int32), vmem(n_hgt * sum(heights), PTS)),
         [SCALARS, WHOLE, WHOLE],
-        [my_col, owners, nodes],
+        [spot, owners, nodes],
         "places",
         8,
     )
-    power = None
+    beyond = below = power = None
     for step in range(STEPS):
         first = step == 0
-        h, to_col, h_high = kernel(
-            h_edge_kernel,
-            (field, planes, two_rows),
-            [WHOLE] * 6,
-            [e, col, hgt, e_rows, h_high, h],
-            f"h_edge_{step}",
-            4,
-            {5: 0},
-        )
-        e_hgt = hgt
-        col = shifted(to_col, 1, 0)
-        hgt = shifted(h_high, 0, 1)
         last = step == STEPS - 1
-        outs = (field,) if last else (field, three_rows)
-        h, *h_rows = kernel(h_rest_kernel, outs, [WHOLE] * 3, [e, e_hgt, h], f"h_rest_{step}", 40, {2: 0})
-        media = [h, ca, cb, sigma]
+        args = [spot, h, e, ca, cb, sigma, own_rows, *col, *others]
+        aliases = {1: 0, 2: 1}
+        if not first:
+            args += [beyond, below, power]
+            aliases[15] = 2
+        outs = [field, field, whole, pair_planes, pair_rows]
         if last:
-            e, power, h_out = pl.pallas_call(
-                functools.partial(e_last_kernel, first),
-                out_shape=(field, whole, pltpu.HBM((3, nx, nz, ny), F32)),
-                in_specs=[WHOLE] * 8,
-                out_specs=(WHOLE, WHOLE, FAR),
-                input_output_aliases={6: 0, 7: 1},
-                scratch_shapes=[sem],
-                compiler_params=params(VMEM_MIB),
-                cost_estimate=cost(cells * 50, cells * 50),
-                name="e_last",
-            )(*media, col, hgt, e, power)
-            break
-        args = media + [col, hgt, media_rows, *h_rows, e_low, e] + ([] if first else [power])
-        e, power, to_col, e_low = kernel(
-            functools.partial(e_edge_kernel, first),
-            (field, whole, planes, two_rows),
-            [WHOLE] * len(args),
-            args,
-            f"e_edge_{step}",
-            5,
-            {9: 0} if first else {9: 0, 10: 1},
-        )
-        h_hgt = hgt
-        col = shifted(to_col, -1, 0)
-        hgt = shifted(e_low, 0, -1)
-        e, power, e_rows = kernel(
-            functools.partial(e_rest_kernel, first),
-            (field, whole, three_rows),
-            [WHOLE] * 7,
-            media + [h_hgt, e, power],
-            f"e_rest_{step}",
-            45,
-            {5: 0, 6: 1},
-        )
+            outs += [pltpu.HBM((3, nx, nz, ny), F32)]
+        else:
+            outs += [pair_rows] + [vmem(3, nz, ny)] * 2 + [vmem(3, nx, ny)] * 2 + [row] * 2
+        deep = 5 if first else 3
+        scratch = [vmem(deep, nz, ny), vmem(3, nz, ny), vmem(deep, nx, ny), vmem(2, nx, ny), row, row]
+        outs = pl.pallas_call(
+            functools.partial(step_kernel, first, last),
+            out_shape=tuple(outs),
+            in_specs=[SCALARS] + [WHOLE] * (len(args) - 1),
+            out_specs=(WHOLE,) * 5 + ((FAR,) if last else (WHOLE,) * 7),
+            input_output_aliases=aliases,
+            scratch_shapes=scratch + ([sem] if last else []),
+            compiler_params=params(VMEM_MIB),
+            cost_estimate=cost(cells * 100, cells * 100),
+            name=f"step_{step}",
+        )(*args)
+        h, e, power, beyond, below = outs[:5]
+        if last:
+            h_out = outs[5]
+        else:
+            own_rows = outs[5]
+            received = exchange(*outs[6:])
+            col, others = received[:2], received[2:]
 
     mine, pair, other, e_out, _ = pl.pallas_call(
         functools.partial(pack_kernel, heights),

time: 141 us -> 167 us (1.18)
  starting transfers between devices: 45.5 us -> 82.1 us
  waiting for transfers between devices: 56.1 us -> 37.2 us
  Pallas kernels: 37.1 us -> 43.6 us
  local copies, waits for them, and re-layouts: 0.5 us -> 2.18 us
    ppermute x16 -> x24, starting transfers between devices: 33.5 us -> 58.1 us  [swapped(): return lax.ppermute(block, ('col', 'hgt'), route)]
    pallas_call x1 -> x4, Pallas kernels: 2.34 us -> 22.6 us  [per_device(): pl.pallas_call(functools.partial(step_kernel, first, last), out_shape=tup...]
    ppermute x16 -> x24, waiting for transfers between devices: 20.2 us -> 2.87 us  [swapped(): return lax.ppermute(block, ('col', 'hgt'), route)]
    pallas_call x20 -> x6, Pallas kernels: 28.7 us -> 14.9 us  [kernel(): pl.pallas_call(body, out_shape=outs, in_specs=ins, out_specs=jax.tree.map...]
    all_to_all x2, starting transfers between devices: 7.73 us -> 15.7 us  [swap(): return lax.all_to_all(x, axis, split_axis=0, concat_axis=0, tiled=True)]
    ppermute x3, starting transfers between devices: 4.28 us -> 8.35 us  [across(): return lax.ppermute(x, 'col', [(c, c ^ turn) for c in range(n_col)])]
    unnamed x8 -> x4, local copies, waits for them, and re-layouts: 0.22 us -> 1.9 us
  transfers between devices with their start and end apart: 21 -> 29, of which waited for: 11 -> 3; matrix products, arithmetic and copies ran while one was open for 0% -> 0% of each run, Pallas kernels for 19% -> 8%
where the time goes in v8:
time: 167 us; the launch traced here: 166 us
  starting transfers between devices  82.1 us (49%)
  Pallas kernels  43.6 us (26%)
  waiting for transfers between devices  37.2 us (22%)
  local copies, waits for them, and re-layouts  2.18 us (1%)
    ppermute x24, starting transfers between devices, swapped(): return lax.ppermute(block, ('col', 'hgt'), route)  58.1 us
    pallas_call x4, Pallas kernels, per_device(): pl.pallas_call(functools.partial(step_kernel, first, last), out_shape=tup...  22.6 us
    ppermute x3, waiting for transfers between devices, across(): return lax.ppermute(x, 'col', [(c, c ^ turn) for c in range(n_col)])  19.1 us
    all_to_all x2, starting transfers between devices, swap(): return lax.all_to_all(x, axis, split_axis=0, concat_axis=0, tiled=True)  15.7 us
    all_to_all x2, waiting for transfers between devices, swap(): return lax.all_to_all(x, axis, split_axis=0, concat_axis=0, tiled=True)  15.2 us
    pallas_call x6, Pallas kernels, kernel(): pl.pallas_call(body, out_shape=outs, in_specs=ins, out_specs=jax.tree.map...  14.9 us
    ppermute x3, starting transfers between devices, across(): return lax.ppermute(x, 'col', [(c, c ^ turn) for c in range(n_col)])  8.35 us
    pallas_call x1, Pallas kernels, per_device(): pl.pallas_call(functools.partial(pack_kernel, heights), out_shape=(pltpu....  5.15 us
  transfers between devices with their start and end apart: 29, of which 3 were waited for; matrix products, arithmetic and copies ran while one was open for 0% of the time, Pallas kernels for 8%

profile of v8, /device:TPU:0, one launch (start us, length us, event | category | flops | bytes accessed | tf_op | source)
XLA Modules:
  0.0 166.3 jit_solution(9814207783838135328)
XLA Ops:
  2.9 1.8 %edge.1 = (f32[5,24,1024]{2,1,0:T(8,128)S(1)}, f32[5,24,1024]{2,1,0:T(8,128)S(1)}) custom-call(s32[2]{0:T(128)S(1)} %pad_add_fusion.my_col.spot.refs_0_, f32[3,16,24,1024]{3,2,1,0:T(8,128)} %e.1, f32[3,16,24,1024]{3,2,1,0:T(8,128)} %h.1, s32[1,3072]{1,0:T(1,128)S(1)} %add.3.order), custom_call_target="tpu_custom_call" | custom-call | flops 1572864 | bytes 1572864 | tf_op jit(solution)/shard_map/edge/pallas_call | solution.py:511
  4.7 3.1 %collective-permute-start = (f32[5,24,1024]{2,1,0:T(8,128)S(1)}, f32[5,24,1024]{2,1,0:T(8,128)S(1)}, u32[]{:S(2)}, u32[]{:S(2)}) collective-permute-start(f32[5,24,1024]{2,1,0:T(8,128)S(1)} %get-tuple-element.69), channel_id=1, source_target_pairs={{0,8},{8,0},{1,9},{9,1},{2,10},{10,2},{3,11},{11,3},{4,12},{12,4},... | collective-permute-start | bytes 1474568 | tf_op jit(solution)/shard_map/ppermute | solution.py:488
  8.5 5.6 %load.1 = (f32[16,24,1024]{2,1,0:T(8,128)S(1)}, f32[16,24,1024]{2,1,0:T(8,128)S(1)}, f32[16,24,1024]{2,1,0:T(8,128)S(1)}, f32[3,16,24,1024]{3,2,1,0:T(8,128)S(1)...) custom-call(s32[2]{0:T(128)S(1)} %pad_add_fusion.my_col.spot.refs_0_, ...), custom_call_target="tpu_custom_call" | custom-call | flops 23592960 | bytes 23592960 | tf_op jit(solution)/shard_map/load/pallas_call | solution.py:511
  16.2 2.8 %collective-permute-done.refs_7_ = f32[5,24,1024]{2,1,0:T(8,128)S(1)} collective-permute-done((f32[5,24,1024]{2,1,0:T(8,128)S(1)}, f32[5,24,1024]{2,1,0:T(8,128)S(1)}, u32[]{:S(2)}, u32[]{:S(2)}) %collective-permute-start) | collective-permute-done | bytes 491552 | tf_op jit(solution)/shard_map/ppermute | solution.py:488
  19.0 5.5 %step_0.1 = (f32[3,16,24,1024]{3,2,1,0:T(8,128)S(1)}, f32[3,16,24,1024]{3,2,1,0:T(8,128)S(1)}, f32[16,24,1024]{2,1,0:T(8,128)S(1)}, f32[2,24,1024]{2,1,0:T(8,128...) custom-call(s32[2]{0:T(128)S(1)} %pad_add_fusion.my_col.spot.refs_0_, ...), custom_call_target="tpu_custom_call", output_to_operand_aliasing={{0}: (1, {}), {1}: (2, {})} | custom-call | flops 39321600 | bytes 39321600 | tf_op jit(solution)/shard_map/step_0/pallas_call | solution.py:589
  24.5 5.9 %collective-permute-start.6 = (f32[3,24,1024]{2,1,0:T(8,128)S(1)}, f32[3,24,1024]{2,1,0:T(8,128)S(1)}, u32[]{:S(2)}, u32[]{:S(2)}) collective-permute-start(f32[3,24,1024]{2,1,0:T(8,128)S(1)} %get-tuple-element.78), channel_id=1, source_target_pairs={{0,8},{8,0},{1,9},{9,1},{2,10},{10,2},{3,11},{11,3},{4,12},{12,4},... | collective-permute-start | bytes 884744 | tf_op jit(solution)/shard_map/ppermute | solution.py:488
  31.1 7.8 %collective-permute-start.8 = (f32[3,16,1024]{2,1,0:T(8,128)S(1)}, f32[3,16,1024]{2,1,0:T(8,128)S(1)}, u32[]{:S(2)}, u32[]{:S(2)}) collective-permute-start(f32[3,16,1024]{2,1,0:T(8,128)S(1)} %get-tuple-element.80), channel_id=1, source_target_pairs={{0,1},{1,0},{2,3},{3,2},{4,5},{5,4},{6,7},{7,6},{8,9},{9,8},{10,11... | collective-permute-start | bytes 589832 | tf_op jit(solution)/shard_map/ppermute | solution.py:488
  41.0 5.6 %step_1.1 = (f32[3,16,24,1024]{3,2,1,0:T(8,128)S(1)}, f32[3,16,24,1024]{3,2,1,0:T(8,128)S(1)}, f32[16,24,1024]{2,1,0:T(8,128)S(1)}, f32[2,24,1024]{2,1,0:T(8,128...) custom-call(s32[2]{0:T(128)S(1)} %pad_add_fusion.my_col.spot.refs_0_, ...), custom_call_target="tpu_custom_call", output_to_operand_aliasing={{0}: (1, {}), {1}: (2, {}), {2}: (15, {})} | custom-call | flops 39321600 | bytes 39321600 | tf_op jit(solution)/shard_map/step_1/pallas_call | solution.py:589
  46.6 8.0 %collective-permute-start.12 = (f32[3,24,1024]{2,1,0:T(8,128)S(1)}, f32[3,24,1024]{2,1,0:T(8,128)S(1)}, u32[]{:S(2)}, u32[]{:S(2)}) collective-permute-start(f32[3,24,1024]{2,1,0:T(8,128)S(1)} %get-tuple-element.90), channel_id=1, source_target_pairs={{0,8},{8,0},{1,9},{9,1},{2,10},{10,2},{3,11},{11,3},{4,12},{12,4},... | collective-permute-start | bytes 884744 | tf_op jit(solution)/shard_map/ppermute | solution.py:488
  55.2 6.5 %collective-permute-start.14 = (f32[3,16,1024]{2,1,0:T(8,128)S(1)}, f32[3,16,1024]{2,1,0:T(8,128)S(1)}, u32[]{:S(2)}, u32[]{:S(2)}) collective-permute-start(f32[3,16,1024]{2,1,0:T(8,128)S(1)} %get-tuple-element.92), channel_id=1, source_target_pairs={{0,1},{1,0},{2,3},{3,2},{4,5},{5,4},{6,7},{7,6},{8,9},{9,8},{10,11... | collective-permute-start | bytes 589832 | tf_op jit(solution)/shard_map/ppermute | solution.py:488
  63.8 5.6 %step_2.1 = (f32[3,16,24,1024]{3,2,1,0:T(8,128)S(1)}, f32[3,16,24,1024]{3,2,1,0:T(8,128)S(1)}, f32[16,24,1024]{2,1,0:T(8,128)S(1)}, f32[2,24,1024]{2,1,0:T(8,128...) custom-call(s32[2]{0:T(128)S(1)} %pad_add_fusion.my_col.spot.refs_0_, ...), custom_call_target="tpu_custom_call", output_to_operand_aliasing={{0}: (1, {}), {1}: (2, {}), {2}: (15, {})} | custom-call | flops 39321600 | bytes 39321600 | tf_op jit(solution)/shard_map/step_2/pallas_call | solution.py:589
  69.4 7.9 %collective-permute-start.18 = (f32[3,24,1024]{2,1,0:T(8,128)S(1)}, f32[3,24,1024]{2,1,0:T(8,128)S(1)}, u32[]{:S(2)}, u32[]{:S(2)}) collective-permute-start(f32[3,24,1024]{2,1,0:T(8,128)S(1)} %get-tuple-element.102), channel_id=1, source_target_pairs={{0,8},{8,0},{1,9},{9,1},{2,10},{10,2},{3,11},{11,3},{4,12},{12,4},... | collective-permute-start | bytes 884744 | tf_op jit(solution)/shard_map/ppermute | solution.py:488
  77.9 8.2 %collective-permute-start.20 = (f32[3,16,1024]{2,1,0:T(8,128)S(1)}, f32[3,16,1024]{2,1,0:T(8,128)S(1)}, u32[]{:S(2)}, u32[]{:S(2)}) collective-permute-start(f32[3,16,1024]{2,1,0:T(8,128)S(1)} %get-tuple-element.104), channel_id=1, source_target_pairs={{0,1},{1,0},{2,3},{3,2},{4,5},{5,4},{6,7},{7,6},{8,9},{9,8},{10,11... | collective-permute-start | bytes 589832 | tf_op jit(solution)/shard_map/ppermute | solution.py:488
  88.1 2.7 %places.1 = (s32[1,3072]{1,0:T(1,128)S(1)}, f32[6336,128]{1,0:T(8,128)S(1)}) custom-call(s32[2]{0:T(128)S(1)} %pad_add_fusion.my_col.spot.refs_0_, s32[1,3072]{1,0:T(1,128)S(1)} %reshape.35.owner, s32[1,3072]{1,0:T(1,128)S(1)} %reshape.36.node), custom_call_target="tpu_custom_call" | custom-call | flops 3145728 | bytes 3145728 | tf_op jit(solution)/shard_map/places/pallas_call | solution.py:511
  90.9 6.0 %step_3.1 = (f32[3,16,24,1024]{3,2,1,0:T(8,128)S(1)}, f32[3,16,24,1024]{3,2,1,0:T(8,128)S(1)}, f32[16,24,1024]{2,1,0:T(8,128)S(1)}, f32[2,24,1024]{2,1,0:T(8,128...) custom-call(s32[2]{0:T(128)S(1)} %pad_add_fusion.my_col.spot.refs_0_, ...), custom_call_target="tpu_custom_call", output_to_operand_aliasing={{0}: (1, {}), {1}: (2, {}), {2}: (15, {})} | custom-call | flops 39321600 | bytes 39321600 | tf_op jit(solution)/shard_map/step_3/pallas_call | solution.py:589
  96.9 5.1 %pack.1 = (f32[8,400,128]{2,1,0:T(8,128)}, f32[8,200,128]{2,1,0:T(8,128)}, f32[8,392,128]{2,1,0:T(8,128)}, f32[3,16,24,1024]{3,2,1,0:T(8,128)}, f32[6336,128]{1,0:T(8,128)S(1)}) custom-call(s32[3072]{0:T(1024)S(1)} %bitcast.9, f32[16,24,1024]{2,1,0:T(8,128)S(1)} %get-tuple-element.111.power, ...), custom_call_target="tpu_custom_call", output_to_operand_aliasing={{4}: (2, {})} | custom-call | flops 393216 | bytes 14155776 | tf_op jit(solution)/shard_map/pack/pallas_call | solution.py:608
  102.1 11.7 %all-to-all-start.1 = ((f32[8,392,128]{2,1,0:T(8,128)}), f32[8,392,128]{2,1,0:T(8,128)S(1)}, u32[]{:S(2)}, u32[]{:S(2)}) async-start(f32[8,392,128]{2,1,0:T(8,128)} %get-tuple-element.118), calls=%async_computation.1 | async-start | bytes 3211264 | tf_op jit(solution)/shard_map/all_to_all | solution.py:627
  113.8 4.2 %collective-permute-start.24 = (f32[8,200,128]{2,1,0:T(8,128)}, f32[8,200,128]{2,1,0:T(8,128)S(1)}, u32[]{:S(2)}, u32[]{:S(2)}) collective-permute-start(f32[8,200,128]{2,1,0:T(8,128)} %get-tuple-element.116), channel_id=1, source_target_pairs={{0,8},{8,0},{16,24},{24,16},{1,9},{9,1},{17,25},{25,17},{2,10},{10... | collective-permute-start | bytes 2457608 | tf_op jit(solution)/shard_map/ppermute | solution.py:630
  118.0 19.1 %collective-permute-done.24.pair = f32[8,200,128]{2,1,0:T(8,128)S(1)} collective-permute-done((f32[8,200,128]{2,1,0:T(8,128)}, f32[8,200,128]{2,1,0:T(8,128)S(1)}, u32[]{:S(2)}, u32[]{:S(2)}) %collective-permute-start.24) | collective-permute-done | bytes 819232 | tf_op jit(solution)/shard_map/ppermute | solution.py:630
  138.1 4.0 %all-to-all-start = ((f32[8,400,128]{2,1,0:T(8,128)}), f32[8,400,128]{2,1,0:T(8,128)S(1)}, u32[]{:S(2)}, u32[]{:S(2)}) async-start(f32[8,400,128]{2,1,0:T(8,128)} %merge.1), calls=%async_computation | async-start | bytes 3276800 | tf_op jit(solution)/shard_map/all_to_all | solution.py:627
  142.1 2.4 %collect_other.1 = (f32[384,128]{1,0:T(8,128)}, f32[384,128]{1,0:T(8,128)}) custom-call(f32[8,392,128]{2,1,0:T(8,128)S(1)} %all-to-all-done.1.blocks), custom_call_target="tpu_custom_call" | custom-call | flops 393216 | bytes 393216 | tf_op jit(solution)/shard_map/collect_other/pallas_call | solution.py:511
  144.6 2.1 %collective-permute-start.25 = (f32[384,128]{1,0:T(8,128)}, f32[384,128]{1,0:T(8,128)S(1)}, u32[]{:S(2)}, u32[]{:S(2)}) collective-permute-start(f32[384,128]{1,0:T(8,128)} %get-tuple-element.119), channel_id=1, source_target_pairs={{0,16},{8,24},{16,0},{24,8},{1,17},{9,25},{17,1},{25,9},{2,18},{10... | collective-permute-start | bytes 589832 | tf_op jit(solution)/shard_map/ppermute | solution.py:630
  146.7 2.0 %collective-permute-start.26 = (f32[384,128]{1,0:T(8,128)}, f32[384,128]{1,0:T(8,128)S(1)}, u32[]{:S(2)}, u32[]{:S(2)}) collective-permute-start(f32[384,128]{1,0:T(8,128)} %get-tuple-element.120), channel_id=1, source_target_pairs={{0,24},{8,16},{16,8},{24,0},{1,25},{9,17},{17,9},{25,1},{2,26},{10... | collective-permute-start | bytes 589832 | tf_op jit(solution)/shard_map/ppermute | solution.py:630
  148.7 15.2 %all-to-all-done.blocks = f32[8,400,128]{2,1,0:T(8,128)S(1)} async-done(((f32[8,400,128]{2,1,0:T(8,128)}), f32[8,400,128]{2,1,0:T(8,128)S(1)}, u32[]{:S(2)}, u32[]{:S(2)}) %all-to-all-start) | async-done | bytes 1638432 | tf_op jit(solution)/shard_map/all_to_all | solution.py:627
  (54 shorter events, 16.5 us)
Async XLA Ops:
  4.7 14.3 %collective-permute-start = (f32[5,24,1024]{2,1,0:T(8,128)S(1)}, f32[5,24,1024]{2,1,0:T(8,128)S(1)}, u32[]{:S(2)}, u32[]{:S(2)}) collective-permute-start(f32[5,24,1024]{2,1,0:T(8,128)S(1)} %get-tuple-element.69), channel_id=1, source_target_pairs={{0,8},{8,0},{1,9},{9,1},{2,10},{10,2},{3,11},{11,3},{4,12},{12,4},... | collective-permute-start | bytes 1474568 | tf_op jit(solution)/shard_map/ppermute | solution.py:488
  7.8 11.2 %collective-permute-start.1 = (f32[5,24,1024]{2,1,0:T(8,128)S(1)}, f32[5,24,1024]{2,1,0:T(8,128)S(1)}, u32[]{:S(2)}, u32[]{:S(2)}) collective-permute-start(f32[5,24,1024]{2,1,0:T(8,128)S(1)} %get-tuple-element.70), channel_id=1, source_target_pairs={{8,16},{16,8},{9,17},{17,9},{10,18},{18,10},{11,19},{19,11},{12,20... | collective-permute-start | bytes 1474568 | tf_op jit(solution)/shard_map/ppermute | solution.py:488
  14.1 2.1 %collective-permute-start.2 = (f32[5,16,1024]{2,1,0:T(8,128)S(1)}, f32[5,16,1024]{2,1,0:T(8,128)S(1)}, u32[]{:S(2)}, u32[]{:S(2)}) collective-permute-start(f32[5,16,1024]{2,1,0:T(8,128)S(1)} %get-tuple-element.71), channel_id=1, source_target_pairs={{0,1},{1,0},{2,3},{3,2},{4,5},{5,4},{6,7},{7,6},{8,9},{9,8},{10,11... | collective-permute-start | bytes 983048 | tf_op jit(solution)/shard_map/ppermute | solution.py:488
  14.2 2.1 %collective-permute-start.3 = (f32[5,16,1024]{2,1,0:T(8,128)S(1)}, f32[5,16,1024]{2,1,0:T(8,128)S(1)}, u32[]{:S(2)}, u32[]{:S(2)}) collective-permute-start(f32[5,16,1024]{2,1,0:T(8,128)S(1)} %get-tuple-element.72), channel_id=1, source_target_pairs={{1,2},{2,1},{3,4},{4,3},{5,6},{6,5},{9,10},{10,9},{11,12},{12,11},... | collective-permute-start | bytes 983048 | tf_op jit(solution)/shard_map/ppermute | solution.py:488
  14.8 0.7 collective-permute-start.4
  15.5 0.7 collective-permute-start.5
  24.5 16.5 %collective-permute-start.6 = (f32[3,24,1024]{2,1,0:T(8,128)S(1)}, f32[3,24,1024]{2,1,0:T(8,128)S(1)}, u32[]{:S(2)}, u32[]{:S(2)}) collective-permute-start(f32[3,24,1024]{2,1,0:T(8,128)S(1)} %get-tuple-element.78), channel_id=1, source_target_pairs={{0,8},{8,0},{1,9},{9,1},{2,10},{10,2},{3,11},{11,3},{4,12},{12,4},... | collective-permute-start | bytes 884744 | tf_op jit(solution)/shard_map/ppermute | solution.py:488
  30.4 10.6 %collective-permute-start.7 = (f32[3,24,1024]{2,1,0:T(8,128)S(1)}, f32[3,24,1024]{2,1,0:T(8,128)S(1)}, u32[]{:S(2)}, u32[]{:S(2)}) collective-permute-start(f32[3,24,1024]{2,1,0:T(8,128)S(1)} %get-tuple-element.79), channel_id=1, source_target_pairs={{8,16},{16,8},{9,17},{17,9},{10,18},{18,10},{11,19},{19,11},{12,20... | collective-permute-start | bytes 884744 | tf_op jit(solution)/shard_map/ppermute | solution.py:488
  31.1 9.9 %collective-permute-start.8 = (f32[3,16,1024]{2,1,0:T(8,128)S(1)}, f32[3,16,1024]{2,1,0:T(8,128)S(1)}, u32[]{:S(2)}, u32[]{:S(2)}) collective-permute-start(f32[3,16,1024]{2,1,0:T(8,128)S(1)} %get-tuple-element.80), channel_id=1, source_target_pairs={{0,1},{1,0},{2,3},{3,2},{4,5},{5,4},{6,7},{7,6},{8,9},{9,8},{10,11... | collective-permute-start | bytes 589832 | tf_op jit(solution)/shard_map/ppermute | solution.py:488
  38.9 2.0 %collective-permute-start.9 = (f32[3,16,1024]{2,1,0:T(8,128)S(1)}, f32[3,16,1024]{2,1,0:T(8,128)S(1)}, u32[]{:S(2)}, u32[]{:S(2)}) collective-permute-start(f32[3,16,1024]{2,1,0:T(8,128)S(1)} %get-tuple-element.81), channel_id=1, source_target_pairs={{1,2},{2,1},{3,4},{4,3},{5,6},{6,5},{9,10},{10,9},{11,12},{12,11},... | collective-permute-start | bytes 589832 | tf_op jit(solution)/shard_map/ppermute | solution.py:488
  46.6 17.2 %collective-permute-start.12 = (f32[3,24,1024]{2,1,0:T(8,128)S(1)}, f32[3,24,1024]{2,1,0:T(8,128)S(1)}, u32[]{:S(2)}, u32[]{:S(2)}) collective-permute-start(f32[3,24,1024]{2,1,0:T(8,128)S(1)} %get-tuple-element.90), channel_id=1, source_target_pairs={{0,8},{8,0},{1,9},{9,1},{2,10},{10,2},{3,11},{11,3},{4,12},{12,4},... | collective-permute-start | bytes 884744 | tf_op jit(solution)/shard_map/ppermute | solution.py:488
  54.5 9.3 %collective-permute-start.13 = (f32[3,24,1024]{2,1,0:T(8,128)S(1)}, f32[3,24,1024]{2,1,0:T(8,128)S(1)}, u32[]{:S(2)}, u32[]{:S(2)}) collective-permute-start(f32[3,24,1024]{2,1,0:T(8,128)S(1)} %get-tuple-element.91), channel_id=1, source_target_pairs={{8,16},{16,8},{9,17},{17,9},{10,18},{18,10},{11,19},{19,11},{12,20... | collective-permute-start | bytes 884744 | tf_op jit(solution)/shard_map/ppermute | solution.py:488
  55.2 8.6 %collective-permute-start.14 = (f32[3,16,1024]{2,1,0:T(8,128)S(1)}, f32[3,16,1024]{2,1,0:T(8,128)S(1)}, u32[]{:S(2)}, u32[]{:S(2)}) collective-permute-start(f32[3,16,1024]{2,1,0:T(8,128)S(1)} %get-tuple-element.92), channel_id=1, source_target_pairs={{0,1},{1,0},{2,3},{3,2},{4,5},{5,4},{6,7},{7,6},{8,9},{9,8},{10,11... | collective-permute-start | bytes 589832 | tf_op jit(solution)/shard_map/ppermute | solution.py:488
  61.7 2.0 %collective-permute-start.15 = (f32[3,16,1024]{2,1,0:T(8,128)S(1)}, f32[3,16,1024]{2,1,0:T(8,128)S(1)}, u32[]{:S(2)}, u32[]{:S(2)}) collective-permute-start(f32[3,16,1024]{2,1,0:T(8,128)S(1)} %get-tuple-element.93), channel_id=1, source_target_pairs={{1,2},{2,1},{3,4},{4,3},{5,6},{6,5},{9,10},{10,9},{11,12},{12,11},... | collective-permute-start | bytes 589832 | tf_op jit(solution)/shard_map/ppermute | solution.py:488
  69.4 21.5 %collective-permute-start.18 = (f32[3,24,1024]{2,1,0:T(8,128)S(1)}, f32[3,24,1024]{2,1,0:T(8,128)S(1)}, u32[]{:S(2)}, u32[]{:S(2)}) collective-permute-start(f32[3,24,1024]{2,1,0:T(8,128)S(1)} %get-tuple-element.102), channel_id=1, source_target_pairs={{0,8},{8,0},{1,9},{9,1},{2,10},{10,2},{3,11},{11,3},{4,12},{12,4},... | collective-permute-start | bytes 884744 | tf_op jit(solution)/shard_map/ppermute | solution.py:488
  77.3 13.6 %collective-permute-start.19 = (f32[3,24,1024]{2,1,0:T(8,128)S(1)}, f32[3,24,1024]{2,1,0:T(8,128)S(1)}, u32[]{:S(2)}, u32[]{:S(2)}) collective-permute-start(f32[3,24,1024]{2,1,0:T(8,128)S(1)} %get-tuple-element.103), channel_id=1, source_target_pairs={{8,16},{16,8},{9,17},{17,9},{10,18},{18,10},{11,19},{19,11},{12,20... | collective-permute-start | bytes 884744 | tf_op jit(solution)/shard_map/ppermute | solution.py:488
  77.9 12.9 %collective-permute-start.20 = (f32[3,16,1024]{2,1,0:T(8,128)S(1)}, f32[3,16,1024]{2,1,0:T(8,128)S(1)}, u32[]{:S(2)}, u32[]{:S(2)}) collective-permute-start(f32[3,16,1024]{2,1,0:T(8,128)S(1)} %get-tuple-element.104), channel_id=1, source_target_pairs={{0,1},{1,0},{2,3},{3,2},{4,5},{5,4},{6,7},{7,6},{8,9},{9,8},{10,11... | collective-permute-start | bytes 589832 | tf_op jit(solution)/shard_map/ppermute | solution.py:488
  86.1 4.8 %collective-permute-start.21 = (f32[3,16,1024]{2,1,0:T(8,128)S(1)}, f32[3,16,1024]{2,1,0:T(8,128)S(1)}, u32[]{:S(2)}, u32[]{:S(2)}) collective-permute-start(f32[3,16,1024]{2,1,0:T(8,128)S(1)} %get-tuple-element.105), channel_id=1, source_target_pairs={{1,2},{2,1},{3,4},{4,3},{5,6},{6,5},{9,10},{10,9},{11,12},{12,11},... | collective-permute-start | bytes 589832 | tf_op jit(solution)/shard_map/ppermute | solution.py:488
  87.5 3.4 %collective-permute-start.23 = (f32[1,1024]{1,0:T(1,128)S(1)}, f32[1,1024]{1,0:T(1,128)S(1)}, u32[]{:S(2)}, u32[]{:S(2)}) collective-permute-start(f32[1,1024]{1,0:T(1,128)S(1)} %get-tuple-element.107), channel_id=1, source_target_pairs={{9,16},{16,9},{10,17},{17,10},{11,18},{18,11},{12,19},{19,12},{13,... | collective-permute-start | bytes 12296 | tf_op jit(solution)/shard_map/ppermute | solution.py:488
  102.1 36.1 %all-to-all-start.1 = ((f32[8,392,128]{2,1,0:T(8,128)}), f32[8,392,128]{2,1,0:T(8,128)S(1)}, u32[]{:S(2)}, u32[]{:S(2)}) async-start(f32[8,392,128]{2,1,0:T(8,128)} %get-tuple-element.118), calls=%async_computation.1 | async-start | bytes 3211264 | tf_op jit(solution)/shard_map/all_to_all | solution.py:627
  113.8 23.4 %collective-permute-start.24 = (f32[8,200,128]{2,1,0:T(8,128)}, f32[8,200,128]{2,1,0:T(8,128)S(1)}, u32[]{:S(2)}, u32[]{:S(2)}) collective-permute-start(f32[8,200,128]{2,1,0:T(8,128)} %get-tuple-element.116), channel_id=1, source_target_pairs={{0,8},{8,0},{16,24},{24,16},{1,9},{9,1},{17,25},{25,17},{2,10},{10... | collective-permute-start | bytes 2457608 | tf_op jit(solution)/shard_map/ppermute | solution.py:630
  138.1 25.7 %all-to-all-start = ((f32[8,400,128]{2,1,0:T(8,128)}), f32[8,400,128]{2,1,0:T(8,128)S(1)}, u32[]{:S(2)}, u32[]{:S(2)}) async-start(f32[8,400,128]{2,1,0:T(8,128)} %merge.1), calls=%async_computation | async-start | bytes 3276800 | tf_op jit(solution)/shard_map/all_to_all | solution.py:627
  144.6 21.0 %collective-permute-start.25 = (f32[384,128]{1,0:T(8,128)}, f32[384,128]{1,0:T(8,128)S(1)}, u32[]{:S(2)}, u32[]{:S(2)}) collective-permute-start(f32[384,128]{1,0:T(8,128)} %get-tuple-element.119), channel_id=1, source_target_pairs={{0,16},{8,24},{16,0},{24,8},{1,17},{9,25},{17,1},{25,9},{2,18},{10... | collective-permute-start | bytes 589832 | tf_op jit(solution)/shard_map/ppermute | solution.py:630
  146.7 18.9 %collective-permute-start.26 = (f32[384,128]{1,0:T(8,128)}, f32[384,128]{1,0:T(8,128)S(1)}, u32[]{:S(2)}, u32[]{:S(2)}) collective-permute-start(f32[384,128]{1,0:T(8,128)} %get-tuple-element.120), channel_id=1, source_target_pairs={{0,24},{8,16},{16,8},{24,0},{1,25},{9,17},{17,9},{25,1},{2,26},{10... | collective-permute-start | bytes 589832 | tf_op jit(solution)/shard_map/ppermute | solution.py:630
  (6 other events, 30.8 us)

commit v9 on v6

--- a/solution.py
+++ b/solution.py
@@ -62,17 +62,20 @@
     return jnp.where(place > 0, pltpu.roll(f, 1, 0), jnp.broadcast_to(row, f.shape))
 
 
-def edge_kernel(e, to_col, to_hgt, low, sems):
+def edge_kernel(e, to_col, sem):
+    copy = pltpu.make_async_copy(e.at[pl.ds(1, 2), 0], to_col, sem)
+    copy.start()
+    copy.wait()
+
+
+def low_kernel(e, order, to_hgt, low, sem):
     nx = e.shape[1]
-    col_copy = pltpu.make_async_copy(e.at[pl.ds(1, 2), 0], to_col, sems.at[0])
-    low_copy = pltpu.make_async_copy(e.at[pl.ds(0, 2), :, pl.ds(0, ROWS)], low, sems.at[1])
-    low_copy.start()
-    col_copy.start()
-    low_copy.wait()
+    copy = pltpu.make_async_copy(e.at[pl.ds(0, 2), :, pl.ds(0, ROWS)], low, sem)
+    copy.start()
+    copy.wait()
     for x in range(nx):
         for comp in range(2):
             to_hgt[comp, x : x + 1, :] = low[comp, x, 0:1, :]
-    col_copy.wait()
 
 
 def load_kernel(
@@ -86,12 +89,14 @@
         here = pl.ds(part * size, size)
         copies.append(pltpu.make_async_copy(temp_far.at[here], temp.at[here], sems.at[0, part]))
         copies.append(pltpu.make_async_copy(tags_far.at[here], tags.at[here], sems.at[1, part]))
-    e_copy = pltpu.make_async_copy(e_far, e, sems.at[2, 0])
-    h_copy = pltpu.make_async_copy(h_far, h, sems.at[2, 1])
-    for copy in copies:
+    fields = []
+    for comp in range(3):
+        for part in range(parts):
+            here = pl.ds(part * size, size)
+            fields.append(pltpu.make_async_copy(e_far.at[comp, here], e.at[comp, here], sems.at[2 + comp, part]))
+            fields.append(pltpu.make_async_copy(h_far.at[comp, here], h.at[comp, here], sems.at[5 + comp, part]))
+    for copy in copies + fields:
         copy.start()
-    e_copy.start()
-    h_copy.start()
 
     def plane(x, carry):
         for z in range(0, nz, ROWS):
@@ -118,8 +123,8 @@
         copies[2 * part].wait()
         copies[2 * part + 1].wait()
         lax.fori_loop(part * size, (part + 1) * size, plane, 0)
-    e_copy.wait()
-    h_copy.wait()
+    for copy in fields:
+        copy.wait()
 
     def rows(x, carry):
         for comp in range(3):
@@ -482,10 +487,11 @@
     two_rows = vmem(2, nx, ny)
     three_rows = vmem(3, nx, ny)
 
-    to_col, e_low = kernel(
-        edge_kernel, (planes, two_rows), [FAR], [e_start], "edge", 4, scratch=[vmem(2, nx, ROWS, ny), sem((2,))]
-    )
+    to_col = kernel(edge_kernel, planes, [FAR], [e_start], "edge", 4, scratch=[sem])
     col = shifted(to_col, -1, 0)
+    e_low = kernel(
+        low_kernel, two_rows, [FAR, WHOLE], [e_start, to_col], "low", 60, scratch=[vmem(2, nx, ROWS, ny), sem]
+    )
     hgt = shifted(e_low, 0, -1)
     ca, cb, sigma, e, h, media_rows, e_rows, h_high = kernel(
         load_kernel,
@@ -494,7 +500,7 @@
         [far(cell_temp), far(region_tags), e_start, h_start, owners + nodes + my_col],
         "load",
         60,
-        scratch=[vmem(nx, nz, ny), pltpu.VMEM((nx, nz, ny), jnp.int32), sem((3, 4))],
+        scratch=[vmem(nx, nz, ny), pltpu.VMEM((nx, nz, ny), jnp.int32), sem((8, 4))],
     )
     begins, heights = starts_of(n_col, n_hgt, cap)
     place, flat = kernel(

time: 141 us -> 142 us (level)
  waiting for transfers between devices: 56.1 us -> 53.7 us
  starting transfers between devices: 45.5 us -> 47.6 us
    ppermute x16, waiting for transfers between devices: 20.2 us -> 17.7 us  [shifted(): return lax.ppermute(block, ('col', 'hgt'), route)]
    ppermute x16, starting transfers between devices: 33.5 us -> 35.6 us  [shifted(): return lax.ppermute(block, ('col', 'hgt'), route)]
    pallas_call x20 -> x21, Pallas kernels: 28.7 us -> 29.7 us  [kernel(): pl.pallas_call(body, out_shape=outs, in_specs=ins, out_specs=jax.tree.map...]
  transfers between devices with their start and end apart: 21 -> 21, of which waited for: 11 -> 12; matrix products, arithmetic and copies ran while one was open for 0% -> 0% of each run, Pallas kernels for 19% -> 20%
where the time goes in v9:
time: 142 us; the launch traced here: 141 us
  waiting for transfers between devices  53.7 us (38%)
  starting transfers between devices  47.6 us (34%)
  Pallas kernels  38.1 us (27%)
    ppermute x16, starting transfers between devices, shifted(): return lax.ppermute(block, ('col', 'hgt'), route)  35.6 us
    pallas_call x21, Pallas kernels, kernel(): pl.pallas_call(body, out_shape=outs, in_specs=ins, out_specs=jax.tree.map...  29.7 us
    ppermute x3, waiting for transfers between devices, across(): return lax.ppermute(x, 'col', [(c, c ^ turn) for c in range(n_col)])  20 us
    ppermute x16, waiting for transfers between devices, shifted(): return lax.ppermute(block, ('col', 'hgt'), route)  17.7 us
    all_to_all x2, waiting for transfers between devices, swap(): return lax.all_to_all(x, axis, split_axis=0, concat_axis=0, tiled=True)  16.1 us
    all_to_all x2, starting transfers between devices, swap(): return lax.all_to_all(x, axis, split_axis=0, concat_axis=0, tiled=True)  7.84 us
    pallas_call x1, Pallas kernels, per_device(): pl.pallas_call(functools.partial(pack_kernel, heights), out_shape=(pltpu....  5.13 us
    ppermute x3, starting transfers between devices, across(): return lax.ppermute(x, 'col', [(c, c ^ turn) for c in range(n_col)])  4.2 us
  transfers between devices with their start and end apart: 21, of which 12 were waited for; matrix products, arithmetic and copies ran while one was open for 0% of the time, Pallas kernels for 20%

profile of v9, /device:TPU:0, one launch (start us, length us, event | category | flops | bytes accessed | tf_op | source)
XLA Modules:
  0.0 141.0 jit_solution(11836039270501103578)
XLA Ops:
  6.1 5.0 %load.1 = (f32[16,24,1024]{2,1,0:T(8,128)S(1)}, f32[16,24,1024]{2,1,0:T(8,128)S(1)}, f32[16,24,1024]{2,1,0:T(8,128)S(1)}, f32[3,16,24,1024]{3,2,1,0:T(8,128)S(1)...) custom-call(f32[16,24,1024]{2,1,0:T(8,128)} %temp_far.1, ...), custom_call_target="tpu_custom_call" | custom-call | flops 23592960 | bytes 23592960 | tf_op jit(solution)/shard_map/load/pallas_call | solution.py:467
  11.6 5.2 %collective-permute-start.3 = (f32[2,24,1024]{2,1,0:T(8,128)S(1)}, f32[2,24,1024]{2,1,0:T(8,128)S(1)}, u32[]{:S(2)}, u32[]{:S(2)}) collective-permute-start(f32[2,24,1024]{2,1,0:T(8,128)S(1)} %get-tuple-element.72), channel_id=1, source_target_pairs={{0,8},{1,9},{2,10},{3,11},{4,12},{5,13},{6,14},{7,15},{8,16},{9,17... | collective-permute-start | bytes 589832 | tf_op jit(solution)/shard_map/ppermute | solution.py:444
  16.8 2.8 %collective-permute-start.2 = (f32[2,16,1024]{2,1,0:T(8,128)S(1)}, f32[2,16,1024]{2,1,0:T(8,128)S(1)}, u32[]{:S(2)}, u32[]{:S(2)}) collective-permute-start(f32[2,16,1024]{2,1,0:T(8,128)S(1)} %get-tuple-element.71.rows_old), channel_id=1, source_target_pairs={{0,1},{1,2},{2,3},{3,4},{4,5},{5,6},{6,7},{8,9},{9,10},{10,11},{11... | collective-permute-start | bytes 393224 | tf_op jit(solution)/shard_map/ppermute | solution.py:444
  19.6 1.9 %h_rest_0.1 = (f32[3,16,24,1024]{3,2,1,0:T(8,128)S(1)}, f32[3,16,1024]{2,1,0:T(8,128)S(1)}) custom-call(f32[3,16,24,1024]{3,2,1,0:T(8,128)S(1)} %get-tuple-element.62.e.refs_0_, f32[2,16,1024]{2,1,0:T(8,128)S(1)} %collective-permute-done.hgt, f32[3,16,24,1024]{3,2,1,0:T(8,128)S(1)} %get-tuple-element.66.h_old), custom_call_target="tpu_custom_call", output_to_operand_aliasing={{0}: (2, {})} | custom-call | flops 15728640 | bytes 15728640 | tf_op jit(solution)/shard_map/h_rest_0/pallas_call | solution.py:467
  24.7 2.2 %e_rest_0.1 = (f32[3,16,24,1024]{3,2,1,0:T(8,128)S(1)}, f32[16,24,1024]{2,1,0:T(8,128)S(1)}, f32[3,16,1024]{2,1,0:T(8,128)S(1)}) custom-call(f32[3,16,24,1024]{3,2,1,0:T(8,128)S(1)} %get-tuple-element.67.h.h_old, f32[16,24,1024]{2,1,0:T(8,128)S(1)} %get-tuple-element.68.ca, ...), custom_call_target="tpu_custom_call", output_to_operand_aliasing={{0}: (5, {}), {1}: (6, {})} | custom-call | flops 17694720 | bytes 17694720 | tf_op jit(solution)/shard_map/e_rest_0/pallas_call | solution.py:467
  27.6 4.6 %collective-permute-done.5.col = f32[2,24,1024]{2,1,0:T(8,128)S(1)} collective-permute-done((f32[2,24,1024]{2,1,0:T(8,128)S(1)}, f32[2,24,1024]{2,1,0:T(8,128)S(1)}, u32[]{:S(2)}, u32[]{:S(2)}) %collective-permute-start.5) | collective-permute-done | bytes 196640 | tf_op jit(solution)/shard_map/ppermute | solution.py:444
  32.4 3.5 %collective-permute-start.7 = (f32[2,24,1024]{2,1,0:T(8,128)S(1)}, f32[2,24,1024]{2,1,0:T(8,128)S(1)}, u32[]{:S(2)}, u32[]{:S(2)}) collective-permute-start(f32[2,24,1024]{2,1,0:T(8,128)S(1)} %get-tuple-element.84), channel_id=1, source_target_pairs={{0,8},{1,9},{2,10},{3,11},{4,12},{5,13},{6,14},{7,15},{8,16},{9,17... | collective-permute-start | bytes 589832 | tf_op jit(solution)/shard_map/ppermute | solution.py:444
  35.9 2.3 %collective-permute-start.6 = (f32[2,16,1024]{2,1,0:T(8,128)S(1)}, f32[2,16,1024]{2,1,0:T(8,128)S(1)}, u32[]{:S(2)}, u32[]{:S(2)}) collective-permute-start(f32[2,16,1024]{2,1,0:T(8,128)S(1)} %get-tuple-element.83.rows_old), channel_id=1, source_target_pairs={{0,1},{1,2},{2,3},{3,4},{4,5},{5,6},{6,7},{8,9},{9,10},{10,11},{11... | collective-permute-start | bytes 393224 | tf_op jit(solution)/shard_map/ppermute | solution.py:444
  43.6 2.3 %e_rest_1.1 = (f32[3,16,24,1024]{3,2,1,0:T(8,128)S(1)}, f32[16,24,1024]{2,1,0:T(8,128)S(1)}, f32[3,16,1024]{2,1,0:T(8,128)S(1)}) custom-call(f32[3,16,24,1024]{3,2,1,0:T(8,128)S(1)} %get-tuple-element.82.h.h_old, f32[16,24,1024]{2,1,0:T(8,128)S(1)} %get-tuple-element.68.ca, ...), custom_call_target="tpu_custom_call", output_to_operand_aliasing={{0}: (5, {}), {1}: (6, {})} | custom-call | flops 17694720 | bytes 17694720 | tf_op jit(solution)/shard_map/e_rest_1/pallas_call | solution.py:467
  46.2 4.7 %collective-permute-done.9.col = f32[2,24,1024]{2,1,0:T(8,128)S(1)} collective-permute-done((f32[2,24,1024]{2,1,0:T(8,128)S(1)}, f32[2,24,1024]{2,1,0:T(8,128)S(1)}, u32[]{:S(2)}, u32[]{:S(2)}) %collective-permute-start.9) | collective-permute-done | bytes 196640 | tf_op jit(solution)/shard_map/ppermute | solution.py:444
  51.0 3.5 %collective-permute-start.11 = (f32[2,24,1024]{2,1,0:T(8,128)S(1)}, f32[2,24,1024]{2,1,0:T(8,128)S(1)}, u32[]{:S(2)}, u32[]{:S(2)}) collective-permute-start(f32[2,24,1024]{2,1,0:T(8,128)S(1)} %get-tuple-element.96), channel_id=1, source_target_pairs={{0,8},{1,9},{2,10},{3,11},{4,12},{5,13},{6,14},{7,15},{8,16},{9,17... | collective-permute-start | bytes 589832 | tf_op jit(solution)/shard_map/ppermute | solution.py:444
  54.5 2.3 %collective-permute-start.10 = (f32[2,16,1024]{2,1,0:T(8,128)S(1)}, f32[2,16,1024]{2,1,0:T(8,128)S(1)}, u32[]{:S(2)}, u32[]{:S(2)}) collective-permute-start(f32[2,16,1024]{2,1,0:T(8,128)S(1)} %get-tuple-element.95.rows_old), channel_id=1, source_target_pairs={{0,1},{1,2},{2,3},{3,4},{4,5},{5,6},{6,7},{8,9},{9,10},{10,11},{11... | collective-permute-start | bytes 393224 | tf_op jit(solution)/shard_map/ppermute | solution.py:444
  62.2 2.3 %e_rest_2.1 = (f32[3,16,24,1024]{3,2,1,0:T(8,128)S(1)}, f32[16,24,1024]{2,1,0:T(8,128)S(1)}, f32[3,16,1024]{2,1,0:T(8,128)S(1)}) custom-call(f32[3,16,24,1024]{3,2,1,0:T(8,128)S(1)} %get-tuple-element.94.h.h_old, f32[16,24,1024]{2,1,0:T(8,128)S(1)} %get-tuple-element.68.ca, ...), custom_call_target="tpu_custom_call", output_to_operand_aliasing={{0}: (5, {}), {1}: (6, {})} | custom-call | flops 17694720 | bytes 17694720 | tf_op jit(solution)/shard_map/e_rest_2/pallas_call | solution.py:467
  65.0 4.7 %collective-permute-done.13.col = f32[2,24,1024]{2,1,0:T(8,128)S(1)} collective-permute-done((f32[2,24,1024]{2,1,0:T(8,128)S(1)}, f32[2,24,1024]{2,1,0:T(8,128)S(1)}, u32[]{:S(2)}, u32[]{:S(2)}) %collective-permute-start.13) | collective-permute-done | bytes 196640 | tf_op jit(solution)/shard_map/ppermute | solution.py:444
  69.8 3.2 %collective-permute-start.14 = (f32[2,24,1024]{2,1,0:T(8,128)S(1)}, f32[2,24,1024]{2,1,0:T(8,128)S(1)}, u32[]{:S(2)}, u32[]{:S(2)}) collective-permute-start(f32[2,24,1024]{2,1,0:T(8,128)S(1)} %get-tuple-element.106), channel_id=1, source_target_pairs={{0,8},{1,9},{2,10},{3,11},{4,12},{5,13},{6,14},{7,15},{8,16},{9,17... | collective-permute-start | bytes 589832 | tf_op jit(solution)/shard_map/ppermute | solution.py:444
  73.0 2.6 %collective-permute-start.15 = (f32[2,16,1024]{2,1,0:T(8,128)S(1)}, f32[2,16,1024]{2,1,0:T(8,128)S(1)}, u32[]{:S(2)}, u32[]{:S(2)}) collective-permute-start(f32[2,16,1024]{2,1,0:T(8,128)S(1)} %get-tuple-element.107), channel_id=1, source_target_pairs={{0,1},{1,2},{2,3},{3,4},{4,5},{5,6},{6,7},{8,9},{9,10},{10,11},{11... | collective-permute-start | bytes 393224 | tf_op jit(solution)/shard_map/ppermute | solution.py:444
  75.6 2.2 %places.1 = (s32[1,3072]{1,0:T(1,128)S(1)}, f32[6336,128]{1,0:T(8,128)S(1)}) custom-call(s32[1]{0:T(128)} %bitcast.my_col, s32[1,3072]{1,0:T(1,128)S(1)} %reshape.46.owner, s32[1,3072]{1,0:T(1,128)S(1)} %reshape.47.node), custom_call_target="tpu_custom_call" | custom-call | flops 3145728 | bytes 3145728 | tf_op jit(solution)/shard_map/places/pallas_call | solution.py:467
  79.7 2.3 %e_last.1 = (f32[3,16,24,1024]{3,2,1,0:T(8,128)S(1)}, f32[16,24,1024]{2,1,0:T(8,128)S(1)}, f32[3,16,24,1024]{3,2,1,0:T(8,128)}) custom-call(f32[3,16,24,1024]{3,2,1,0:T(8,128)S(1)} %h_rest_3.1.h, f32[16,24,1024]{2,1,0:T(8,128)S(1)} %get-tuple-element.68.ca, f32[16,24,1024]{2,1,0:T(8,128)S(1)} %get-tuple-element.69.cb, ...), custom_call_target="tpu_custom_call", output_to_operand_aliasing={{0}: (6, {}), {1}: (7, {})} | custom-call | flops 19660800 | bytes 19660800 | tf_op jit(solution)/shard_map/e_last/pallas_call | solution.py:534
  82.0 5.1 %pack.1 = (f32[8,400,128]{2,1,0:T(8,128)}, f32[8,200,128]{2,1,0:T(8,128)}, f32[8,392,128]{2,1,0:T(8,128)}, f32[3,16,24,1024]{3,2,1,0:T(8,128)}, f32[6336,128]{1,0:T(8,128)S(1)}) custom-call(s32[3072]{0:T(1024)S(1)} %bitcast.8, f32[16,24,1024]{2,1,0:T(8,128)S(1)} %get-tuple-element.109.power, ...), custom_call_target="tpu_custom_call", output_to_operand_aliasing={{4}: (2, {})} | custom-call | flops 393216 | bytes 14155776 | tf_op jit(solution)/shard_map/pack/pallas_call | solution.py:569
  87.1 4.0 %all-to-all-start.1 = ((f32[8,392,128]{2,1,0:T(8,128)}), f32[8,392,128]{2,1,0:T(8,128)S(1)}, u32[]{:S(2)}, u32[]{:S(2)}) async-start(f32[8,392,128]{2,1,0:T(8,128)} %get-tuple-element.116), calls=%async_computation.1 | async-start | bytes 3211264 | tf_op jit(solution)/shard_map/all_to_all | solution.py:588
  92.1 19.9 %collective-permute-done.16.pair = f32[8,200,128]{2,1,0:T(8,128)S(1)} collective-permute-done((f32[8,200,128]{2,1,0:T(8,128)}, f32[8,200,128]{2,1,0:T(8,128)S(1)}, u32[]{:S(2)}, u32[]{:S(2)}) %collective-permute-start.16) | collective-permute-done | bytes 819232 | tf_op jit(solution)/shard_map/ppermute | solution.py:591
  113.0 3.8 %all-to-all-start = ((f32[8,400,128]{2,1,0:T(8,128)}), f32[8,400,128]{2,1,0:T(8,128)S(1)}, u32[]{:S(2)}, u32[]{:S(2)}) async-start(f32[8,400,128]{2,1,0:T(8,128)} %merge.1), calls=%async_computation | async-start | bytes 3276800 | tf_op jit(solution)/shard_map/all_to_all | solution.py:588
  116.9 2.4 %collect_other.1 = (f32[384,128]{1,0:T(8,128)}, f32[384,128]{1,0:T(8,128)}) custom-call(f32[8,392,128]{2,1,0:T(8,128)S(1)} %all-to-all-done.1.blocks), custom_call_target="tpu_custom_call" | custom-call | flops 393216 | bytes 393216 | tf_op jit(solution)/shard_map/collect_other/pallas_call | solution.py:467
  122.5 16.1 %all-to-all-done.blocks = f32[8,400,128]{2,1,0:T(8,128)S(1)} async-done(((f32[8,400,128]{2,1,0:T(8,128)}), f32[8,400,128]{2,1,0:T(8,128)S(1)}, u32[]{:S(2)}, u32[]{:S(2)}) %all-to-all-start) | async-done | bytes 1638432 | tf_op jit(solution)/shard_map/all_to_all | solution.py:588
  (53 shorter events, 31.2 us)
Async XLA Ops:
  0.6 4.9 %copy-start.1 = (s32[1,1,16,24,8,1]{3,5,4,2,1,0:T(1,128)S(1)}, s32[1,1,16,24,8,1]{3,5,4,2,1,0:T(1,128)}, u32[]{:S(2)}) copy-start(s32[1,1,16,24,8,1]{3,5,4,2,1,0:T(1,128)} %param.11) | copy-start | bytes 36868
  0.6 5.1 %copy-start.2 = (s32[1,1,16,24,8]{3,4,2,1,0:T(8,128)S(1)}, s32[1,1,16,24,8]{3,4,2,1,0:T(8,128)}, u32[]{:S(2)}) copy-start(s32[1,1,16,24,8]{3,4,2,1,0:T(8,128)} %param.12) | copy-start | bytes 36868
  1.6 9.8 %collective-permute-start.1 = (f32[2,24,1024]{2,1,0:T(8,128)S(1)}, f32[2,24,1024]{2,1,0:T(8,128)S(1)}, u32[]{:S(2)}, u32[]{:S(2)}) collective-permute-start(f32[2,24,1024]{2,1,0:T(8,128)S(1)} %edge.1.order), channel_id=1, source_target_pairs={{8,0},{9,1},{10,2},{11,3},{12,4},{13,5},{14,6},{15,7},{16,8},{17,9... | collective-permute-start | bytes 589832 | tf_op jit(solution)/shard_map/ppermute | solution.py:444
  4.2 6.9 %collective-permute-start = (f32[2,16,1024]{2,1,0:T(8,128)S(1)}, f32[2,16,1024]{2,1,0:T(8,128)S(1)}, u32[]{:S(2)}, u32[]{:S(2)}) collective-permute-start(f32[2,16,1024]{2,1,0:T(8,128)S(1)} %low.1.rows_old), channel_id=1, source_target_pairs={{1,0},{2,1},{3,2},{4,3},{5,4},{6,5},{7,6},{9,8},{10,9},{11,10},{12... | collective-permute-start | bytes 393224 | tf_op jit(solution)/shard_map/ppermute | solution.py:444
  11.6 10.3 %collective-permute-start.3 = (f32[2,24,1024]{2,1,0:T(8,128)S(1)}, f32[2,24,1024]{2,1,0:T(8,128)S(1)}, u32[]{:S(2)}, u32[]{:S(2)}) collective-permute-start(f32[2,24,1024]{2,1,0:T(8,128)S(1)} %get-tuple-element.72), channel_id=1, source_target_pairs={{0,8},{1,9},{2,10},{3,11},{4,12},{5,13},{6,14},{7,15},{8,16},{9,17... | collective-permute-start | bytes 589832 | tf_op jit(solution)/shard_map/ppermute | solution.py:444
  16.8 4.7 %collective-permute-start.2 = (f32[2,16,1024]{2,1,0:T(8,128)S(1)}, f32[2,16,1024]{2,1,0:T(8,128)S(1)}, u32[]{:S(2)}, u32[]{:S(2)}) collective-permute-start(f32[2,16,1024]{2,1,0:T(8,128)S(1)} %get-tuple-element.71.rows_old), channel_id=1, source_target_pairs={{0,1},{1,2},{2,3},{3,4},{4,5},{5,6},{6,7},{8,9},{9,10},{10,11},{11... | collective-permute-start | bytes 393224 | tf_op jit(solution)/shard_map/ppermute | solution.py:444
  22.1 10.1 %collective-permute-start.5 = (f32[2,24,1024]{2,1,0:T(8,128)S(1)}, f32[2,24,1024]{2,1,0:T(8,128)S(1)}, u32[]{:S(2)}, u32[]{:S(2)}) collective-permute-start(f32[2,24,1024]{2,1,0:T(8,128)S(1)} %get-tuple-element.79), channel_id=1, source_target_pairs={{8,0},{9,1},{10,2},{11,3},{12,4},{13,5},{14,6},{15,7},{16,8},{17,9... | collective-permute-start | bytes 589832 | tf_op jit(solution)/shard_map/ppermute | solution.py:444
  23.4 4.2 %collective-permute-start.4 = (f32[2,16,1024]{2,1,0:T(8,128)S(1)}, f32[2,16,1024]{2,1,0:T(8,128)S(1)}, u32[]{:S(2)}, u32[]{:S(2)}) collective-permute-start(f32[2,16,1024]{2,1,0:T(8,128)S(1)} %get-tuple-element.78.rows_old), channel_id=1, source_target_pairs={{1,0},{2,1},{3,2},{4,3},{5,4},{6,5},{7,6},{9,8},{10,9},{11,10},{12... | collective-permute-start | bytes 393224 | tf_op jit(solution)/shard_map/ppermute | solution.py:444
  32.4 8.4 %collective-permute-start.7 = (f32[2,24,1024]{2,1,0:T(8,128)S(1)}, f32[2,24,1024]{2,1,0:T(8,128)S(1)}, u32[]{:S(2)}, u32[]{:S(2)}) collective-permute-start(f32[2,24,1024]{2,1,0:T(8,128)S(1)} %get-tuple-element.84), channel_id=1, source_target_pairs={{0,8},{1,9},{2,10},{3,11},{4,12},{5,13},{6,14},{7,15},{8,16},{9,17... | collective-permute-start | bytes 589832 | tf_op jit(solution)/shard_map/ppermute | solution.py:444
  35.9 4.2 %collective-permute-start.6 = (f32[2,16,1024]{2,1,0:T(8,128)S(1)}, f32[2,16,1024]{2,1,0:T(8,128)S(1)}, u32[]{:S(2)}, u32[]{:S(2)}) collective-permute-start(f32[2,16,1024]{2,1,0:T(8,128)S(1)} %get-tuple-element.83.rows_old), channel_id=1, source_target_pairs={{0,1},{1,2},{2,3},{3,4},{4,5},{5,6},{6,7},{8,9},{9,10},{10,11},{11... | collective-permute-start | bytes 393224 | tf_op jit(solution)/shard_map/ppermute | solution.py:444
  41.0 9.8 %collective-permute-start.9 = (f32[2,24,1024]{2,1,0:T(8,128)S(1)}, f32[2,24,1024]{2,1,0:T(8,128)S(1)}, u32[]{:S(2)}, u32[]{:S(2)}) collective-permute-start(f32[2,24,1024]{2,1,0:T(8,128)S(1)} %get-tuple-element.91), channel_id=1, source_target_pairs={{8,0},{9,1},{10,2},{11,3},{12,4},{13,5},{14,6},{15,7},{16,8},{17,9... | collective-permute-start | bytes 589832 | tf_op jit(solution)/shard_map/ppermute | solution.py:444
  42.3 3.9 %collective-permute-start.8 = (f32[2,16,1024]{2,1,0:T(8,128)S(1)}, f32[2,16,1024]{2,1,0:T(8,128)S(1)}, u32[]{:S(2)}, u32[]{:S(2)}) collective-permute-start(f32[2,16,1024]{2,1,0:T(8,128)S(1)} %get-tuple-element.90.rows_old), channel_id=1, source_target_pairs={{1,0},{2,1},{3,2},{4,3},{5,4},{6,5},{7,6},{9,8},{10,9},{11,10},{12... | collective-permute-start | bytes 393224 | tf_op jit(solution)/shard_map/ppermute | solution.py:444
  51.0 8.4 %collective-permute-start.11 = (f32[2,24,1024]{2,1,0:T(8,128)S(1)}, f32[2,24,1024]{2,1,0:T(8,128)S(1)}, u32[]{:S(2)}, u32[]{:S(2)}) collective-permute-start(f32[2,24,1024]{2,1,0:T(8,128)S(1)} %get-tuple-element.96), channel_id=1, source_target_pairs={{0,8},{1,9},{2,10},{3,11},{4,12},{5,13},{6,14},{7,15},{8,16},{9,17... | collective-permute-start | bytes 589832 | tf_op jit(solution)/shard_map/ppermute | solution.py:444
  54.5 4.2 %collective-permute-start.10 = (f32[2,16,1024]{2,1,0:T(8,128)S(1)}, f32[2,16,1024]{2,1,0:T(8,128)S(1)}, u32[]{:S(2)}, u32[]{:S(2)}) collective-permute-start(f32[2,16,1024]{2,1,0:T(8,128)S(1)} %get-tuple-element.95.rows_old), channel_id=1, source_target_pairs={{0,1},{1,2},{2,3},{3,4},{4,5},{5,6},{6,7},{8,9},{9,10},{10,11},{11... | collective-permute-start | bytes 393224 | tf_op jit(solution)/shard_map/ppermute | solution.py:444
  59.6 10.1 %collective-permute-start.13 = (f32[2,24,1024]{2,1,0:T(8,128)S(1)}, f32[2,24,1024]{2,1,0:T(8,128)S(1)}, u32[]{:S(2)}, u32[]{:S(2)}) collective-permute-start(f32[2,24,1024]{2,1,0:T(8,128)S(1)} %get-tuple-element.103), channel_id=1, source_target_pairs={{8,0},{9,1},{10,2},{11,3},{12,4},{13,5},{14,6},{15,7},{16,8},{17,9... | collective-permute-start | bytes 589832 | tf_op jit(solution)/shard_map/ppermute | solution.py:444
  60.9 4.1 %collective-permute-start.12 = (f32[2,16,1024]{2,1,0:T(8,128)S(1)}, f32[2,16,1024]{2,1,0:T(8,128)S(1)}, u32[]{:S(2)}, u32[]{:S(2)}) collective-permute-start(f32[2,16,1024]{2,1,0:T(8,128)S(1)} %get-tuple-element.102), channel_id=1, source_target_pairs={{1,0},{2,1},{3,2},{4,3},{5,4},{6,5},{7,6},{9,8},{10,9},{11,10},{12... | collective-permute-start | bytes 393224 | tf_op jit(solution)/shard_map/ppermute | solution.py:444
  69.8 9.8 %collective-permute-start.14 = (f32[2,24,1024]{2,1,0:T(8,128)S(1)}, f32[2,24,1024]{2,1,0:T(8,128)S(1)}, u32[]{:S(2)}, u32[]{:S(2)}) collective-permute-start(f32[2,24,1024]{2,1,0:T(8,128)S(1)} %get-tuple-element.106), channel_id=1, source_target_pairs={{0,8},{1,9},{2,10},{3,11},{4,12},{5,13},{6,14},{7,15},{8,16},{9,17... | collective-permute-start | bytes 589832 | tf_op jit(solution)/shard_map/ppermute | solution.py:444
  73.0 6.6 %collective-permute-start.15 = (f32[2,16,1024]{2,1,0:T(8,128)S(1)}, f32[2,16,1024]{2,1,0:T(8,128)S(1)}, u32[]{:S(2)}, u32[]{:S(2)}) collective-permute-start(f32[2,16,1024]{2,1,0:T(8,128)S(1)} %get-tuple-element.107), channel_id=1, source_target_pairs={{0,1},{1,2},{2,3},{3,4},{4,5},{5,6},{6,7},{8,9},{9,10},{10,11},{11... | collective-permute-start | bytes 393224 | tf_op jit(solution)/shard_map/ppermute | solution.py:444
  87.1 25.9 %all-to-all-start.1 = ((f32[8,392,128]{2,1,0:T(8,128)}), f32[8,392,128]{2,1,0:T(8,128)S(1)}, u32[]{:S(2)}, u32[]{:S(2)}) async-start(f32[8,392,128]{2,1,0:T(8,128)} %get-tuple-element.116), calls=%async_computation.1 | async-start | bytes 3211264 | tf_op jit(solution)/shard_map/all_to_all | solution.py:588
  91.1 20.9 %collective-permute-start.16 = (f32[8,200,128]{2,1,0:T(8,128)}, f32[8,200,128]{2,1,0:T(8,128)S(1)}, u32[]{:S(2)}, u32[]{:S(2)}) collective-permute-start(f32[8,200,128]{2,1,0:T(8,128)} %get-tuple-element.114), channel_id=1, source_target_pairs={{0,8},{8,0},{16,24},{24,16},{1,9},{9,1},{17,25},{25,17},{2,10},{10... | collective-permute-start | bytes 2457608 | tf_op jit(solution)/shard_map/ppermute | solution.py:591
  112.0 28.3 %copy-start = (f32[384,128]{1,0:T(8,128)S(1)}, f32[384,128]{1,0:T(8,128)}, u32[]{:S(2)}) copy-start(f32[384,128]{1,0:T(8,128)} %enthalpy.1) | copy-start | bytes 589828
  113.0 25.6 %all-to-all-start = ((f32[8,400,128]{2,1,0:T(8,128)}), f32[8,400,128]{2,1,0:T(8,128)S(1)}, u32[]{:S(2)}, u32[]{:S(2)}) async-start(f32[8,400,128]{2,1,0:T(8,128)} %merge.1), calls=%async_computation | async-start | bytes 3276800 | tf_op jit(solution)/shard_map/all_to_all | solution.py:588
  119.3 21.0 %collective-permute-start.17 = (f32[384,128]{1,0:T(8,128)}, f32[384,128]{1,0:T(8,128)S(1)}, u32[]{:S(2)}, u32[]{:S(2)}) collective-permute-start(f32[384,128]{1,0:T(8,128)} %get-tuple-element.117), channel_id=1, source_target_pairs={{0,16},{8,24},{16,0},{24,8},{1,17},{9,25},{17,1},{25,9},{2,18},{10... | collective-permute-start | bytes 589832 | tf_op jit(solution)/shard_map/ppermute | solution.py:591
  120.8 19.5 %collective-permute-start.18 = (f32[384,128]{1,0:T(8,128)}, f32[384,128]{1,0:T(8,128)S(1)}, u32[]{:S(2)}, u32[]{:S(2)}) collective-permute-start(f32[384,128]{1,0:T(8,128)} %get-tuple-element.118), channel_id=1, source_target_pairs={{0,24},{8,16},{16,8},{24,0},{1,25},{9,17},{17,9},{25,1},{2,26},{10... | collective-permute-start | bytes 589832 | tf_op jit(solution)/shard_map/ppermute | solution.py:591

commit v10 on v6

--- a/solution.py
+++ b/solution.py
@@ -251,18 +251,56 @@
     over(1, nx, plane)
 
 
-def e_last_kernel(first, h, ca, cb, sigma, col, hgt, e_old, power_old, e, power, h_out, sem):
-    nx, nz = e.shape[1:3]
-    copy = pltpu.make_async_copy(h, h_out, sem)
-    copy.start()
-
-    def plane(x):
+def e_last_kernel(
+    heights, place, h, ca, cb, sigma, col, hgt, e_old, power_old, flat_old, e, power, flat, h_out, e_out, *refs
+):
+    mine, pair, other, sems = refs
+    nx, nz, ny = power.shape
+    per_row = ny // PTS
+    h_copy = pltpu.make_async_copy(h, h_out, sems.at[0])
+    h_copy.start()
+
+    def e_copy(x):
+        return pltpu.make_async_copy(e.at[:, x], e_out.at[:, x], sems.at[1])
+
+    def scatter(x, z):
+        for row in range(z, z + ROWS):
+            for k in range(per_row):
+                spot = place[x * (nz * per_row) + row * per_row + k]
+                flat[pl.ds(spot, 1), :] = power[x, row : row + 1, k * PTS : (k + 1) * PTS]
+
+    for z in range(0, nz, ROWS):
+        e_tile(False, h, e, power, ca, cb, sigma, col, hgt, 0, z)
+
+    def plane(x, carry):
+        e_copy(x - 1).start()
         for z in range(0, nz, ROWS):
-            e_tile(first, h, e, power, ca, cb, sigma, col if isinstance(x, int) else None, hgt, x, z)
-
-    plane(0)
-    over(1, nx, plane)
-    copy.wait()
+            e_tile(False, h, e, power, ca, cb, sigma, None, hgt, x, z)
+            scatter(x - 1, z)
+        return carry
+
+    lax.fori_loop(1, nx, plane, 0)
+    e_copy(nx - 1).start()
+    for z in range(0, nz, ROWS):
+        scatter(nx - 1, z)
+    copies = []
+    first = 0
+    for out, rows in zip((mine, pair, other), heights):
+        for group in range(out.shape[0]):
+            target = out.at[group, pl.ds(0, rows)]
+            copies.append(pltpu.make_async_copy(flat.at[pl.ds(first, rows)], target, sems.at[2 + len(copies)]))
+            first += rows
+    for copy in copies:
+        copy.start()
+    for copy in copies:
+        copy.wait()
+    h_copy.wait()
+
+    def finish(x, carry):
+        e_copy(x).wait()
+        return carry
+
+    lax.fori_loop(0, nx, finish, 0)
 
 
 def places_kernel(n_col, n_hgt, cap, my_col, owner, node, place, flat):
@@ -343,34 +381,6 @@
     return [0, n_hgt * heights[0], n_hgt * (heights[0] + heights[1])], heights
 
 
-def pack_kernel(heights, place, power, flat_old, e, mine, pair, other, e_out, flat, sems):
-    nx, nz, ny = power.shape
-    e_copy = pltpu.make_async_copy(e, e_out, sems.at[0])
-    e_copy.start()
-    per_row = ny // PTS
-
-    def plane(x, carry):
-        for z in range(nz):
-            for k in range(per_row):
-                spot = place[x * (nz * per_row) + z * per_row + k]
-                flat[pl.ds(spot, 1), :] = power[x, z : z + 1, k * PTS : (k + 1) * PTS]
-        return carry
-
-    lax.fori_loop(0, nx, plane, 0)
-    copies = []
-    first = 0
-    for out, rows in zip((mine, pair, other), heights):
-        for group in range(out.shape[0]):
-            target = out.at[group, pl.ds(0, rows)]
-            copies.append(pltpu.make_async_copy(flat.at[pl.ds(first, rows)], target, sems.at[1 + len(copies)]))
-            first += rows
-    for copy in copies:
-        copy.start()
-    for copy in copies:
-        copy.wait()
-    e_copy.wait()
-
-
 def summed(blocks, first, cap, node_row, chosen, split, node_count):
     ids = lax.broadcasted_iota(jnp.int32, (node_count, LANES), 0).astype(F32)
     n_from, _, pts = blocks.shape
@@ -525,17 +535,27 @@
         h, *h_rows = kernel(h_rest_kernel, outs, [WHOLE] * 3, [e, e_hgt, h], f"h_rest_{step}", 40, {2: 0})
         media = [h, ca, cb, sigma]
         if last:
-            e, power, h_out = pl.pallas_call(
-                functools.partial(e_last_kernel, first),
-                out_shape=(field, whole, pltpu.HBM((3, nx, nz, ny), F32)),
-                in_specs=[WHOLE] * 8,
-                out_specs=(WHOLE, WHOLE, FAR),
-                input_output_aliases={6: 0, 7: 1},
-                scratch_shapes=[sem],
+            flat_rows = n_hgt * sum(heights)
+            _, _, _, h_out, e_out, mine, pair, other = pl.pallas_call(
+                functools.partial(e_last_kernel, heights),
+                out_shape=(
+                    field,
+                    whole,
+                    vmem(flat_rows, PTS),
+                    pltpu.HBM((3, nx, nz, ny), F32),
+                    pltpu.HBM((3, nx, nz, ny), F32),
+                    pltpu.HBM((n_hgt, 2 * heights[0], PTS), F32),
+                    pltpu.HBM((n_hgt, heights[1], PTS), F32),
+                    pltpu.HBM((n_hgt, heights[2], PTS), F32),
+                ),
+                in_specs=[SCALARS] + [WHOLE] * 9,
+                out_specs=(WHOLE,) * 3 + (FAR,) * 5,
+                input_output_aliases={7: 0, 8: 1, 9: 2},
+                scratch_shapes=[sem((2 + 3 * n_hgt,))],
                 compiler_params=params(VMEM_MIB),
                 cost_estimate=cost(cells * 50, cells * 50),
                 name="e_last",
-            )(*media, col, hgt, e, power)
+            )(place.reshape(count), *media, col, hgt, e, power, flat)
             break
         args = media + [col, hgt, media_rows, *h_rows, e_low, e] + ([] if first else [power])
         e, power, to_col, e_low = kernel(
@@ -560,24 +580,6 @@
             {5: 0, 6: 1},
         )
 
-    mine, pair, other, e_out, _ = pl.pallas_call(
-        functools.partial(pack_kernel, heights),
-        out_shape=(
-            pltpu.HBM((n_hgt, 2 * heights[0], PTS), F32),
-            pltpu.HBM((n_hgt, heights[1], PTS), F32),
-            pltpu.HBM((n_hgt, heights[2], PTS), F32),
-            pltpu.HBM((3, nx, nz, ny), F32),
-            vmem(n_hgt * sum(heights), PTS),
-        ),
-        in_specs=[SCALARS] + [WHOLE] * 3,
-        out_specs=(FAR,) * 4 + (WHOLE,),
-        input_output_aliases={2: 4},
-        scratch_shapes=[sem((1 + 3 * n_hgt,))],
-        compiler_params=params(VMEM_MIB),
-        cost_estimate=cost(cells, cells * 36),
-        name="pack",
-    )(place.reshape(count), power, flat, e)
-
     def swap(x, axis):
         return lax.all_to_all(x, axis, split_axis=0, concat_axis=0, tiled=True)
 

time: 141 us -> 142 us (level)
    pallas_call x2 -> x1, Pallas kernels: 7.45 us -> 8.23 us  [per_device(): pl.pallas_call(functools.partial(e_last_kernel, heights), out_shape=(fiel...]
where the time goes in v10:
time: 142 us; the launch traced here: 141 us
  waiting for transfers between devices  56.1 us (40%)
  starting transfers between devices  45.5 us (32%)
  Pallas kernels  37.9 us (27%)
    ppermute x16, starting transfers between devices, shifted(): return lax.ppermute(block, ('col', 'hgt'), route)  33.5 us
    pallas_call x20, Pallas kernels, kernel(): pl.pallas_call(body, out_shape=outs, in_specs=ins, out_specs=jax.tree.map...  28.7 us
    ppermute x16, waiting for transfers between devices, shifted(): return lax.ppermute(block, ('col', 'hgt'), route)  20.2 us
    ppermute x3, waiting for transfers between devices, across(): return lax.ppermute(x, 'col', [(c, c ^ turn) for c in range(n_col)])  19.9 us
    all_to_all x2, waiting for transfers between devices, swap(): return lax.all_to_all(x, axis, split_axis=0, concat_axis=0, tiled=True)  16 us
    pallas_call x1, Pallas kernels, per_device(): pl.pallas_call(functools.partial(e_last_kernel, heights), out_shape=(fiel...  8.23 us
    all_to_all x2, starting transfers between devices, swap(): return lax.all_to_all(x, axis, split_axis=0, concat_axis=0, tiled=True)  7.73 us
    ppermute x3, starting transfers between devices, across(): return lax.ppermute(x, 'col', [(c, c ^ turn) for c in range(n_col)])  4.29 us
  transfers between devices with their start and end apart: 21, of which 11 were waited for; matrix products, arithmetic and copies ran while one was open for 0% of the time, Pallas kernels for 19%

profile of v10, /device:TPU:0, one launch (start us, length us, event | category | flops | bytes accessed | tf_op | source)
XLA Modules:
  0.0 141.1 jit_solution(17529078819646204837)
XLA Ops:
  5.1 4.9 %load.1 = (f32[16,24,1024]{2,1,0:T(8,128)S(1)}, f32[16,24,1024]{2,1,0:T(8,128)S(1)}, f32[16,24,1024]{2,1,0:T(8,128)S(1)}, f32[3,16,24,1024]{3,2,1,0:T(8,128)S(1)...) custom-call(f32[16,24,1024]{2,1,0:T(8,128)} %temp_far.1, ...), custom_call_target="tpu_custom_call" | custom-call | flops 23592960 | bytes 23592960 | tf_op jit(solution)/shard_map/load/pallas_call | solution.py:472
  10.1 3.5 %collective-permute-done.1.col = f32[2,24,1024]{2,1,0:T(8,128)S(1)} collective-permute-done((f32[2,24,1024]{2,1,0:T(8,128)S(1)}, f32[2,24,1024]{2,1,0:T(8,128)S(1)}, u32[]{:S(2)}, u32[]{:S(2)}) %collective-permute-start.1) | collective-permute-done | bytes 196640 | tf_op jit(solution)/shard_map/ppermute | solution.py:449
  13.8 4.1 %collective-permute-start.3 = (f32[2,24,1024]{2,1,0:T(8,128)S(1)}, f32[2,24,1024]{2,1,0:T(8,128)S(1)}, u32[]{:S(2)}, u32[]{:S(2)}) collective-permute-start(f32[2,24,1024]{2,1,0:T(8,128)S(1)} %get-tuple-element.74), channel_id=1, source_target_pairs={{0,8},{1,9},{2,10},{3,11},{4,12},{5,13},{6,14},{7,15},{8,16},{9,17... | collective-permute-start | bytes 589832 | tf_op jit(solution)/shard_map/ppermute | solution.py:449
  19.6 1.9 %h_rest_0.1 = (f32[3,16,24,1024]{3,2,1,0:T(8,128)S(1)}, f32[3,16,1024]{2,1,0:T(8,128)S(1)}) custom-call(f32[3,16,24,1024]{3,2,1,0:T(8,128)S(1)} %get-tuple-element.62.e.refs_0_, f32[2,16,1024]{2,1,0:T(8,128)S(1)} %collective-permute-done.hgt, f32[3,16,24,1024]{3,2,1,0:T(8,128)S(1)} %get-tuple-element.68.h_old), custom_call_target="tpu_custom_call", output_to_operand_aliasing={{0}: (2, {})} | custom-call | flops 15728640 | bytes 15728640 | tf_op jit(solution)/shard_map/h_rest_0/pallas_call | solution.py:472
  25.1 2.2 %e_rest_0.1 = (f32[3,16,24,1024]{3,2,1,0:T(8,128)S(1)}, f32[16,24,1024]{2,1,0:T(8,128)S(1)}, f32[3,16,1024]{2,1,0:T(8,128)S(1)}) custom-call(f32[3,16,24,1024]{3,2,1,0:T(8,128)S(1)} %get-tuple-element.69.h.h_old, f32[16,24,1024]{2,1,0:T(8,128)S(1)} %get-tuple-element.70.ca, ...), custom_call_target="tpu_custom_call", output_to_operand_aliasing={{0}: (5, {}), {1}: (6, {})} | custom-call | flops 17694720 | bytes 17694720 | tf_op jit(solution)/shard_map/e_rest_0/pallas_call | solution.py:472
  27.9 4.7 %collective-permute-done.5.col = f32[2,24,1024]{2,1,0:T(8,128)S(1)} collective-permute-done((f32[2,24,1024]{2,1,0:T(8,128)S(1)}, f32[2,24,1024]{2,1,0:T(8,128)S(1)}, u32[]{:S(2)}, u32[]{:S(2)}) %collective-permute-start.5) | collective-permute-done | bytes 196640 | tf_op jit(solution)/shard_map/ppermute | solution.py:449
  32.7 3.5 %collective-permute-start.7 = (f32[2,24,1024]{2,1,0:T(8,128)S(1)}, f32[2,24,1024]{2,1,0:T(8,128)S(1)}, u32[]{:S(2)}, u32[]{:S(2)}) collective-permute-start(f32[2,24,1024]{2,1,0:T(8,128)S(1)} %get-tuple-element.86), channel_id=1, source_target_pairs={{0,8},{1,9},{2,10},{3,11},{4,12},{5,13},{6,14},{7,15},{8,16},{9,17... | collective-permute-start | bytes 589832 | tf_op jit(solution)/shard_map/ppermute | solution.py:449
  36.2 2.3 %collective-permute-start.6 = (f32[2,16,1024]{2,1,0:T(8,128)S(1)}, f32[2,16,1024]{2,1,0:T(8,128)S(1)}, u32[]{:S(2)}, u32[]{:S(2)}) collective-permute-start(f32[2,16,1024]{2,1,0:T(8,128)S(1)} %get-tuple-element.85.rows_old), channel_id=1, source_target_pairs={{0,1},{1,2},{2,3},{3,4},{4,5},{5,6},{6,7},{8,9},{9,10},{10,11},{11... | collective-permute-start | bytes 393224 | tf_op jit(solution)/shard_map/ppermute | solution.py:449
  38.5 1.9 %h_rest_1.1 = (f32[3,16,24,1024]{3,2,1,0:T(8,128)S(1)}, f32[3,16,1024]{2,1,0:T(8,128)S(1)}) custom-call(f32[3,16,24,1024]{3,2,1,0:T(8,128)S(1)} %get-tuple-element.79.e.refs_0_, f32[2,16,1024]{2,1,0:T(8,128)S(1)} %collective-permute-done.4.hgt, f32[3,16,24,1024]{3,2,1,0:T(8,128)S(1)} %get-tuple-element.83.h_old), custom_call_target="tpu_custom_call", output_to_operand_aliasing={{0}: (2, {})} | custom-call | flops 15728640 | bytes 15728640 | tf_op jit(solution)/shard_map/h_rest_1/pallas_call | solution.py:472
  43.9 2.3 %e_rest_1.1 = (f32[3,16,24,1024]{3,2,1,0:T(8,128)S(1)}, f32[16,24,1024]{2,1,0:T(8,128)S(1)}, f32[3,16,1024]{2,1,0:T(8,128)S(1)}) custom-call(f32[3,16,24,1024]{3,2,1,0:T(8,128)S(1)} %get-tuple-element.84.h.h_old, f32[16,24,1024]{2,1,0:T(8,128)S(1)} %get-tuple-element.70.ca, ...), custom_call_target="tpu_custom_call", output_to_operand_aliasing={{0}: (5, {}), {1}: (6, {})} | custom-call | flops 17694720 | bytes 17694720 | tf_op jit(solution)/shard_map/e_rest_1/pallas_call | solution.py:472
  46.2 4.4 %collective-permute-done.9.col = f32[2,24,1024]{2,1,0:T(8,128)S(1)} collective-permute-done((f32[2,24,1024]{2,1,0:T(8,128)S(1)}, f32[2,24,1024]{2,1,0:T(8,128)S(1)}, u32[]{:S(2)}, u32[]{:S(2)}) %collective-permute-start.9) | collective-permute-done | bytes 196640 | tf_op jit(solution)/shard_map/ppermute | solution.py:449
  50.7 3.6 %collective-permute-start.11 = (f32[2,24,1024]{2,1,0:T(8,128)S(1)}, f32[2,24,1024]{2,1,0:T(8,128)S(1)}, u32[]{:S(2)}, u32[]{:S(2)}) collective-permute-start(f32[2,24,1024]{2,1,0:T(8,128)S(1)} %get-tuple-element.98), channel_id=1, source_target_pairs={{0,8},{1,9},{2,10},{3,11},{4,12},{5,13},{6,14},{7,15},{8,16},{9,17... | collective-permute-start | bytes 589832 | tf_op jit(solution)/shard_map/ppermute | solution.py:449
  54.4 2.1 %collective-permute-start.10 = (f32[2,16,1024]{2,1,0:T(8,128)S(1)}, f32[2,16,1024]{2,1,0:T(8,128)S(1)}, u32[]{:S(2)}, u32[]{:S(2)}) collective-permute-start(f32[2,16,1024]{2,1,0:T(8,128)S(1)} %get-tuple-element.97.rows_old), channel_id=1, source_target_pairs={{0,1},{1,2},{2,3},{3,4},{4,5},{5,6},{6,7},{8,9},{9,10},{10,11},{11... | collective-permute-start | bytes 393224 | tf_op jit(solution)/shard_map/ppermute | solution.py:449
  61.9 2.3 %e_rest_2.1 = (f32[3,16,24,1024]{3,2,1,0:T(8,128)S(1)}, f32[16,24,1024]{2,1,0:T(8,128)S(1)}, f32[3,16,1024]{2,1,0:T(8,128)S(1)}) custom-call(f32[3,16,24,1024]{3,2,1,0:T(8,128)S(1)} %get-tuple-element.96.h.h_old, f32[16,24,1024]{2,1,0:T(8,128)S(1)} %get-tuple-element.70.ca, ...), custom_call_target="tpu_custom_call", output_to_operand_aliasing={{0}: (5, {}), {1}: (6, {})} | custom-call | flops 17694720 | bytes 17694720 | tf_op jit(solution)/shard_map/e_rest_2/pallas_call | solution.py:472
  64.4 4.7 %collective-permute-done.13.col = f32[2,24,1024]{2,1,0:T(8,128)S(1)} collective-permute-done((f32[2,24,1024]{2,1,0:T(8,128)S(1)}, f32[2,24,1024]{2,1,0:T(8,128)S(1)}, u32[]{:S(2)}, u32[]{:S(2)}) %collective-permute-start.13) | collective-permute-done | bytes 196640 | tf_op jit(solution)/shard_map/ppermute | solution.py:449
  69.2 3.0 %collective-permute-start.14 = (f32[2,24,1024]{2,1,0:T(8,128)S(1)}, f32[2,24,1024]{2,1,0:T(8,128)S(1)}, u32[]{:S(2)}, u32[]{:S(2)}) collective-permute-start(f32[2,24,1024]{2,1,0:T(8,128)S(1)} %get-tuple-element.108), channel_id=1, source_target_pairs={{0,8},{1,9},{2,10},{3,11},{4,12},{5,13},{6,14},{7,15},{8,16},{9,17... | collective-permute-start | bytes 589832 | tf_op jit(solution)/shard_map/ppermute | solution.py:449
  72.3 2.7 %collective-permute-start.15 = (f32[2,16,1024]{2,1,0:T(8,128)S(1)}, f32[2,16,1024]{2,1,0:T(8,128)S(1)}, u32[]{:S(2)}, u32[]{:S(2)}) collective-permute-start(f32[2,16,1024]{2,1,0:T(8,128)S(1)} %get-tuple-element.109), channel_id=1, source_target_pairs={{0,1},{1,2},{2,3},{3,4},{4,5},{5,6},{6,7},{8,9},{9,10},{10,11},{11... | collective-permute-start | bytes 393224 | tf_op jit(solution)/shard_map/ppermute | solution.py:449
  75.0 2.2 %places.1 = (s32[1,3072]{1,0:T(1,128)S(1)}, f32[6336,128]{1,0:T(8,128)S(1)}) custom-call(s32[1]{0:T(128)} %bitcast.my_col, s32[1,3072]{1,0:T(1,128)S(1)} %reshape.46.owner, s32[1,3072]{1,0:T(1,128)S(1)} %reshape.47.node), custom_call_target="tpu_custom_call" | custom-call | flops 3145728 | bytes 3145728 | tf_op jit(solution)/shard_map/places/pallas_call | solution.py:472
  79.1 8.2 %e_last.1 = (f32[3,16,24,1024]{3,2,1,0:T(8,128)S(1)}, f32[16,24,1024]{2,1,0:T(8,128)S(1)}, f32[6336,128]{1,0:T(8,128)S(1)}, f32[3,16,24,1024]{3,2,1,0:T(8,128)},...) custom-call(s32[3072]{0:T(1024)S(1)} %bitcast.8, ...), custom_call_target="tpu_custom_call", output_to_operand_aliasing={{0}: (7, {}), {1}: (8, {}), {2}: (9, {})} | custom-call | flops 19660800 | bytes 19660800 | tf_op jit(solution)/shard_map/e_last/pallas_call | solution.py:539
  87.3 3.9 %all-to-all-start.1 = ((f32[8,392,128]{2,1,0:T(8,128)}), f32[8,392,128]{2,1,0:T(8,128)S(1)}, u32[]{:S(2)}, u32[]{:S(2)}) async-start(f32[8,392,128]{2,1,0:T(8,128)} %get-tuple-element.116), calls=%async_computation.1 | async-start | bytes 3211264 | tf_op jit(solution)/shard_map/all_to_all | solution.py:584
  92.2 19.9 %collective-permute-done.16.pair = f32[8,200,128]{2,1,0:T(8,128)S(1)} collective-permute-done((f32[8,200,128]{2,1,0:T(8,128)}, f32[8,200,128]{2,1,0:T(8,128)S(1)}, u32[]{:S(2)}, u32[]{:S(2)}) %collective-permute-start.16) | collective-permute-done | bytes 819232 | tf_op jit(solution)/shard_map/ppermute | solution.py:587
  113.0 3.9 %all-to-all-start = ((f32[8,400,128]{2,1,0:T(8,128)}), f32[8,400,128]{2,1,0:T(8,128)S(1)}, u32[]{:S(2)}, u32[]{:S(2)}) async-start(f32[8,400,128]{2,1,0:T(8,128)} %merge.1), calls=%async_computation | async-start | bytes 3276800 | tf_op jit(solution)/shard_map/all_to_all | solution.py:584
  116.9 2.4 %collect_other.1 = (f32[384,128]{1,0:T(8,128)}, f32[384,128]{1,0:T(8,128)}) custom-call(f32[8,392,128]{2,1,0:T(8,128)S(1)} %all-to-all-done.1.blocks), custom_call_target="tpu_custom_call" | custom-call | flops 393216 | bytes 393216 | tf_op jit(solution)/shard_map/collect_other/pallas_call | solution.py:472
  122.6 16.0 %all-to-all-done.blocks = f32[8,400,128]{2,1,0:T(8,128)S(1)} async-done(((f32[8,400,128]{2,1,0:T(8,128)}), f32[8,400,128]{2,1,0:T(8,128)S(1)}, u32[]{:S(2)}, u32[]{:S(2)}) %all-to-all-start) | async-done | bytes 1638432 | tf_op jit(solution)/shard_map/all_to_all | solution.py:584
  (51 shorter events, 29.5 us)
Async XLA Ops:
  0.6 4.0 %copy-start.1 = (s32[1,1,16,24,8,1]{3,5,4,2,1,0:T(1,128)S(1)}, s32[1,1,16,24,8,1]{3,5,4,2,1,0:T(1,128)}, u32[]{:S(2)}) copy-start(s32[1,1,16,24,8,1]{3,5,4,2,1,0:T(1,128)} %param.11) | copy-start | bytes 36868
  0.6 4.2 %copy-start.2 = (s32[1,1,16,24,8]{3,4,2,1,0:T(8,128)S(1)}, s32[1,1,16,24,8]{3,4,2,1,0:T(8,128)}, u32[]{:S(2)}) copy-start(s32[1,1,16,24,8]{3,4,2,1,0:T(8,128)} %param.12) | copy-start | bytes 36868
  2.0 8.1 %collective-permute-start = (f32[2,16,1024]{2,1,0:T(8,128)S(1)}, f32[2,16,1024]{2,1,0:T(8,128)S(1)}, u32[]{:S(2)}, u32[]{:S(2)}) collective-permute-start(f32[2,16,1024]{2,1,0:T(8,128)S(1)} %get-tuple-element.63.rows_old), channel_id=1, source_target_pairs={{1,0},{2,1},{3,2},{4,3},{5,4},{6,5},{7,6},{9,8},{10,9},{11,10},{12... | collective-permute-start | bytes 393224 | tf_op jit(solution)/shard_map/ppermute | solution.py:449
  3.3 10.3 %collective-permute-start.1 = (f32[2,24,1024]{2,1,0:T(8,128)S(1)}, f32[2,24,1024]{2,1,0:T(8,128)S(1)}, u32[]{:S(2)}, u32[]{:S(2)}) collective-permute-start(f32[2,24,1024]{2,1,0:T(8,128)S(1)} %get-tuple-element.64), channel_id=1, source_target_pairs={{8,0},{9,1},{10,2},{11,3},{12,4},{13,5},{14,6},{15,7},{16,8},{17,9... | collective-permute-start | bytes 589832 | tf_op jit(solution)/shard_map/ppermute | solution.py:449
  13.8 8.5 %collective-permute-start.3 = (f32[2,24,1024]{2,1,0:T(8,128)S(1)}, f32[2,24,1024]{2,1,0:T(8,128)S(1)}, u32[]{:S(2)}, u32[]{:S(2)}) collective-permute-start(f32[2,24,1024]{2,1,0:T(8,128)S(1)} %get-tuple-element.74), channel_id=1, source_target_pairs={{0,8},{1,9},{2,10},{3,11},{4,12},{5,13},{6,14},{7,15},{8,16},{9,17... | collective-permute-start | bytes 589832 | tf_op jit(solution)/shard_map/ppermute | solution.py:449
  17.9 3.7 %collective-permute-start.2 = (f32[2,16,1024]{2,1,0:T(8,128)S(1)}, f32[2,16,1024]{2,1,0:T(8,128)S(1)}, u32[]{:S(2)}, u32[]{:S(2)}) collective-permute-start(f32[2,16,1024]{2,1,0:T(8,128)S(1)} %get-tuple-element.73.rows_old), channel_id=1, source_target_pairs={{0,1},{1,2},{2,3},{3,4},{4,5},{5,6},{6,7},{8,9},{9,10},{10,11},{11... | collective-permute-start | bytes 393224 | tf_op jit(solution)/shard_map/ppermute | solution.py:449
  22.5 10.1 %collective-permute-start.5 = (f32[2,24,1024]{2,1,0:T(8,128)S(1)}, f32[2,24,1024]{2,1,0:T(8,128)S(1)}, u32[]{:S(2)}, u32[]{:S(2)}) collective-permute-start(f32[2,24,1024]{2,1,0:T(8,128)S(1)} %get-tuple-element.81), channel_id=1, source_target_pairs={{8,0},{9,1},{10,2},{11,3},{12,4},{13,5},{14,6},{15,7},{16,8},{17,9... | collective-permute-start | bytes 589832 | tf_op jit(solution)/shard_map/ppermute | solution.py:449
  23.8 4.1 %collective-permute-start.4 = (f32[2,16,1024]{2,1,0:T(8,128)S(1)}, f32[2,16,1024]{2,1,0:T(8,128)S(1)}, u32[]{:S(2)}, u32[]{:S(2)}) collective-permute-start(f32[2,16,1024]{2,1,0:T(8,128)S(1)} %get-tuple-element.80.rows_old), channel_id=1, source_target_pairs={{1,0},{2,1},{3,2},{4,3},{5,4},{6,5},{7,6},{9,8},{10,9},{11,10},{12... | collective-permute-start | bytes 393224 | tf_op jit(solution)/shard_map/ppermute | solution.py:449
  32.7 8.4 %collective-permute-start.7 = (f32[2,24,1024]{2,1,0:T(8,128)S(1)}, f32[2,24,1024]{2,1,0:T(8,128)S(1)}, u32[]{:S(2)}, u32[]{:S(2)}) collective-permute-start(f32[2,24,1024]{2,1,0:T(8,128)S(1)} %get-tuple-element.86), channel_id=1, source_target_pairs={{0,8},{1,9},{2,10},{3,11},{4,12},{5,13},{6,14},{7,15},{8,16},{9,17... | collective-permute-start | bytes 589832 | tf_op jit(solution)/shard_map/ppermute | solution.py:449
  36.2 4.2 %collective-permute-start.6 = (f32[2,16,1024]{2,1,0:T(8,128)S(1)}, f32[2,16,1024]{2,1,0:T(8,128)S(1)}, u32[]{:S(2)}, u32[]{:S(2)}) collective-permute-start(f32[2,16,1024]{2,1,0:T(8,128)S(1)} %get-tuple-element.85.rows_old), channel_id=1, source_target_pairs={{0,1},{1,2},{2,3},{3,4},{4,5},{5,6},{6,7},{8,9},{9,10},{10,11},{11... | collective-permute-start | bytes 393224 | tf_op jit(solution)/shard_map/ppermute | solution.py:449
  41.3 9.3 %collective-permute-start.9 = (f32[2,24,1024]{2,1,0:T(8,128)S(1)}, f32[2,24,1024]{2,1,0:T(8,128)S(1)}, u32[]{:S(2)}, u32[]{:S(2)}) collective-permute-start(f32[2,24,1024]{2,1,0:T(8,128)S(1)} %get-tuple-element.93), channel_id=1, source_target_pairs={{8,0},{9,1},{10,2},{11,3},{12,4},{13,5},{14,6},{15,7},{16,8},{17,9... | collective-permute-start | bytes 589832 | tf_op jit(solution)/shard_map/ppermute | solution.py:449
  42.6 3.6 %collective-permute-start.8 = (f32[2,16,1024]{2,1,0:T(8,128)S(1)}, f32[2,16,1024]{2,1,0:T(8,128)S(1)}, u32[]{:S(2)}, u32[]{:S(2)}) collective-permute-start(f32[2,16,1024]{2,1,0:T(8,128)S(1)} %get-tuple-element.92.rows_old), channel_id=1, source_target_pairs={{1,0},{2,1},{3,2},{4,3},{5,4},{6,5},{7,6},{9,8},{10,9},{11,10},{12... | collective-permute-start | bytes 393224 | tf_op jit(solution)/shard_map/ppermute | solution.py:449
  50.7 8.4 %collective-permute-start.11 = (f32[2,24,1024]{2,1,0:T(8,128)S(1)}, f32[2,24,1024]{2,1,0:T(8,128)S(1)}, u32[]{:S(2)}, u32[]{:S(2)}) collective-permute-start(f32[2,24,1024]{2,1,0:T(8,128)S(1)} %get-tuple-element.98), channel_id=1, source_target_pairs={{0,8},{1,9},{2,10},{3,11},{4,12},{5,13},{6,14},{7,15},{8,16},{9,17... | collective-permute-start | bytes 589832 | tf_op jit(solution)/shard_map/ppermute | solution.py:449
  54.4 4.1 %collective-permute-start.10 = (f32[2,16,1024]{2,1,0:T(8,128)S(1)}, f32[2,16,1024]{2,1,0:T(8,128)S(1)}, u32[]{:S(2)}, u32[]{:S(2)}) collective-permute-start(f32[2,16,1024]{2,1,0:T(8,128)S(1)} %get-tuple-element.97.rows_old), channel_id=1, source_target_pairs={{0,1},{1,2},{2,3},{3,4},{4,5},{5,6},{6,7},{8,9},{9,10},{10,11},{11... | collective-permute-start | bytes 393224 | tf_op jit(solution)/shard_map/ppermute | solution.py:449
  59.3 9.8 %collective-permute-start.13 = (f32[2,24,1024]{2,1,0:T(8,128)S(1)}, f32[2,24,1024]{2,1,0:T(8,128)S(1)}, u32[]{:S(2)}, u32[]{:S(2)}) collective-permute-start(f32[2,24,1024]{2,1,0:T(8,128)S(1)} %get-tuple-element.105), channel_id=1, source_target_pairs={{8,0},{9,1},{10,2},{11,3},{12,4},{13,5},{14,6},{15,7},{16,8},{17,9... | collective-permute-start | bytes 589832 | tf_op jit(solution)/shard_map/ppermute | solution.py:449
  60.6 3.8 %collective-permute-start.12 = (f32[2,16,1024]{2,1,0:T(8,128)S(1)}, f32[2,16,1024]{2,1,0:T(8,128)S(1)}, u32[]{:S(2)}, u32[]{:S(2)}) collective-permute-start(f32[2,16,1024]{2,1,0:T(8,128)S(1)} %get-tuple-element.104), channel_id=1, source_target_pairs={{1,0},{2,1},{3,2},{4,3},{5,4},{6,5},{7,6},{9,8},{10,9},{11,10},{12... | collective-permute-start | bytes 393224 | tf_op jit(solution)/shard_map/ppermute | solution.py:449
  69.2 9.8 %collective-permute-start.14 = (f32[2,24,1024]{2,1,0:T(8,128)S(1)}, f32[2,24,1024]{2,1,0:T(8,128)S(1)}, u32[]{:S(2)}, u32[]{:S(2)}) collective-permute-start(f32[2,24,1024]{2,1,0:T(8,128)S(1)} %get-tuple-element.108), channel_id=1, source_target_pairs={{0,8},{1,9},{2,10},{3,11},{4,12},{5,13},{6,14},{7,15},{8,16},{9,17... | collective-permute-start | bytes 589832 | tf_op jit(solution)/shard_map/ppermute | solution.py:449
  72.3 6.8 %collective-permute-start.15 = (f32[2,16,1024]{2,1,0:T(8,128)S(1)}, f32[2,16,1024]{2,1,0:T(8,128)S(1)}, u32[]{:S(2)}, u32[]{:S(2)}) collective-permute-start(f32[2,16,1024]{2,1,0:T(8,128)S(1)} %get-tuple-element.109), channel_id=1, source_target_pairs={{0,1},{1,2},{2,3},{3,4},{4,5},{5,6},{6,7},{8,9},{9,10},{10,11},{11... | collective-permute-start | bytes 393224 | tf_op jit(solution)/shard_map/ppermute | solution.py:449
  87.3 25.7 %all-to-all-start.1 = ((f32[8,392,128]{2,1,0:T(8,128)}), f32[8,392,128]{2,1,0:T(8,128)S(1)}, u32[]{:S(2)}, u32[]{:S(2)}) async-start(f32[8,392,128]{2,1,0:T(8,128)} %get-tuple-element.116), calls=%async_computation.1 | async-start | bytes 3211264 | tf_op jit(solution)/shard_map/all_to_all | solution.py:584
  91.2 20.9 %collective-permute-start.16 = (f32[8,200,128]{2,1,0:T(8,128)}, f32[8,200,128]{2,1,0:T(8,128)S(1)}, u32[]{:S(2)}, u32[]{:S(2)}) collective-permute-start(f32[8,200,128]{2,1,0:T(8,128)} %get-tuple-element.114), channel_id=1, source_target_pairs={{0,8},{8,0},{16,24},{24,16},{1,9},{9,1},{17,25},{25,17},{2,10},{10... | collective-permute-start | bytes 2457608 | tf_op jit(solution)/shard_map/ppermute | solution.py:587
  112.0 28.3 %copy-start = (f32[384,128]{1,0:T(8,128)S(1)}, f32[384,128]{1,0:T(8,128)}, u32[]{:S(2)}) copy-start(f32[384,128]{1,0:T(8,128)} %enthalpy.1) | copy-start | bytes 589828
  113.0 25.6 %all-to-all-start = ((f32[8,400,128]{2,1,0:T(8,128)}), f32[8,400,128]{2,1,0:T(8,128)S(1)}, u32[]{:S(2)}, u32[]{:S(2)}) async-start(f32[8,400,128]{2,1,0:T(8,128)} %merge.1), calls=%async_computation | async-start | bytes 3276800 | tf_op jit(solution)/shard_map/all_to_all | solution.py:584
  119.3 21.0 %collective-permute-start.17 = (f32[384,128]{1,0:T(8,128)}, f32[384,128]{1,0:T(8,128)S(1)}, u32[]{:S(2)}, u32[]{:S(2)}) collective-permute-start(f32[384,128]{1,0:T(8,128)} %get-tuple-element.117), channel_id=1, source_target_pairs={{0,16},{8,24},{16,0},{24,8},{1,17},{9,25},{17,1},{25,9},{2,18},{10... | collective-permute-start | bytes 589832 | tf_op jit(solution)/shard_map/ppermute | solution.py:587
  120.8 19.5 %collective-permute-start.18 = (f32[384,128]{1,0:T(8,128)}, f32[384,128]{1,0:T(8,128)S(1)}, u32[]{:S(2)}, u32[]{:S(2)}) collective-permute-start(f32[384,128]{1,0:T(8,128)} %get-tuple-element.118), channel_id=1, source_target_pairs={{0,24},{8,16},{16,8},{24,0},{1,25},{9,17},{17,9},{25,1},{2,26},{10... | collective-permute-start | bytes 589832 | tf_op jit(solution)/shard_map/ppermute | solution.py:587

commit v11 on v6

--- a/solution.py
+++ b/solution.py
@@ -343,7 +343,7 @@
     return [0, n_hgt * heights[0], n_hgt * (heights[0] + heights[1])], heights
 
 
-def pack_kernel(heights, place, power, flat_old, e, mine, pair, other, e_out, flat, sems):
+def pack_kernel(heights, place, power, flat_old, e, pair, other, e_out, flat, sems):
     nx, nz, ny = power.shape
     e_copy = pltpu.make_async_copy(e, e_out, sems.at[0])
     e_copy.start()
@@ -358,8 +358,8 @@
 
     lax.fori_loop(0, nx, plane, 0)
     copies = []
-    first = 0
-    for out, rows in zip((mine, pair, other), heights):
+    first = pair.shape[0] * heights[0]
+    for out, rows in zip((pair, other), heights[1:]):
         for group in range(out.shape[0]):
             target = out.at[group, pl.ds(0, rows)]
             copies.append(pltpu.make_async_copy(flat.at[pl.ds(first, rows)], target, sems.at[1 + len(copies)]))
@@ -392,30 +392,61 @@
     return both[:, 0:pts] + both[:, pts : 2 * pts]
 
 
-def collect_kernel(cap, blocks, *refs):
-    *outs, chosen, split = refs
+def collect_kernel(part, cap, blocks, out, chosen, split, mine, sems):
+    n_from = blocks.shape[0]
+    rest = mine.shape[1] - cap
+    begin = blocks.shape[1] - rest
+    per = -(-cap // LANES)
+    copies = []
+    for source in range(n_from):
+        rows = blocks.at[source, pl.ds(part * cap, cap)]
+        nodes = blocks.at[source, pl.ds(begin, rest)]
+        copies.append(pltpu.make_async_copy(rows, mine.at[source, pl.ds(0, cap)], sems.at[0, source]))
+        copies.append(pltpu.make_async_copy(nodes, mine.at[source, pl.ds(cap, rest)], sems.at[1, source]))
+    for copy in copies:
+        copy.start()
+    split[...] = jnp.zeros(split.shape, split.dtype)
+    for copy in copies:
+        copy.wait()
+    out[...] = summed(mine, [0], cap, [cap + part * per], chosen, split, out.shape[0])
+
+
+def own_kernel(cap, height, flat, mine, sems):
+    copies = [
+        pltpu.make_async_copy(flat.at[pl.ds(group * height, cap)], mine.at[group, pl.ds(0, cap)], sems.at[group])
+        for group in range(mine.shape[0])
+    ]
+    for copy in copies:
+        copy.start()
+    for copy in copies:
+        copy.wait()
+
+
+def merge_kernel(cap, height, flat, pair, mine_old, mine, tile, sems):
+    per = -(-cap // LANES)
+    groups = mine.shape[0]
+    copies = []
+    for group in range(groups):
+        target = mine.at[group, pl.ds(cap, cap)]
+        copies.append(pltpu.make_async_copy(pair.at[group, pl.ds(0, cap)], target, sems.at[0, group]))
+    for copy in copies:
+        copy.start()
+    rest = tile.shape[1]
+    tile[...] = jnp.full(tile.shape, -1.0, F32)
+    for group in range(groups):
+        tile[group, 0:per, :] = pair[group, cap : cap + per, :]
+        tile[group, per : 2 * per, :] = flat[group * height + cap : group * height + cap + per, :]
+        target = mine.at[group, pl.ds(2 * cap, rest)]
+        copies.append(pltpu.make_async_copy(tile.at[group], target, sems.at[1, group]))
+        copies[-1].start()
+    for copy in copies:
+        copy.wait()
+
+
+def collect_mine_kernel(cap, blocks, out, chosen, split):
     per = -(-cap // LANES)
     split[...] = jnp.zeros(split.shape, split.dtype)
-    for part, out in enumerate(outs):
-        out[...] = summed(blocks, [part * cap], cap, [len(outs) * cap + part * per], chosen, split, out.shape[0])
-
-
-def merge_kernel(pair, mine_old, mine, sems):
-    rows = pair.shape[1]
-    copies = [
-        pltpu.make_async_copy(pair.at[group], mine.at[group, pl.ds(rows, rows)], sems.at[group])
-        for group in range(mine.shape[0])
-    ]
-    for copy in copies:
-        copy.start()
-    for copy in copies:
-        copy.wait()
-
-
-def collect_mine_kernel(cap, blocks, out, chosen, split):
-    half = blocks.shape[1] // 2
-    split[...] = jnp.zeros(split.shape, split.dtype)
-    out[...] = summed(blocks, [0, half], cap, [cap, half + cap], chosen, split, out.shape[0])
+    out[...] = summed(blocks, [0, cap], cap, [2 * cap + per, 2 * cap], chosen, split, out.shape[0])
 
 
 def finish_kernel(enthalpy, *refs):
@@ -560,19 +591,18 @@
             {5: 0, 6: 1},
         )
 
-    mine, pair, other, e_out, _ = pl.pallas_call(
+    pair, other, e_out, flat = pl.pallas_call(
         functools.partial(pack_kernel, heights),
         out_shape=(
-            pltpu.HBM((n_hgt, 2 * heights[0], PTS), F32),
             pltpu.HBM((n_hgt, heights[1], PTS), F32),
             pltpu.HBM((n_hgt, heights[2], PTS), F32),
             pltpu.HBM((3, nx, nz, ny), F32),
             vmem(n_hgt * sum(heights), PTS),
         ),
         in_specs=[SCALARS] + [WHOLE] * 3,
-        out_specs=(FAR,) * 4 + (WHOLE,),
-        input_output_aliases={2: 4},
-        scratch_shapes=[sem((1 + 3 * n_hgt,))],
+        out_specs=(FAR,) * 3 + (WHOLE,),
+        input_output_aliases={2: 3},
+        scratch_shapes=[sem((1 + 2 * n_hgt,))],
         compiler_params=params(VMEM_MIB),
         cost_estimate=cost(cells, cells * 36),
         name="pack",
@@ -591,27 +621,41 @@
     node_rows = jax.ShapeDtypeStruct((node_count, PTS), F32)
     from_pair = across(pair, 1)
     other_blocks = swap(other, "hgt")
-    sums = kernel(
-        functools.partial(collect_kernel, cap),
-        (node_rows,) * (n_col - 2),
-        [WHOLE],
-        [other_blocks],
-        "collect_other",
-        1,
-        scratch=one_hot_space(n_hgt),
-    )
+    sums = [
+        kernel(
+            functools.partial(collect_kernel, part, cap),
+            node_rows,
+            [pl.BlockSpec(memory_space=pl.ANY)],
+            [other_blocks],
+            f"collect_other_{part}",
+            1,
+            scratch=one_hot_space(n_hgt) + [vmem(n_hgt, cap + table_rows(n_col - 2, cap), PTS), sem((2, n_hgt))],
+        )
+        for part in range(n_col - 2)
+    ]
     parts = [across(sums[turn - 2], turn) for turn in range(2, n_col)]
+    both = pltpu.HBM((n_hgt, 2 * cap + table_rows(2, cap), PTS), F32)
     mine = pl.pallas_call(
-        merge_kernel,
-        out_shape=pltpu.HBM((n_hgt, 2 * heights[0], PTS), F32),
-        in_specs=[pl.BlockSpec(memory_space=pl.ANY), FAR],
+        functools.partial(own_kernel, cap, heights[0]),
+        out_shape=both,
+        in_specs=[WHOLE],
         out_specs=FAR,
-        input_output_aliases={1: 0},
         scratch_shapes=[sem((n_hgt,))],
+        compiler_params=params(VMEM_MIB),
+        cost_estimate=cost(cells, cells * 20),
+        name="own",
+    )(flat)
+    mine = pl.pallas_call(
+        functools.partial(merge_kernel, cap, heights[0]),
+        out_shape=both,
+        in_specs=[WHOLE, WHOLE, FAR],
+        out_specs=FAR,
+        input_output_aliases={2: 0},
+        scratch_shapes=[vmem(n_hgt, table_rows(2, cap), PTS), sem((2, n_hgt))],
         compiler_params=params(VMEM_MIB),
         cost_estimate=cost(1, 1),
         name="merge",
-    )(from_pair, mine)
+    )(flat, from_pair, mine)
     mine_blocks = swap(mine, "hgt")
     own = kernel(
         functools.partial(collect_mine_kernel, cap),

time: 141 us -> 141 us (level)
  waiting for transfers between devices: 56.1 us -> 52 us
  Pallas kernels: 37.1 us -> 40 us
    all_to_all x2, waiting for transfers between devices: 16 us -> 13.3 us  [swap(): return lax.all_to_all(x, axis, split_axis=0, concat_axis=0, tiled=True)]
    pallas_call x20 -> x21, Pallas kernels: 28.7 us -> 30.7 us  [kernel(): pl.pallas_call(body, out_shape=outs, in_specs=ins, out_specs=jax.tree.map...]
  transfers between devices with their start and end apart: 21 -> 21, of which waited for: 11 -> 11; matrix products, arithmetic and copies ran while one was open for 0% -> 0% of each run, Pallas kernels for 19% -> 21%
where the time goes in v11:
time: 141 us; the launch traced here: 140 us
  waiting for transfers between devices  52 us (37%)
  starting transfers between devices  46.7 us (33%)
  Pallas kernels  40 us (28%)
    ppermute x16, starting transfers between devices, shifted(): return lax.ppermute(block, ('col', 'hgt'), route)  33.5 us
    pallas_call x21, Pallas kernels, kernel(): pl.pallas_call(body, out_shape=outs, in_specs=ins, out_specs=jax.tree.map...  30.7 us
    ppermute x16, waiting for transfers between devices, shifted(): return lax.ppermute(block, ('col', 'hgt'), route)  20.2 us
    ppermute x3, waiting for transfers between devices, across(): return lax.ppermute(x, 'col', [(c, c ^ turn) for c in range(n_col)])  18.5 us
    all_to_all x2, waiting for transfers between devices, swap(): return lax.all_to_all(x, axis, split_axis=0, concat_axis=0, tiled=True)  13.3 us
    all_to_all x2, starting transfers between devices, swap(): return lax.all_to_all(x, axis, split_axis=0, concat_axis=0, tiled=True)  8.38 us
    pallas_call x1, Pallas kernels, per_device(): pl.pallas_call(functools.partial(pack_kernel, heights), out_shape=(pltpu....  4.86 us
    ppermute x3, starting transfers between devices, across(): return lax.ppermute(x, 'col', [(c, c ^ turn) for c in range(n_col)])  4.82 us
  transfers between devices with their start and end apart: 21, of which 11 were waited for; matrix products, arithmetic and copies ran while one was open for 0% of the time, Pallas kernels for 21%

profile of v11, /device:TPU:0, one launch (start us, length us, event | category | flops | bytes accessed | tf_op | source)
XLA Modules:
  0.0 140.3 jit_solution(13783388437300834188)
XLA Ops:
  5.1 4.9 %load.1 = (f32[16,24,1024]{2,1,0:T(8,128)S(1)}, f32[16,24,1024]{2,1,0:T(8,128)S(1)}, f32[16,24,1024]{2,1,0:T(8,128)S(1)}, f32[3,16,24,1024]{3,2,1,0:T(8,128)S(1)...) custom-call(f32[16,24,1024]{2,1,0:T(8,128)} %temp_far.1, ...), custom_call_target="tpu_custom_call" | custom-call | flops 23592960 | bytes 23592960 | tf_op jit(solution)/shard_map/load/pallas_call | solution.py:493
  10.1 3.5 %collective-permute-done.1.col = f32[2,24,1024]{2,1,0:T(8,128)S(1)} collective-permute-done((f32[2,24,1024]{2,1,0:T(8,128)S(1)}, f32[2,24,1024]{2,1,0:T(8,128)S(1)}, u32[]{:S(2)}, u32[]{:S(2)}) %collective-permute-start.1) | collective-permute-done | bytes 196640 | tf_op jit(solution)/shard_map/ppermute | solution.py:470
  13.8 4.1 %collective-permute-start.3 = (f32[2,24,1024]{2,1,0:T(8,128)S(1)}, f32[2,24,1024]{2,1,0:T(8,128)S(1)}, u32[]{:S(2)}, u32[]{:S(2)}) collective-permute-start(f32[2,24,1024]{2,1,0:T(8,128)S(1)} %get-tuple-element.74), channel_id=1, source_target_pairs={{0,8},{1,9},{2,10},{3,11},{4,12},{5,13},{6,14},{7,15},{8,16},{9,17... | collective-permute-start | bytes 589832 | tf_op jit(solution)/shard_map/ppermute | solution.py:470
  25.1 2.2 %e_rest_0.1 = (f32[3,16,24,1024]{3,2,1,0:T(8,128)S(1)}, f32[16,24,1024]{2,1,0:T(8,128)S(1)}, f32[3,16,1024]{2,1,0:T(8,128)S(1)}) custom-call(f32[3,16,24,1024]{3,2,1,0:T(8,128)S(1)} %get-tuple-element.69.h.h_old, f32[16,24,1024]{2,1,0:T(8,128)S(1)} %get-tuple-element.70.ca, ...), custom_call_target="tpu_custom_call", output_to_operand_aliasing={{0}: (5, {}), {1}: (6, {})} | custom-call | flops 17694720 | bytes 17694720 | tf_op jit(solution)/shard_map/e_rest_0/pallas_call | solution.py:493
  27.9 4.7 %collective-permute-done.5.col = f32[2,24,1024]{2,1,0:T(8,128)S(1)} collective-permute-done((f32[2,24,1024]{2,1,0:T(8,128)S(1)}, f32[2,24,1024]{2,1,0:T(8,128)S(1)}, u32[]{:S(2)}, u32[]{:S(2)}) %collective-permute-start.5) | collective-permute-done | bytes 196640 | tf_op jit(solution)/shard_map/ppermute | solution.py:470
  32.7 3.5 %collective-permute-start.7 = (f32[2,24,1024]{2,1,0:T(8,128)S(1)}, f32[2,24,1024]{2,1,0:T(8,128)S(1)}, u32[]{:S(2)}, u32[]{:S(2)}) collective-permute-start(f32[2,24,1024]{2,1,0:T(8,128)S(1)} %get-tuple-element.86), channel_id=1, source_target_pairs={{0,8},{1,9},{2,10},{3,11},{4,12},{5,13},{6,14},{7,15},{8,16},{9,17... | collective-permute-start | bytes 589832 | tf_op jit(solution)/shard_map/ppermute | solution.py:470
  36.2 2.3 %collective-permute-start.6 = (f32[2,16,1024]{2,1,0:T(8,128)S(1)}, f32[2,16,1024]{2,1,0:T(8,128)S(1)}, u32[]{:S(2)}, u32[]{:S(2)}) collective-permute-start(f32[2,16,1024]{2,1,0:T(8,128)S(1)} %get-tuple-element.85.rows_old), channel_id=1, source_target_pairs={{0,1},{1,2},{2,3},{3,4},{4,5},{5,6},{6,7},{8,9},{9,10},{10,11},{11... | collective-permute-start | bytes 393224 | tf_op jit(solution)/shard_map/ppermute | solution.py:470
  43.9 2.3 %e_rest_1.1 = (f32[3,16,24,1024]{3,2,1,0:T(8,128)S(1)}, f32[16,24,1024]{2,1,0:T(8,128)S(1)}, f32[3,16,1024]{2,1,0:T(8,128)S(1)}) custom-call(f32[3,16,24,1024]{3,2,1,0:T(8,128)S(1)} %get-tuple-element.84.h.h_old, f32[16,24,1024]{2,1,0:T(8,128)S(1)} %get-tuple-element.70.ca, ...), custom_call_target="tpu_custom_call", output_to_operand_aliasing={{0}: (5, {}), {1}: (6, {})} | custom-call | flops 17694720 | bytes 17694720 | tf_op jit(solution)/shard_map/e_rest_1/pallas_call | solution.py:493
  46.2 4.4 %collective-permute-done.9.col = f32[2,24,1024]{2,1,0:T(8,128)S(1)} collective-permute-done((f32[2,24,1024]{2,1,0:T(8,128)S(1)}, f32[2,24,1024]{2,1,0:T(8,128)S(1)}, u32[]{:S(2)}, u32[]{:S(2)}) %collective-permute-start.9) | collective-permute-done | bytes 196640 | tf_op jit(solution)/shard_map/ppermute | solution.py:470
  50.7 3.6 %collective-permute-start.11 = (f32[2,24,1024]{2,1,0:T(8,128)S(1)}, f32[2,24,1024]{2,1,0:T(8,128)S(1)}, u32[]{:S(2)}, u32[]{:S(2)}) collective-permute-start(f32[2,24,1024]{2,1,0:T(8,128)S(1)} %get-tuple-element.98), channel_id=1, source_target_pairs={{0,8},{1,9},{2,10},{3,11},{4,12},{5,13},{6,14},{7,15},{8,16},{9,17... | collective-permute-start | bytes 589832 | tf_op jit(solution)/shard_map/ppermute | solution.py:470
  54.4 2.1 %collective-permute-start.10 = (f32[2,16,1024]{2,1,0:T(8,128)S(1)}, f32[2,16,1024]{2,1,0:T(8,128)S(1)}, u32[]{:S(2)}, u32[]{:S(2)}) collective-permute-start(f32[2,16,1024]{2,1,0:T(8,128)S(1)} %get-tuple-element.97.rows_old), channel_id=1, source_target_pairs={{0,1},{1,2},{2,3},{3,4},{4,5},{5,6},{6,7},{8,9},{9,10},{10,11},{11... | collective-permute-start | bytes 393224 | tf_op jit(solution)/shard_map/ppermute | solution.py:470
  61.9 2.3 %e_rest_2.1 = (f32[3,16,24,1024]{3,2,1,0:T(8,128)S(1)}, f32[16,24,1024]{2,1,0:T(8,128)S(1)}, f32[3,16,1024]{2,1,0:T(8,128)S(1)}) custom-call(f32[3,16,24,1024]{3,2,1,0:T(8,128)S(1)} %get-tuple-element.96.h.h_old, f32[16,24,1024]{2,1,0:T(8,128)S(1)} %get-tuple-element.70.ca, ...), custom_call_target="tpu_custom_call", output_to_operand_aliasing={{0}: (5, {}), {1}: (6, {})} | custom-call | flops 17694720 | bytes 17694720 | tf_op jit(solution)/shard_map/e_rest_2/pallas_call | solution.py:493
  64.4 4.7 %collective-permute-done.13.col = f32[2,24,1024]{2,1,0:T(8,128)S(1)} collective-permute-done((f32[2,24,1024]{2,1,0:T(8,128)S(1)}, f32[2,24,1024]{2,1,0:T(8,128)S(1)}, u32[]{:S(2)}, u32[]{:S(2)}) %collective-permute-start.13) | collective-permute-done | bytes 196640 | tf_op jit(solution)/shard_map/ppermute | solution.py:470
  69.2 3.0 %collective-permute-start.14 = (f32[2,24,1024]{2,1,0:T(8,128)S(1)}, f32[2,24,1024]{2,1,0:T(8,128)S(1)}, u32[]{:S(2)}, u32[]{:S(2)}) collective-permute-start(f32[2,24,1024]{2,1,0:T(8,128)S(1)} %get-tuple-element.108), channel_id=1, source_target_pairs={{0,8},{1,9},{2,10},{3,11},{4,12},{5,13},{6,14},{7,15},{8,16},{9,17... | collective-permute-start | bytes 589832 | tf_op jit(solution)/shard_map/ppermute | solution.py:470
  72.3 2.7 %collective-permute-start.15 = (f32[2,16,1024]{2,1,0:T(8,128)S(1)}, f32[2,16,1024]{2,1,0:T(8,128)S(1)}, u32[]{:S(2)}, u32[]{:S(2)}) collective-permute-start(f32[2,16,1024]{2,1,0:T(8,128)S(1)} %get-tuple-element.109), channel_id=1, source_target_pairs={{0,1},{1,2},{2,3},{3,4},{4,5},{5,6},{6,7},{8,9},{9,10},{10,11},{11... | collective-permute-start | bytes 393224 | tf_op jit(solution)/shard_map/ppermute | solution.py:470
  75.0 2.2 %places.1 = (s32[1,3072]{1,0:T(1,128)S(1)}, f32[6336,128]{1,0:T(8,128)S(1)}) custom-call(s32[1]{0:T(128)} %bitcast.my_col, s32[1,3072]{1,0:T(1,128)S(1)} %reshape.46.owner, s32[1,3072]{1,0:T(1,128)S(1)} %reshape.47.node), custom_call_target="tpu_custom_call" | custom-call | flops 3145728 | bytes 3145728 | tf_op jit(solution)/shard_map/places/pallas_call | solution.py:493
  79.1 2.3 %e_last.1 = (f32[3,16,24,1024]{3,2,1,0:T(8,128)S(1)}, f32[16,24,1024]{2,1,0:T(8,128)S(1)}, f32[3,16,24,1024]{3,2,1,0:T(8,128)}) custom-call(f32[3,16,24,1024]{3,2,1,0:T(8,128)S(1)} %h_rest_3.1.h, f32[16,24,1024]{2,1,0:T(8,128)S(1)} %get-tuple-element.70.ca, f32[16,24,1024]{2,1,0:T(8,128)S(1)} %get-tuple-element.71.cb, ...), custom_call_target="tpu_custom_call", output_to_operand_aliasing={{0}: (6, {}), {1}: (7, {})} | custom-call | flops 19660800 | bytes 19660800 | tf_op jit(solution)/shard_map/e_last/pallas_call | solution.py:559
  81.4 4.9 %pack.1 = (f32[8,200,128]{2,1,0:T(8,128)}, f32[8,392,128]{2,1,0:T(8,128)}, f32[3,16,24,1024]{3,2,1,0:T(8,128)}, f32[6336,128]{1,0:T(8,128)S(1)}) custom-call(s32[3072]{0:T(1024)S(1)} %bitcast.8, f32[16,24,1024]{2,1,0:T(8,128)S(1)} %get-tuple-element.111.power, f32[6336,128]{1,0:T(8,128)S(1)} %get-tuple-element.112.flat_old, ...), custom_call_target="tpu_custom_call", output_to_operand_aliasing={{3}: (2, {})} | custom-call | flops 393216 | bytes 14155776 | tf_op jit(solution)/shard_map/pack/pallas_call | solution.py:594
  86.3 4.3 %all-to-all-start.1 = ((f32[8,392,128]{2,1,0:T(8,128)}), f32[8,392,128]{2,1,0:T(8,128)}, u32[]{:S(2)}, u32[]{:S(2)}) async-start(f32[8,392,128]{2,1,0:T(8,128)} %get-tuple-element.118), calls=%async_computation.1 | async-start | bytes 3211264 | tf_op jit(solution)/shard_map/all_to_all | solution.py:612
  92.8 18.5 %collective-permute-done.16.pair = f32[8,200,128]{2,1,0:T(8,128)S(1)} collective-permute-done((f32[8,200,128]{2,1,0:T(8,128)}, f32[8,200,128]{2,1,0:T(8,128)S(1)}, u32[]{:S(2)}, u32[]{:S(2)}) %collective-permute-start.16) | collective-permute-done | bytes 819232 | tf_op jit(solution)/shard_map/ppermute | solution.py:615
  112.4 4.1 %all-to-all-start = ((f32[8,392,128]{2,1,0:T(8,128)}), f32[8,392,128]{2,1,0:T(8,128)S(1)}, u32[]{:S(2)}, u32[]{:S(2)}) async-start(f32[8,392,128]{2,1,0:T(8,128)} %merge.1), calls=%async_computation | async-start | bytes 3211264 | tf_op jit(solution)/shard_map/all_to_all | solution.py:612
  116.5 2.2 %collect_other_0.1 = f32[384,128]{1,0:T(8,128)S(1)} custom-call(f32[8,392,128]{2,1,0:T(8,128)} %all-to-all-done.1.blocks), custom_call_target="tpu_custom_call" | custom-call | flops 393216 | bytes 393216 | tf_op jit(solution)/shard_map/collect_other_0/pallas_call | solution.py:493
  120.5 2.2 %collect_other_1.1 = f32[384,128]{1,0:T(8,128)S(1)} custom-call(f32[8,392,128]{2,1,0:T(8,128)} %all-to-all-done.1.blocks), custom_call_target="tpu_custom_call" | custom-call | flops 393216 | bytes 393216 | tf_op jit(solution)/shard_map/collect_other_1/pallas_call | solution.py:493
  124.6 13.3 %all-to-all-done.blocks = f32[8,392,128]{2,1,0:T(8,128)S(1)} async-done(((f32[8,392,128]{2,1,0:T(8,128)}), f32[8,392,128]{2,1,0:T(8,128)S(1)}, u32[]{:S(2)}, u32[]{:S(2)}) %all-to-all-start) | async-done | bytes 1605664 | tf_op jit(solution)/shard_map/all_to_all | solution.py:612
  (54 shorter events, 35.0 us)
Async XLA Ops:
  0.6 3.9 %copy-start.1 = (s32[1,1,16,24,8,1]{3,5,4,2,1,0:T(1,128)S(1)}, s32[1,1,16,24,8,1]{3,5,4,2,1,0:T(1,128)}, u32[]{:S(2)}) copy-start(s32[1,1,16,24,8,1]{3,5,4,2,1,0:T(1,128)} %param.11) | copy-start | bytes 36868
  0.6 4.2 %copy-start.2 = (s32[1,1,16,24,8]{3,4,2,1,0:T(8,128)S(1)}, s32[1,1,16,24,8]{3,4,2,1,0:T(8,128)}, u32[]{:S(2)}) copy-start(s32[1,1,16,24,8]{3,4,2,1,0:T(8,128)} %param.12) | copy-start | bytes 36868
  2.0 8.1 %collective-permute-start = (f32[2,16,1024]{2,1,0:T(8,128)S(1)}, f32[2,16,1024]{2,1,0:T(8,128)S(1)}, u32[]{:S(2)}, u32[]{:S(2)}) collective-permute-start(f32[2,16,1024]{2,1,0:T(8,128)S(1)} %get-tuple-element.63.rows_old), channel_id=1, source_target_pairs={{1,0},{2,1},{3,2},{4,3},{5,4},{6,5},{7,6},{9,8},{10,9},{11,10},{12... | collective-permute-start | bytes 393224 | tf_op jit(solution)/shard_map/ppermute | solution.py:470
  3.3 10.3 %collective-permute-start.1 = (f32[2,24,1024]{2,1,0:T(8,128)S(1)}, f32[2,24,1024]{2,1,0:T(8,128)S(1)}, u32[]{:S(2)}, u32[]{:S(2)}) collective-permute-start(f32[2,24,1024]{2,1,0:T(8,128)S(1)} %get-tuple-element.64), channel_id=1, source_target_pairs={{8,0},{9,1},{10,2},{11,3},{12,4},{13,5},{14,6},{15,7},{16,8},{17,9... | collective-permute-start | bytes 589832 | tf_op jit(solution)/shard_map/ppermute | solution.py:470
  13.8 8.5 %collective-permute-start.3 = (f32[2,24,1024]{2,1,0:T(8,128)S(1)}, f32[2,24,1024]{2,1,0:T(8,128)S(1)}, u32[]{:S(2)}, u32[]{:S(2)}) collective-permute-start(f32[2,24,1024]{2,1,0:T(8,128)S(1)} %get-tuple-element.74), channel_id=1, source_target_pairs={{0,8},{1,9},{2,10},{3,11},{4,12},{5,13},{6,14},{7,15},{8,16},{9,17... | collective-permute-start | bytes 589832 | tf_op jit(solution)/shard_map/ppermute | solution.py:470
  17.9 3.7 %collective-permute-start.2 = (f32[2,16,1024]{2,1,0:T(8,128)S(1)}, f32[2,16,1024]{2,1,0:T(8,128)S(1)}, u32[]{:S(2)}, u32[]{:S(2)}) collective-permute-start(f32[2,16,1024]{2,1,0:T(8,128)S(1)} %get-tuple-element.73.rows_old), channel_id=1, source_target_pairs={{0,1},{1,2},{2,3},{3,4},{4,5},{5,6},{6,7},{8,9},{9,10},{10,11},{11... | collective-permute-start | bytes 393224 | tf_op jit(solution)/shard_map/ppermute | solution.py:470
  22.5 10.1 %collective-permute-start.5 = (f32[2,24,1024]{2,1,0:T(8,128)S(1)}, f32[2,24,1024]{2,1,0:T(8,128)S(1)}, u32[]{:S(2)}, u32[]{:S(2)}) collective-permute-start(f32[2,24,1024]{2,1,0:T(8,128)S(1)} %get-tuple-element.81), channel_id=1, source_target_pairs={{8,0},{9,1},{10,2},{11,3},{12,4},{13,5},{14,6},{15,7},{16,8},{17,9... | collective-permute-start | bytes 589832 | tf_op jit(solution)/shard_map/ppermute | solution.py:470
  23.8 4.1 %collective-permute-start.4 = (f32[2,16,1024]{2,1,0:T(8,128)S(1)}, f32[2,16,1024]{2,1,0:T(8,128)S(1)}, u32[]{:S(2)}, u32[]{:S(2)}) collective-permute-start(f32[2,16,1024]{2,1,0:T(8,128)S(1)} %get-tuple-element.80.rows_old), channel_id=1, source_target_pairs={{1,0},{2,1},{3,2},{4,3},{5,4},{6,5},{7,6},{9,8},{10,9},{11,10},{12... | collective-permute-start | bytes 393224 | tf_op jit(solution)/shard_map/ppermute | solution.py:470
  32.7 8.4 %collective-permute-start.7 = (f32[2,24,1024]{2,1,0:T(8,128)S(1)}, f32[2,24,1024]{2,1,0:T(8,128)S(1)}, u32[]{:S(2)}, u32[]{:S(2)}) collective-permute-start(f32[2,24,1024]{2,1,0:T(8,128)S(1)} %get-tuple-element.86), channel_id=1, source_target_pairs={{0,8},{1,9},{2,10},{3,11},{4,12},{5,13},{6,14},{7,15},{8,16},{9,17... | collective-permute-start | bytes 589832 | tf_op jit(solution)/shard_map/ppermute | solution.py:470
  36.2 4.2 %collective-permute-start.6 = (f32[2,16,1024]{2,1,0:T(8,128)S(1)}, f32[2,16,1024]{2,1,0:T(8,128)S(1)}, u32[]{:S(2)}, u32[]{:S(2)}) collective-permute-start(f32[2,16,1024]{2,1,0:T(8,128)S(1)} %get-tuple-element.85.rows_old), channel_id=1, source_target_pairs={{0,1},{1,2},{2,3},{3,4},{4,5},{5,6},{6,7},{8,9},{9,10},{10,11},{11... | collective-permute-start | bytes 393224 | tf_op jit(solution)/shard_map/ppermute | solution.py:470
  41.3 9.3 %collective-permute-start.9 = (f32[2,24,1024]{2,1,0:T(8,128)S(1)}, f32[2,24,1024]{2,1,0:T(8,128)S(1)}, u32[]{:S(2)}, u32[]{:S(2)}) collective-permute-start(f32[2,24,1024]{2,1,0:T(8,128)S(1)} %get-tuple-element.93), channel_id=1, source_target_pairs={{8,0},{9,1},{10,2},{11,3},{12,4},{13,5},{14,6},{15,7},{16,8},{17,9... | collective-permute-start | bytes 589832 | tf_op jit(solution)/shard_map/ppermute | solution.py:470
  42.6 3.6 %collective-permute-start.8 = (f32[2,16,1024]{2,1,0:T(8,128)S(1)}, f32[2,16,1024]{2,1,0:T(8,128)S(1)}, u32[]{:S(2)}, u32[]{:S(2)}) collective-permute-start(f32[2,16,1024]{2,1,0:T(8,128)S(1)} %get-tuple-element.92.rows_old), channel_id=1, source_target_pairs={{1,0},{2,1},{3,2},{4,3},{5,4},{6,5},{7,6},{9,8},{10,9},{11,10},{12... | collective-permute-start | bytes 393224 | tf_op jit(solution)/shard_map/ppermute | solution.py:470
  50.7 8.4 %collective-permute-start.11 = (f32[2,24,1024]{2,1,0:T(8,128)S(1)}, f32[2,24,1024]{2,1,0:T(8,128)S(1)}, u32[]{:S(2)}, u32[]{:S(2)}) collective-permute-start(f32[2,24,1024]{2,1,0:T(8,128)S(1)} %get-tuple-element.98), channel_id=1, source_target_pairs={{0,8},{1,9},{2,10},{3,11},{4,12},{5,13},{6,14},{7,15},{8,16},{9,17... | collective-permute-start | bytes 589832 | tf_op jit(solution)/shard_map/ppermute | solution.py:470
  54.4 4.1 %collective-permute-start.10 = (f32[2,16,1024]{2,1,0:T(8,128)S(1)}, f32[2,16,1024]{2,1,0:T(8,128)S(1)}, u32[]{:S(2)}, u32[]{:S(2)}) collective-permute-start(f32[2,16,1024]{2,1,0:T(8,128)S(1)} %get-tuple-element.97.rows_old), channel_id=1, source_target_pairs={{0,1},{1,2},{2,3},{3,4},{4,5},{5,6},{6,7},{8,9},{9,10},{10,11},{11... | collective-permute-start | bytes 393224 | tf_op jit(solution)/shard_map/ppermute | solution.py:470
  59.3 9.8 %collective-permute-start.13 = (f32[2,24,1024]{2,1,0:T(8,128)S(1)}, f32[2,24,1024]{2,1,0:T(8,128)S(1)}, u32[]{:S(2)}, u32[]{:S(2)}) collective-permute-start(f32[2,24,1024]{2,1,0:T(8,128)S(1)} %get-tuple-element.105), channel_id=1, source_target_pairs={{8,0},{9,1},{10,2},{11,3},{12,4},{13,5},{14,6},{15,7},{16,8},{17,9... | collective-permute-start | bytes 589832 | tf_op jit(solution)/shard_map/ppermute | solution.py:470
  60.6 3.8 %collective-permute-start.12 = (f32[2,16,1024]{2,1,0:T(8,128)S(1)}, f32[2,16,1024]{2,1,0:T(8,128)S(1)}, u32[]{:S(2)}, u32[]{:S(2)}) collective-permute-start(f32[2,16,1024]{2,1,0:T(8,128)S(1)} %get-tuple-element.104), channel_id=1, source_target_pairs={{1,0},{2,1},{3,2},{4,3},{5,4},{6,5},{7,6},{9,8},{10,9},{11,10},{12... | collective-permute-start | bytes 393224 | tf_op jit(solution)/shard_map/ppermute | solution.py:470
  69.2 9.8 %collective-permute-start.14 = (f32[2,24,1024]{2,1,0:T(8,128)S(1)}, f32[2,24,1024]{2,1,0:T(8,128)S(1)}, u32[]{:S(2)}, u32[]{:S(2)}) collective-permute-start(f32[2,24,1024]{2,1,0:T(8,128)S(1)} %get-tuple-element.108), channel_id=1, source_target_pairs={{0,8},{1,9},{2,10},{3,11},{4,12},{5,13},{6,14},{7,15},{8,16},{9,17... | collective-permute-start | bytes 589832 | tf_op jit(solution)/shard_map/ppermute | solution.py:470
  72.3 6.8 %collective-permute-start.15 = (f32[2,16,1024]{2,1,0:T(8,128)S(1)}, f32[2,16,1024]{2,1,0:T(8,128)S(1)}, u32[]{:S(2)}, u32[]{:S(2)}) collective-permute-start(f32[2,16,1024]{2,1,0:T(8,128)S(1)} %get-tuple-element.109), channel_id=1, source_target_pairs={{0,1},{1,2},{2,3},{3,4},{4,5},{5,6},{6,7},{8,9},{9,10},{10,11},{11... | collective-permute-start | bytes 393224 | tf_op jit(solution)/shard_map/ppermute | solution.py:470
  86.3 26.1 %all-to-all-start.1 = ((f32[8,392,128]{2,1,0:T(8,128)}), f32[8,392,128]{2,1,0:T(8,128)}, u32[]{:S(2)}, u32[]{:S(2)}) async-start(f32[8,392,128]{2,1,0:T(8,128)} %get-tuple-element.118), calls=%async_computation.1 | async-start | bytes 3211264 | tf_op jit(solution)/shard_map/all_to_all | solution.py:612
  90.6 20.7 %collective-permute-start.16 = (f32[8,200,128]{2,1,0:T(8,128)}, f32[8,200,128]{2,1,0:T(8,128)S(1)}, u32[]{:S(2)}, u32[]{:S(2)}) collective-permute-start(f32[8,200,128]{2,1,0:T(8,128)} %get-tuple-element.117), channel_id=1, source_target_pairs={{0,8},{8,0},{16,24},{24,16},{1,9},{9,1},{17,25},{25,17},{2,10},{10... | collective-permute-start | bytes 2457608 | tf_op jit(solution)/shard_map/ppermute | solution.py:615
  112.4 27.2 %copy-start = (f32[384,128]{1,0:T(8,128)S(1)}, f32[384,128]{1,0:T(8,128)}, u32[]{:S(2)}) copy-start(f32[384,128]{1,0:T(8,128)} %enthalpy.1) | copy-start | bytes 589828
  112.4 25.4 %all-to-all-start = ((f32[8,392,128]{2,1,0:T(8,128)}), f32[8,392,128]{2,1,0:T(8,128)S(1)}, u32[]{:S(2)}, u32[]{:S(2)}) async-start(f32[8,392,128]{2,1,0:T(8,128)} %merge.1), calls=%async_computation | async-start | bytes 3211264 | tf_op jit(solution)/shard_map/all_to_all | solution.py:612
  118.7 20.8 %collective-permute-start.17 = (f32[384,128]{1,0:T(8,128)S(1)}, f32[384,128]{1,0:T(8,128)S(1)}, u32[]{:S(2)}, u32[]{:S(2)}) collective-permute-start(f32[384,128]{1,0:T(8,128)S(1)} %collect_other_0.1), channel_id=1, source_target_pairs={{0,16},{8,24},{16,0},{24,8},{1,17},{9,25},{17,1},{25,9},{2,18},{10... | collective-permute-start | bytes 589832 | tf_op jit(solution)/shard_map/ppermute | solution.py:615
  122.7 16.8 %collective-permute-start.18 = (f32[384,128]{1,0:T(8,128)S(1)}, f32[384,128]{1,0:T(8,128)S(1)}, u32[]{:S(2)}, u32[]{:S(2)}) collective-permute-start(f32[384,128]{1,0:T(8,128)S(1)} %collect_other_1.1), channel_id=1, source_target_pairs={{0,24},{8,16},{16,8},{24,0},{1,25},{9,17},{17,9},{25,1},{2,26},{10... | collective-permute-start | bytes 589832 | tf_op jit(solution)/shard_map/ppermute | solution.py:615

commit v12 on v11

--- a/solution.py
+++ b/solution.py
@@ -392,23 +392,22 @@
     return both[:, 0:pts] + both[:, pts : 2 * pts]
 
 
-def collect_kernel(part, cap, blocks, out, chosen, split, mine, sems):
-    n_from = blocks.shape[0]
-    rest = mine.shape[1] - cap
-    begin = blocks.shape[1] - rest
+def collect_kernel(cap, blocks, *refs):
+    *outs, chosen, split, near, sems = refs
+    n_from, rows, _ = blocks.shape
     per = -(-cap // LANES)
+    after = len(outs) * cap
+    pieces = [(after, rows - after)] + [(part * cap, cap) for part in range(len(outs))]
     copies = []
-    for source in range(n_from):
-        rows = blocks.at[source, pl.ds(part * cap, cap)]
-        nodes = blocks.at[source, pl.ds(begin, rest)]
-        copies.append(pltpu.make_async_copy(rows, mine.at[source, pl.ds(0, cap)], sems.at[0, source]))
-        copies.append(pltpu.make_async_copy(nodes, mine.at[source, pl.ds(cap, rest)], sems.at[1, source]))
-    for copy in copies:
-        copy.start()
+    for i, (begin, size) in enumerate(pieces):
+        here = pl.ds(begin, size)
+        copies.append(pltpu.make_async_copy(blocks.at[:, here], near.at[:, here], sems.at[i]))
+        copies[i].start()
     split[...] = jnp.zeros(split.shape, split.dtype)
-    for copy in copies:
-        copy.wait()
-    out[...] = summed(mine, [0], cap, [cap + part * per], chosen, split, out.shape[0])
+    copies[0].wait()
+    for part, out in enumerate(outs):
+        copies[1 + part].wait()
+        out[...] = summed(near, [part * cap], cap, [after + part * per], chosen, split, out.shape[0])
 
 
 def own_kernel(cap, height, flat, mine, sems):
@@ -621,18 +620,15 @@
     node_rows = jax.ShapeDtypeStruct((node_count, PTS), F32)
     from_pair = across(pair, 1)
     other_blocks = swap(other, "hgt")
-    sums = [
-        kernel(
-            functools.partial(collect_kernel, part, cap),
-            node_rows,
-            [pl.BlockSpec(memory_space=pl.ANY)],
-            [other_blocks],
-            f"collect_other_{part}",
-            1,
-            scratch=one_hot_space(n_hgt) + [vmem(n_hgt, cap + table_rows(n_col - 2, cap), PTS), sem((2, n_hgt))],
-        )
-        for part in range(n_col - 2)
-    ]
+    sums = kernel(
+        functools.partial(collect_kernel, cap),
+        (node_rows,) * (n_col - 2),
+        [pl.BlockSpec(memory_space=pl.ANY)],
+        [other_blocks],
+        "collect_other",
+        1,
+        scratch=one_hot_space(n_hgt) + [vmem(n_hgt, heights[2], PTS), sem((n_col - 1,))],
+    )
     parts = [across(sums[turn - 2], turn) for turn in range(2, n_col)]
     both = pltpu.HBM((n_hgt, 2 * cap + table_rows(2, cap), PTS), F32)
     mine = pl.pallas_call(

time: 141 us -> 141 us (level)
    pallas_call x21 -> x20, Pallas kernels: 30.7 us -> 29.4 us  [kernel(): pl.pallas_call(body, out_shape=outs, in_specs=ins, out_specs=jax.tree.map...]
  transfers between devices with their start and end apart: 21 -> 21, of which waited for: 11 -> 11; matrix products, arithmetic and copies ran while one was open for 0% -> 0% of each run, Pallas kernels for 21% -> 20%
where the time goes in v12:
time: 141 us; the launch traced here: 140 us
  waiting for transfers between devices  53.4 us (38%)
  starting transfers between devices  46.6 us (33%)
  Pallas kernels  38.6 us (27%)
    ppermute x16, starting transfers between devices, shifted(): return lax.ppermute(block, ('col', 'hgt'), route)  33.5 us
    pallas_call x20, Pallas kernels, kernel(): pl.pallas_call(body, out_shape=outs, in_specs=ins, out_specs=jax.tree.map...  29.4 us
    ppermute x16, waiting for transfers between devices, shifted(): return lax.ppermute(block, ('col', 'hgt'), route)  20.2 us
    ppermute x3, waiting for transfers between devices, across(): return lax.ppermute(x, 'col', [(c, c ^ turn) for c in range(n_col)])  18.5 us
    all_to_all x2, waiting for transfers between devices, swap(): return lax.all_to_all(x, axis, split_axis=0, concat_axis=0, tiled=True)  14.7 us
    all_to_all x2, starting transfers between devices, swap(): return lax.all_to_all(x, axis, split_axis=0, concat_axis=0, tiled=True)  8.38 us
    pallas_call x1, Pallas kernels, per_device(): pl.pallas_call(functools.partial(pack_kernel, heights), out_shape=(pltpu....  4.86 us
    ppermute x3, starting transfers between devices, across(): return lax.ppermute(x, 'col', [(c, c ^ turn) for c in range(n_col)])  4.74 us
  transfers between devices with their start and end apart: 21, of which 11 were waited for; matrix products, arithmetic and copies ran while one was open for 0% of the time, Pallas kernels for 20%

profile of v12, /device:TPU:0, one launch (start us, length us, event | category | flops | bytes accessed | tf_op | source)
XLA Modules:
  0.0 140.3 jit_solution(2893401739441371895)
XLA Ops:
  5.1 4.9 %load.1 = (f32[16,24,1024]{2,1,0:T(8,128)S(1)}, f32[16,24,1024]{2,1,0:T(8,128)S(1)}, f32[16,24,1024]{2,1,0:T(8,128)S(1)}, f32[3,16,24,1024]{3,2,1,0:T(8,128)S(1)...) custom-call(f32[16,24,1024]{2,1,0:T(8,128)} %temp_far.1, ...), custom_call_target="tpu_custom_call" | custom-call | flops 23592960 | bytes 23592960 | tf_op jit(solution)/shard_map/load/pallas_call | solution.py:492
  10.1 3.5 %collective-permute-done.1.col = f32[2,24,1024]{2,1,0:T(8,128)S(1)} collective-permute-done((f32[2,24,1024]{2,1,0:T(8,128)S(1)}, f32[2,24,1024]{2,1,0:T(8,128)S(1)}, u32[]{:S(2)}, u32[]{:S(2)}) %collective-permute-start.1) | collective-permute-done | bytes 196640 | tf_op jit(solution)/shard_map/ppermute | solution.py:469
  13.7 4.1 %collective-permute-start.3 = (f32[2,24,1024]{2,1,0:T(8,128)S(1)}, f32[2,24,1024]{2,1,0:T(8,128)S(1)}, u32[]{:S(2)}, u32[]{:S(2)}) collective-permute-start(f32[2,24,1024]{2,1,0:T(8,128)S(1)} %get-tuple-element.76), channel_id=1, source_target_pairs={{0,8},{1,9},{2,10},{3,11},{4,12},{5,13},{6,14},{7,15},{8,16},{9,17... | collective-permute-start | bytes 589832 | tf_op jit(solution)/shard_map/ppermute | solution.py:469
  19.6 1.9 %h_rest_0.1 = (f32[3,16,24,1024]{3,2,1,0:T(8,128)S(1)}, f32[3,16,1024]{2,1,0:T(8,128)S(1)}) custom-call(f32[3,16,24,1024]{3,2,1,0:T(8,128)S(1)} %get-tuple-element.64.e.refs_0_, f32[2,16,1024]{2,1,0:T(8,128)S(1)} %collective-permute-done.hgt, f32[3,16,24,1024]{3,2,1,0:T(8,128)S(1)} %get-tuple-element.70.h_old), custom_call_target="tpu_custom_call", output_to_operand_aliasing={{0}: (2, {})} | custom-call | flops 15728640 | bytes 15728640 | tf_op jit(solution)/shard_map/h_rest_0/pallas_call | solution.py:492
  25.1 2.2 %e_rest_0.1 = (f32[3,16,24,1024]{3,2,1,0:T(8,128)S(1)}, f32[16,24,1024]{2,1,0:T(8,128)S(1)}, f32[3,16,1024]{2,1,0:T(8,128)S(1)}) custom-call(f32[3,16,24,1024]{3,2,1,0:T(8,128)S(1)} %get-tuple-element.71.h.h_old, f32[16,24,1024]{2,1,0:T(8,128)S(1)} %get-tuple-element.72.ca, ...), custom_call_target="tpu_custom_call", output_to_operand_aliasing={{0}: (5, {}), {1}: (6, {})} | custom-call | flops 17694720 | bytes 17694720 | tf_op jit(solution)/shard_map/e_rest_0/pallas_call | solution.py:492
  27.9 4.7 %collective-permute-done.5.col = f32[2,24,1024]{2,1,0:T(8,128)S(1)} collective-permute-done((f32[2,24,1024]{2,1,0:T(8,128)S(1)}, f32[2,24,1024]{2,1,0:T(8,128)S(1)}, u32[]{:S(2)}, u32[]{:S(2)}) %collective-permute-start.5) | collective-permute-done | bytes 196640 | tf_op jit(solution)/shard_map/ppermute | solution.py:469
  32.7 3.5 %collective-permute-start.7 = (f32[2,24,1024]{2,1,0:T(8,128)S(1)}, f32[2,24,1024]{2,1,0:T(8,128)S(1)}, u32[]{:S(2)}, u32[]{:S(2)}) collective-permute-start(f32[2,24,1024]{2,1,0:T(8,128)S(1)} %get-tuple-element.88), channel_id=1, source_target_pairs={{0,8},{1,9},{2,10},{3,11},{4,12},{5,13},{6,14},{7,15},{8,16},{9,17... | collective-permute-start | bytes 589832 | tf_op jit(solution)/shard_map/ppermute | solution.py:469
  36.2 2.3 %collective-permute-start.6 = (f32[2,16,1024]{2,1,0:T(8,128)S(1)}, f32[2,16,1024]{2,1,0:T(8,128)S(1)}, u32[]{:S(2)}, u32[]{:S(2)}) collective-permute-start(f32[2,16,1024]{2,1,0:T(8,128)S(1)} %get-tuple-element.87.rows_old), channel_id=1, source_target_pairs={{0,1},{1,2},{2,3},{3,4},{4,5},{5,6},{6,7},{8,9},{9,10},{10,11},{11... | collective-permute-start | bytes 393224 | tf_op jit(solution)/shard_map/ppermute | solution.py:469
  43.9 2.3 %e_rest_1.1 = (f32[3,16,24,1024]{3,2,1,0:T(8,128)S(1)}, f32[16,24,1024]{2,1,0:T(8,128)S(1)}, f32[3,16,1024]{2,1,0:T(8,128)S(1)}) custom-call(f32[3,16,24,1024]{3,2,1,0:T(8,128)S(1)} %get-tuple-element.86.h.h_old, f32[16,24,1024]{2,1,0:T(8,128)S(1)} %get-tuple-element.72.ca, ...), custom_call_target="tpu_custom_call", output_to_operand_aliasing={{0}: (5, {}), {1}: (6, {})} | custom-call | flops 17694720 | bytes 17694720 | tf_op jit(solution)/shard_map/e_rest_1/pallas_call | solution.py:492
  46.2 4.4 %collective-permute-done.9.col = f32[2,24,1024]{2,1,0:T(8,128)S(1)} collective-permute-done((f32[2,24,1024]{2,1,0:T(8,128)S(1)}, f32[2,24,1024]{2,1,0:T(8,128)S(1)}, u32[]{:S(2)}, u32[]{:S(2)}) %collective-permute-start.9) | collective-permute-done | bytes 196640 | tf_op jit(solution)/shard_map/ppermute | solution.py:469
  50.7 3.6 %collective-permute-start.11 = (f32[2,24,1024]{2,1,0:T(8,128)S(1)}, f32[2,24,1024]{2,1,0:T(8,128)S(1)}, u32[]{:S(2)}, u32[]{:S(2)}) collective-permute-start(f32[2,24,1024]{2,1,0:T(8,128)S(1)} %get-tuple-element.100), channel_id=1, source_target_pairs={{0,8},{1,9},{2,10},{3,11},{4,12},{5,13},{6,14},{7,15},{8,16},{9,17... | collective-permute-start | bytes 589832 | tf_op jit(solution)/shard_map/ppermute | solution.py:469
  54.3 2.1 %collective-permute-start.10 = (f32[2,16,1024]{2,1,0:T(8,128)S(1)}, f32[2,16,1024]{2,1,0:T(8,128)S(1)}, u32[]{:S(2)}, u32[]{:S(2)}) collective-permute-start(f32[2,16,1024]{2,1,0:T(8,128)S(1)} %get-tuple-element.99.rows_old), channel_id=1, source_target_pairs={{0,1},{1,2},{2,3},{3,4},{4,5},{5,6},{6,7},{8,9},{9,10},{10,11},{11... | collective-permute-start | bytes 393224 | tf_op jit(solution)/shard_map/ppermute | solution.py:469
  61.9 2.3 %e_rest_2.1 = (f32[3,16,24,1024]{3,2,1,0:T(8,128)S(1)}, f32[16,24,1024]{2,1,0:T(8,128)S(1)}, f32[3,16,1024]{2,1,0:T(8,128)S(1)}) custom-call(f32[3,16,24,1024]{3,2,1,0:T(8,128)S(1)} %get-tuple-element.98.h.h_old, f32[16,24,1024]{2,1,0:T(8,128)S(1)} %get-tuple-element.72.ca, ...), custom_call_target="tpu_custom_call", output_to_operand_aliasing={{0}: (5, {}), {1}: (6, {})} | custom-call | flops 17694720 | bytes 17694720 | tf_op jit(solution)/shard_map/e_rest_2/pallas_call | solution.py:492
  64.4 4.7 %collective-permute-done.13.col = f32[2,24,1024]{2,1,0:T(8,128)S(1)} collective-permute-done((f32[2,24,1024]{2,1,0:T(8,128)S(1)}, f32[2,24,1024]{2,1,0:T(8,128)S(1)}, u32[]{:S(2)}, u32[]{:S(2)}) %collective-permute-start.13) | collective-permute-done | bytes 196640 | tf_op jit(solution)/shard_map/ppermute | solution.py:469
  69.2 3.1 %collective-permute-start.14 = (f32[2,24,1024]{2,1,0:T(8,128)S(1)}, f32[2,24,1024]{2,1,0:T(8,128)S(1)}, u32[]{:S(2)}, u32[]{:S(2)}) collective-permute-start(f32[2,24,1024]{2,1,0:T(8,128)S(1)} %get-tuple-element.110), channel_id=1, source_target_pairs={{0,8},{1,9},{2,10},{3,11},{4,12},{5,13},{6,14},{7,15},{8,16},{9,17... | collective-permute-start | bytes 589832 | tf_op jit(solution)/shard_map/ppermute | solution.py:469
  72.3 2.7 %collective-permute-start.15 = (f32[2,16,1024]{2,1,0:T(8,128)S(1)}, f32[2,16,1024]{2,1,0:T(8,128)S(1)}, u32[]{:S(2)}, u32[]{:S(2)}) collective-permute-start(f32[2,16,1024]{2,1,0:T(8,128)S(1)} %get-tuple-element.111), channel_id=1, source_target_pairs={{0,1},{1,2},{2,3},{3,4},{4,5},{5,6},{6,7},{8,9},{9,10},{10,11},{11... | collective-permute-start | bytes 393224 | tf_op jit(solution)/shard_map/ppermute | solution.py:469
  75.0 2.2 %places.1 = (s32[1,3072]{1,0:T(1,128)S(1)}, f32[6336,128]{1,0:T(8,128)S(1)}) custom-call(s32[1]{0:T(128)} %bitcast.my_col, s32[1,3072]{1,0:T(1,128)S(1)} %reshape.46.owner, s32[1,3072]{1,0:T(1,128)S(1)} %reshape.47.node), custom_call_target="tpu_custom_call" | custom-call | flops 3145728 | bytes 3145728 | tf_op jit(solution)/shard_map/places/pallas_call | solution.py:492
  79.1 2.3 %e_last.1 = (f32[3,16,24,1024]{3,2,1,0:T(8,128)S(1)}, f32[16,24,1024]{2,1,0:T(8,128)S(1)}, f32[3,16,24,1024]{3,2,1,0:T(8,128)}) custom-call(f32[3,16,24,1024]{3,2,1,0:T(8,128)S(1)} %h_rest_3.1.h, f32[16,24,1024]{2,1,0:T(8,128)S(1)} %get-tuple-element.72.ca, f32[16,24,1024]{2,1,0:T(8,128)S(1)} %get-tuple-element.73.cb, ...), custom_call_target="tpu_custom_call", output_to_operand_aliasing={{0}: (6, {}), {1}: (7, {})} | custom-call | flops 19660800 | bytes 19660800 | tf_op jit(solution)/shard_map/e_last/pallas_call | solution.py:558
  81.4 4.9 %pack.1 = (f32[8,200,128]{2,1,0:T(8,128)}, f32[8,392,128]{2,1,0:T(8,128)}, f32[3,16,24,1024]{3,2,1,0:T(8,128)}, f32[6336,128]{1,0:T(8,128)S(1)}) custom-call(s32[3072]{0:T(1024)S(1)} %bitcast.8, f32[16,24,1024]{2,1,0:T(8,128)S(1)} %get-tuple-element.113.power, f32[6336,128]{1,0:T(8,128)S(1)} %get-tuple-element.114.flat_old, ...), custom_call_target="tpu_custom_call", output_to_operand_aliasing={{3}: (2, {})} | custom-call | flops 393216 | bytes 14155776 | tf_op jit(solution)/shard_map/pack/pallas_call | solution.py:593
  86.3 4.3 %all-to-all-start.1 = ((f32[8,392,128]{2,1,0:T(8,128)}), f32[8,392,128]{2,1,0:T(8,128)}, u32[]{:S(2)}, u32[]{:S(2)}) async-start(f32[8,392,128]{2,1,0:T(8,128)} %get-tuple-element.120), calls=%async_computation.1 | async-start | bytes 3211264 | tf_op jit(solution)/shard_map/all_to_all | solution.py:611
  92.8 18.5 %collective-permute-done.16.pair = f32[8,200,128]{2,1,0:T(8,128)S(1)} collective-permute-done((f32[8,200,128]{2,1,0:T(8,128)}, f32[8,200,128]{2,1,0:T(8,128)S(1)}, u32[]{:S(2)}, u32[]{:S(2)}) %collective-permute-start.16) | collective-permute-done | bytes 819232 | tf_op jit(solution)/shard_map/ppermute | solution.py:614
  112.4 4.1 %all-to-all-start = ((f32[8,392,128]{2,1,0:T(8,128)}), f32[8,392,128]{2,1,0:T(8,128)S(1)}, u32[]{:S(2)}, u32[]{:S(2)}) async-start(f32[8,392,128]{2,1,0:T(8,128)} %merge.1), calls=%async_computation | async-start | bytes 3211264 | tf_op jit(solution)/shard_map/all_to_all | solution.py:611
  116.5 3.2 %collect_other.1 = (f32[384,128]{1,0:T(8,128)S(1)}, f32[384,128]{1,0:T(8,128)S(1)}) custom-call(f32[8,392,128]{2,1,0:T(8,128)} %all-to-all-done.1.blocks), custom_call_target="tpu_custom_call" | custom-call | flops 393216 | bytes 393216 | tf_op jit(solution)/shard_map/collect_other/pallas_call | solution.py:492
  123.2 14.7 %all-to-all-done.blocks = f32[8,392,128]{2,1,0:T(8,128)S(1)} async-done(((f32[8,392,128]{2,1,0:T(8,128)}), f32[8,392,128]{2,1,0:T(8,128)S(1)}, u32[]{:S(2)}, u32[]{:S(2)}) %all-to-all-start) | async-done | bytes 1605664 | tf_op jit(solution)/shard_map/all_to_all | solution.py:611
  (53 shorter events, 32.9 us)
Async XLA Ops:
  0.6 3.9 %copy-start.1 = (s32[1,1,16,24,8,1]{3,5,4,2,1,0:T(1,128)S(1)}, s32[1,1,16,24,8,1]{3,5,4,2,1,0:T(1,128)}, u32[]{:S(2)}) copy-start(s32[1,1,16,24,8,1]{3,5,4,2,1,0:T(1,128)} %param.11) | copy-start | bytes 36868
  0.6 4.2 %copy-start.2 = (s32[1,1,16,24,8]{3,4,2,1,0:T(8,128)S(1)}, s32[1,1,16,24,8]{3,4,2,1,0:T(8,128)}, u32[]{:S(2)}) copy-start(s32[1,1,16,24,8]{3,4,2,1,0:T(8,128)} %param.12) | copy-start | bytes 36868
  2.0 8.1 %collective-permute-start = (f32[2,16,1024]{2,1,0:T(8,128)S(1)}, f32[2,16,1024]{2,1,0:T(8,128)S(1)}, u32[]{:S(2)}, u32[]{:S(2)}) collective-permute-start(f32[2,16,1024]{2,1,0:T(8,128)S(1)} %get-tuple-element.65.rows_old), channel_id=1, source_target_pairs={{1,0},{2,1},{3,2},{4,3},{5,4},{6,5},{7,6},{9,8},{10,9},{11,10},{12... | collective-permute-start | bytes 393224 | tf_op jit(solution)/shard_map/ppermute | solution.py:469
  3.3 10.3 %collective-permute-start.1 = (f32[2,24,1024]{2,1,0:T(8,128)S(1)}, f32[2,24,1024]{2,1,0:T(8,128)S(1)}, u32[]{:S(2)}, u32[]{:S(2)}) collective-permute-start(f32[2,24,1024]{2,1,0:T(8,128)S(1)} %get-tuple-element.66), channel_id=1, source_target_pairs={{8,0},{9,1},{10,2},{11,3},{12,4},{13,5},{14,6},{15,7},{16,8},{17,9... | collective-permute-start | bytes 589832 | tf_op jit(solution)/shard_map/ppermute | solution.py:469
  13.7 8.5 %collective-permute-start.3 = (f32[2,24,1024]{2,1,0:T(8,128)S(1)}, f32[2,24,1024]{2,1,0:T(8,128)S(1)}, u32[]{:S(2)}, u32[]{:S(2)}) collective-permute-start(f32[2,24,1024]{2,1,0:T(8,128)S(1)} %get-tuple-element.76), channel_id=1, source_target_pairs={{0,8},{1,9},{2,10},{3,11},{4,12},{5,13},{6,14},{7,15},{8,16},{9,17... | collective-permute-start | bytes 589832 | tf_op jit(solution)/shard_map/ppermute | solution.py:469
  17.9 3.7 %collective-permute-start.2 = (f32[2,16,1024]{2,1,0:T(8,128)S(1)}, f32[2,16,1024]{2,1,0:T(8,128)S(1)}, u32[]{:S(2)}, u32[]{:S(2)}) collective-permute-start(f32[2,16,1024]{2,1,0:T(8,128)S(1)} %get-tuple-element.75.rows_old), channel_id=1, source_target_pairs={{0,1},{1,2},{2,3},{3,4},{4,5},{5,6},{6,7},{8,9},{9,10},{10,11},{11... | collective-permute-start | bytes 393224 | tf_op jit(solution)/shard_map/ppermute | solution.py:469
  22.5 10.1 %collective-permute-start.5 = (f32[2,24,1024]{2,1,0:T(8,128)S(1)}, f32[2,24,1024]{2,1,0:T(8,128)S(1)}, u32[]{:S(2)}, u32[]{:S(2)}) collective-permute-start(f32[2,24,1024]{2,1,0:T(8,128)S(1)} %get-tuple-element.83), channel_id=1, source_target_pairs={{8,0},{9,1},{10,2},{11,3},{12,4},{13,5},{14,6},{15,7},{16,8},{17,9... | collective-permute-start | bytes 589832 | tf_op jit(solution)/shard_map/ppermute | solution.py:469
  23.8 4.1 %collective-permute-start.4 = (f32[2,16,1024]{2,1,0:T(8,128)S(1)}, f32[2,16,1024]{2,1,0:T(8,128)S(1)}, u32[]{:S(2)}, u32[]{:S(2)}) collective-permute-start(f32[2,16,1024]{2,1,0:T(8,128)S(1)} %get-tuple-element.82.rows_old), channel_id=1, source_target_pairs={{1,0},{2,1},{3,2},{4,3},{5,4},{6,5},{7,6},{9,8},{10,9},{11,10},{12... | collective-permute-start | bytes 393224 | tf_op jit(solution)/shard_map/ppermute | solution.py:469
  32.7 8.4 %collective-permute-start.7 = (f32[2,24,1024]{2,1,0:T(8,128)S(1)}, f32[2,24,1024]{2,1,0:T(8,128)S(1)}, u32[]{:S(2)}, u32[]{:S(2)}) collective-permute-start(f32[2,24,1024]{2,1,0:T(8,128)S(1)} %get-tuple-element.88), channel_id=1, source_target_pairs={{0,8},{1,9},{2,10},{3,11},{4,12},{5,13},{6,14},{7,15},{8,16},{9,17... | collective-permute-start | bytes 589832 | tf_op jit(solution)/shard_map/ppermute | solution.py:469
  36.2 4.2 %collective-permute-start.6 = (f32[2,16,1024]{2,1,0:T(8,128)S(1)}, f32[2,16,1024]{2,1,0:T(8,128)S(1)}, u32[]{:S(2)}, u32[]{:S(2)}) collective-permute-start(f32[2,16,1024]{2,1,0:T(8,128)S(1)} %get-tuple-element.87.rows_old), channel_id=1, source_target_pairs={{0,1},{1,2},{2,3},{3,4},{4,5},{5,6},{6,7},{8,9},{9,10},{10,11},{11... | collective-permute-start | bytes 393224 | tf_op jit(solution)/shard_map/ppermute | solution.py:469
  41.3 9.3 %collective-permute-start.9 = (f32[2,24,1024]{2,1,0:T(8,128)S(1)}, f32[2,24,1024]{2,1,0:T(8,128)S(1)}, u32[]{:S(2)}, u32[]{:S(2)}) collective-permute-start(f32[2,24,1024]{2,1,0:T(8,128)S(1)} %get-tuple-element.95), channel_id=1, source_target_pairs={{8,0},{9,1},{10,2},{11,3},{12,4},{13,5},{14,6},{15,7},{16,8},{17,9... | collective-permute-start | bytes 589832 | tf_op jit(solution)/shard_map/ppermute | solution.py:469
  42.6 3.6 %collective-permute-start.8 = (f32[2,16,1024]{2,1,0:T(8,128)S(1)}, f32[2,16,1024]{2,1,0:T(8,128)S(1)}, u32[]{:S(2)}, u32[]{:S(2)}) collective-permute-start(f32[2,16,1024]{2,1,0:T(8,128)S(1)} %get-tuple-element.94.rows_old), channel_id=1, source_target_pairs={{1,0},{2,1},{3,2},{4,3},{5,4},{6,5},{7,6},{9,8},{10,9},{11,10},{12... | collective-permute-start | bytes 393224 | tf_op jit(solution)/shard_map/ppermute | solution.py:469
  50.7 8.4 %collective-permute-start.11 = (f32[2,24,1024]{2,1,0:T(8,128)S(1)}, f32[2,24,1024]{2,1,0:T(8,128)S(1)}, u32[]{:S(2)}, u32[]{:S(2)}) collective-permute-start(f32[2,24,1024]{2,1,0:T(8,128)S(1)} %get-tuple-element.100), channel_id=1, source_target_pairs={{0,8},{1,9},{2,10},{3,11},{4,12},{5,13},{6,14},{7,15},{8,16},{9,17... | collective-permute-start | bytes 589832 | tf_op jit(solution)/shard_map/ppermute | solution.py:469
  54.3 4.1 %collective-permute-start.10 = (f32[2,16,1024]{2,1,0:T(8,128)S(1)}, f32[2,16,1024]{2,1,0:T(8,128)S(1)}, u32[]{:S(2)}, u32[]{:S(2)}) collective-permute-start(f32[2,16,1024]{2,1,0:T(8,128)S(1)} %get-tuple-element.99.rows_old), channel_id=1, source_target_pairs={{0,1},{1,2},{2,3},{3,4},{4,5},{5,6},{6,7},{8,9},{9,10},{10,11},{11... | collective-permute-start | bytes 393224 | tf_op jit(solution)/shard_map/ppermute | solution.py:469
  59.3 9.8 %collective-permute-start.13 = (f32[2,24,1024]{2,1,0:T(8,128)S(1)}, f32[2,24,1024]{2,1,0:T(8,128)S(1)}, u32[]{:S(2)}, u32[]{:S(2)}) collective-permute-start(f32[2,24,1024]{2,1,0:T(8,128)S(1)} %get-tuple-element.107), channel_id=1, source_target_pairs={{8,0},{9,1},{10,2},{11,3},{12,4},{13,5},{14,6},{15,7},{16,8},{17,9... | collective-permute-start | bytes 589832 | tf_op jit(solution)/shard_map/ppermute | solution.py:469
  60.6 3.8 %collective-permute-start.12 = (f32[2,16,1024]{2,1,0:T(8,128)S(1)}, f32[2,16,1024]{2,1,0:T(8,128)S(1)}, u32[]{:S(2)}, u32[]{:S(2)}) collective-permute-start(f32[2,16,1024]{2,1,0:T(8,128)S(1)} %get-tuple-element.106), channel_id=1, source_target_pairs={{1,0},{2,1},{3,2},{4,3},{5,4},{6,5},{7,6},{9,8},{10,9},{11,10},{12... | collective-permute-start | bytes 393224 | tf_op jit(solution)/shard_map/ppermute | solution.py:469
  69.2 9.8 %collective-permute-start.14 = (f32[2,24,1024]{2,1,0:T(8,128)S(1)}, f32[2,24,1024]{2,1,0:T(8,128)S(1)}, u32[]{:S(2)}, u32[]{:S(2)}) collective-permute-start(f32[2,24,1024]{2,1,0:T(8,128)S(1)} %get-tuple-element.110), channel_id=1, source_target_pairs={{0,8},{1,9},{2,10},{3,11},{4,12},{5,13},{6,14},{7,15},{8,16},{9,17... | collective-permute-start | bytes 589832 | tf_op jit(solution)/shard_map/ppermute | solution.py:469
  72.3 6.8 %collective-permute-start.15 = (f32[2,16,1024]{2,1,0:T(8,128)S(1)}, f32[2,16,1024]{2,1,0:T(8,128)S(1)}, u32[]{:S(2)}, u32[]{:S(2)}) collective-permute-start(f32[2,16,1024]{2,1,0:T(8,128)S(1)} %get-tuple-element.111), channel_id=1, source_target_pairs={{0,1},{1,2},{2,3},{3,4},{4,5},{5,6},{6,7},{8,9},{9,10},{10,11},{11... | collective-permute-start | bytes 393224 | tf_op jit(solution)/shard_map/ppermute | solution.py:469
  86.3 26.1 %all-to-all-start.1 = ((f32[8,392,128]{2,1,0:T(8,128)}), f32[8,392,128]{2,1,0:T(8,128)}, u32[]{:S(2)}, u32[]{:S(2)}) async-start(f32[8,392,128]{2,1,0:T(8,128)} %get-tuple-element.120), calls=%async_computation.1 | async-start | bytes 3211264 | tf_op jit(solution)/shard_map/all_to_all | solution.py:611
  90.6 20.7 %collective-permute-start.16 = (f32[8,200,128]{2,1,0:T(8,128)}, f32[8,200,128]{2,1,0:T(8,128)S(1)}, u32[]{:S(2)}, u32[]{:S(2)}) collective-permute-start(f32[8,200,128]{2,1,0:T(8,128)} %get-tuple-element.119), channel_id=1, source_target_pairs={{0,8},{8,0},{16,24},{24,16},{1,9},{9,1},{17,25},{25,17},{2,10},{10... | collective-permute-start | bytes 2457608 | tf_op jit(solution)/shard_map/ppermute | solution.py:614
  112.4 27.2 %copy-start = (f32[384,128]{1,0:T(8,128)S(1)}, f32[384,128]{1,0:T(8,128)}, u32[]{:S(2)}) copy-start(f32[384,128]{1,0:T(8,128)} %enthalpy.1) | copy-start | bytes 589828
  112.4 25.4 %all-to-all-start = ((f32[8,392,128]{2,1,0:T(8,128)}), f32[8,392,128]{2,1,0:T(8,128)S(1)}, u32[]{:S(2)}, u32[]{:S(2)}) async-start(f32[8,392,128]{2,1,0:T(8,128)} %merge.1), calls=%async_computation | async-start | bytes 3211264 | tf_op jit(solution)/shard_map/all_to_all | solution.py:611
  119.6 19.9 %collective-permute-start.17 = (f32[384,128]{1,0:T(8,128)S(1)}, f32[384,128]{1,0:T(8,128)S(1)}, u32[]{:S(2)}, u32[]{:S(2)}) collective-permute-start(f32[384,128]{1,0:T(8,128)S(1)} %get-tuple-element.121), channel_id=1, source_target_pairs={{0,16},{8,24},{16,0},{24,8},{1,17},{9,25},{17,1},{25,9},{2,18},{10... | collective-permute-start | bytes 589832 | tf_op jit(solution)/shard_map/ppermute | solution.py:614
  121.4 18.1 %collective-permute-start.18 = (f32[384,128]{1,0:T(8,128)S(1)}, f32[384,128]{1,0:T(8,128)S(1)}, u32[]{:S(2)}, u32[]{:S(2)}) collective-permute-start(f32[384,128]{1,0:T(8,128)S(1)} %get-tuple-element.122), channel_id=1, source_target_pairs={{0,24},{8,16},{16,8},{24,0},{1,25},{9,17},{17,9},{25,1},{2,26},{10... | collective-permute-start | bytes 589832 | tf_op jit(solution)/shard_map/ppermute | solution.py:614

commit v13 on v12

--- a/solution.py
+++ b/solution.py
@@ -392,12 +392,12 @@
     return both[:, 0:pts] + both[:, pts : 2 * pts]
 
 
-def collect_kernel(cap, blocks, *refs):
+def collect_kernel(cap, parts, n_part, blocks, *refs):
     *outs, chosen, split, near, sems = refs
-    n_from, rows, _ = blocks.shape
+    rows = blocks.shape[1]
     per = -(-cap // LANES)
-    after = len(outs) * cap
-    pieces = [(after, rows - after)] + [(part * cap, cap) for part in range(len(outs))]
+    after = n_part * cap
+    pieces = [(after, rows - after)] + [(part * cap, cap) for part in parts]
     copies = []
     for i, (begin, size) in enumerate(pieces):
         here = pl.ds(begin, size)
@@ -405,9 +405,15 @@
         copies[i].start()
     split[...] = jnp.zeros(split.shape, split.dtype)
     copies[0].wait()
-    for part, out in enumerate(outs):
-        copies[1 + part].wait()
+    for i, (part, out) in enumerate(zip(parts, outs)):
+        copies[1 + i].wait()
         out[...] = summed(near, [part * cap], cap, [after + part * per], chosen, split, out.shape[0])
+
+
+def add_kernel(*refs):
+    n = len(refs) // 3
+    for own, other, out in zip(refs[:n], refs[n : 2 * n], refs[2 * n :]):
+        out[...] = own[...] + other[...]
 
 
 def own_kernel(cap, height, flat, mine, sems):
@@ -620,16 +626,24 @@
     node_rows = jax.ShapeDtypeStruct((node_count, PTS), F32)
     from_pair = across(pair, 1)
     other_blocks = swap(other, "hgt")
+    def collect(turns, name):
+        return kernel(
+            functools.partial(collect_kernel, cap, [turn - 2 for turn in turns], n_col - 2),
+            (node_rows,) * len(turns),
+            [pl.BlockSpec(memory_space=pl.ANY)],
+            [other_blocks],
+            name,
+            8,
+            scratch=one_hot_space(n_hgt) + [vmem(n_hgt, heights[2], PTS), sem((1 + len(turns),))],
+        )
+
+    turns = list(range(2, n_col, 2))
+    swapped = [across(part, 1) for part in collect([turn + 1 for turn in turns], "collect_odd")]
+    kept = collect(turns, "collect_even")
     sums = kernel(
-        functools.partial(collect_kernel, cap),
-        (node_rows,) * (n_col - 2),
-        [pl.BlockSpec(memory_space=pl.ANY)],
-        [other_blocks],
-        "collect_other",
-        1,
-        scratch=one_hot_space(n_hgt) + [vmem(n_hgt, heights[2], PTS), sem((n_col - 1,))],
+        add_kernel, (node_rows,) * len(turns), [WHOLE] * (2 * len(turns)), [*kept, *swapped], "add", 1
     )
-    parts = [across(sums[turn - 2], turn) for turn in range(2, n_col)]
+    parts = [across(part, turn) for part, turn in zip(sums, turns)]
     both = pltpu.HBM((n_hgt, 2 * cap + table_rows(2, cap), PTS), F32)
     mine = pl.pallas_call(
         functools.partial(own_kernel, cap, heights[0]),
@@ -663,7 +677,7 @@
         scratch=one_hot_space(2 * n_hgt),
     )
     node_temp = kernel(
-        finish_kernel, node_rows, [WHOLE] * (n_col), [node_enthalpy, own, *parts], "finish", 1
+        finish_kernel, node_rows, [WHOLE] * (2 + len(parts)), [node_enthalpy, own, *parts], "finish", 1
     )
     return e_out, h_out, node_temp
 

time: 141 us -> 141 us (level)
    all_to_all x2, waiting for transfers between devices: 14.7 us -> 10.3 us  [swap(): return lax.all_to_all(x, axis, split_axis=0, concat_axis=0, tiled=True)]
    ppermute x3, waiting for transfers between devices: 18.5 us -> 22.7 us  [across(): return lax.ppermute(x, 'col', [(c, c ^ turn) for c in range(n_col)])]
    pallas_call x20 -> x22, Pallas kernels: 29.4 us -> 30.3 us  [kernel(): pl.pallas_call(body, out_shape=outs, in_specs=ins, out_specs=jax.tree.map...]
  transfers between devices with their start and end apart: 21 -> 21, of which waited for: 11 -> 12; matrix products, arithmetic and copies ran while one was open for 0% -> 0% of each run, Pallas kernels for 20% -> 21%
where the time goes in v13:
time: 141 us; the launch traced here: 140 us
  waiting for transfers between devices  53.2 us (38%)
  starting transfers between devices  45.9 us (33%)
  Pallas kernels  39.6 us (28%)
    ppermute x16, starting transfers between devices, shifted(): return lax.ppermute(block, ('col', 'hgt'), route)  33.5 us
    pallas_call x22, Pallas kernels, kernel(): pl.pallas_call(body, out_shape=outs, in_specs=ins, out_specs=jax.tree.map...  30.3 us
    ppermute x3, waiting for transfers between devices, across(): return lax.ppermute(x, 'col', [(c, c ^ turn) for c in range(n_col)])  22.7 us
    ppermute x16, waiting for transfers between devices, shifted(): return lax.ppermute(block, ('col', 'hgt'), route)  20.2 us
    all_to_all x2, waiting for transfers between devices, swap(): return lax.all_to_all(x, axis, split_axis=0, concat_axis=0, tiled=True)  10.3 us
    all_to_all x2, starting transfers between devices, swap(): return lax.all_to_all(x, axis, split_axis=0, concat_axis=0, tiled=True)  8.37 us
    pallas_call x1, Pallas kernels, per_device(): pl.pallas_call(functools.partial(pack_kernel, heights), out_shape=(pltpu....  4.86 us
    ppermute x3, starting transfers between devices, across(): return lax.ppermute(x, 'col', [(c, c ^ turn) for c in range(n_col)])  4.08 us
  transfers between devices with their start and end apart: 21, of which 12 were waited for; matrix products, arithmetic and copies ran while one was open for 0% of the time, Pallas kernels for 21%

profile of v13, /device:TPU:0, one launch (start us, length us, event | category | flops | bytes accessed | tf_op | source)
XLA Modules:
  0.0 140.3 jit_solution(1527597130138293409)
XLA Ops:
  5.1 4.9 %load.1 = (f32[16,24,1024]{2,1,0:T(8,128)S(1)}, f32[16,24,1024]{2,1,0:T(8,128)S(1)}, f32[16,24,1024]{2,1,0:T(8,128)S(1)}, f32[3,16,24,1024]{3,2,1,0:T(8,128)S(1)...) custom-call(f32[16,24,1024]{2,1,0:T(8,128)} %temp_far.1, ...), custom_call_target="tpu_custom_call" | custom-call | flops 23592960 | bytes 23592960 | tf_op jit(solution)/shard_map/load/pallas_call | solution.py:498
  10.1 3.5 %collective-permute-done.1.col = f32[2,24,1024]{2,1,0:T(8,128)S(1)} collective-permute-done((f32[2,24,1024]{2,1,0:T(8,128)S(1)}, f32[2,24,1024]{2,1,0:T(8,128)S(1)}, u32[]{:S(2)}, u32[]{:S(2)}) %collective-permute-start.1) | collective-permute-done | bytes 196640 | tf_op jit(solution)/shard_map/ppermute | solution.py:475
  13.7 4.1 %collective-permute-start.3 = (f32[2,24,1024]{2,1,0:T(8,128)S(1)}, f32[2,24,1024]{2,1,0:T(8,128)S(1)}, u32[]{:S(2)}, u32[]{:S(2)}) collective-permute-start(f32[2,24,1024]{2,1,0:T(8,128)S(1)} %get-tuple-element.74), channel_id=1, source_target_pairs={{0,8},{1,9},{2,10},{3,11},{4,12},{5,13},{6,14},{7,15},{8,16},{9,17... | collective-permute-start | bytes 589832 | tf_op jit(solution)/shard_map/ppermute | solution.py:475
  25.1 2.2 %e_rest_0.1 = (f32[3,16,24,1024]{3,2,1,0:T(8,128)S(1)}, f32[16,24,1024]{2,1,0:T(8,128)S(1)}, f32[3,16,1024]{2,1,0:T(8,128)S(1)}) custom-call(f32[3,16,24,1024]{3,2,1,0:T(8,128)S(1)} %get-tuple-element.69.h.h_old, f32[16,24,1024]{2,1,0:T(8,128)S(1)} %get-tuple-element.70.ca, ...), custom_call_target="tpu_custom_call", output_to_operand_aliasing={{0}: (5, {}), {1}: (6, {})} | custom-call | flops 17694720 | bytes 17694720 | tf_op jit(solution)/shard_map/e_rest_0/pallas_call | solution.py:498
  27.9 4.7 %collective-permute-done.5.col = f32[2,24,1024]{2,1,0:T(8,128)S(1)} collective-permute-done((f32[2,24,1024]{2,1,0:T(8,128)S(1)}, f32[2,24,1024]{2,1,0:T(8,128)S(1)}, u32[]{:S(2)}, u32[]{:S(2)}) %collective-permute-start.5) | collective-permute-done | bytes 196640 | tf_op jit(solution)/shard_map/ppermute | solution.py:475
  32.7 3.5 %collective-permute-start.7 = (f32[2,24,1024]{2,1,0:T(8,128)S(1)}, f32[2,24,1024]{2,1,0:T(8,128)S(1)}, u32[]{:S(2)}, u32[]{:S(2)}) collective-permute-start(f32[2,24,1024]{2,1,0:T(8,128)S(1)} %get-tuple-element.86), channel_id=1, source_target_pairs={{0,8},{1,9},{2,10},{3,11},{4,12},{5,13},{6,14},{7,15},{8,16},{9,17... | collective-permute-start | bytes 589832 | tf_op jit(solution)/shard_map/ppermute | solution.py:475
  36.2 2.3 %collective-permute-start.6 = (f32[2,16,1024]{2,1,0:T(8,128)S(1)}, f32[2,16,1024]{2,1,0:T(8,128)S(1)}, u32[]{:S(2)}, u32[]{:S(2)}) collective-permute-start(f32[2,16,1024]{2,1,0:T(8,128)S(1)} %get-tuple-element.85.rows_old), channel_id=1, source_target_pairs={{0,1},{1,2},{2,3},{3,4},{4,5},{5,6},{6,7},{8,9},{9,10},{10,11},{11... | collective-permute-start | bytes 393224 | tf_op jit(solution)/shard_map/ppermute | solution.py:475
  43.9 2.3 %e_rest_1.1 = (f32[3,16,24,1024]{3,2,1,0:T(8,128)S(1)}, f32[16,24,1024]{2,1,0:T(8,128)S(1)}, f32[3,16,1024]{2,1,0:T(8,128)S(1)}) custom-call(f32[3,16,24,1024]{3,2,1,0:T(8,128)S(1)} %get-tuple-element.84.h.h_old, f32[16,24,1024]{2,1,0:T(8,128)S(1)} %get-tuple-element.70.ca, ...), custom_call_target="tpu_custom_call", output_to_operand_aliasing={{0}: (5, {}), {1}: (6, {})} | custom-call | flops 17694720 | bytes 17694720 | tf_op jit(solution)/shard_map/e_rest_1/pallas_call | solution.py:498
  46.2 4.4 %collective-permute-done.9.col = f32[2,24,1024]{2,1,0:T(8,128)S(1)} collective-permute-done((f32[2,24,1024]{2,1,0:T(8,128)S(1)}, f32[2,24,1024]{2,1,0:T(8,128)S(1)}, u32[]{:S(2)}, u32[]{:S(2)}) %collective-permute-start.9) | collective-permute-done | bytes 196640 | tf_op jit(solution)/shard_map/ppermute | solution.py:475
  50.7 3.6 %collective-permute-start.11 = (f32[2,24,1024]{2,1,0:T(8,128)S(1)}, f32[2,24,1024]{2,1,0:T(8,128)S(1)}, u32[]{:S(2)}, u32[]{:S(2)}) collective-permute-start(f32[2,24,1024]{2,1,0:T(8,128)S(1)} %get-tuple-element.98), channel_id=1, source_target_pairs={{0,8},{1,9},{2,10},{3,11},{4,12},{5,13},{6,14},{7,15},{8,16},{9,17... | collective-permute-start | bytes 589832 | tf_op jit(solution)/shard_map/ppermute | solution.py:475
  54.3 2.1 %collective-permute-start.10 = (f32[2,16,1024]{2,1,0:T(8,128)S(1)}, f32[2,16,1024]{2,1,0:T(8,128)S(1)}, u32[]{:S(2)}, u32[]{:S(2)}) collective-permute-start(f32[2,16,1024]{2,1,0:T(8,128)S(1)} %get-tuple-element.97.rows_old), channel_id=1, source_target_pairs={{0,1},{1,2},{2,3},{3,4},{4,5},{5,6},{6,7},{8,9},{9,10},{10,11},{11... | collective-permute-start | bytes 393224 | tf_op jit(solution)/shard_map/ppermute | solution.py:475
  61.9 2.3 %e_rest_2.1 = (f32[3,16,24,1024]{3,2,1,0:T(8,128)S(1)}, f32[16,24,1024]{2,1,0:T(8,128)S(1)}, f32[3,16,1024]{2,1,0:T(8,128)S(1)}) custom-call(f32[3,16,24,1024]{3,2,1,0:T(8,128)S(1)} %get-tuple-element.96.h.h_old, f32[16,24,1024]{2,1,0:T(8,128)S(1)} %get-tuple-element.70.ca, ...), custom_call_target="tpu_custom_call", output_to_operand_aliasing={{0}: (5, {}), {1}: (6, {})} | custom-call | flops 17694720 | bytes 17694720 | tf_op jit(solution)/shard_map/e_rest_2/pallas_call | solution.py:498
  64.4 4.7 %collective-permute-done.13.col = f32[2,24,1024]{2,1,0:T(8,128)S(1)} collective-permute-done((f32[2,24,1024]{2,1,0:T(8,128)S(1)}, f32[2,24,1024]{2,1,0:T(8,128)S(1)}, u32[]{:S(2)}, u32[]{:S(2)}) %collective-permute-start.13) | collective-permute-done | bytes 196640 | tf_op jit(solution)/shard_map/ppermute | solution.py:475
  69.2 3.1 %collective-permute-start.14 = (f32[2,24,1024]{2,1,0:T(8,128)S(1)}, f32[2,24,1024]{2,1,0:T(8,128)S(1)}, u32[]{:S(2)}, u32[]{:S(2)}) collective-permute-start(f32[2,24,1024]{2,1,0:T(8,128)S(1)} %get-tuple-element.108), channel_id=1, source_target_pairs={{0,8},{1,9},{2,10},{3,11},{4,12},{5,13},{6,14},{7,15},{8,16},{9,17... | collective-permute-start | bytes 589832 | tf_op jit(solution)/shard_map/ppermute | solution.py:475
  72.3 2.7 %collective-permute-start.15 = (f32[2,16,1024]{2,1,0:T(8,128)S(1)}, f32[2,16,1024]{2,1,0:T(8,128)S(1)}, u32[]{:S(2)}, u32[]{:S(2)}) collective-permute-start(f32[2,16,1024]{2,1,0:T(8,128)S(1)} %get-tuple-element.109), channel_id=1, source_target_pairs={{0,1},{1,2},{2,3},{3,4},{4,5},{5,6},{6,7},{8,9},{9,10},{10,11},{11... | collective-permute-start | bytes 393224 | tf_op jit(solution)/shard_map/ppermute | solution.py:475
  75.0 2.2 %places.1 = (s32[1,3072]{1,0:T(1,128)S(1)}, f32[6336,128]{1,0:T(8,128)S(1)}) custom-call(s32[1]{0:T(128)} %bitcast.my_col, s32[1,3072]{1,0:T(1,128)S(1)} %reshape.46.owner, s32[1,3072]{1,0:T(1,128)S(1)} %reshape.47.node), custom_call_target="tpu_custom_call" | custom-call | flops 3145728 | bytes 3145728 | tf_op jit(solution)/shard_map/places/pallas_call | solution.py:498
  79.1 2.3 %e_last.1 = (f32[3,16,24,1024]{3,2,1,0:T(8,128)S(1)}, f32[16,24,1024]{2,1,0:T(8,128)S(1)}, f32[3,16,24,1024]{3,2,1,0:T(8,128)}) custom-call(f32[3,16,24,1024]{3,2,1,0:T(8,128)S(1)} %h_rest_3.1.h, f32[16,24,1024]{2,1,0:T(8,128)S(1)} %get-tuple-element.70.ca, f32[16,24,1024]{2,1,0:T(8,128)S(1)} %get-tuple-element.71.cb, ...), custom_call_target="tpu_custom_call", output_to_operand_aliasing={{0}: (6, {}), {1}: (7, {})} | custom-call | flops 19660800 | bytes 19660800 | tf_op jit(solution)/shard_map/e_last/pallas_call | solution.py:564
  81.4 4.9 %pack.1 = (f32[8,200,128]{2,1,0:T(8,128)}, f32[8,392,128]{2,1,0:T(8,128)}, f32[3,16,24,1024]{3,2,1,0:T(8,128)}, f32[6336,128]{1,0:T(8,128)S(1)}) custom-call(s32[3072]{0:T(1024)S(1)} %bitcast.8, f32[16,24,1024]{2,1,0:T(8,128)S(1)} %get-tuple-element.111.power, f32[6336,128]{1,0:T(8,128)S(1)} %get-tuple-element.112.flat_old, ...), custom_call_target="tpu_custom_call", output_to_operand_aliasing={{3}: (2, {})} | custom-call | flops 393216 | bytes 14155776 | tf_op jit(solution)/shard_map/pack/pallas_call | solution.py:599
  86.3 4.3 %all-to-all-start.1 = ((f32[8,392,128]{2,1,0:T(8,128)}), f32[8,392,128]{2,1,0:T(8,128)}, u32[]{:S(2)}, u32[]{:S(2)}) async-start(f32[8,392,128]{2,1,0:T(8,128)} %get-tuple-element.118), calls=%async_computation.1 | async-start | bytes 3211264 | tf_op jit(solution)/shard_map/all_to_all | solution.py:617
  92.8 18.5 %collective-permute-done.16.pair = f32[8,200,128]{2,1,0:T(8,128)S(1)} collective-permute-done((f32[8,200,128]{2,1,0:T(8,128)}, f32[8,200,128]{2,1,0:T(8,128)S(1)}, u32[]{:S(2)}, u32[]{:S(2)}) %collective-permute-start.16) | collective-permute-done | bytes 819232 | tf_op jit(solution)/shard_map/ppermute | solution.py:620
  112.4 4.1 %all-to-all-start = ((f32[8,392,128]{2,1,0:T(8,128)}), f32[8,392,128]{2,1,0:T(8,128)S(1)}, u32[]{:S(2)}, u32[]{:S(2)}) async-start(f32[8,392,128]{2,1,0:T(8,128)} %merge.1), calls=%async_computation | async-start | bytes 3211264 | tf_op jit(solution)/shard_map/all_to_all | solution.py:617
  116.5 2.0 %collect_odd.1 = f32[384,128]{1,0:T(8,128)S(1)} custom-call(f32[8,392,128]{2,1,0:T(8,128)} %all-to-all-done.1.blocks), custom_call_target="tpu_custom_call" | custom-call | flops 3145728 | bytes 3145728 | tf_op jit(solution)/shard_map/collect_odd/pallas_call | solution.py:498
  121.7 4.2 %collective-permute-done.17.refs_1_ = f32[384,128]{1,0:T(8,128)S(1)} collective-permute-done((f32[384,128]{1,0:T(8,128)S(1)}, f32[384,128]{1,0:T(8,128)S(1)}, u32[]{:S(2)}, u32[]{:S(2)}) %collective-permute-start.17) | collective-permute-done | bytes 196640 | tf_op jit(solution)/shard_map/ppermute | solution.py:620
  127.6 10.3 %all-to-all-done.blocks = f32[8,392,128]{2,1,0:T(8,128)S(1)} async-done(((f32[8,392,128]{2,1,0:T(8,128)}), f32[8,392,128]{2,1,0:T(8,128)S(1)}, u32[]{:S(2)}, u32[]{:S(2)}) %all-to-all-start) | async-done | bytes 1605664 | tf_op jit(solution)/shard_map/all_to_all | solution.py:617
  (55 shorter events, 36.3 us)
Async XLA Ops:
  0.6 3.9 %copy-start.1 = (s32[1,1,16,24,8,1]{3,5,4,2,1,0:T(1,128)S(1)}, s32[1,1,16,24,8,1]{3,5,4,2,1,0:T(1,128)}, u32[]{:S(2)}) copy-start(s32[1,1,16,24,8,1]{3,5,4,2,1,0:T(1,128)} %param.11) | copy-start | bytes 36868
  0.6 4.2 %copy-start.2 = (s32[1,1,16,24,8]{3,4,2,1,0:T(8,128)S(1)}, s32[1,1,16,24,8]{3,4,2,1,0:T(8,128)}, u32[]{:S(2)}) copy-start(s32[1,1,16,24,8]{3,4,2,1,0:T(8,128)} %param.12) | copy-start | bytes 36868
  2.0 8.1 %collective-permute-start = (f32[2,16,1024]{2,1,0:T(8,128)S(1)}, f32[2,16,1024]{2,1,0:T(8,128)S(1)}, u32[]{:S(2)}, u32[]{:S(2)}) collective-permute-start(f32[2,16,1024]{2,1,0:T(8,128)S(1)} %get-tuple-element.63.rows_old), channel_id=1, source_target_pairs={{1,0},{2,1},{3,2},{4,3},{5,4},{6,5},{7,6},{9,8},{10,9},{11,10},{12... | collective-permute-start | bytes 393224 | tf_op jit(solution)/shard_map/ppermute | solution.py:475
  3.3 10.3 %collective-permute-start.1 = (f32[2,24,1024]{2,1,0:T(8,128)S(1)}, f32[2,24,1024]{2,1,0:T(8,128)S(1)}, u32[]{:S(2)}, u32[]{:S(2)}) collective-permute-start(f32[2,24,1024]{2,1,0:T(8,128)S(1)} %get-tuple-element.64), channel_id=1, source_target_pairs={{8,0},{9,1},{10,2},{11,3},{12,4},{13,5},{14,6},{15,7},{16,8},{17,9... | collective-permute-start | bytes 589832 | tf_op jit(solution)/shard_map/ppermute | solution.py:475
  13.7 8.5 %collective-permute-start.3 = (f32[2,24,1024]{2,1,0:T(8,128)S(1)}, f32[2,24,1024]{2,1,0:T(8,128)S(1)}, u32[]{:S(2)}, u32[]{:S(2)}) collective-permute-start(f32[2,24,1024]{2,1,0:T(8,128)S(1)} %get-tuple-element.74), channel_id=1, source_target_pairs={{0,8},{1,9},{2,10},{3,11},{4,12},{5,13},{6,14},{7,15},{8,16},{9,17... | collective-permute-start | bytes 589832 | tf_op jit(solution)/shard_map/ppermute | solution.py:475
  17.9 3.7 %collective-permute-start.2 = (f32[2,16,1024]{2,1,0:T(8,128)S(1)}, f32[2,16,1024]{2,1,0:T(8,128)S(1)}, u32[]{:S(2)}, u32[]{:S(2)}) collective-permute-start(f32[2,16,1024]{2,1,0:T(8,128)S(1)} %get-tuple-element.73.rows_old), channel_id=1, source_target_pairs={{0,1},{1,2},{2,3},{3,4},{4,5},{5,6},{6,7},{8,9},{9,10},{10,11},{11... | collective-permute-start | bytes 393224 | tf_op jit(solution)/shard_map/ppermute | solution.py:475
  22.5 10.1 %collective-permute-start.5 = (f32[2,24,1024]{2,1,0:T(8,128)S(1)}, f32[2,24,1024]{2,1,0:T(8,128)S(1)}, u32[]{:S(2)}, u32[]{:S(2)}) collective-permute-start(f32[2,24,1024]{2,1,0:T(8,128)S(1)} %get-tuple-element.81), channel_id=1, source_target_pairs={{8,0},{9,1},{10,2},{11,3},{12,4},{13,5},{14,6},{15,7},{16,8},{17,9... | collective-permute-start | bytes 589832 | tf_op jit(solution)/shard_map/ppermute | solution.py:475
  23.8 4.1 %collective-permute-start.4 = (f32[2,16,1024]{2,1,0:T(8,128)S(1)}, f32[2,16,1024]{2,1,0:T(8,128)S(1)}, u32[]{:S(2)}, u32[]{:S(2)}) collective-permute-start(f32[2,16,1024]{2,1,0:T(8,128)S(1)} %get-tuple-element.80.rows_old), channel_id=1, source_target_pairs={{1,0},{2,1},{3,2},{4,3},{5,4},{6,5},{7,6},{9,8},{10,9},{11,10},{12... | collective-permute-start | bytes 393224 | tf_op jit(solution)/shard_map/ppermute | solution.py:475
  32.7 8.4 %collective-permute-start.7 = (f32[2,24,1024]{2,1,0:T(8,128)S(1)}, f32[2,24,1024]{2,1,0:T(8,128)S(1)}, u32[]{:S(2)}, u32[]{:S(2)}) collective-permute-start(f32[2,24,1024]{2,1,0:T(8,128)S(1)} %get-tuple-element.86), channel_id=1, source_target_pairs={{0,8},{1,9},{2,10},{3,11},{4,12},{5,13},{6,14},{7,15},{8,16},{9,17... | collective-permute-start | bytes 589832 | tf_op jit(solution)/shard_map/ppermute | solution.py:475
  36.2 4.2 %collective-permute-start.6 = (f32[2,16,1024]{2,1,0:T(8,128)S(1)}, f32[2,16,1024]{2,1,0:T(8,128)S(1)}, u32[]{:S(2)}, u32[]{:S(2)}) collective-permute-start(f32[2,16,1024]{2,1,0:T(8,128)S(1)} %get-tuple-element.85.rows_old), channel_id=1, source_target_pairs={{0,1},{1,2},{2,3},{3,4},{4,5},{5,6},{6,7},{8,9},{9,10},{10,11},{11... | collective-permute-start | bytes 393224 | tf_op jit(solution)/shard_map/ppermute | solution.py:475
  41.3 9.3 %collective-permute-start.9 = (f32[2,24,1024]{2,1,0:T(8,128)S(1)}, f32[2,24,1024]{2,1,0:T(8,128)S(1)}, u32[]{:S(2)}, u32[]{:S(2)}) collective-permute-start(f32[2,24,1024]{2,1,0:T(8,128)S(1)} %get-tuple-element.93), channel_id=1, source_target_pairs={{8,0},{9,1},{10,2},{11,3},{12,4},{13,5},{14,6},{15,7},{16,8},{17,9... | collective-permute-start | bytes 589832 | tf_op jit(solution)/shard_map/ppermute | solution.py:475
  42.6 3.6 %collective-permute-start.8 = (f32[2,16,1024]{2,1,0:T(8,128)S(1)}, f32[2,16,1024]{2,1,0:T(8,128)S(1)}, u32[]{:S(2)}, u32[]{:S(2)}) collective-permute-start(f32[2,16,1024]{2,1,0:T(8,128)S(1)} %get-tuple-element.92.rows_old), channel_id=1, source_target_pairs={{1,0},{2,1},{3,2},{4,3},{5,4},{6,5},{7,6},{9,8},{10,9},{11,10},{12... | collective-permute-start | bytes 393224 | tf_op jit(solution)/shard_map/ppermute | solution.py:475
  50.7 8.4 %collective-permute-start.11 = (f32[2,24,1024]{2,1,0:T(8,128)S(1)}, f32[2,24,1024]{2,1,0:T(8,128)S(1)}, u32[]{:S(2)}, u32[]{:S(2)}) collective-permute-start(f32[2,24,1024]{2,1,0:T(8,128)S(1)} %get-tuple-element.98), channel_id=1, source_target_pairs={{0,8},{1,9},{2,10},{3,11},{4,12},{5,13},{6,14},{7,15},{8,16},{9,17... | collective-permute-start | bytes 589832 | tf_op jit(solution)/shard_map/ppermute | solution.py:475
  54.3 4.1 %collective-permute-start.10 = (f32[2,16,1024]{2,1,0:T(8,128)S(1)}, f32[2,16,1024]{2,1,0:T(8,128)S(1)}, u32[]{:S(2)}, u32[]{:S(2)}) collective-permute-start(f32[2,16,1024]{2,1,0:T(8,128)S(1)} %get-tuple-element.97.rows_old), channel_id=1, source_target_pairs={{0,1},{1,2},{2,3},{3,4},{4,5},{5,6},{6,7},{8,9},{9,10},{10,11},{11... | collective-permute-start | bytes 393224 | tf_op jit(solution)/shard_map/ppermute | solution.py:475
  59.3 9.8 %collective-permute-start.13 = (f32[2,24,1024]{2,1,0:T(8,128)S(1)}, f32[2,24,1024]{2,1,0:T(8,128)S(1)}, u32[]{:S(2)}, u32[]{:S(2)}) collective-permute-start(f32[2,24,1024]{2,1,0:T(8,128)S(1)} %get-tuple-element.105), channel_id=1, source_target_pairs={{8,0},{9,1},{10,2},{11,3},{12,4},{13,5},{14,6},{15,7},{16,8},{17,9... | collective-permute-start | bytes 589832 | tf_op jit(solution)/shard_map/ppermute | solution.py:475
  60.6 3.8 %collective-permute-start.12 = (f32[2,16,1024]{2,1,0:T(8,128)S(1)}, f32[2,16,1024]{2,1,0:T(8,128)S(1)}, u32[]{:S(2)}, u32[]{:S(2)}) collective-permute-start(f32[2,16,1024]{2,1,0:T(8,128)S(1)} %get-tuple-element.104), channel_id=1, source_target_pairs={{1,0},{2,1},{3,2},{4,3},{5,4},{6,5},{7,6},{9,8},{10,9},{11,10},{12... | collective-permute-start | bytes 393224 | tf_op jit(solution)/shard_map/ppermute | solution.py:475
  69.2 9.8 %collective-permute-start.14 = (f32[2,24,1024]{2,1,0:T(8,128)S(1)}, f32[2,24,1024]{2,1,0:T(8,128)S(1)}, u32[]{:S(2)}, u32[]{:S(2)}) collective-permute-start(f32[2,24,1024]{2,1,0:T(8,128)S(1)} %get-tuple-element.108), channel_id=1, source_target_pairs={{0,8},{1,9},{2,10},{3,11},{4,12},{5,13},{6,14},{7,15},{8,16},{9,17... | collective-permute-start | bytes 589832 | tf_op jit(solution)/shard_map/ppermute | solution.py:475
  72.3 6.8 %collective-permute-start.15 = (f32[2,16,1024]{2,1,0:T(8,128)S(1)}, f32[2,16,1024]{2,1,0:T(8,128)S(1)}, u32[]{:S(2)}, u32[]{:S(2)}) collective-permute-start(f32[2,16,1024]{2,1,0:T(8,128)S(1)} %get-tuple-element.109), channel_id=1, source_target_pairs={{0,1},{1,2},{2,3},{3,4},{4,5},{5,6},{6,7},{8,9},{9,10},{10,11},{11... | collective-permute-start | bytes 393224 | tf_op jit(solution)/shard_map/ppermute | solution.py:475
  86.3 26.1 %all-to-all-start.1 = ((f32[8,392,128]{2,1,0:T(8,128)}), f32[8,392,128]{2,1,0:T(8,128)}, u32[]{:S(2)}, u32[]{:S(2)}) async-start(f32[8,392,128]{2,1,0:T(8,128)} %get-tuple-element.118), calls=%async_computation.1 | async-start | bytes 3211264 | tf_op jit(solution)/shard_map/all_to_all | solution.py:617
  90.6 20.7 %collective-permute-start.16 = (f32[8,200,128]{2,1,0:T(8,128)}, f32[8,200,128]{2,1,0:T(8,128)S(1)}, u32[]{:S(2)}, u32[]{:S(2)}) collective-permute-start(f32[8,200,128]{2,1,0:T(8,128)} %get-tuple-element.117), channel_id=1, source_target_pairs={{0,8},{8,0},{16,24},{24,16},{1,9},{9,1},{17,25},{25,17},{2,10},{10... | collective-permute-start | bytes 2457608 | tf_op jit(solution)/shard_map/ppermute | solution.py:620
  112.4 27.1 %copy-start = (f32[384,128]{1,0:T(8,128)S(1)}, f32[384,128]{1,0:T(8,128)}, u32[]{:S(2)}) copy-start(f32[384,128]{1,0:T(8,128)} %enthalpy.1) | copy-start | bytes 589828
  112.4 25.4 %all-to-all-start = ((f32[8,392,128]{2,1,0:T(8,128)}), f32[8,392,128]{2,1,0:T(8,128)S(1)}, u32[]{:S(2)}, u32[]{:S(2)}) async-start(f32[8,392,128]{2,1,0:T(8,128)} %merge.1), calls=%async_computation | async-start | bytes 3211264 | tf_op jit(solution)/shard_map/all_to_all | solution.py:617
  118.5 7.4 %collective-permute-start.17 = (f32[384,128]{1,0:T(8,128)S(1)}, f32[384,128]{1,0:T(8,128)S(1)}, u32[]{:S(2)}, u32[]{:S(2)}) collective-permute-start(f32[384,128]{1,0:T(8,128)S(1)} %collect_odd.1), channel_id=1, source_target_pairs={{0,8},{8,0},{16,24},{24,16},{1,9},{9,1},{17,25},{25,17},{2,10},{10... | collective-permute-start | bytes 589832 | tf_op jit(solution)/shard_map/ppermute | solution.py:620
  125.9 13.6 %collective-permute-start.18 = (f32[384,128]{1,0:T(8,128)S(1)}, f32[384,128]{1,0:T(8,128)S(1)}, u32[]{:S(2)}, u32[]{:S(2)}) collective-permute-start(f32[384,128]{1,0:T(8,128)S(1)} %add.26), channel_id=1, source_target_pairs={{0,16},{8,24},{16,0},{24,8},{1,17},{9,25},{17,1},{25,9},{2,18},{10... | collective-permute-start | bytes 589832 | tf_op jit(solution)/shard_map/ppermute | solution.py:620

commit v14 on v13

--- a/solution.py
+++ b/solution.py
@@ -280,6 +280,8 @@
     parts_of = jnp.zeros((2 * n_dev, room_for), F32)
     nt = (((1,), (1,)), ((), ()))
     begins, heights = starts_of(n_col, n_hgt, cap)
+    cut = cut_of(cap)
+    behind = [cut, cap, (n_col - 2) * cap + cap - cut]
     for start in range(0, count, width):
         own = owner[:, start : start + width]
         hit = jnp.where(rows == own, 1.0, 0.0)
@@ -290,7 +292,7 @@
         own_hgt = lax.rem(own, n_hgt)
         begin = jnp.where(
             turn == 0,
-            begins[0] + own_hgt * heights[0],
+            jnp.where(rank < cut, begins[0] + own_hgt * heights[0], begins[2] + own_hgt * heights[2] + behind[2] - cap),
             jnp.where(
                 turn == 1,
                 begins[1] + own_hgt * heights[1],
@@ -315,7 +317,6 @@
     lax.fori_loop(0, flat.shape[0] // chunk, clear, 0)
     for at in range(flat.shape[0] // chunk * chunk, flat.shape[0], ROWS):
         flat[at : at + ROWS, :] = jnp.zeros((ROWS, PTS), F32)
-    behind = [cap, cap, (n_col - 2) * cap]
     for begin, height, skip in zip(begins, heights, behind):
         for part in range(n_hgt):
             at = begin + part * height
@@ -324,22 +325,35 @@
         turn = lax.bitwise_xor(jnp.int32(group), my_col[0])
         kind = jnp.minimum(turn, 2)
         begin = jnp.where(kind == 0, begins[0], jnp.where(kind == 1, begins[1], begins[2]))
-        height = jnp.where(kind == 2, heights[2], heights[0])
-        skip = jnp.where(kind == 2, behind[2] + (turn - 2) * per, cap)
+        height = jnp.where(kind == 0, heights[0], jnp.where(kind == 1, heights[1], heights[2]))
+        skip = jnp.where(kind == 0, cut, jnp.where(kind == 1, cap, behind[2] + (turn - 2) * per))
         for part in range(n_hgt):
             at = group * n_hgt + part
             for piece in range(per):
                 row = table[at : at + 1, piece * LANES : (piece + 1) * LANES]
                 flat[pl.ds(begin + part * height + skip + piece, 1), :] = row
 
+        @pl.when(turn == 0)
+        def _():
+            piece = cut // LANES
+            for part in range(n_hgt):
+                row = begins[2] + part * heights[2] + behind[2] + (n_col - 2) * per
+                at = group * n_hgt + part
+                flat[row : row + 1, :] = table[at : at + 1, piece * LANES : (piece + 1) * LANES]
+
+
+def cut_of(cap):
+    return cap - cap // 6 // ROWS * ROWS
+
 
 def table_rows(parts, cap):
     return -(-parts * -(-cap // LANES) // ROWS) * ROWS
 
 
 def starts_of(n_col, n_hgt, cap):
-    one = cap + table_rows(1, cap)
-    heights = [one, one, (n_col - 2) * cap + table_rows(n_col - 2, cap)]
+    cut = cut_of(cap)
+    others = (n_col - 2) * cap + cap - cut + table_rows(n_col - 1, cap)
+    heights = [cut + table_rows(1, cap), cap + table_rows(1, cap), others]
     return [0, n_hgt * heights[0], n_hgt * (heights[0] + heights[1])], heights
 
 
@@ -371,10 +385,10 @@
     e_copy.wait()
 
 
-def summed(blocks, first, cap, node_row, chosen, split, node_count):
+def summed(blocks, first, caps, node_row, chosen, split, node_count):
     ids = lax.broadcasted_iota(jnp.int32, (node_count, LANES), 0).astype(F32)
     n_from, _, pts = blocks.shape
-    per = -(-cap // LANES)
+    per = -(-max(caps) // LANES)
     many = len(first)
     for source in range(n_from):
         for i in range(many):
@@ -384,6 +398,7 @@
                 lanes = slice(seat + piece * LANES, seat + (piece + 1) * LANES)
                 hit = ids == blocks[source, row : row + 1, :]
                 chosen[:, lanes] = jnp.where(hit, 1.0, 0.0).astype(jnp.bfloat16)
+            cap = caps[i]
             values = blocks[source, first[i] : first[i] + cap, :]
             high = values.astype(jnp.bfloat16)
             split[seat : seat + cap, 0:pts] = high
@@ -397,6 +412,7 @@
     rows = blocks.shape[1]
     per = -(-cap // LANES)
     after = n_part * cap
+    table = after + cap - cut_of(cap)
     pieces = [(after, rows - after)] + [(part * cap, cap) for part in parts]
     copies = []
     for i, (begin, size) in enumerate(pieces):
@@ -407,7 +423,29 @@
     copies[0].wait()
     for i, (part, out) in enumerate(zip(parts, outs)):
         copies[1 + i].wait()
-        out[...] = summed(near, [part * cap], cap, [after + part * per], chosen, split, out.shape[0])
+        out[...] = summed(near, [part * cap], [cap], [table + part * per], chosen, split, out.shape[0])
+
+
+def collect_tail_kernel(cap, n_part, blocks, out, chosen, split, near, sem):
+    n_from, rows, pts = blocks.shape
+    cut = cut_of(cap)
+    begin = n_part * cap
+    copy = pltpu.make_async_copy(blocks.at[:, pl.ds(begin, rows - begin)], near, sem)
+    copy.start()
+    split[...] = jnp.zeros(split.shape, split.dtype)
+    copy.wait()
+    ids = lax.broadcasted_iota(jnp.int32, (out.shape[0], LANES), 0).astype(F32)
+    row = cap - cut + n_part * -(-cap // LANES)
+    for source in range(n_from):
+        hit = ids == near[source, row : row + 1, :]
+        chosen[:, source * LANES : (source + 1) * LANES] = jnp.where(hit, 1.0, 0.0).astype(jnp.bfloat16)
+        values = near[source, 0 : cap - cut, :]
+        high = values.astype(jnp.bfloat16)
+        here = slice(source * LANES + cut % LANES, source * LANES + cut % LANES + cap - cut)
+        split[here, 0:pts] = high
+        split[here, pts : 2 * pts] = (values - high.astype(F32)).astype(jnp.bfloat16)
+    both = jnp.dot(chosen[...], split[...], preferred_element_type=F32)
+    out[...] = both[:, 0:pts] + both[:, pts : 2 * pts]
 
 
 def add_kernel(*refs):
@@ -417,6 +455,7 @@
 
 
 def own_kernel(cap, height, flat, mine, sems):
+    cap = cut_of(cap)
     copies = [
         pltpu.make_async_copy(flat.at[pl.ds(group * height, cap)], mine.at[group, pl.ds(0, cap)], sems.at[group])
         for group in range(mine.shape[0])
@@ -429,10 +468,11 @@
 
 def merge_kernel(cap, height, flat, pair, mine_old, mine, tile, sems):
     per = -(-cap // LANES)
+    cut = cut_of(cap)
     groups = mine.shape[0]
     copies = []
     for group in range(groups):
-        target = mine.at[group, pl.ds(cap, cap)]
+        target = mine.at[group, pl.ds(cut, cap)]
         copies.append(pltpu.make_async_copy(pair.at[group, pl.ds(0, cap)], target, sems.at[0, group]))
     for copy in copies:
         copy.start()
@@ -440,8 +480,8 @@
     tile[...] = jnp.full(tile.shape, -1.0, F32)
     for group in range(groups):
         tile[group, 0:per, :] = pair[group, cap : cap + per, :]
-        tile[group, per : 2 * per, :] = flat[group * height + cap : group * height + cap + per, :]
-        target = mine.at[group, pl.ds(2 * cap, rest)]
+        tile[group, per : 2 * per, :] = flat[group * height + cut : group * height + cut + per, :]
+        target = mine.at[group, pl.ds(cut + cap, rest)]
         copies.append(pltpu.make_async_copy(tile.at[group], target, sems.at[1, group]))
         copies[-1].start()
     for copy in copies:
@@ -451,7 +491,9 @@
 def collect_mine_kernel(cap, blocks, out, chosen, split):
     per = -(-cap // LANES)
     split[...] = jnp.zeros(split.shape, split.dtype)
-    out[...] = summed(blocks, [0, cap], cap, [2 * cap + per, 2 * cap], chosen, split, out.shape[0])
+    cut = cut_of(cap)
+    nodes = [cut + cap + per, cut + cap]
+    out[...] = summed(blocks, [0, cut], [cut, cap], nodes, chosen, split, out.shape[0])
 
 
 def finish_kernel(enthalpy, *refs):
@@ -644,7 +686,21 @@
         add_kernel, (node_rows,) * len(turns), [WHOLE] * (2 * len(turns)), [*kept, *swapped], "add", 1
     )
     parts = [across(part, turn) for part, turn in zip(sums, turns)]
-    both = pltpu.HBM((n_hgt, 2 * cap + table_rows(2, cap), PTS), F32)
+    tail = kernel(
+        functools.partial(collect_tail_kernel, cap, n_col - 2),
+        node_rows,
+        [pl.BlockSpec(memory_space=pl.ANY)],
+        [other_blocks],
+        "collect_tail",
+        8,
+        scratch=[
+            pltpu.VMEM((node_count, n_hgt * LANES), jnp.bfloat16),
+            pltpu.VMEM((n_hgt * LANES, 2 * PTS), jnp.bfloat16),
+            vmem(n_hgt, heights[2] - (n_col - 2) * cap, PTS),
+            sem,
+        ],
+    )
+    both = pltpu.HBM((n_hgt, cut_of(cap) + cap + table_rows(2, cap), PTS), F32)
     mine = pl.pallas_call(
         functools.partial(own_kernel, cap, heights[0]),
         out_shape=both,
@@ -677,7 +733,7 @@
         scratch=one_hot_space(2 * n_hgt),
     )
     node_temp = kernel(
-        finish_kernel, node_rows, [WHOLE] * (2 + len(parts)), [node_enthalpy, own, *parts], "finish", 1
+        finish_kernel, node_rows, [WHOLE] * (3 + len(parts)), [node_enthalpy, own, tail, *parts], "finish", 1
     )
     return e_out, h_out, node_temp
 

time: 141 us -> 140 us (level)
  waiting for transfers between devices: 53.2 us -> 51.2 us
    all_to_all x2, waiting for transfers between devices: 10.3 us -> 8.42 us  [swap(): return lax.all_to_all(x, axis, split_axis=0, concat_axis=0, tiled=True)]
    pallas_call x22 -> x23, Pallas kernels: 30.3 us -> 31.8 us  [kernel(): pl.pallas_call(body, out_shape=outs, in_specs=ins, out_specs=jax.tree.map...]
  transfers between devices with their start and end apart: 21 -> 21, of which waited for: 12 -> 13; matrix products, arithmetic and copies ran while one was open for 0% -> 0% of each run, Pallas kernels for 21% -> 22%
where the time goes in v14:
time: 140 us; the launch traced here: 139 us
  waiting for transfers between devices  51.2 us (37%)
  starting transfers between devices  45.5 us (32%)
  Pallas kernels  41 us (29%)
    ppermute x16, starting transfers between devices, shifted(): return lax.ppermute(block, ('col', 'hgt'), route)  33.5 us
    pallas_call x23, Pallas kernels, kernel(): pl.pallas_call(body, out_shape=outs, in_specs=ins, out_specs=jax.tree.map...  31.8 us
    ppermute x3, waiting for transfers between devices, across(): return lax.ppermute(x, 'col', [(c, c ^ turn) for c in range(n_col)])  22.5 us
    ppermute x16, waiting for transfers between devices, shifted(): return lax.ppermute(block, ('col', 'hgt'), route)  20.2 us
    all_to_all x2, waiting for transfers between devices, swap(): return lax.all_to_all(x, axis, split_axis=0, concat_axis=0, tiled=True)  8.42 us
    all_to_all x2, starting transfers between devices, swap(): return lax.all_to_all(x, axis, split_axis=0, concat_axis=0, tiled=True)  7.9 us
    pallas_call x1, Pallas kernels, per_device(): pl.pallas_call(functools.partial(pack_kernel, heights), out_shape=(pltpu....  4.83 us
    ppermute x3, starting transfers between devices, across(): return lax.ppermute(x, 'col', [(c, c ^ turn) for c in range(n_col)])  4.08 us
  transfers between devices with their start and end apart: 21, of which 13 were waited for; matrix products, arithmetic and copies ran while one was open for 0% of the time, Pallas kernels for 22%

profile of v14, /device:TPU:0, one launch (start us, length us, event | category | flops | bytes accessed | tf_op | source)
XLA Modules:
  0.0 139.3 jit_solution(10525928165916736371)
XLA Ops:
  5.1 4.9 %load.1 = (f32[16,24,1024]{2,1,0:T(8,128)S(1)}, f32[16,24,1024]{2,1,0:T(8,128)S(1)}, f32[16,24,1024]{2,1,0:T(8,128)S(1)}, f32[3,16,24,1024]{3,2,1,0:T(8,128)S(1)...) custom-call(f32[16,24,1024]{2,1,0:T(8,128)} %temp_far.1, ...), custom_call_target="tpu_custom_call" | custom-call | flops 23592960 | bytes 23592960 | tf_op jit(solution)/shard_map/load/pallas_call | solution.py:540
  10.1 3.5 %collective-permute-done.1.col = f32[2,24,1024]{2,1,0:T(8,128)S(1)} collective-permute-done((f32[2,24,1024]{2,1,0:T(8,128)S(1)}, f32[2,24,1024]{2,1,0:T(8,128)S(1)}, u32[]{:S(2)}, u32[]{:S(2)}) %collective-permute-start.1) | collective-permute-done | bytes 196640 | tf_op jit(solution)/shard_map/ppermute | solution.py:517
  13.7 4.1 %collective-permute-start.3 = (f32[2,24,1024]{2,1,0:T(8,128)S(1)}, f32[2,24,1024]{2,1,0:T(8,128)S(1)}, u32[]{:S(2)}, u32[]{:S(2)}) collective-permute-start(f32[2,24,1024]{2,1,0:T(8,128)S(1)} %get-tuple-element.74), channel_id=1, source_target_pairs={{0,8},{1,9},{2,10},{3,11},{4,12},{5,13},{6,14},{7,15},{8,16},{9,17... | collective-permute-start | bytes 589832 | tf_op jit(solution)/shard_map/ppermute | solution.py:517
  25.1 2.2 %e_rest_0.1 = (f32[3,16,24,1024]{3,2,1,0:T(8,128)S(1)}, f32[16,24,1024]{2,1,0:T(8,128)S(1)}, f32[3,16,1024]{2,1,0:T(8,128)S(1)}) custom-call(f32[3,16,24,1024]{3,2,1,0:T(8,128)S(1)} %get-tuple-element.69.h.h_old, f32[16,24,1024]{2,1,0:T(8,128)S(1)} %get-tuple-element.70.ca, ...), custom_call_target="tpu_custom_call", output_to_operand_aliasing={{0}: (5, {}), {1}: (6, {})} | custom-call | flops 17694720 | bytes 17694720 | tf_op jit(solution)/shard_map/e_rest_0/pallas_call | solution.py:540
  27.9 4.7 %collective-permute-done.5.col = f32[2,24,1024]{2,1,0:T(8,128)S(1)} collective-permute-done((f32[2,24,1024]{2,1,0:T(8,128)S(1)}, f32[2,24,1024]{2,1,0:T(8,128)S(1)}, u32[]{:S(2)}, u32[]{:S(2)}) %collective-permute-start.5) | collective-permute-done | bytes 196640 | tf_op jit(solution)/shard_map/ppermute | solution.py:517
  32.7 3.5 %collective-permute-start.7 = (f32[2,24,1024]{2,1,0:T(8,128)S(1)}, f32[2,24,1024]{2,1,0:T(8,128)S(1)}, u32[]{:S(2)}, u32[]{:S(2)}) collective-permute-start(f32[2,24,1024]{2,1,0:T(8,128)S(1)} %get-tuple-element.86), channel_id=1, source_target_pairs={{0,8},{1,9},{2,10},{3,11},{4,12},{5,13},{6,14},{7,15},{8,16},{9,17... | collective-permute-start | bytes 589832 | tf_op jit(solution)/shard_map/ppermute | solution.py:517
  36.2 2.3 %collective-permute-start.6 = (f32[2,16,1024]{2,1,0:T(8,128)S(1)}, f32[2,16,1024]{2,1,0:T(8,128)S(1)}, u32[]{:S(2)}, u32[]{:S(2)}) collective-permute-start(f32[2,16,1024]{2,1,0:T(8,128)S(1)} %get-tuple-element.85.rows_old), channel_id=1, source_target_pairs={{0,1},{1,2},{2,3},{3,4},{4,5},{5,6},{6,7},{8,9},{9,10},{10,11},{11... | collective-permute-start | bytes 393224 | tf_op jit(solution)/shard_map/ppermute | solution.py:517
  43.9 2.3 %e_rest_1.1 = (f32[3,16,24,1024]{3,2,1,0:T(8,128)S(1)}, f32[16,24,1024]{2,1,0:T(8,128)S(1)}, f32[3,16,1024]{2,1,0:T(8,128)S(1)}) custom-call(f32[3,16,24,1024]{3,2,1,0:T(8,128)S(1)} %get-tuple-element.84.h.h_old, f32[16,24,1024]{2,1,0:T(8,128)S(1)} %get-tuple-element.70.ca, ...), custom_call_target="tpu_custom_call", output_to_operand_aliasing={{0}: (5, {}), {1}: (6, {})} | custom-call | flops 17694720 | bytes 17694720 | tf_op jit(solution)/shard_map/e_rest_1/pallas_call | solution.py:540
  46.2 4.4 %collective-permute-done.9.col = f32[2,24,1024]{2,1,0:T(8,128)S(1)} collective-permute-done((f32[2,24,1024]{2,1,0:T(8,128)S(1)}, f32[2,24,1024]{2,1,0:T(8,128)S(1)}, u32[]{:S(2)}, u32[]{:S(2)}) %collective-permute-start.9) | collective-permute-done | bytes 196640 | tf_op jit(solution)/shard_map/ppermute | solution.py:517
  50.7 3.6 %collective-permute-start.11 = (f32[2,24,1024]{2,1,0:T(8,128)S(1)}, f32[2,24,1024]{2,1,0:T(8,128)S(1)}, u32[]{:S(2)}, u32[]{:S(2)}) collective-permute-start(f32[2,24,1024]{2,1,0:T(8,128)S(1)} %get-tuple-element.98), channel_id=1, source_target_pairs={{0,8},{1,9},{2,10},{3,11},{4,12},{5,13},{6,14},{7,15},{8,16},{9,17... | collective-permute-start | bytes 589832 | tf_op jit(solution)/shard_map/ppermute | solution.py:517
  54.3 2.1 %collective-permute-start.10 = (f32[2,16,1024]{2,1,0:T(8,128)S(1)}, f32[2,16,1024]{2,1,0:T(8,128)S(1)}, u32[]{:S(2)}, u32[]{:S(2)}) collective-permute-start(f32[2,16,1024]{2,1,0:T(8,128)S(1)} %get-tuple-element.97.rows_old), channel_id=1, source_target_pairs={{0,1},{1,2},{2,3},{3,4},{4,5},{5,6},{6,7},{8,9},{9,10},{10,11},{11... | collective-permute-start | bytes 393224 | tf_op jit(solution)/shard_map/ppermute | solution.py:517
  61.9 2.3 %e_rest_2.1 = (f32[3,16,24,1024]{3,2,1,0:T(8,128)S(1)}, f32[16,24,1024]{2,1,0:T(8,128)S(1)}, f32[3,16,1024]{2,1,0:T(8,128)S(1)}) custom-call(f32[3,16,24,1024]{3,2,1,0:T(8,128)S(1)} %get-tuple-element.96.h.h_old, f32[16,24,1024]{2,1,0:T(8,128)S(1)} %get-tuple-element.70.ca, ...), custom_call_target="tpu_custom_call", output_to_operand_aliasing={{0}: (5, {}), {1}: (6, {})} | custom-call | flops 17694720 | bytes 17694720 | tf_op jit(solution)/shard_map/e_rest_2/pallas_call | solution.py:540
  64.4 4.7 %collective-permute-done.13.col = f32[2,24,1024]{2,1,0:T(8,128)S(1)} collective-permute-done((f32[2,24,1024]{2,1,0:T(8,128)S(1)}, f32[2,24,1024]{2,1,0:T(8,128)S(1)}, u32[]{:S(2)}, u32[]{:S(2)}) %collective-permute-start.13) | collective-permute-done | bytes 196640 | tf_op jit(solution)/shard_map/ppermute | solution.py:517
  69.2 3.1 %collective-permute-start.14 = (f32[2,24,1024]{2,1,0:T(8,128)S(1)}, f32[2,24,1024]{2,1,0:T(8,128)S(1)}, u32[]{:S(2)}, u32[]{:S(2)}) collective-permute-start(f32[2,24,1024]{2,1,0:T(8,128)S(1)} %get-tuple-element.108), channel_id=1, source_target_pairs={{0,8},{1,9},{2,10},{3,11},{4,12},{5,13},{6,14},{7,15},{8,16},{9,17... | collective-permute-start | bytes 589832 | tf_op jit(solution)/shard_map/ppermute | solution.py:517
  72.3 2.7 %collective-permute-start.15 = (f32[2,16,1024]{2,1,0:T(8,128)S(1)}, f32[2,16,1024]{2,1,0:T(8,128)S(1)}, u32[]{:S(2)}, u32[]{:S(2)}) collective-permute-start(f32[2,16,1024]{2,1,0:T(8,128)S(1)} %get-tuple-element.109), channel_id=1, source_target_pairs={{0,1},{1,2},{2,3},{3,4},{4,5},{5,6},{6,7},{8,9},{9,10},{10,11},{11... | collective-permute-start | bytes 393224 | tf_op jit(solution)/shard_map/ppermute | solution.py:517
  75.0 2.2 %places.1 = (s32[1,3072]{1,0:T(1,128)S(1)}, f32[6336,128]{1,0:T(8,128)S(1)}) custom-call(s32[1]{0:T(128)} %bitcast.my_col, s32[1,3072]{1,0:T(1,128)S(1)} %reshape.46.owner, s32[1,3072]{1,0:T(1,128)S(1)} %reshape.47.node), custom_call_target="tpu_custom_call" | custom-call | flops 3145728 | bytes 3145728 | tf_op jit(solution)/shard_map/places/pallas_call | solution.py:540
  79.1 2.3 %e_last.1 = (f32[3,16,24,1024]{3,2,1,0:T(8,128)S(1)}, f32[16,24,1024]{2,1,0:T(8,128)S(1)}, f32[3,16,24,1024]{3,2,1,0:T(8,128)}) custom-call(f32[3,16,24,1024]{3,2,1,0:T(8,128)S(1)} %h_rest_3.1.h, f32[16,24,1024]{2,1,0:T(8,128)S(1)} %get-tuple-element.70.ca, f32[16,24,1024]{2,1,0:T(8,128)S(1)} %get-tuple-element.71.cb, ...), custom_call_target="tpu_custom_call", output_to_operand_aliasing={{0}: (6, {}), {1}: (7, {})} | custom-call | flops 19660800 | bytes 19660800 | tf_op jit(solution)/shard_map/e_last/pallas_call | solution.py:606
  81.4 4.8 %pack.1 = (f32[8,200,128]{2,1,0:T(8,128)}, f32[8,424,128]{2,1,0:T(8,128)}, f32[3,16,24,1024]{3,2,1,0:T(8,128)}, f32[6336,128]{1,0:T(8,128)S(1)}) custom-call(s32[3072]{0:T(1024)S(1)} %bitcast.8, f32[16,24,1024]{2,1,0:T(8,128)S(1)} %get-tuple-element.111.power, f32[6336,128]{1,0:T(8,128)S(1)} %get-tuple-element.112.flat_old, ...), custom_call_target="tpu_custom_call", output_to_operand_aliasing={{3}: (2, {})} | custom-call | flops 393216 | bytes 14155776 | tf_op jit(solution)/shard_map/pack/pallas_call | solution.py:641
  86.3 4.3 %all-to-all-start.1 = ((f32[8,424,128]{2,1,0:T(8,128)}), f32[8,424,128]{2,1,0:T(8,128)}, u32[]{:S(2)}, u32[]{:S(2)}) async-start(f32[8,424,128]{2,1,0:T(8,128)} %get-tuple-element.118), calls=%async_computation.1 | async-start | bytes 3473408 | tf_op jit(solution)/shard_map/all_to_all | solution.py:659
  92.7 18.6 %collective-permute-done.16.pair = f32[8,200,128]{2,1,0:T(8,128)S(1)} collective-permute-done((f32[8,200,128]{2,1,0:T(8,128)}, f32[8,200,128]{2,1,0:T(8,128)S(1)}, u32[]{:S(2)}, u32[]{:S(2)}) %collective-permute-start.16) | collective-permute-done | bytes 819232 | tf_op jit(solution)/shard_map/ppermute | solution.py:662
  113.4 3.6 %all-to-all-start = ((f32[8,360,128]{2,1,0:T(8,128)}), f32[8,360,128]{2,1,0:T(8,128)S(1)}, u32[]{:S(2)}, u32[]{:S(2)}) async-start(f32[8,360,128]{2,1,0:T(8,128)} %merge.1), calls=%async_computation | async-start | bytes 2949120 | tf_op jit(solution)/shard_map/all_to_all | solution.py:659
  117.0 2.1 %collect_odd.1 = f32[384,128]{1,0:T(8,128)S(1)} custom-call(f32[8,424,128]{2,1,0:T(8,128)} %all-to-all-done.1.blocks), custom_call_target="tpu_custom_call" | custom-call | flops 3145728 | bytes 3145728 | tf_op jit(solution)/shard_map/collect_odd/pallas_call | solution.py:540
  122.4 3.9 %collective-permute-done.17.refs_1_ = f32[384,128]{1,0:T(8,128)S(1)} collective-permute-done((f32[384,128]{1,0:T(8,128)S(1)}, f32[384,128]{1,0:T(8,128)S(1)}, u32[]{:S(2)}, u32[]{:S(2)}) %collective-permute-start.17) | collective-permute-done | bytes 196640 | tf_op jit(solution)/shard_map/ppermute | solution.py:662
  129.5 7.4 %all-to-all-done.blocks = f32[8,360,128]{2,1,0:T(8,128)S(1)} async-done(((f32[8,360,128]{2,1,0:T(8,128)}), f32[8,360,128]{2,1,0:T(8,128)S(1)}, u32[]{:S(2)}, u32[]{:S(2)}) %all-to-all-start) | async-done | bytes 1474592 | tf_op jit(solution)/shard_map/all_to_all | solution.py:659
  (56 shorter events, 38.6 us)
Async XLA Ops:
  0.6 3.9 %copy-start.1 = (s32[1,1,16,24,8,1]{3,5,4,2,1,0:T(1,128)S(1)}, s32[1,1,16,24,8,1]{3,5,4,2,1,0:T(1,128)}, u32[]{:S(2)}) copy-start(s32[1,1,16,24,8,1]{3,5,4,2,1,0:T(1,128)} %param.11) | copy-start | bytes 36868
  0.6 4.2 %copy-start.2 = (s32[1,1,16,24,8]{3,4,2,1,0:T(8,128)S(1)}, s32[1,1,16,24,8]{3,4,2,1,0:T(8,128)}, u32[]{:S(2)}) copy-start(s32[1,1,16,24,8]{3,4,2,1,0:T(8,128)} %param.12) | copy-start | bytes 36868
  2.0 8.1 %collective-permute-start = (f32[2,16,1024]{2,1,0:T(8,128)S(1)}, f32[2,16,1024]{2,1,0:T(8,128)S(1)}, u32[]{:S(2)}, u32[]{:S(2)}) collective-permute-start(f32[2,16,1024]{2,1,0:T(8,128)S(1)} %get-tuple-element.63.rows_old), channel_id=1, source_target_pairs={{1,0},{2,1},{3,2},{4,3},{5,4},{6,5},{7,6},{9,8},{10,9},{11,10},{12... | collective-permute-start | bytes 393224 | tf_op jit(solution)/shard_map/ppermute | solution.py:517
  3.3 10.3 %collective-permute-start.1 = (f32[2,24,1024]{2,1,0:T(8,128)S(1)}, f32[2,24,1024]{2,1,0:T(8,128)S(1)}, u32[]{:S(2)}, u32[]{:S(2)}) collective-permute-start(f32[2,24,1024]{2,1,0:T(8,128)S(1)} %get-tuple-element.64), channel_id=1, source_target_pairs={{8,0},{9,1},{10,2},{11,3},{12,4},{13,5},{14,6},{15,7},{16,8},{17,9... | collective-permute-start | bytes 589832 | tf_op jit(solution)/shard_map/ppermute | solution.py:517
  13.7 8.5 %collective-permute-start.3 = (f32[2,24,1024]{2,1,0:T(8,128)S(1)}, f32[2,24,1024]{2,1,0:T(8,128)S(1)}, u32[]{:S(2)}, u32[]{:S(2)}) collective-permute-start(f32[2,24,1024]{2,1,0:T(8,128)S(1)} %get-tuple-element.74), channel_id=1, source_target_pairs={{0,8},{1,9},{2,10},{3,11},{4,12},{5,13},{6,14},{7,15},{8,16},{9,17... | collective-permute-start | bytes 589832 | tf_op jit(solution)/shard_map/ppermute | solution.py:517
  17.9 3.7 %collective-permute-start.2 = (f32[2,16,1024]{2,1,0:T(8,128)S(1)}, f32[2,16,1024]{2,1,0:T(8,128)S(1)}, u32[]{:S(2)}, u32[]{:S(2)}) collective-permute-start(f32[2,16,1024]{2,1,0:T(8,128)S(1)} %get-tuple-element.73.rows_old), channel_id=1, source_target_pairs={{0,1},{1,2},{2,3},{3,4},{4,5},{5,6},{6,7},{8,9},{9,10},{10,11},{11... | collective-permute-start | bytes 393224 | tf_op jit(solution)/shard_map/ppermute | solution.py:517
  22.5 10.1 %collective-permute-start.5 = (f32[2,24,1024]{2,1,0:T(8,128)S(1)}, f32[2,24,1024]{2,1,0:T(8,128)S(1)}, u32[]{:S(2)}, u32[]{:S(2)}) collective-permute-start(f32[2,24,1024]{2,1,0:T(8,128)S(1)} %get-tuple-element.81), channel_id=1, source_target_pairs={{8,0},{9,1},{10,2},{11,3},{12,4},{13,5},{14,6},{15,7},{16,8},{17,9... | collective-permute-start | bytes 589832 | tf_op jit(solution)/shard_map/ppermute | solution.py:517
  23.8 4.1 %collective-permute-start.4 = (f32[2,16,1024]{2,1,0:T(8,128)S(1)}, f32[2,16,1024]{2,1,0:T(8,128)S(1)}, u32[]{:S(2)}, u32[]{:S(2)}) collective-permute-start(f32[2,16,1024]{2,1,0:T(8,128)S(1)} %get-tuple-element.80.rows_old), channel_id=1, source_target_pairs={{1,0},{2,1},{3,2},{4,3},{5,4},{6,5},{7,6},{9,8},{10,9},{11,10},{12... | collective-permute-start | bytes 393224 | tf_op jit(solution)/shard_map/ppermute | solution.py:517
  32.7 8.4 %collective-permute-start.7 = (f32[2,24,1024]{2,1,0:T(8,128)S(1)}, f32[2,24,1024]{2,1,0:T(8,128)S(1)}, u32[]{:S(2)}, u32[]{:S(2)}) collective-permute-start(f32[2,24,1024]{2,1,0:T(8,128)S(1)} %get-tuple-element.86), channel_id=1, source_target_pairs={{0,8},{1,9},{2,10},{3,11},{4,12},{5,13},{6,14},{7,15},{8,16},{9,17... | collective-permute-start | bytes 589832 | tf_op jit(solution)/shard_map/ppermute | solution.py:517
  36.2 4.2 %collective-permute-start.6 = (f32[2,16,1024]{2,1,0:T(8,128)S(1)}, f32[2,16,1024]{2,1,0:T(8,128)S(1)}, u32[]{:S(2)}, u32[]{:S(2)}) collective-permute-start(f32[2,16,1024]{2,1,0:T(8,128)S(1)} %get-tuple-element.85.rows_old), channel_id=1, source_target_pairs={{0,1},{1,2},{2,3},{3,4},{4,5},{5,6},{6,7},{8,9},{9,10},{10,11},{11... | collective-permute-start | bytes 393224 | tf_op jit(solution)/shard_map/ppermute | solution.py:517
  41.3 9.3 %collective-permute-start.9 = (f32[2,24,1024]{2,1,0:T(8,128)S(1)}, f32[2,24,1024]{2,1,0:T(8,128)S(1)}, u32[]{:S(2)}, u32[]{:S(2)}) collective-permute-start(f32[2,24,1024]{2,1,0:T(8,128)S(1)} %get-tuple-element.93), channel_id=1, source_target_pairs={{8,0},{9,1},{10,2},{11,3},{12,4},{13,5},{14,6},{15,7},{16,8},{17,9... | collective-permute-start | bytes 589832 | tf_op jit(solution)/shard_map/ppermute | solution.py:517
  42.6 3.6 %collective-permute-start.8 = (f32[2,16,1024]{2,1,0:T(8,128)S(1)}, f32[2,16,1024]{2,1,0:T(8,128)S(1)}, u32[]{:S(2)}, u32[]{:S(2)}) collective-permute-start(f32[2,16,1024]{2,1,0:T(8,128)S(1)} %get-tuple-element.92.rows_old), channel_id=1, source_target_pairs={{1,0},{2,1},{3,2},{4,3},{5,4},{6,5},{7,6},{9,8},{10,9},{11,10},{12... | collective-permute-start | bytes 393224 | tf_op jit(solution)/shard_map/ppermute | solution.py:517
  50.7 8.4 %collective-permute-start.11 = (f32[2,24,1024]{2,1,0:T(8,128)S(1)}, f32[2,24,1024]{2,1,0:T(8,128)S(1)}, u32[]{:S(2)}, u32[]{:S(2)}) collective-permute-start(f32[2,24,1024]{2,1,0:T(8,128)S(1)} %get-tuple-element.98), channel_id=1, source_target_pairs={{0,8},{1,9},{2,10},{3,11},{4,12},{5,13},{6,14},{7,15},{8,16},{9,17... | collective-permute-start | bytes 589832 | tf_op jit(solution)/shard_map/ppermute | solution.py:517
  54.3 4.1 %collective-permute-start.10 = (f32[2,16,1024]{2,1,0:T(8,128)S(1)}, f32[2,16,1024]{2,1,0:T(8,128)S(1)}, u32[]{:S(2)}, u32[]{:S(2)}) collective-permute-start(f32[2,16,1024]{2,1,0:T(8,128)S(1)} %get-tuple-element.97.rows_old), channel_id=1, source_target_pairs={{0,1},{1,2},{2,3},{3,4},{4,5},{5,6},{6,7},{8,9},{9,10},{10,11},{11... | collective-permute-start | bytes 393224 | tf_op jit(solution)/shard_map/ppermute | solution.py:517
  59.3 9.8 %collective-permute-start.13 = (f32[2,24,1024]{2,1,0:T(8,128)S(1)}, f32[2,24,1024]{2,1,0:T(8,128)S(1)}, u32[]{:S(2)}, u32[]{:S(2)}) collective-permute-start(f32[2,24,1024]{2,1,0:T(8,128)S(1)} %get-tuple-element.105), channel_id=1, source_target_pairs={{8,0},{9,1},{10,2},{11,3},{12,4},{13,5},{14,6},{15,7},{16,8},{17,9... | collective-permute-start | bytes 589832 | tf_op jit(solution)/shard_map/ppermute | solution.py:517
  60.6 3.8 %collective-permute-start.12 = (f32[2,16,1024]{2,1,0:T(8,128)S(1)}, f32[2,16,1024]{2,1,0:T(8,128)S(1)}, u32[]{:S(2)}, u32[]{:S(2)}) collective-permute-start(f32[2,16,1024]{2,1,0:T(8,128)S(1)} %get-tuple-element.104), channel_id=1, source_target_pairs={{1,0},{2,1},{3,2},{4,3},{5,4},{6,5},{7,6},{9,8},{10,9},{11,10},{12... | collective-permute-start | bytes 393224 | tf_op jit(solution)/shard_map/ppermute | solution.py:517
  69.2 9.9 %collective-permute-start.14 = (f32[2,24,1024]{2,1,0:T(8,128)S(1)}, f32[2,24,1024]{2,1,0:T(8,128)S(1)}, u32[]{:S(2)}, u32[]{:S(2)}) collective-permute-start(f32[2,24,1024]{2,1,0:T(8,128)S(1)} %get-tuple-element.108), channel_id=1, source_target_pairs={{0,8},{1,9},{2,10},{3,11},{4,12},{5,13},{6,14},{7,15},{8,16},{9,17... | collective-permute-start | bytes 589832 | tf_op jit(solution)/shard_map/ppermute | solution.py:517
  72.3 6.8 %collective-permute-start.15 = (f32[2,16,1024]{2,1,0:T(8,128)S(1)}, f32[2,16,1024]{2,1,0:T(8,128)S(1)}, u32[]{:S(2)}, u32[]{:S(2)}) collective-permute-start(f32[2,16,1024]{2,1,0:T(8,128)S(1)} %get-tuple-element.109), channel_id=1, source_target_pairs={{0,1},{1,2},{2,3},{3,4},{4,5},{5,6},{6,7},{8,9},{9,10},{10,11},{11... | collective-permute-start | bytes 393224 | tf_op jit(solution)/shard_map/ppermute | solution.py:517
  86.3 27.1 %all-to-all-start.1 = ((f32[8,424,128]{2,1,0:T(8,128)}), f32[8,424,128]{2,1,0:T(8,128)}, u32[]{:S(2)}, u32[]{:S(2)}) async-start(f32[8,424,128]{2,1,0:T(8,128)} %get-tuple-element.118), calls=%async_computation.1 | async-start | bytes 3473408 | tf_op jit(solution)/shard_map/all_to_all | solution.py:659
  90.6 20.7 %collective-permute-start.16 = (f32[8,200,128]{2,1,0:T(8,128)}, f32[8,200,128]{2,1,0:T(8,128)S(1)}, u32[]{:S(2)}, u32[]{:S(2)}) collective-permute-start(f32[8,200,128]{2,1,0:T(8,128)} %get-tuple-element.117), channel_id=1, source_target_pairs={{0,8},{8,0},{16,24},{24,16},{1,9},{9,1},{17,25},{25,17},{2,10},{10... | collective-permute-start | bytes 2457608 | tf_op jit(solution)/shard_map/ppermute | solution.py:662
  113.4 23.5 %all-to-all-start = ((f32[8,360,128]{2,1,0:T(8,128)}), f32[8,360,128]{2,1,0:T(8,128)S(1)}, u32[]{:S(2)}, u32[]{:S(2)}) async-start(f32[8,360,128]{2,1,0:T(8,128)} %merge.1), calls=%async_computation | async-start | bytes 2949120 | tf_op jit(solution)/shard_map/all_to_all | solution.py:659
  117.0 21.5 %copy-start = (f32[384,128]{1,0:T(8,128)S(1)}, f32[384,128]{1,0:T(8,128)}, u32[]{:S(2)}) copy-start(f32[384,128]{1,0:T(8,128)} %enthalpy.1) | copy-start | bytes 589828
  119.1 7.3 %collective-permute-start.17 = (f32[384,128]{1,0:T(8,128)S(1)}, f32[384,128]{1,0:T(8,128)S(1)}, u32[]{:S(2)}, u32[]{:S(2)}) collective-permute-start(f32[384,128]{1,0:T(8,128)S(1)} %collect_odd.1), channel_id=1, source_target_pairs={{0,8},{8,0},{16,24},{24,16},{1,9},{9,1},{17,25},{25,17},{2,10},{10... | collective-permute-start | bytes 589832 | tf_op jit(solution)/shard_map/ppermute | solution.py:662
  126.4 12.1 %collective-permute-start.18 = (f32[384,128]{1,0:T(8,128)S(1)}, f32[384,128]{1,0:T(8,128)S(1)}, u32[]{:S(2)}, u32[]{:S(2)}) collective-permute-start(f32[384,128]{1,0:T(8,128)S(1)} %add.26), channel_id=1, source_target_pairs={{0,16},{8,24},{16,0},{24,8},{1,17},{9,25},{17,1},{25,9},{2,18},{10... | collective-permute-start | bytes 589832 | tf_op jit(solution)/shard_map/ppermute | solution.py:662

commit v15 on v14

--- a/solution.py
+++ b/solution.py
@@ -343,7 +343,7 @@
 
 
 def cut_of(cap):
-    return cap - cap // 6 // ROWS * ROWS
+    return cap - max(2 * ROWS, cap // 6 // (2 * ROWS) * (2 * ROWS))
 
 
 def table_rows(parts, cap):
@@ -401,6 +401,8 @@
             cap = caps[i]
             values = blocks[source, first[i] : first[i] + cap, :]
             high = values.astype(jnp.bfloat16)
+            if cap < per * LANES:
+                split[seat + cap : seat + per * LANES, :] = jnp.zeros((per * LANES - cap, 2 * pts), split.dtype)
             split[seat : seat + cap, 0:pts] = high
             split[seat : seat + cap, pts : 2 * pts] = (values - high.astype(F32)).astype(jnp.bfloat16)
     both = jnp.dot(chosen[...], split[...], preferred_element_type=F32)
@@ -419,7 +421,6 @@
         here = pl.ds(begin, size)
         copies.append(pltpu.make_async_copy(blocks.at[:, here], near.at[:, here], sems.at[i]))
         copies[i].start()
-    split[...] = jnp.zeros(split.shape, split.dtype)
     copies[0].wait()
     for i, (part, out) in enumerate(zip(parts, outs)):
         copies[1 + i].wait()
@@ -490,7 +491,6 @@
 
 def collect_mine_kernel(cap, blocks, out, chosen, split):
     per = -(-cap // LANES)
-    split[...] = jnp.zeros(split.shape, split.dtype)
     cut = cut_of(cap)
     nodes = [cut + cap + per, cut + cap]
     out[...] = summed(blocks, [0, cut], [cut, cap], nodes, chosen, split, out.shape[0])

time: 140 us -> 140 us (level)
  no operation moved by 1% of the time
where the time goes in v15:
time: 140 us; the launch traced here: 139 us
  waiting for transfers between devices  51.1 us (36%)
  starting transfers between devices  45.5 us (32%)
  Pallas kernels  41 us (29%)
    ppermute x16, starting transfers between devices, shifted(): return lax.ppermute(block, ('col', 'hgt'), route)  33.5 us
    pallas_call x23, Pallas kernels, kernel(): pl.pallas_call(body, out_shape=outs, in_specs=ins, out_specs=jax.tree.map...  31.8 us
    ppermute x3, waiting for transfers between devices, across(): return lax.ppermute(x, 'col', [(c, c ^ turn) for c in range(n_col)])  22.5 us
    ppermute x16, waiting for transfers between devices, shifted(): return lax.ppermute(block, ('col', 'hgt'), route)  20.2 us
    all_to_all x2, waiting for transfers between devices, swap(): return lax.all_to_all(x, axis, split_axis=0, concat_axis=0, tiled=True)  8.4 us
    all_to_all x2, starting transfers between devices, swap(): return lax.all_to_all(x, axis, split_axis=0, concat_axis=0, tiled=True)  7.9 us
    pallas_call x1, Pallas kernels, per_device(): pl.pallas_call(functools.partial(pack_kernel, heights), out_shape=(pltpu....  4.83 us
    ppermute x3, starting transfers between devices, across(): return lax.ppermute(x, 'col', [(c, c ^ turn) for c in range(n_col)])  4.08 us
  transfers between devices with their start and end apart: 21, of which 13 were waited for; matrix products, arithmetic and copies ran while one was open for 0% of the time, Pallas kernels for 22%

profile of v15, /device:TPU:0, one launch (start us, length us, event | category | flops | bytes accessed | tf_op | source)
XLA Modules:
  0.0 139.2 jit_solution(12635747475616579635)
XLA Ops:
  5.1 4.9 %load.1 = (f32[16,24,1024]{2,1,0:T(8,128)S(1)}, f32[16,24,1024]{2,1,0:T(8,128)S(1)}, f32[16,24,1024]{2,1,0:T(8,128)S(1)}, f32[3,16,24,1024]{3,2,1,0:T(8,128)S(1)...) custom-call(f32[16,24,1024]{2,1,0:T(8,128)} %temp_far.1, ...), custom_call_target="tpu_custom_call" | custom-call | flops 23592960 | bytes 23592960 | tf_op jit(solution)/shard_map/load/pallas_call | solution.py:540
  10.1 3.5 %collective-permute-done.1.col = f32[2,24,1024]{2,1,0:T(8,128)S(1)} collective-permute-done((f32[2,24,1024]{2,1,0:T(8,128)S(1)}, f32[2,24,1024]{2,1,0:T(8,128)S(1)}, u32[]{:S(2)}, u32[]{:S(2)}) %collective-permute-start.1) | collective-permute-done | bytes 196640 | tf_op jit(solution)/shard_map/ppermute | solution.py:517
  13.7 4.1 %collective-permute-start.3 = (f32[2,24,1024]{2,1,0:T(8,128)S(1)}, f32[2,24,1024]{2,1,0:T(8,128)S(1)}, u32[]{:S(2)}, u32[]{:S(2)}) collective-permute-start(f32[2,24,1024]{2,1,0:T(8,128)S(1)} %get-tuple-element.74), channel_id=1, source_target_pairs={{0,8},{1,9},{2,10},{3,11},{4,12},{5,13},{6,14},{7,15},{8,16},{9,17... | collective-permute-start | bytes 589832 | tf_op jit(solution)/shard_map/ppermute | solution.py:517
  25.1 2.2 %e_rest_0.1 = (f32[3,16,24,1024]{3,2,1,0:T(8,128)S(1)}, f32[16,24,1024]{2,1,0:T(8,128)S(1)}, f32[3,16,1024]{2,1,0:T(8,128)S(1)}) custom-call(f32[3,16,24,1024]{3,2,1,0:T(8,128)S(1)} %get-tuple-element.69.h.h_old, f32[16,24,1024]{2,1,0:T(8,128)S(1)} %get-tuple-element.70.ca, ...), custom_call_target="tpu_custom_call", output_to_operand_aliasing={{0}: (5, {}), {1}: (6, {})} | custom-call | flops 17694720 | bytes 17694720 | tf_op jit(solution)/shard_map/e_rest_0/pallas_call | solution.py:540
  27.9 4.7 %collective-permute-done.5.col = f32[2,24,1024]{2,1,0:T(8,128)S(1)} collective-permute-done((f32[2,24,1024]{2,1,0:T(8,128)S(1)}, f32[2,24,1024]{2,1,0:T(8,128)S(1)}, u32[]{:S(2)}, u32[]{:S(2)}) %collective-permute-start.5) | collective-permute-done | bytes 196640 | tf_op jit(solution)/shard_map/ppermute | solution.py:517
  32.7 3.5 %collective-permute-start.7 = (f32[2,24,1024]{2,1,0:T(8,128)S(1)}, f32[2,24,1024]{2,1,0:T(8,128)S(1)}, u32[]{:S(2)}, u32[]{:S(2)}) collective-permute-start(f32[2,24,1024]{2,1,0:T(8,128)S(1)} %get-tuple-element.86), channel_id=1, source_target_pairs={{0,8},{1,9},{2,10},{3,11},{4,12},{5,13},{6,14},{7,15},{8,16},{9,17... | collective-permute-start | bytes 589832 | tf_op jit(solution)/shard_map/ppermute | solution.py:517
  36.2 2.3 %collective-permute-start.6 = (f32[2,16,1024]{2,1,0:T(8,128)S(1)}, f32[2,16,1024]{2,1,0:T(8,128)S(1)}, u32[]{:S(2)}, u32[]{:S(2)}) collective-permute-start(f32[2,16,1024]{2,1,0:T(8,128)S(1)} %get-tuple-element.85.rows_old), channel_id=1, source_target_pairs={{0,1},{1,2},{2,3},{3,4},{4,5},{5,6},{6,7},{8,9},{9,10},{10,11},{11... | collective-permute-start | bytes 393224 | tf_op jit(solution)/shard_map/ppermute | solution.py:517
  43.9 2.3 %e_rest_1.1 = (f32[3,16,24,1024]{3,2,1,0:T(8,128)S(1)}, f32[16,24,1024]{2,1,0:T(8,128)S(1)}, f32[3,16,1024]{2,1,0:T(8,128)S(1)}) custom-call(f32[3,16,24,1024]{3,2,1,0:T(8,128)S(1)} %get-tuple-element.84.h.h_old, f32[16,24,1024]{2,1,0:T(8,128)S(1)} %get-tuple-element.70.ca, ...), custom_call_target="tpu_custom_call", output_to_operand_aliasing={{0}: (5, {}), {1}: (6, {})} | custom-call | flops 17694720 | bytes 17694720 | tf_op jit(solution)/shard_map/e_rest_1/pallas_call | solution.py:540
  46.2 4.4 %collective-permute-done.9.col = f32[2,24,1024]{2,1,0:T(8,128)S(1)} collective-permute-done((f32[2,24,1024]{2,1,0:T(8,128)S(1)}, f32[2,24,1024]{2,1,0:T(8,128)S(1)}, u32[]{:S(2)}, u32[]{:S(2)}) %collective-permute-start.9) | collective-permute-done | bytes 196640 | tf_op jit(solution)/shard_map/ppermute | solution.py:517
  50.7 3.6 %collective-permute-start.11 = (f32[2,24,1024]{2,1,0:T(8,128)S(1)}, f32[2,24,1024]{2,1,0:T(8,128)S(1)}, u32[]{:S(2)}, u32[]{:S(2)}) collective-permute-start(f32[2,24,1024]{2,1,0:T(8,128)S(1)} %get-tuple-element.98), channel_id=1, source_target_pairs={{0,8},{1,9},{2,10},{3,11},{4,12},{5,13},{6,14},{7,15},{8,16},{9,17... | collective-permute-start | bytes 589832 | tf_op jit(solution)/shard_map/ppermute | solution.py:517
  54.3 2.1 %collective-permute-start.10 = (f32[2,16,1024]{2,1,0:T(8,128)S(1)}, f32[2,16,1024]{2,1,0:T(8,128)S(1)}, u32[]{:S(2)}, u32[]{:S(2)}) collective-permute-start(f32[2,16,1024]{2,1,0:T(8,128)S(1)} %get-tuple-element.97.rows_old), channel_id=1, source_target_pairs={{0,1},{1,2},{2,3},{3,4},{4,5},{5,6},{6,7},{8,9},{9,10},{10,11},{11... | collective-permute-start | bytes 393224 | tf_op jit(solution)/shard_map/ppermute | solution.py:517
  61.9 2.3 %e_rest_2.1 = (f32[3,16,24,1024]{3,2,1,0:T(8,128)S(1)}, f32[16,24,1024]{2,1,0:T(8,128)S(1)}, f32[3,16,1024]{2,1,0:T(8,128)S(1)}) custom-call(f32[3,16,24,1024]{3,2,1,0:T(8,128)S(1)} %get-tuple-element.96.h.h_old, f32[16,24,1024]{2,1,0:T(8,128)S(1)} %get-tuple-element.70.ca, ...), custom_call_target="tpu_custom_call", output_to_operand_aliasing={{0}: (5, {}), {1}: (6, {})} | custom-call | flops 17694720 | bytes 17694720 | tf_op jit(solution)/shard_map/e_rest_2/pallas_call | solution.py:540
  64.4 4.7 %collective-permute-done.13.col = f32[2,24,1024]{2,1,0:T(8,128)S(1)} collective-permute-done((f32[2,24,1024]{2,1,0:T(8,128)S(1)}, f32[2,24,1024]{2,1,0:T(8,128)S(1)}, u32[]{:S(2)}, u32[]{:S(2)}) %collective-permute-start.13) | collective-permute-done | bytes 196640 | tf_op jit(solution)/shard_map/ppermute | solution.py:517
  69.2 3.1 %collective-permute-start.14 = (f32[2,24,1024]{2,1,0:T(8,128)S(1)}, f32[2,24,1024]{2,1,0:T(8,128)S(1)}, u32[]{:S(2)}, u32[]{:S(2)}) collective-permute-start(f32[2,24,1024]{2,1,0:T(8,128)S(1)} %get-tuple-element.108), channel_id=1, source_target_pairs={{0,8},{1,9},{2,10},{3,11},{4,12},{5,13},{6,14},{7,15},{8,16},{9,17... | collective-permute-start | bytes 589832 | tf_op jit(solution)/shard_map/ppermute | solution.py:517
  72.3 2.7 %collective-permute-start.15 = (f32[2,16,1024]{2,1,0:T(8,128)S(1)}, f32[2,16,1024]{2,1,0:T(8,128)S(1)}, u32[]{:S(2)}, u32[]{:S(2)}) collective-permute-start(f32[2,16,1024]{2,1,0:T(8,128)S(1)} %get-tuple-element.109), channel_id=1, source_target_pairs={{0,1},{1,2},{2,3},{3,4},{4,5},{5,6},{6,7},{8,9},{9,10},{10,11},{11... | collective-permute-start | bytes 393224 | tf_op jit(solution)/shard_map/ppermute | solution.py:517
  75.0 2.2 %places.1 = (s32[1,3072]{1,0:T(1,128)S(1)}, f32[6336,128]{1,0:T(8,128)S(1)}) custom-call(s32[1]{0:T(128)} %bitcast.my_col, s32[1,3072]{1,0:T(1,128)S(1)} %reshape.46.owner, s32[1,3072]{1,0:T(1,128)S(1)} %reshape.47.node), custom_call_target="tpu_custom_call" | custom-call | flops 3145728 | bytes 3145728 | tf_op jit(solution)/shard_map/places/pallas_call | solution.py:540
  79.1 2.3 %e_last.1 = (f32[3,16,24,1024]{3,2,1,0:T(8,128)S(1)}, f32[16,24,1024]{2,1,0:T(8,128)S(1)}, f32[3,16,24,1024]{3,2,1,0:T(8,128)}) custom-call(f32[3,16,24,1024]{3,2,1,0:T(8,128)S(1)} %h_rest_3.1.h, f32[16,24,1024]{2,1,0:T(8,128)S(1)} %get-tuple-element.70.ca, f32[16,24,1024]{2,1,0:T(8,128)S(1)} %get-tuple-element.71.cb, ...), custom_call_target="tpu_custom_call", output_to_operand_aliasing={{0}: (6, {}), {1}: (7, {})} | custom-call | flops 19660800 | bytes 19660800 | tf_op jit(solution)/shard_map/e_last/pallas_call | solution.py:606
  81.4 4.8 %pack.1 = (f32[8,200,128]{2,1,0:T(8,128)}, f32[8,424,128]{2,1,0:T(8,128)}, f32[3,16,24,1024]{3,2,1,0:T(8,128)}, f32[6336,128]{1,0:T(8,128)S(1)}) custom-call(s32[3072]{0:T(1024)S(1)} %bitcast.8, f32[16,24,1024]{2,1,0:T(8,128)S(1)} %get-tuple-element.111.power, f32[6336,128]{1,0:T(8,128)S(1)} %get-tuple-element.112.flat_old, ...), custom_call_target="tpu_custom_call", output_to_operand_aliasing={{3}: (2, {})} | custom-call | flops 393216 | bytes 14155776 | tf_op jit(solution)/shard_map/pack/pallas_call | solution.py:641
  86.3 4.3 %all-to-all-start.1 = ((f32[8,424,128]{2,1,0:T(8,128)}), f32[8,424,128]{2,1,0:T(8,128)}, u32[]{:S(2)}, u32[]{:S(2)}) async-start(f32[8,424,128]{2,1,0:T(8,128)} %get-tuple-element.118), calls=%async_computation.1 | async-start | bytes 3473408 | tf_op jit(solution)/shard_map/all_to_all | solution.py:659
  92.7 18.6 %collective-permute-done.16.pair = f32[8,200,128]{2,1,0:T(8,128)S(1)} collective-permute-done((f32[8,200,128]{2,1,0:T(8,128)}, f32[8,200,128]{2,1,0:T(8,128)S(1)}, u32[]{:S(2)}, u32[]{:S(2)}) %collective-permute-start.16) | collective-permute-done | bytes 819232 | tf_op jit(solution)/shard_map/ppermute | solution.py:662
  113.4 3.6 %all-to-all-start = ((f32[8,360,128]{2,1,0:T(8,128)}), f32[8,360,128]{2,1,0:T(8,128)S(1)}, u32[]{:S(2)}, u32[]{:S(2)}) async-start(f32[8,360,128]{2,1,0:T(8,128)} %merge.1), calls=%async_computation | async-start | bytes 2949120 | tf_op jit(solution)/shard_map/all_to_all | solution.py:659
  117.0 2.1 %collect_odd.1 = f32[384,128]{1,0:T(8,128)S(1)} custom-call(f32[8,424,128]{2,1,0:T(8,128)} %all-to-all-done.1.blocks), custom_call_target="tpu_custom_call" | custom-call | flops 3145728 | bytes 3145728 | tf_op jit(solution)/shard_map/collect_odd/pallas_call | solution.py:540
  122.5 3.9 %collective-permute-done.17.refs_1_ = f32[384,128]{1,0:T(8,128)S(1)} collective-permute-done((f32[384,128]{1,0:T(8,128)S(1)}, f32[384,128]{1,0:T(8,128)S(1)}, u32[]{:S(2)}, u32[]{:S(2)}) %collective-permute-start.17) | collective-permute-done | bytes 196640 | tf_op jit(solution)/shard_map/ppermute | solution.py:662
  129.5 7.4 %all-to-all-done.blocks = f32[8,360,128]{2,1,0:T(8,128)S(1)} async-done(((f32[8,360,128]{2,1,0:T(8,128)}), f32[8,360,128]{2,1,0:T(8,128)S(1)}, u32[]{:S(2)}, u32[]{:S(2)}) %all-to-all-start) | async-done | bytes 1474592 | tf_op jit(solution)/shard_map/all_to_all | solution.py:659
  (56 shorter events, 38.6 us)
Async XLA Ops:
  0.6 3.9 %copy-start.1 = (s32[1,1,16,24,8,1]{3,5,4,2,1,0:T(1,128)S(1)}, s32[1,1,16,24,8,1]{3,5,4,2,1,0:T(1,128)}, u32[]{:S(2)}) copy-start(s32[1,1,16,24,8,1]{3,5,4,2,1,0:T(1,128)} %param.11) | copy-start | bytes 36868
  0.6 4.2 %copy-start.2 = (s32[1,1,16,24,8]{3,4,2,1,0:T(8,128)S(1)}, s32[1,1,16,24,8]{3,4,2,1,0:T(8,128)}, u32[]{:S(2)}) copy-start(s32[1,1,16,24,8]{3,4,2,1,0:T(8,128)} %param.12) | copy-start | bytes 36868
  2.0 8.1 %collective-permute-start = (f32[2,16,1024]{2,1,0:T(8,128)S(1)}, f32[2,16,1024]{2,1,0:T(8,128)S(1)}, u32[]{:S(2)}, u32[]{:S(2)}) collective-permute-start(f32[2,16,1024]{2,1,0:T(8,128)S(1)} %get-tuple-element.63.rows_old), channel_id=1, source_target_pairs={{1,0},{2,1},{3,2},{4,3},{5,4},{6,5},{7,6},{9,8},{10,9},{11,10},{12... | collective-permute-start | bytes 393224 | tf_op jit(solution)/shard_map/ppermute | solution.py:517
  3.3 10.3 %collective-permute-start.1 = (f32[2,24,1024]{2,1,0:T(8,128)S(1)}, f32[2,24,1024]{2,1,0:T(8,128)S(1)}, u32[]{:S(2)}, u32[]{:S(2)}) collective-permute-start(f32[2,24,1024]{2,1,0:T(8,128)S(1)} %get-tuple-element.64), channel_id=1, source_target_pairs={{8,0},{9,1},{10,2},{11,3},{12,4},{13,5},{14,6},{15,7},{16,8},{17,9... | collective-permute-start | bytes 589832 | tf_op jit(solution)/shard_map/ppermute | solution.py:517
  13.7 8.5 %collective-permute-start.3 = (f32[2,24,1024]{2,1,0:T(8,128)S(1)}, f32[2,24,1024]{2,1,0:T(8,128)S(1)}, u32[]{:S(2)}, u32[]{:S(2)}) collective-permute-start(f32[2,24,1024]{2,1,0:T(8,128)S(1)} %get-tuple-element.74), channel_id=1, source_target_pairs={{0,8},{1,9},{2,10},{3,11},{4,12},{5,13},{6,14},{7,15},{8,16},{9,17... | collective-permute-start | bytes 589832 | tf_op jit(solution)/shard_map/ppermute | solution.py:517
  17.9 3.7 %collective-permute-start.2 = (f32[2,16,1024]{2,1,0:T(8,128)S(1)}, f32[2,16,1024]{2,1,0:T(8,128)S(1)}, u32[]{:S(2)}, u32[]{:S(2)}) collective-permute-start(f32[2,16,1024]{2,1,0:T(8,128)S(1)} %get-tuple-element.73.rows_old), channel_id=1, source_target_pairs={{0,1},{1,2},{2,3},{3,4},{4,5},{5,6},{6,7},{8,9},{9,10},{10,11},{11... | collective-permute-start | bytes 393224 | tf_op jit(solution)/shard_map/ppermute | solution.py:517
  22.5 10.1 %collective-permute-start.5 = (f32[2,24,1024]{2,1,0:T(8,128)S(1)}, f32[2,24,1024]{2,1,0:T(8,128)S(1)}, u32[]{:S(2)}, u32[]{:S(2)}) collective-permute-start(f32[2,24,1024]{2,1,0:T(8,128)S(1)} %get-tuple-element.81), channel_id=1, source_target_pairs={{8,0},{9,1},{10,2},{11,3},{12,4},{13,5},{14,6},{15,7},{16,8},{17,9... | collective-permute-start | bytes 589832 | tf_op jit(solution)/shard_map/ppermute | solution.py:517
  23.8 4.1 %collective-permute-start.4 = (f32[2,16,1024]{2,1,0:T(8,128)S(1)}, f32[2,16,1024]{2,1,0:T(8,128)S(1)}, u32[]{:S(2)}, u32[]{:S(2)}) collective-permute-start(f32[2,16,1024]{2,1,0:T(8,128)S(1)} %get-tuple-element.80.rows_old), channel_id=1, source_target_pairs={{1,0},{2,1},{3,2},{4,3},{5,4},{6,5},{7,6},{9,8},{10,9},{11,10},{12... | collective-permute-start | bytes 393224 | tf_op jit(solution)/shard_map/ppermute | solution.py:517
  32.7 8.4 %collective-permute-start.7 = (f32[2,24,1024]{2,1,0:T(8,128)S(1)}, f32[2,24,1024]{2,1,0:T(8,128)S(1)}, u32[]{:S(2)}, u32[]{:S(2)}) collective-permute-start(f32[2,24,1024]{2,1,0:T(8,128)S(1)} %get-tuple-element.86), channel_id=1, source_target_pairs={{0,8},{1,9},{2,10},{3,11},{4,12},{5,13},{6,14},{7,15},{8,16},{9,17... | collective-permute-start | bytes 589832 | tf_op jit(solution)/shard_map/ppermute | solution.py:517
  36.2 4.2 %collective-permute-start.6 = (f32[2,16,1024]{2,1,0:T(8,128)S(1)}, f32[2,16,1024]{2,1,0:T(8,128)S(1)}, u32[]{:S(2)}, u32[]{:S(2)}) collective-permute-start(f32[2,16,1024]{2,1,0:T(8,128)S(1)} %get-tuple-element.85.rows_old), channel_id=1, source_target_pairs={{0,1},{1,2},{2,3},{3,4},{4,5},{5,6},{6,7},{8,9},{9,10},{10,11},{11... | collective-permute-start | bytes 393224 | tf_op jit(solution)/shard_map/ppermute | solution.py:517
  41.3 9.3 %collective-permute-start.9 = (f32[2,24,1024]{2,1,0:T(8,128)S(1)}, f32[2,24,1024]{2,1,0:T(8,128)S(1)}, u32[]{:S(2)}, u32[]{:S(2)}) collective-permute-start(f32[2,24,1024]{2,1,0:T(8,128)S(1)} %get-tuple-element.93), channel_id=1, source_target_pairs={{8,0},{9,1},{10,2},{11,3},{12,4},{13,5},{14,6},{15,7},{16,8},{17,9... | collective-permute-start | bytes 589832 | tf_op jit(solution)/shard_map/ppermute | solution.py:517
  42.6 3.6 %collective-permute-start.8 = (f32[2,16,1024]{2,1,0:T(8,128)S(1)}, f32[2,16,1024]{2,1,0:T(8,128)S(1)}, u32[]{:S(2)}, u32[]{:S(2)}) collective-permute-start(f32[2,16,1024]{2,1,0:T(8,128)S(1)} %get-tuple-element.92.rows_old), channel_id=1, source_target_pairs={{1,0},{2,1},{3,2},{4,3},{5,4},{6,5},{7,6},{9,8},{10,9},{11,10},{12... | collective-permute-start | bytes 393224 | tf_op jit(solution)/shard_map/ppermute | solution.py:517
  50.7 8.4 %collective-permute-start.11 = (f32[2,24,1024]{2,1,0:T(8,128)S(1)}, f32[2,24,1024]{2,1,0:T(8,128)S(1)}, u32[]{:S(2)}, u32[]{:S(2)}) collective-permute-start(f32[2,24,1024]{2,1,0:T(8,128)S(1)} %get-tuple-element.98), channel_id=1, source_target_pairs={{0,8},{1,9},{2,10},{3,11},{4,12},{5,13},{6,14},{7,15},{8,16},{9,17... | collective-permute-start | bytes 589832 | tf_op jit(solution)/shard_map/ppermute | solution.py:517
  54.3 4.1 %collective-permute-start.10 = (f32[2,16,1024]{2,1,0:T(8,128)S(1)}, f32[2,16,1024]{2,1,0:T(8,128)S(1)}, u32[]{:S(2)}, u32[]{:S(2)}) collective-permute-start(f32[2,16,1024]{2,1,0:T(8,128)S(1)} %get-tuple-element.97.rows_old), channel_id=1, source_target_pairs={{0,1},{1,2},{2,3},{3,4},{4,5},{5,6},{6,7},{8,9},{9,10},{10,11},{11... | collective-permute-start | bytes 393224 | tf_op jit(solution)/shard_map/ppermute | solution.py:517
  59.3 9.8 %collective-permute-start.13 = (f32[2,24,1024]{2,1,0:T(8,128)S(1)}, f32[2,24,1024]{2,1,0:T(8,128)S(1)}, u32[]{:S(2)}, u32[]{:S(2)}) collective-permute-start(f32[2,24,1024]{2,1,0:T(8,128)S(1)} %get-tuple-element.105), channel_id=1, source_target_pairs={{8,0},{9,1},{10,2},{11,3},{12,4},{13,5},{14,6},{15,7},{16,8},{17,9... | collective-permute-start | bytes 589832 | tf_op jit(solution)/shard_map/ppermute | solution.py:517
  60.6 3.8 %collective-permute-start.12 = (f32[2,16,1024]{2,1,0:T(8,128)S(1)}, f32[2,16,1024]{2,1,0:T(8,128)S(1)}, u32[]{:S(2)}, u32[]{:S(2)}) collective-permute-start(f32[2,16,1024]{2,1,0:T(8,128)S(1)} %get-tuple-element.104), channel_id=1, source_target_pairs={{1,0},{2,1},{3,2},{4,3},{5,4},{6,5},{7,6},{9,8},{10,9},{11,10},{12... | collective-permute-start | bytes 393224 | tf_op jit(solution)/shard_map/ppermute | solution.py:517
  69.2 9.9 %collective-permute-start.14 = (f32[2,24,1024]{2,1,0:T(8,128)S(1)}, f32[2,24,1024]{2,1,0:T(8,128)S(1)}, u32[]{:S(2)}, u32[]{:S(2)}) collective-permute-start(f32[2,24,1024]{2,1,0:T(8,128)S(1)} %get-tuple-element.108), channel_id=1, source_target_pairs={{0,8},{1,9},{2,10},{3,11},{4,12},{5,13},{6,14},{7,15},{8,16},{9,17... | collective-permute-start | bytes 589832 | tf_op jit(solution)/shard_map/ppermute | solution.py:517
  72.3 6.8 %collective-permute-start.15 = (f32[2,16,1024]{2,1,0:T(8,128)S(1)}, f32[2,16,1024]{2,1,0:T(8,128)S(1)}, u32[]{:S(2)}, u32[]{:S(2)}) collective-permute-start(f32[2,16,1024]{2,1,0:T(8,128)S(1)} %get-tuple-element.109), channel_id=1, source_target_pairs={{0,1},{1,2},{2,3},{3,4},{4,5},{5,6},{6,7},{8,9},{9,10},{10,11},{11... | collective-permute-start | bytes 393224 | tf_op jit(solution)/shard_map/ppermute | solution.py:517
  86.3 27.1 %all-to-all-start.1 = ((f32[8,424,128]{2,1,0:T(8,128)}), f32[8,424,128]{2,1,0:T(8,128)}, u32[]{:S(2)}, u32[]{:S(2)}) async-start(f32[8,424,128]{2,1,0:T(8,128)} %get-tuple-element.118), calls=%async_computation.1 | async-start | bytes 3473408 | tf_op jit(solution)/shard_map/all_to_all | solution.py:659
  90.6 20.7 %collective-permute-start.16 = (f32[8,200,128]{2,1,0:T(8,128)}, f32[8,200,128]{2,1,0:T(8,128)S(1)}, u32[]{:S(2)}, u32[]{:S(2)}) collective-permute-start(f32[8,200,128]{2,1,0:T(8,128)} %get-tuple-element.117), channel_id=1, source_target_pairs={{0,8},{8,0},{16,24},{24,16},{1,9},{9,1},{17,25},{25,17},{2,10},{10... | collective-permute-start | bytes 2457608 | tf_op jit(solution)/shard_map/ppermute | solution.py:662
  113.4 23.5 %all-to-all-start = ((f32[8,360,128]{2,1,0:T(8,128)}), f32[8,360,128]{2,1,0:T(8,128)S(1)}, u32[]{:S(2)}, u32[]{:S(2)}) async-start(f32[8,360,128]{2,1,0:T(8,128)} %merge.1), calls=%async_computation | async-start | bytes 2949120 | tf_op jit(solution)/shard_map/all_to_all | solution.py:659
  117.0 21.5 %copy-start = (f32[384,128]{1,0:T(8,128)S(1)}, f32[384,128]{1,0:T(8,128)}, u32[]{:S(2)}) copy-start(f32[384,128]{1,0:T(8,128)} %enthalpy.1) | copy-start | bytes 589828
  119.1 7.3 %collective-permute-start.17 = (f32[384,128]{1,0:T(8,128)S(1)}, f32[384,128]{1,0:T(8,128)S(1)}, u32[]{:S(2)}, u32[]{:S(2)}) collective-permute-start(f32[384,128]{1,0:T(8,128)S(1)} %collect_odd.1), channel_id=1, source_target_pairs={{0,8},{8,0},{16,24},{24,16},{1,9},{9,1},{17,25},{25,17},{2,10},{10... | collective-permute-start | bytes 589832 | tf_op jit(solution)/shard_map/ppermute | solution.py:662
  126.4 12.0 %collective-permute-start.18 = (f32[384,128]{1,0:T(8,128)S(1)}, f32[384,128]{1,0:T(8,128)S(1)}, u32[]{:S(2)}, u32[]{:S(2)}) collective-permute-start(f32[384,128]{1,0:T(8,128)S(1)} %add.26), channel_id=1, source_target_pairs={{0,16},{8,24},{16,0},{24,8},{1,17},{9,25},{17,1},{25,9},{2,18},{10... | collective-permute-start | bytes 589832 | tf_op jit(solution)/shard_map/ppermute | solution.py:662
